TPU v7x, 32 devices: a whole 2x2x4 slice. The times are simulated.
32 devices in a mesh: groups: 2 (over y), leaf: 16 (over z, x, core).
Axes of the slice: x: 2, y: 2, z: 4, core: 2. Of those that a mesh axis runs over, the one named last changes fastest.
Arguments:
- right_side: float32 [64, 262144], P(None, ('groups', 'leaf')), parts along dimension 1
- scaling: float32 [262144], P(('groups', 'leaf')), parts along dimension 0, may hold values from 0.5 to 2
- embeddings: float32 [32, 262144], P(None, ('groups', 'leaf')), parts along dimension 1
- near_leaves: int32 [512, 3], P(('groups', 'leaf')), parts along dimension 0, may hold values from 0 to 255, as said below
- far_leaves: int32 [512, 8], P(('groups', 'leaf')), parts along dimension 0, may hold values from 0 to 255, as said below
- leaf_basis: bfloat16 [512, 64, 512], P(('groups', 'leaf')), parts along dimension 0, may hold values from -0.25 to 0.25
- leaf_coupling: bfloat16 [512, 8, 4096], P(('groups', 'leaf')), parts along dimension 0, may hold values from -0.25 to 0.25
- transfer: bfloat16 [512, 4096], P(('groups', 'leaf')), parts along dimension 0, may hold values from -0.25 to 0.25
- coarse_coupling: bfloat16 [4, 2, 4096], P('groups'), parts along dimension 0, may hold values from -0.5 to 0.5
Outputs:
- solution: float32 [64, 262144], P(None, ('groups', 'leaf')), parts along dimension 1
- residual: float32 [64, 262144], P(None, ('groups', 'leaf')), parts along dimension 1
There are 2 independent parts, one for each index of `groups`. A program takes and returns all parts, laid end to end along the dimension named above; each array names one. Nothing has to cross between parts.
Inputs may be any that keep to these rules, and one draw needn't show every extreme that they name: `near_leaves`: the first entry of a row is the leaf itself; the entries of a row are distinct and lie among the leaves of the owner's device and the 8 leaves on either side of them. `far_leaves`: the entries of a row are distinct leaves that lie on devices 2 to 4 places below or above the owner's device.
All inputs are finite; a program needn't handle non-finite values.
Results may differ from a plain program's by a relative error of at most 0.006.
Values may be sent and summed in bfloat16 or wider, within the bound.
No kernel may reach another device: no remote copies, remote signals or barrier semaphores. Data moves between devices by JAX's collectives and lax.ppermute only.
A program may use at most 128 MiB of HBM per device.

v0:
```python
import jax
import jax.numpy as jnp
from jax import lax
from jax.sharding import PartitionSpec as P

FARDEV = 4
CDEV = 8
ITERS = 2


KERNEL_SCALE = 0.0625
RIDGE_TERM = 1.0
EPSILON = 1e-06
HIGHEST = lax.Precision.HIGHEST


def extended(block, sides, width):
    for axis, dim in sides:
        count = lax.axis_size(axis)
        forward = [(i, i + 1) for i in range(count - 1)]
        backward = [(target, source) for source, target in forward]
        low = lax.ppermute(
            lax.slice_in_dim(block, block.shape[dim] - width, None, axis=dim), axis, forward
        )
        high = lax.ppermute(lax.slice_in_dim(block, 0, width, axis=dim), axis, backward)
        block = jnp.concatenate([low, block, high], axis=dim)
    return block


def passed_along(value, axis, steps):
    count = lax.axis_size(axis)
    first, last = (max(0, -steps), min(count, count - steps))
    return lax.ppermute(value, axis, [(source, source + steps) for source in range(first, last)])


def body(
    right_side,
    scaling,
    embeddings,
    near_leaves,
    far_leaves,
    leaf_basis,
    leaf_coupling,
    transfer,
    coarse_coupling,
):
    columns, local_points = right_side.shape
    per_device, rank_size, leaf_size = leaf_basis.shape
    features = embeddings.shape[0]
    device_count = lax.axis_size("leaf")
    position = lax.axis_index("leaf")
    margin_leaves = per_device // 2
    margin_points = margin_leaves * leaf_size
    window_leaves = per_device + 2 * margin_leaves
    near_index = near_leaves - (position * per_device - margin_leaves)
    far_index = far_leaves - (position - FARDEV) * per_device
    cluster = position // CDEV
    coarse_count = device_count // CDEV
    padded_points = extended(embeddings, (("leaf", 1),), margin_points)
    window_points = padded_points.reshape(features, window_leaves, leaf_size)
    chosen_points = jnp.take(window_points, near_index, axis=1)
    own_points = embeddings.reshape(features, per_device, leaf_size)
    own_square = jnp.sum(own_points * own_points, axis=0)
    chosen_square = jnp.sum(chosen_points * chosen_points, axis=0)
    crossed = jnp.einsum(
        "dip,disq->ispq",
        own_points,
        chosen_points,
        precision=HIGHEST,
        preferred_element_type=jnp.float32,
    )
    distance = own_square[:, None, :, None] + chosen_square[:, :, None, :] - 2.0 * crossed
    near_blocks = jnp.exp(-distance * KERNEL_SCALE).astype(jnp.bfloat16)
    basis_transfer = transfer.reshape(per_device, rank_size, rank_size)
    transfer_wide = basis_transfer.astype(jnp.float32)
    couplings = leaf_coupling.reshape(per_device, -1, rank_size, rank_size)
    coarse_row = lax.dynamic_index_in_dim(coarse_coupling, cluster, 0, keepdims=False)
    coarse_row = coarse_row.reshape(coarse_count, rank_size, rank_size).astype(jnp.float32)
    others = (jnp.arange(coarse_count) != cluster).astype(jnp.float32)
    coarse_row = coarse_row * others[:, None, None]
    solution = jnp.zeros_like(right_side)
    residual = right_side
    direction = right_side
    direction_image = right_side
    curvature = jnp.zeros((columns,), jnp.float32)
    aligned = jnp.zeros((columns,), jnp.float32)
    for iteration in range(ITERS):
        scaled = scaling[None, :] * residual
        rounded = scaled.astype(jnp.bfloat16)
        padded = extended(rounded, (("leaf", 1),), margin_points)
        chosen = jnp.take(padded.reshape(columns, window_leaves, leaf_size), near_index, axis=1)
        near_part = jnp.einsum(
            "ispq,nisq->nip", near_blocks, chosen, preferred_element_type=jnp.float32
        )
        leaf_values = rounded.reshape(columns, per_device, leaf_size)
        coefficients = jnp.einsum(
            "iap,nip->ian", leaf_basis, leaf_values, preferred_element_type=jnp.float32
        ).astype(jnp.bfloat16)
        below_list = [coefficients] * (FARDEV + 1)
        above_list = [coefficients] * (FARDEV + 1)
        moving = coefficients
        for spacing in range(1, FARDEV + 1):
            moving = passed_along(moving, "leaf", 1)
            below_list[spacing] = moving
        moving = coefficients
        for spacing in range(1, FARDEV + 1):
            moving = passed_along(moving, "leaf", -1)
            above_list[spacing] = moving
        pieces = [below_list[spacing] for spacing in range(FARDEV, 0, -1)] + [coefficients]
        pieces = pieces + [above_list[spacing] for spacing in range(1, FARDEV + 1)]
        window = jnp.concatenate(pieces, axis=0)
        picked = jnp.take(window, far_index.reshape(-1), axis=0).reshape(
            per_device, -1, rank_size, columns
        )
        coupled = jnp.einsum(
            "isab,isbn->ian", couplings, picked, preferred_element_type=jnp.float32
        )
        partial_value = jnp.einsum(
            "iab,ian->bn", basis_transfer, coefficients, preferred_element_type=jnp.float32
        )
        gathered = lax.all_gather(partial_value[None], "leaf", axis=0, tiled=True)
        member = (
            jnp.arange(device_count)[None, :] // CDEV == jnp.arange(coarse_count)[:, None]
        ).astype(jnp.float32)
        totals = jnp.einsum("cd,drn->crn", member, gathered, precision=HIGHEST)
        from_coarse = jnp.einsum("bxy,byn->xn", coarse_row, totals, precision=HIGHEST)
        combined = coupled + jnp.einsum(
            "iab,bn->ian", transfer_wide, from_coarse, precision=HIGHEST
        )
        far_part = jnp.einsum(
            "iap,ian->nip",
            leaf_basis,
            combined.astype(jnp.bfloat16),
            preferred_element_type=jnp.float32,
        )
        product_now = RIDGE_TERM * scaled + (near_part + far_part).reshape(columns, local_points)
        if iteration == 0:
            aligned, curvature = lax.psum(
                (
                    jnp.sum(residual * product_now, axis=1),
                    jnp.sum(product_now * product_now, axis=1),
                ),
                "leaf",
            )
            direction = scaled
            direction_image = product_now
        else:
            cross_term = lax.psum(jnp.sum(product_now * direction_image, axis=1), "leaf")
            beta_factor = -cross_term / (curvature + EPSILON)
            direction = scaled + beta_factor[:, None] * direction
            direction_image = product_now + beta_factor[:, None] * direction_image
            aligned, curvature = lax.psum(
                (
                    jnp.sum(residual * direction_image, axis=1),
                    jnp.sum(direction_image * direction_image, axis=1),
                ),
                "leaf",
            )
        step_size = aligned / (curvature + EPSILON)
        solution = solution + step_size[:, None] * direction
        residual = residual - step_size[:, None] * direction_image
    return (solution, residual)


def solution(mesh):
    return jax.shard_map(
        body,
        mesh=mesh,
        in_specs=(
            P(None, ("groups", "leaf")),
            P(("groups", "leaf")),
            P(None, ("groups", "leaf")),
            P(("groups", "leaf"), None),
            P(("groups", "leaf"), None),
            P(("groups", "leaf"), None, None),
            P(("groups", "leaf"), None, None),
            P(("groups", "leaf"), None),
            P("groups", None, None),
        ),
        out_specs=(P(None, ("groups", "leaf")), P(None, ("groups", "leaf"))),
        check_vma=False,
    )
```

profile of v0, /device:TPU:0, one launch (start us, length us, event | category | flops | bytes accessed | tf_op | source)
XLA Modules:
  0.0 390.9 jit_solution(15214140192127718205)
XLA Ops:
  10.5 5.9 %collective-permute-start.2 = (f32[32,4096]{1,0:T(8,128)}, f32[32,4096]{1,0:T(8,128)}, u32[]{:S(2)}, u32[]{:S(2)}) collective-permute-start(f32[32,4096]{1,0:T(8,128)} %get-tuple-element.24), channel_id=1, source_target_pairs={{0,1},{1,2},{2,3},{3,4},{4,5},{5,6},{6,7},{7,8},{8,9},{9,10},{10,1... | collective-permute-start | bytes 1572872 | tf_op jit(solution)/shard_map/ppermute | solution.py:22
  20.4 27.9 %all-gather = f32[1024,64]{1,0:T(8,128)} all-gather(f32[64,64]{1,0:T(8,128)S(1)} %copy.96), channel_id=2, replica_groups=mesh['groups'=2,'leaf'=16] {'leaf'}, dimensions={0}, use_global_device_ids=true | all-gather | bytes 278528 | tf_op jit(solution)/shard_map/all_gather | solution.py:121
  57.1 7.5 %collective-permute-start.6 = (bf16[16,64,64]{1,2,0:T(8,128)(2,1)S(1)}, bf16[16,64,64]{1,2,0:T(8,128)(2,1)}, u32[]{:S(2)}, u32[]{:S(2)}) collective-permute-start(bf16[16,64,64]{1,2,0:T(8,128)(2,1)S(1)} %collective-permute-done.5), channel_id=1, source_target_pairs={{0,1},{1,2},{2,3},{3,4},{4,5},{5,6},{6,7},{7,8},{8,9},{9,10},{10,1... | collective-permute-start | bytes 393224 | tf_op jit(solution)/shard_map/ppermute | solution.py:33
  66.1 6.1 %collective-permute-start.7 = (bf16[16,64,64]{1,2,0:T(8,128)(2,1)}, bf16[16,64,64]{1,2,0:T(8,128)(2,1)}, u32[]{:S(2)}, u32[]{:S(2)}) collective-permute-start(bf16[16,64,64]{1,2,0:T(8,128)(2,1)} %collective-permute-done.6), channel_id=1, source_target_pairs={{0,1},{1,2},{2,3},{3,4},{4,5},{5,6},{6,7},{7,8},{8,9},{9,10},{10,1... | collective-permute-start | bytes 393224 | tf_op jit(solution)/shard_map/ppermute | solution.py:33
  72.2 4.2 %reshape.119 = bf16[16,8,64,64]{3,2,1,0:T(8,128)(2,1)} reshape(bf16[16,8,4096]{2,1,0:T(8,128)(2,1)} %param.19) | data formatting | bytes 2097152 | tf_op jit(solution)/shard_map/reshape | solution.py:76
  78.8 3.8 collective-permute-start
  98.1 4.1 %gather_fusion.1 = bf16[48,64,512]{2,1,0:T(8,128)(2,1)} fusion(bf16[64,32,512]{2,0,1:T(8,128)(2,1)} %bitcast.143, s32[1024]{0:T(1024)S(1)} %pad_clamp_fusion.1), kind=kCustom, calls=%fused_computation.clone | custom fusion | bytes 6291648 | tf_op jit(solution)/shard_map/jit(_take)/gather | solution.py:91
  112.0 4.0 %fusion.29 = f32[16,64,512]{2,1,0:T(8,128)} fusion(bf16[16,64,512]{2,1,0:T(8,128)(2,1)S(1)} %copy-done, f32[16,64,64]{1,2,0:T(8,128)} %convolution_bitcast_fusion.3, bf16[16,8,64,64]{2,3,1,0:T(8,128)(2,1)} %bitcast.155, bf16[16,8,64,64]{3,2,1,0:T(8,128)(2,1)S(1)} %copy-done.5), kind=kOutput, calls=%fused_computation.61 | convolution fusion | flops 134348800 | bytes 5505024 | tf_op jit(solution)/shard_map/iap,ian->nip/dot_general | solution.py:130
  116.0 54.2 %fusion.3 = bf16[16,3,512,512]{2,3,1,0:T(8,128)(2,1)} fusion(f32[16,3,512]{2,1,0:T(4,128)} %fusion.7, f32[16,512]{1,0:T(8,128)S(1)} %add.98, f32[16,3,32,512]{3,2,1,0:T(8,128)} %bitcast.145, pred[16,3]{1,0:T(8,128)(4,1)S(1)} %copy.86, f32[32,16,512,1]{2,1,0,3:T(8,128)} %bitcast.158), kind=kOutput, calls=%fused_computation.9 | convolution fusion | flops 4908122112 | bytes 29491248 | tf_op jit(solution)/shard_map/dip,disq->ispq/dot_general | solution.py:65
  170.3 10.6 %fusion.16 = f32[16,8,8,512]{3,2,1,0:T(8,128)S(1)} fusion(f32[16,64,512]{2,1,0:T(8,128)S(1)} %copy-done.8, bf16[16,3,512,512]{2,3,1,0:T(8,128)(2,1)} %fusion.3, bf16[16,3,64,512]{3,2,1,0:T(8,128)(2,1)S(1)} %bitcast.138, pred[16,3]{1,0:T(8,128)(4,1)S(1)} %copy.86), kind=kOutput, calls=%fused_computation.31 | convolution fusion | flops 1612709888 | bytes 32505904 | tf_op jit(solution)/shard_map/ispq,nisq->nip/dot_general | solution.py:92
  183.2 31.7 %all-reduce.1 = (f32[64]{0:T(128)S(1)}, f32[64]{0:T(128)S(1)}) all-reduce(f32[64]{0:T(128)S(1)} %get-tuple-element.7, f32[64]{0:T(128)S(1)} %get-tuple-element.6), channel_id=1, replica_groups=mesh['groups'=2,'leaf'=16] {'leaf'}, use_global_device_ids=true, to_apply=%region_3.6 | all-reduce | flops 128 | bytes 1024 | tf_op jit(solution)/shard_map/psum | solution.py:138
  214.9 3.3 multiply_convert_fusion
  227.7 4.5 %collective-permute-start.12 = (bf16[64,4096]{1,0:T(8,128)(2,1)}, bf16[64,4096]{1,0:T(8,128)(2,1)}, u32[]{:S(2)}, u32[]{:S(2)}) collective-permute-start(bf16[64,4096]{1,0:T(8,128)(2,1)} %get-tuple-element.20), channel_id=1, source_target_pairs={{0,1},{1,2},{2,3},{3,4},{4,5},{5,6},{6,7},{7,8},{8,9},{9,10},{10,1... | collective-permute-start | bytes 1572872 | tf_op jit(solution)/shard_map/ppermute | solution.py:22
  232.2 20.7 %all-gather.1 = f32[1024,64]{1,0:T(8,128)S(1)} all-gather(f32[64,64]{1,0:T(8,128)S(1)} %copy.107), channel_id=3, replica_groups=mesh['groups'=2,'leaf'=16] {'leaf'}, dimensions={0}, use_global_device_ids=true | all-gather | bytes 278528 | tf_op jit(solution)/shard_map/all_gather | solution.py:121
  257.5 4.4 %collective-permute-start.16 = (bf16[16,64,64]{1,2,0:T(8,128)(2,1)S(1)}, bf16[16,64,64]{1,2,0:T(8,128)(2,1)S(1)}, u32[]{:S(2)}, u32[]{:S(2)}) collective-permute-start(bf16[16,64,64]{1,2,0:T(8,128)(2,1)S(1)} %collective-permute-done.15), channel_id=1, source_target_pairs={{0,1},{1,2},{2,3},{3,4},{4,5},{5,6},{6,7},{7,8},{8,9},{9,10},{10,1... | collective-permute-start | bytes 393224 | tf_op jit(solution)/shard_map/ppermute | solution.py:33
  264.3 5.3 %collective-permute-start.17 = (bf16[16,64,64]{1,2,0:T(8,128)(2,1)S(1)}, bf16[16,64,64]{1,2,0:T(8,128)(2,1)S(1)}, u32[]{:S(2)}, u32[]{:S(2)}) collective-permute-start(bf16[16,64,64]{1,2,0:T(8,128)(2,1)S(1)} %collective-permute-done.16), channel_id=1, source_target_pairs={{0,1},{1,2},{2,3},{3,4},{4,5},{5,6},{6,7},{7,8},{8,9},{9,10},{10,1... | collective-permute-start | bytes 393224 | tf_op jit(solution)/shard_map/ppermute | solution.py:33
  282.0 3.8 gather_fusion.4
  292.2 4.1 %gather_fusion.3 = bf16[48,64,512]{2,1,0:T(8,128)(2,1)} fusion(bf16[64,32,512]{2,0,1:T(8,128)(2,1)} %bitcast.144, s32[1024]{0:T(1024)S(1)} %pad_clamp_fusion.1), kind=kCustom, calls=%fused_computation.2.clone | custom fusion | bytes 6291648 | tf_op jit(solution)/shard_map/jit(_take)/gather | solution.py:91
  296.3 4.7 %fusion.30 = f32[16,64,512]{2,1,0:T(8,128)} fusion(bf16[16,64,512]{2,1,0:T(8,128)(2,1)S(1)} %copy-done, f32[16,64,64]{1,2,0:T(8,128)} %convolution_bitcast_fusion.2, bf16[16,8,64,64]{2,3,1,0:T(8,128)(2,1)} %bitcast.154, bf16[16,8,64,64]{3,2,1,0:T(8,128)(2,1)} %reshape.119), kind=kOutput, calls=%fused_computation.62 | convolution fusion | flops 134348800 | bytes 5505024 | tf_op jit(solution)/shard_map/iap,ian->nip/dot_general | solution.py:130
  301.0 14.1 %fusion.15 = f32[16,8,8,512]{3,2,1,0:T(8,128)S(1)} fusion(f32[16,64,512]{2,1,0:T(8,128)} %fusion.30, bf16[16,3,512,512]{2,3,1,0:T(8,128)(2,1)} %fusion.3, bf16[16,3,64,512]{3,2,1,0:T(8,128)(2,1)} %bitcast.139, pred[16,3]{1,0:T(8,128)(4,1)S(1)} %copy.86), kind=kOutput, calls=%fused_computation.29 | convolution fusion | flops 1612709888 | bytes 32505904 | tf_op jit(solution)/shard_map/ispq,nisq->nip/dot_general | solution.py:92
  318.0 33.6 %psum.37 = f32[64]{0:T(128)S(1)} all-reduce(f32[64]{0:T(128)S(1)} %multiply_reduce_fusion.2), channel_id=1, replica_groups=mesh['groups'=2,'leaf'=16] {'leaf'}, use_global_device_ids=true, to_apply=%region_7.10 | all-reduce | flops 64 | bytes 512 | tf_op jit(solution)/shard_map/psum | solution.py:148
  351.6 4.2 %multiply_reduce_fusion = (f32[64]{0:T(128)S(1)}, f32[64]{0:T(128)S(1)}, f32[64,8192]{1,0:T(8,128)}) fusion(f32[64,8192]{1,0:T(8,128)} %get-tuple-element.14, f32[64,8192]{1,0:T(8,128)S(1)} %get-tuple-element.15, f32[64]{0:T(128)S(1)} %negate_divide_fusion, f32[64,8192]{1,0:T(8,128)} %bitcast.141, f32[8192]{0:T(1024)S(1)} %copy-done.12), kind=kLoop, calls=%fused_computation.34 | loop fusion | flops 4194176 | bytes 8422144 | tf_op jit(solution)/shard_map/reduce_sum | solution.py:155
  355.9 29.5 %all-reduce = (f32[64]{0:T(128)S(1)}, f32[64]{0:T(128)S(1)}) all-reduce(f32[64]{0:T(128)S(1)} %get-tuple-element.5, f32[64]{0:T(128)S(1)} %get-tuple-element.4), channel_id=1, replica_groups=mesh['groups'=2,'leaf'=16] {'leaf'}, use_global_device_ids=true, to_apply=%region_9.12 | all-reduce | flops 128 | bytes 1024 | tf_op jit(solution)/shard_map/psum | solution.py:152
  385.4 5.5 %multiply_subtract_fusion = (f32[64,8192]{1,0:T(8,128)}, f32[64,8192]{1,0:T(8,128)}) fusion(f32[64,8192]{1,0:T(8,128)} %get-tuple-element.14, f32[64,8192]{1,0:T(8,128)} %get-tuple-element.12, f32[64]{0:T(128)S(1)} %add_divide_fusion, f32[64]{0:T(128)S(1)} %negate_divide_fusion, f32[64,8192]{1,0:T(8,128)} %param.13, f32[8192]{0:T(1024)S(1)} %copy-done.12, ...), kind=kLoop, calls=%fused_computation.32 | loop fusion | flops 4718592 | bytes 10519296 | tf_op jit(solution)/shard_map/sub | solution.py:161
  (160 shorter events, 91.7 us)
Async XLA Ops:
  3.6 49.3 %collective-permute-start.4 = (bf16[16,64,64]{1,2,0:T(8,128)(2,1)}, bf16[16,64,64]{1,2,0:T(8,128)(2,1)}, u32[]{:S(2)}, u32[]{:S(2)}) collective-permute-start(bf16[16,64,64]{1,2,0:T(8,128)(2,1)} %fusion.31), channel_id=1, source_target_pairs={{0,1},{1,2},{2,3},{3,4},{4,5},{5,6},{6,7},{7,8},{8,9},{9,10},{10,1... | collective-permute-start | bytes 393224 | tf_op jit(solution)/shard_map/ppermute | solution.py:33
  6.8 48.3 %collective-permute-start.8 = (bf16[16,64,64]{1,2,0:T(8,128)(2,1)}, bf16[16,64,64]{1,2,0:T(8,128)(2,1)}, u32[]{:S(2)}, u32[]{:S(2)}) collective-permute-start(bf16[16,64,64]{1,2,0:T(8,128)(2,1)} %fusion.31), channel_id=1, source_target_pairs={{1,0},{2,1},{3,2},{4,3},{5,4},{6,5},{7,6},{8,7},{9,8},{10,9},{11,1... | collective-permute-start | bytes 393224 | tf_op jit(solution)/shard_map/ppermute | solution.py:33
  9.2 75.8 %collective-permute-start.3 = (f32[32,4096]{1,0:T(8,128)}, f32[32,4096]{1,0:T(8,128)}, u32[]{:S(2)}, u32[]{:S(2)}) collective-permute-start(f32[32,4096]{1,0:T(8,128)} %get-tuple-element.25), channel_id=1, source_target_pairs={{1,0},{2,1},{3,2},{4,3},{5,4},{6,5},{7,6},{8,7},{9,8},{10,9},{11,1... | collective-permute-start | bytes 1572872 | tf_op jit(solution)/shard_map/ppermute | solution.py:25
  10.5 74.5 %collective-permute-start.2 = (f32[32,4096]{1,0:T(8,128)}, f32[32,4096]{1,0:T(8,128)}, u32[]{:S(2)}, u32[]{:S(2)}) collective-permute-start(f32[32,4096]{1,0:T(8,128)} %get-tuple-element.24), channel_id=1, source_target_pairs={{0,1},{1,2},{2,3},{3,4},{4,5},{5,6},{6,7},{7,8},{8,9},{9,10},{10,1... | collective-permute-start | bytes 1572872 | tf_op jit(solution)/shard_map/ppermute | solution.py:22
  17.4 73.0 %collective-permute-start.1 = (bf16[64,4096]{1,0:T(8,128)(2,1)}, bf16[64,4096]{1,0:T(8,128)(2,1)}, u32[]{:S(2)}, u32[]{:S(2)}) collective-permute-start(bf16[64,4096]{1,0:T(8,128)(2,1)} %get-tuple-element.23), channel_id=1, source_target_pairs={{1,0},{2,1},{3,2},{4,3},{5,4},{6,5},{7,6},{8,7},{9,8},{10,9},{11,1... | collective-permute-start | bytes 1572872 | tf_op jit(solution)/shard_map/ppermute | solution.py:25
  53.0 3.4 collective-permute-start.5
  55.1 9.6 %collective-permute-start.9 = (bf16[16,64,64]{1,2,0:T(8,128)(2,1)}, bf16[16,64,64]{1,2,0:T(8,128)(2,1)}, u32[]{:S(2)}, u32[]{:S(2)}) collective-permute-start(bf16[16,64,64]{1,2,0:T(8,128)(2,1)} %collective-permute-done.8), channel_id=1, source_target_pairs={{1,0},{2,1},{3,2},{4,3},{5,4},{6,5},{7,6},{8,7},{9,8},{10,9},{11,1... | collective-permute-start | bytes 393224 | tf_op jit(solution)/shard_map/ppermute | solution.py:33
  57.1 8.9 %collective-permute-start.6 = (bf16[16,64,64]{1,2,0:T(8,128)(2,1)S(1)}, bf16[16,64,64]{1,2,0:T(8,128)(2,1)}, u32[]{:S(2)}, u32[]{:S(2)}) collective-permute-start(bf16[16,64,64]{1,2,0:T(8,128)(2,1)S(1)} %collective-permute-done.5), channel_id=1, source_target_pairs={{0,1},{1,2},{2,3},{3,4},{4,5},{5,6},{6,7},{7,8},{8,9},{9,10},{10,1... | collective-permute-start | bytes 393224 | tf_op jit(solution)/shard_map/ppermute | solution.py:33
  64.7 14.1 %collective-permute-start.10 = (bf16[16,64,64]{1,2,0:T(8,128)(2,1)}, bf16[16,64,64]{1,2,0:T(8,128)(2,1)}, u32[]{:S(2)}, u32[]{:S(2)}) collective-permute-start(bf16[16,64,64]{1,2,0:T(8,128)(2,1)} %collective-permute-done.9), channel_id=1, source_target_pairs={{1,0},{2,1},{3,2},{4,3},{5,4},{6,5},{7,6},{8,7},{9,8},{10,9},{11,1... | collective-permute-start | bytes 393224 | tf_op jit(solution)/shard_map/ppermute | solution.py:33
  66.1 16.6 %collective-permute-start.7 = (bf16[16,64,64]{1,2,0:T(8,128)(2,1)}, bf16[16,64,64]{1,2,0:T(8,128)(2,1)}, u32[]{:S(2)}, u32[]{:S(2)}) collective-permute-start(bf16[16,64,64]{1,2,0:T(8,128)(2,1)} %collective-permute-done.6), channel_id=1, source_target_pairs={{0,1},{1,2},{2,3},{3,4},{4,5},{5,6},{6,7},{7,8},{8,9},{9,10},{10,1... | collective-permute-start | bytes 393224 | tf_op jit(solution)/shard_map/ppermute | solution.py:33
  78.8 11.6 %collective-permute-start = (bf16[64,4096]{1,0:T(8,128)(2,1)S(1)}, bf16[64,4096]{1,0:T(8,128)(2,1)S(1)}, u32[]{:S(2)}, u32[]{:S(2)}) collective-permute-start(bf16[64,4096]{1,0:T(8,128)(2,1)S(1)} %copy-done.13), channel_id=1, source_target_pairs={{0,1},{1,2},{2,3},{3,4},{4,5},{5,6},{6,7},{7,8},{8,9},{9,10},{10,1... | collective-permute-start | bytes 1572872 | tf_op jit(solution)/shard_map/ppermute | solution.py:22
  82.7 21.2 %collective-permute-start.11 = (bf16[16,64,64]{1,2,0:T(8,128)(2,1)}, bf16[16,64,64]{1,2,0:T(8,128)(2,1)}, u32[]{:S(2)}, u32[]{:S(2)}) collective-permute-start(bf16[16,64,64]{1,2,0:T(8,128)(2,1)} %collective-permute-done.10), channel_id=1, source_target_pairs={{1,0},{2,1},{3,2},{4,3},{5,4},{6,5},{7,6},{8,7},{9,8},{10,9},{11,1... | collective-permute-start | bytes 393224 | tf_op jit(solution)/shard_map/ppermute | solution.py:33
  116.0 54.2 %copy-start.3 = (bf16[48,64,512]{2,1,0:T(8,128)(2,1)S(1)}, bf16[48,64,512]{2,1,0:T(8,128)(2,1)}, u32[]{:S(2)}) copy-start(bf16[48,64,512]{2,1,0:T(8,128)(2,1)} %gather_fusion.1) | copy-start | bytes 9437188
  116.0 54.2 %copy-start.8 = (f32[16,64,512]{2,1,0:T(8,128)S(1)}, f32[16,64,512]{2,1,0:T(8,128)}, u32[]{:S(2)}) copy-start(f32[16,64,512]{2,1,0:T(8,128)} %fusion.29) | copy-start | bytes 6291460
  219.4 33.5 %collective-permute-start.14 = (bf16[16,64,64]{1,2,0:T(8,128)(2,1)}, bf16[16,64,64]{1,2,0:T(8,128)(2,1)}, u32[]{:S(2)}, u32[]{:S(2)}) collective-permute-start(bf16[16,64,64]{1,2,0:T(8,128)(2,1)} %fusion.32), channel_id=1, source_target_pairs={{0,1},{1,2},{2,3},{3,4},{4,5},{5,6},{6,7},{7,8},{8,9},{9,10},{10,1... | collective-permute-start | bytes 393224 | tf_op jit(solution)/shard_map/ppermute | solution.py:33
  221.4 34.8 %collective-permute-start.18 = (bf16[16,64,64]{1,2,0:T(8,128)(2,1)}, bf16[16,64,64]{1,2,0:T(8,128)(2,1)}, u32[]{:S(2)}, u32[]{:S(2)}) collective-permute-start(bf16[16,64,64]{1,2,0:T(8,128)(2,1)} %fusion.32), channel_id=1, source_target_pairs={{1,0},{2,1},{3,2},{4,3},{5,4},{6,5},{7,6},{8,7},{9,8},{10,9},{11,1... | collective-permute-start | bytes 393224 | tf_op jit(solution)/shard_map/ppermute | solution.py:33
  226.4 62.7 %collective-permute-start.13 = (bf16[64,4096]{1,0:T(8,128)(2,1)}, bf16[64,4096]{1,0:T(8,128)(2,1)}, u32[]{:S(2)}, u32[]{:S(2)}) collective-permute-start(bf16[64,4096]{1,0:T(8,128)(2,1)} %get-tuple-element.21), channel_id=1, source_target_pairs={{1,0},{2,1},{3,2},{4,3},{5,4},{6,5},{7,6},{8,7},{9,8},{10,9},{11,1... | collective-permute-start | bytes 1572872 | tf_op jit(solution)/shard_map/ppermute | solution.py:25
  227.7 61.4 %collective-permute-start.12 = (bf16[64,4096]{1,0:T(8,128)(2,1)}, bf16[64,4096]{1,0:T(8,128)(2,1)}, u32[]{:S(2)}, u32[]{:S(2)}) collective-permute-start(bf16[64,4096]{1,0:T(8,128)(2,1)} %get-tuple-element.20), channel_id=1, source_target_pairs={{0,1},{1,2},{2,3},{3,4},{4,5},{5,6},{6,7},{7,8},{8,9},{9,10},{10,1... | collective-permute-start | bytes 1572872 | tf_op jit(solution)/shard_map/ppermute | solution.py:22
  252.9 4.6 %collective-permute-start.15 = (bf16[16,64,64]{1,2,0:T(8,128)(2,1)}, bf16[16,64,64]{1,2,0:T(8,128)(2,1)S(1)}, u32[]{:S(2)}, u32[]{:S(2)}) collective-permute-start(bf16[16,64,64]{1,2,0:T(8,128)(2,1)} %collective-permute-done.14), channel_id=1, source_target_pairs={{0,1},{1,2},{2,3},{3,4},{4,5},{5,6},{6,7},{7,8},{8,9},{9,10},{10,1... | collective-permute-start | bytes 393224 | tf_op jit(solution)/shard_map/ppermute | solution.py:33
  256.2 6.7 %collective-permute-start.19 = (bf16[16,64,64]{1,2,0:T(8,128)(2,1)}, bf16[16,64,64]{1,2,0:T(8,128)(2,1)S(1)}, u32[]{:S(2)}, u32[]{:S(2)}) collective-permute-start(bf16[16,64,64]{1,2,0:T(8,128)(2,1)} %collective-permute-done.18), channel_id=1, source_target_pairs={{1,0},{2,1},{3,2},{4,3},{5,4},{6,5},{7,6},{8,7},{9,8},{10,9},{11,1... | collective-permute-start | bytes 393224 | tf_op jit(solution)/shard_map/ppermute | solution.py:33
  257.5 6.7 %collective-permute-start.16 = (bf16[16,64,64]{1,2,0:T(8,128)(2,1)S(1)}, bf16[16,64,64]{1,2,0:T(8,128)(2,1)S(1)}, u32[]{:S(2)}, u32[]{:S(2)}) collective-permute-start(bf16[16,64,64]{1,2,0:T(8,128)(2,1)S(1)} %collective-permute-done.15), channel_id=1, source_target_pairs={{0,1},{1,2},{2,3},{3,4},{4,5},{5,6},{6,7},{7,8},{8,9},{9,10},{10,1... | collective-permute-start | bytes 393224 | tf_op jit(solution)/shard_map/ppermute | solution.py:33
  263.0 8.3 %collective-permute-start.20 = (bf16[16,64,64]{1,2,0:T(8,128)(2,1)S(1)}, bf16[16,64,64]{1,2,0:T(8,128)(2,1)S(1)}, u32[]{:S(2)}, u32[]{:S(2)}) collective-permute-start(bf16[16,64,64]{1,2,0:T(8,128)(2,1)S(1)} %collective-permute-done.19), channel_id=1, source_target_pairs={{1,0},{2,1},{3,2},{4,3},{5,4},{6,5},{7,6},{8,7},{9,8},{10,9},{11,1... | collective-permute-start | bytes 393224 | tf_op jit(solution)/shard_map/ppermute | solution.py:33
  264.3 8.3 %collective-permute-start.17 = (bf16[16,64,64]{1,2,0:T(8,128)(2,1)S(1)}, bf16[16,64,64]{1,2,0:T(8,128)(2,1)S(1)}, u32[]{:S(2)}, u32[]{:S(2)}) collective-permute-start(bf16[16,64,64]{1,2,0:T(8,128)(2,1)S(1)} %collective-permute-done.16), channel_id=1, source_target_pairs={{0,1},{1,2},{2,3},{3,4},{4,5},{5,6},{6,7},{7,8},{8,9},{9,10},{10,1... | collective-permute-start | bytes 393224 | tf_op jit(solution)/shard_map/ppermute | solution.py:33
  271.2 10.1 %collective-permute-start.21 = (bf16[16,64,64]{1,2,0:T(8,128)(2,1)S(1)}, bf16[16,64,64]{1,2,0:T(8,128)(2,1)S(1)}, u32[]{:S(2)}, u32[]{:S(2)}) collective-permute-start(bf16[16,64,64]{1,2,0:T(8,128)(2,1)S(1)} %collective-permute-done.20), channel_id=1, source_target_pairs={{1,0},{2,1},{3,2},{4,3},{5,4},{6,5},{7,6},{8,7},{9,8},{10,9},{11,1... | collective-permute-start | bytes 393224 | tf_op jit(solution)/shard_map/ppermute | solution.py:33
  (24 other events, 276.6 us)
where the time goes:
time: 393 us; the launch traced here: 391 us
  blocking collectives  143 us (36%)
  matrix products  100 us (25%)
  starting transfers between devices  61.1 us (16%)
  local copies, waits for them, and re-layouts  57.6 us (15%)
  other arithmetic  27.1 us (7%)
    dot_general x1, matrix products, body(): jnp.einsum('dip,disq->ispq', own_points, chosen_points, precision=HIGHEST...  54.2 us
    all_gather x2, blocking collectives, body(): gathered = lax.all_gather(partial_value[None], 'leaf', axis=0, tiled=True)  48.6 us
    ppermute x16, starting transfers between devices, passed_along(): lax.ppermute(value, axis, [(source, source + steps) for source in range(f...  42.9 us
    psum x1, blocking collectives, body(): lax.psum(jnp.sum(product_now * direction_image, axis=1), 'leaf')  33.6 us
    psum x1, blocking collectives, body(): lax.psum((jnp.sum(residual * product_now, axis=1), jnp.sum(product_now *...  31.7 us
    psum x1, blocking collectives, body(): lax.psum((jnp.sum(residual * direction_image, axis=1), jnp.sum(direction_...  29.5 us
    dot_general x2, matrix products, body(): jnp.einsum('ispq,nisq->nip', near_blocks, chosen, preferred_element_type=...  24.7 us
    unnamed x69, local copies, waits for them, and re-layouts  24.5 us
  transfers between devices with their start and end apart: 22, of which 0 were waited for; matrix products, arithmetic and copies ran while one was open for 15% of the time, Pallas kernels for 0%

commit v1 on v0

v1 whole, which is shorter than its diff:
```python
import math

import jax
import jax.numpy as jnp
from jax import lax
from jax.experimental import pallas as pl
from jax.experimental.pallas import tpu as pltpu
from jax.sharding import PartitionSpec as P

FARDEV = 4
NEARDEV = 2
CDEV = 8
KERNEL_SCALE = 0.0625
RIDGE_TERM = 1.0
EPSILON = 1e-06
F32 = jnp.float32
BF16 = jnp.bfloat16
HALF_SCALE = math.sqrt(2.0 * KERNEL_SCALE * math.log2(math.e))
BLOCK = 2
VMEM_LIMIT = 56 * 1024 * 1024
FAR_SHIFTS = (-4, -3, -2, 2, 3, 4)


def shifted(value, steps):
    count = lax.axis_size("leaf")
    pairs = [(i, i + steps) for i in range(count) if 0 <= i + steps < count]
    return lax.ppermute(value, "leaf", pairs)


def swapped(value, mask):
    count = lax.axis_size("leaf")
    return lax.ppermute(value, "leaf", [(i, i ^ mask) for i in range(count)])


def dot(a, b, ca, cb):
    return lax.dot_general(a, b, (((ca,), (cb,)), ((), ())), preferred_element_type=F32)


def split3(value):
    high = value.astype(BF16)
    rest = value - high.astype(F32)
    mid = rest.astype(BF16)
    low = (rest - mid.astype(F32)).astype(BF16)
    return high, mid, low


def point_pieces(points):
    scaled = points * HALF_SCALE
    high, mid, low = split3(scaled)
    square = 0.5 * jnp.sum(scaled * scaled, axis=0, keepdims=True)
    s_high, s_mid, s_low = split3(square)
    return high, mid, low, s_high.astype(F32), s_mid.astype(F32), s_low.astype(F32)


def norm_rows(first, second, third, width, swap, sign):
    row = lax.broadcasted_iota(jnp.int32, (16, width), 0)
    base = 3 if swap else 0
    ones = 0 if swap else 3
    out = jnp.where((row >= ones) & (row < ones + 3), sign, 0.0)
    for at, piece in enumerate((first, second, third)):
        out = jnp.where(row == base + at, sign * piece, out)
    return out.astype(BF16)


def own_rows(points):
    high, mid, low, a, b, c = point_pieces(points)
    norms = norm_rows(a, b, c, points.shape[1], False, 1.0)
    return jnp.concatenate([high, mid, high, mid, low, high, norms], axis=0)


def other_rows(points):
    high, mid, low, a, b, c = point_pieces(points)
    norms = norm_rows(a, b, c, points.shape[1], True, -1.0)
    return jnp.concatenate([high, high, mid, mid, high, low, norms], axis=0)


def tile_of(other, own):
    return jnp.exp2(dot(other, own, 0, 0)).astype(BF16)


def pack_pair(block):
    half = block.shape[0] // 2
    return jnp.concatenate([block[:half], block[half:]], axis=1)


def leaf_coefficients(basis, rounded, trans):
    coef = dot(basis, rounded, 1, 1).astype(BF16)
    return pack_pair(coef), dot(trans, coef, 0, 0)


def prep_kernel(rs_ref, sc_ref, basis_ref, trans_ref, lo_ref, hi_ref, coef_ref, part_ref):
    step = pl.program_id(0)
    block, rank, leaf = basis_ref.shape
    half = lo_ref.shape[1] // leaf
    total = jnp.zeros(part_ref.shape, F32)
    for j in range(block):
        cols = slice(j * leaf, (j + 1) * leaf)
        rounded = (rs_ref[:, cols] * sc_ref[:, cols]).astype(BF16)
        packed, share = leaf_coefficients(basis_ref[j], rounded, trans_ref[j])
        coef_ref[j] = packed
        total += share
        at = step * block + j

        @pl.when(at < half)
        def _():
            lo_ref[:, pl.ds(pl.multiple_of(at * leaf, leaf), leaf)] = rounded

        @pl.when(at >= half)
        def _():
            hi_ref[:, pl.ds(pl.multiple_of((at - half) * leaf, leaf), leaf)] = rounded

    @pl.when(step == 0)
    def _():
        part_ref[...] = total

    @pl.when(step > 0)
    def _():
        part_ref[...] += total


def self_kernel(e_ref, tile_ref):
    leaf = tile_ref.shape[1]
    for j in range(tile_ref.shape[0]):
        points = e_ref[:, j * leaf : (j + 1) * leaf]
        tile_ref[j] = tile_of(other_rows(points), own_rows(points))


def load_windows(refs, vw, cw):
    vl, vo_lo, vo_hi, vh = refs[:4]
    leaf = vw.shape[2]
    for at in range(vw.shape[0]):
        src = (vl, vo_lo, vo_hi, vh)[at // (vw.shape[0] // 4)]
        place = at % (vw.shape[0] // 4)
        vw[at] = src[:, place * leaf : (place + 1) * leaf]
    for slot, ref in enumerate(refs[4:]):
        per = ref.shape[0]
        cw[slot * per : (slot + 1) * per] = ref[...]


def coarse_rows(coarse_ref, sums_ref, fc):
    acc = jnp.zeros(sums_ref.shape[1:], F32)
    for at in range(sums_ref.shape[0]):
        for piece in split3(sums_ref[at]):
            acc += dot(coarse_ref[at], piece, 1, 0)
    fc[...] = jnp.concatenate(split3(acc), axis=1)


def far_columns(j, l, pos, far_ref, cw, coup_ref, trans_ref, fc, basis_ref):
    per = cw.shape[0] // len(FAR_SHIFTS)
    rank = basis_ref.shape[1]
    picks = []
    for s in range(far_ref.shape[1]):
        leaf_id = far_ref[l, s]
        gap = leaf_id // per - pos
        slot = jnp.where(gap < 0, gap + 4, gap + 1)
        picks.append(cw[slot * per + leaf_id % per])
    wide = dot(coup_ref[j], jnp.concatenate(picks, axis=0), 1, 0)
    coupled = wide[:rank, :rank] + wide[rank:, rank:]
    moved = dot(trans_ref[j], fc[...], 1, 0)
    combined = coupled + moved[:, :rank] + moved[:, rank : 2 * rank] + moved[:, 2 * rank :]
    return dot(combined.astype(BF16), basis_ref[j], 0, 0)


def first_kernel(
    near_ref, far_ref, pos_ref,
    tself_ref, rs_ref, sc_ref, basis_ref, coup_ref, trans_ref, coarse_ref, sums_ref,
    el_ref, eo_ref, eh_ref, *rest,
):
    window_refs, rest = rest[:10], rest[10:]
    tile_ref, u_ref, lo_ref, hi_ref, coef_ref, part_ref, msg_ref = rest[:7]
    ew, vw, cw, fc, acc_uu, acc_ru = rest[7:]
    step = pl.program_id(0)
    steps = pl.num_programs(0)
    block, rank, leaf = basis_ref.shape
    half = lo_ref.shape[1] // leaf
    pos = pos_ref[0]

    @pl.when(step == 0)
    def _():
        load_windows(window_refs, vw, cw)
        for at in range(ew.shape[0]):
            quarter = ew.shape[0] // 4
            if at < quarter:
                ew[at] = el_ref[:, at * leaf : (at + 1) * leaf]
            elif at < 3 * quarter:
                ew[at] = eo_ref[:, (at - quarter) * leaf : (at - quarter + 1) * leaf]
            else:
                ew[at] = eh_ref[:, (at - 3 * quarter) * leaf : (at - 3 * quarter + 1) * leaf]
        coarse_rows(coarse_ref, sums_ref, fc)
        acc_uu[...] = jnp.zeros_like(acc_uu)
        acc_ru[...] = jnp.zeros_like(acc_ru)
        part_ref[...] = jnp.zeros_like(part_ref)

    base = pos * 2 * half - half
    for j in range(block):
        l = step * block + j
        cols = slice(j * leaf, (j + 1) * leaf)
        own = own_rows(ew[l + half])
        near = dot(vw[l + half], tself_ref[j], 1, 0)
        for s in range(1, near_ref.shape[1]):
            m = near_ref[l, s] - base
            tile = tile_of(other_rows(ew[m]), own)
            tile_ref[j, s - 1] = tile
            near += dot(vw[m], tile, 1, 0)
        far = far_columns(j, l, pos, far_ref, cw, coup_ref, trans_ref, fc, basis_ref)
        right = rs_ref[:, cols]
        scale = sc_ref[:, cols]
        image = RIDGE_TERM * (right * scale) + (near + far)
        u_ref[:, cols] = image
        acc_uu[...] += image * image
        acc_ru[...] += right * image
        rounded = (image * scale).astype(BF16)
        packed, share = leaf_coefficients(basis_ref[j], rounded, trans_ref[j])
        coef_ref[j] = packed
        part_ref[...] += share

        @pl.when(l < half)
        def _():
            lo_ref[:, pl.ds(pl.multiple_of(l * leaf, leaf), leaf)] = rounded

        @pl.when(l >= half)
        def _():
            hi_ref[:, pl.ds(pl.multiple_of((l - half) * leaf, leaf), leaf)] = rounded

    @pl.when(step == steps - 1)
    def _():
        lane = lax.broadcasted_iota(jnp.int32, msg_ref.shape, 1)
        out = jnp.where(lane == 0, jnp.sum(acc_uu[...], axis=1, keepdims=True), 0.0)
        out = jnp.where(lane == 1, jnp.sum(acc_ru[...], axis=1, keepdims=True), out)
        msg_ref[...] = out


def second_kernel(
    near_ref, far_ref, pos_ref,
    tself_ref, tile_ref, rs_ref, sc_ref, u_ref, basis_ref, coup_ref, trans_ref, coarse_ref,
    sums_ref, prev_ref, *rest,
):
    window_refs, rest = rest[:10], rest[10:]
    w_ref, msg_ref = rest[:2]
    vw, cw, fc, acc_uw, acc_ww, acc_rw = rest[2:]
    step = pl.program_id(0)
    steps = pl.num_programs(0)
    block, rank, leaf = basis_ref.shape
    half = vw.shape[0] // 4
    pos = pos_ref[0]

    @pl.when(step == 0)
    def _():
        load_windows(window_refs, vw, cw)
        coarse_rows(coarse_ref, sums_ref, fc)
        for acc in (acc_uw, acc_ww, acc_rw):
            acc[...] = jnp.zeros_like(acc)

    base = pos * 2 * half - half
    for j in range(block):
        l = step * block + j
        cols = slice(j * leaf, (j + 1) * leaf)
        near = dot(vw[l + half], tself_ref[j], 1, 0)
        for s in range(1, near_ref.shape[1]):
            near += dot(vw[near_ref[l, s] - base], tile_ref[j, s - 1], 1, 0)
        far = far_columns(j, l, pos, far_ref, cw, coup_ref, trans_ref, fc, basis_ref)
        image = u_ref[:, cols]
        second = RIDGE_TERM * (image * sc_ref[:, cols]) + (near + far)
        w_ref[:, cols] = second
        acc_uw[...] += image * second
        acc_ww[...] += second * second
        acc_rw[...] += rs_ref[:, cols] * second

    @pl.when(step == steps - 1)
    def _():
        lane = lax.broadcasted_iota(jnp.int32, msg_ref.shape, 1)
        out = prev_ref[...]
        for at, acc in enumerate((acc_uw, acc_ww, acc_rw)):
            out = jnp.where(lane == 2 + at, jnp.sum(acc[...], axis=1, keepdims=True), out)
        msg_ref[...] = out


def whole(shape):
    return pl.BlockSpec(shape, lambda i, *_: (0,) * len(shape))


def column_block(rows, width):
    return pl.BlockSpec((rows, width), lambda i, *_: (0, i))


def lead_block(shape):
    return pl.BlockSpec(shape, lambda i, *_: (i,) + (0,) * (len(shape) - 1))


def cluster_exchange(part):
    count = lax.axis_size("leaf")
    mask = 1
    while mask < CDEV:
        part = part + swapped(part, mask)
        mask *= 2
    sums = part[None]
    while mask < count:
        sums = jnp.concatenate([sums, swapped(sums, mask)], axis=0)
        mask *= 2
    return sums[1:]


def exchange(lo, hi, coef, part):
    coefs = [shifted(coef, -gap) for gap in FAR_SHIFTS]
    sums = cluster_exchange(part)
    below = shifted(hi, 1)
    above = shifted(lo, -1)
    return [below, lo, hi, above] + coefs, sums


def body(
    right_side, scaling, embeddings, near_leaves, far_leaves, leaf_basis, leaf_coupling,
    transfer, coarse_coupling,
):
    columns, local_points = right_side.shape
    per, rank, leaf = leaf_basis.shape
    features = embeddings.shape[0]
    near_count = near_leaves.shape[1]
    far_count = far_leaves.shape[1]
    half = per // 2
    margin = half * leaf
    steps = per // BLOCK
    width = BLOCK * leaf
    count = lax.axis_size("leaf")
    pos = lax.axis_index("leaf")
    position = pos.reshape(1).astype(jnp.int32)
    cluster = pos // CDEV
    coarse_count = count // CDEV
    scale_row = scaling.reshape(1, local_points)
    trans = transfer.reshape(per, rank, rank)
    coup = leaf_coupling.reshape(per, far_count, rank, 2, rank // 2)
    coup = coup.transpose(0, 3, 2, 1, 4).reshape(per, 2 * rank, far_count * rank // 2)
    row = lax.dynamic_index_in_dim(coarse_coupling, cluster, 0, keepdims=False)
    order = jnp.arange(1, coarse_count, dtype=jnp.int32) ^ cluster
    coarse = jnp.take(row, order, axis=0).reshape(coarse_count - 1, rank, rank)
    params = pltpu.CompilerParams(vmem_limit_bytes=VMEM_LIMIT)

    e_below = shifted(embeddings[:, local_points - margin :], 1)
    e_above = shifted(embeddings[:, :margin], -1)

    half_shape = jax.ShapeDtypeStruct((columns, margin), BF16)
    coef_shape = jax.ShapeDtypeStruct((per, rank // 2, 2 * columns), BF16)
    part_shape = jax.ShapeDtypeStruct((rank, columns), F32)
    msg_shape = jax.ShapeDtypeStruct((columns, 128), F32)
    block_specs = dict(
        rs=column_block(columns, width), sc=column_block(1, width),
        basis=lead_block((BLOCK, rank, leaf)),
        coup=lead_block((BLOCK,) + coup.shape[1:]),
        trans=lead_block((BLOCK, rank, rank)),
        coef=lead_block((BLOCK, rank // 2, 2 * columns)),
        tself=lead_block((BLOCK, leaf, leaf)),
        tile=lead_block((BLOCK, near_count - 1, leaf, leaf)),
    )
    lo, hi, coef, part = pl.pallas_call(
        prep_kernel,
        grid=(per // 4,),
        in_specs=[
            column_block(columns, 4 * leaf), column_block(1, 4 * leaf),
            lead_block((4, rank, leaf)), lead_block((4, rank, rank)),
        ],
        out_specs=[
            whole((columns, margin)), whole((columns, margin)),
            lead_block((4, rank // 2, 2 * columns)), whole((rank, columns)),
        ],
        out_shape=[half_shape, half_shape, coef_shape, part_shape],
        compiler_params=params,
        name="prep",
    )(right_side, scale_row, leaf_basis, trans)

    windows, sums = exchange(lo, hi, coef, part)

    tself = pl.pallas_call(
        self_kernel,
        grid=(steps,),
        in_specs=[column_block(features, width)],
        out_specs=block_specs["tself"],
        out_shape=jax.ShapeDtypeStruct((per, leaf, leaf), BF16),
        compiler_params=params,
        cost_estimate=pl.CostEstimate(
            flops=2 * per * leaf * leaf * 256, bytes_accessed=per * leaf * leaf * 2,
            transcendentals=per * leaf * leaf,
        ),
        name="self_tiles",
    )(embeddings)

    vw_shape = pltpu.VMEM((4 * half, columns, leaf), BF16)
    cw_shape = pltpu.VMEM((len(FAR_SHIFTS) * per, rank // 2, 2 * columns), BF16)
    fc_shape = pltpu.VMEM((rank, 3 * columns), BF16)
    acc_shape = pltpu.VMEM((columns, leaf), F32)
    window_specs = [whole((columns, margin))] * 4
    window_specs += [whole(coef_shape.shape)] * len(FAR_SHIFTS)
    tiles, image, lo, hi, coef, part, msg = pl.pallas_call(
        first_kernel,
        grid_spec=pltpu.PrefetchScalarGridSpec(
            num_scalar_prefetch=3,
            grid=(steps,),
            in_specs=[
                block_specs["tself"], block_specs["rs"], block_specs["sc"], block_specs["basis"],
                block_specs["coup"], block_specs["trans"], whole(coarse.shape), whole(sums.shape),
                whole((features, margin)), whole(embeddings.shape), whole((features, margin)),
            ] + window_specs,
            out_specs=[
                block_specs["tile"], block_specs["rs"], whole((columns, margin)),
                whole((columns, margin)), block_specs["coef"], whole((rank, columns)),
                whole((columns, 128)),
            ],
            scratch_shapes=[
                pltpu.VMEM((4 * half, features, leaf), F32), vw_shape, cw_shape, fc_shape,
                acc_shape, acc_shape,
            ],
        ),
        out_shape=[
            jax.ShapeDtypeStruct((per, near_count - 1, leaf, leaf), BF16),
            jax.ShapeDtypeStruct(right_side.shape, F32),
            half_shape, half_shape, coef_shape, part_shape, msg_shape,
        ],
        compiler_params=params,
        name="first_product",
    )(
        near_leaves, far_leaves, position, tself, right_side, scale_row, leaf_basis, coup, trans,
        coarse, sums, e_below, embeddings, e_above, *windows,
    )

    windows, sums = exchange(lo, hi, coef, part)

    second, msg = pl.pallas_call(
        second_kernel,
        grid_spec=pltpu.PrefetchScalarGridSpec(
            num_scalar_prefetch=3,
            grid=(steps,),
            in_specs=[
                block_specs["tself"], block_specs["tile"], block_specs["rs"], block_specs["sc"],
                block_specs["rs"], block_specs["basis"], block_specs["coup"], block_specs["trans"],
                whole(coarse.shape), whole(sums.shape), whole((columns, 128)),
            ] + window_specs,
            out_specs=[block_specs["rs"], whole((columns, 128))],
            scratch_shapes=[vw_shape, cw_shape, fc_shape, acc_shape, acc_shape, acc_shape],
        ),
        out_shape=[jax.ShapeDtypeStruct(right_side.shape, F32), msg_shape],
        compiler_params=params,
        name="second_product",
    )(
        near_leaves, far_leaves, position, tself, tiles, right_side, scale_row, image, leaf_basis,
        coup, trans, coarse, sums, msg, *windows,
    )

    mask = 1
    while mask < count:
        msg = msg + swapped(msg, mask)
        mask *= 2
    uu, ru, uw, ww, rw = [msg[:, k : k + 1] for k in range(5)]
    step_one = ru / (uu + EPSILON)
    beta = -(uu - step_one * uw) / (uu + EPSILON)
    lead = 1.0 + beta
    curvature = lead * lead * uu - 2.0 * lead * step_one * uw + step_one * step_one * ww
    aligned = lead * (ru - step_one * uu) - step_one * (rw - step_one * uw)
    step_two = aligned / (curvature + EPSILON)
    first_weight = step_one + step_two * lead
    second_weight = step_two * step_one
    solution = scale_row * (first_weight * right_side - second_weight * image)
    residual = right_side - first_weight * image + second_weight * second
    return (solution, residual)


def solution(mesh):
    return jax.shard_map(
        body,
        mesh=mesh,
        in_specs=(
            P(None, ("groups", "leaf")),
            P(("groups", "leaf")),
            P(None, ("groups", "leaf")),
            P(("groups", "leaf"), None),
            P(("groups", "leaf"), None),
            P(("groups", "leaf"), None, None),
            P(("groups", "leaf"), None, None),
            P(("groups", "leaf"), None),
            P("groups", None, None),
        ),
        out_specs=(P(None, ("groups", "leaf")), P(None, ("groups", "leaf"))),
        check_vma=False,
    )
```

time: 393 us -> 207 us (0.53)
  blocking collectives: 143 us -> 0 us
  matrix products: 100 us -> 0 us
  Pallas kernels: 0 us -> 65.4 us
  waiting for transfers between devices: 0.07 us -> 39.2 us
  local copies, waits for them, and re-layouts: 57.6 us -> 23.1 us
  other arithmetic: 27.1 us -> 6.84 us
  starting transfers between devices: 61.1 us -> 70.1 us
    dot_general x15 -> x0, matrix products: 100 us -> none  [the longest x1 54.2 us: body(): jnp.einsum('dip,disq->ispq', own_points, chosen_points, precision=HIGHEST...]
    psum x3 -> x0, blocking collectives: 94.8 us -> none  [the longest x1 33.6 us: body(): lax.psum(jnp.sum(product_now * direction_image, axis=1), 'leaf')]
    pallas_call x0 -> x4, Pallas kernels: none -> 65.4 us  [the longest x1 31.3 us: body(): pl.pallas_call(first_kernel, grid_spec=pltpu.PrefetchScalarGridSpec(num_s...]
    all_gather x2 -> x0, blocking collectives: 48.6 us -> none  [body(): gathered = lax.all_gather(partial_value[None], 'leaf', axis=0, tiled=True)]
    ppermute x22 -> x30, waiting for transfers between devices: 0.07 us -> 39.2 us  [the longest x12 27.2 us: swapped(): return lax.ppermute(value, 'leaf', [(i, i ^ mask) for i in range(count)])]
    unnamed x69 -> x48, local copies, waits for them, and re-layouts: 24.5 us -> 2.97 us
    gather x5 -> x0, local copies, waits for them, and re-layouts: 17.1 us -> none  [the longest x2 8.25 us: body(): jnp.take(padded.reshape(columns, window_leaves, leaf_size), near_index, a...]
    transpose x0 -> x1, local copies, waits for them, and re-layouts: none -> 9.72 us  [body(): coup.transpose(0, 3, 2, 1, 4).reshape(per, 2 * rank, far_count * rank // 2)]
  transfers between devices with their start and end apart: 22 -> 30, of which waited for: 0 -> 14; matrix products, arithmetic and copies ran while one was open for 15% -> 10% of each run, Pallas kernels for 0% -> 4%
where the time goes in v1:
time: 207 us; the launch traced here: 206 us
  starting transfers between devices  70.1 us (34%)
  Pallas kernels  65.4 us (32%)
  waiting for transfers between devices  39.2 us (19%)
  local copies, waits for them, and re-layouts  23.1 us (11%)
  other arithmetic  6.84 us (3%)
    ppermute x18, starting transfers between devices, shifted(): return lax.ppermute(value, 'leaf', pairs)  48.1 us
    pallas_call x1, Pallas kernels, body(): pl.pallas_call(first_kernel, grid_spec=pltpu.PrefetchScalarGridSpec(num_s...  31.3 us
    ppermute x12, waiting for transfers between devices, swapped(): return lax.ppermute(value, 'leaf', [(i, i ^ mask) for i in range(count)])  27.2 us
    ppermute x12, starting transfers between devices, swapped(): return lax.ppermute(value, 'leaf', [(i, i ^ mask) for i in range(count)])  22.1 us
    pallas_call x1, Pallas kernels, body(): pl.pallas_call(second_kernel, grid_spec=pltpu.PrefetchScalarGridSpec(num_...  19.5 us
    ppermute x18, waiting for transfers between devices, shifted(): return lax.ppermute(value, 'leaf', pairs)  12 us
    transpose x1, local copies, waits for them, and re-layouts, body(): coup.transpose(0, 3, 2, 1, 4).reshape(per, 2 * rank, far_count * rank // 2)  9.72 us
    pallas_call x1, Pallas kernels, body(): pl.pallas_call(self_kernel, grid=(steps,), in_specs=[column_block(feature...  8.2 us
  transfers between devices with their start and end apart: 30, of which 14 were waited for; matrix products, arithmetic and copies ran while one was open for 10% of the time, Pallas kernels for 4%

profile of v1, /device:TPU:0, one launch (start us, length us, event | category | flops | bytes accessed | tf_op | source)
XLA Modules:
  0.0 205.7 jit_solution(6546419092276306547)
XLA Ops:
  2.6 6.3 %prep.1 = (bf16[64,4096]{1,0:T(8,128)(2,1)}, bf16[64,4096]{1,0:T(8,128)(2,1)}, bf16[16,32,128]{2,1,0:T(8,128)(2,1)}, f32[64,64]{1,0:T(8,128)}) custom-call(f32[64,8192]{1,0:T(8,128)} %rs_ref.5, f32[1,8192]{1,0:T(1,128)} %bitcast.13, bf16[16,64,512]{2,1,0:T(8,128)(2,1)} %basis_ref.5, bf16[16,64,64]{2,1,0:T(8,128)(2,1)} %reshape.45.trans_ref), custom_call_target="tpu_custom_call" | custom-call | tf_op jit(solution)/shard_map/prep/pallas_call | solution.py:354
  11.4 2.8 %collective-permute-start.1 = (f32[64,64]{1,0:T(8,128)S(1)}, f32[64,64]{1,0:T(8,128)S(1)}, u32[]{:S(2)}, u32[]{:S(2)}) collective-permute-start(f32[64,64]{1,0:T(8,128)S(1)} %add.63), channel_id=1, source_target_pairs={{0,2},{1,3},{2,0},{3,1},{4,6},{5,7},{6,4},{7,5},{8,10},{9,11},{10,... | collective-permute-start | bytes 49160 | tf_op jit(solution)/shard_map/ppermute | solution.py:32
  22.1 6.4 %collective-permute-start.3 = (f32[1,64,64]{2,1,0:T(8,128)S(1)}, f32[1,64,64]{2,1,0:T(8,128)S(1)}, u32[]{:S(2)}, u32[]{:S(2)}) collective-permute-start(f32[1,64,64]{2,1,0:T(8,128)S(1)} %add_bitcast_fusion.1), channel_id=1, source_target_pairs={{0,8},{1,9},{2,10},{3,11},{4,12},{5,13},{6,14},{7,15},{8,0},{9,1},... | collective-permute-start | bytes 49160 | tf_op jit(solution)/shard_map/ppermute | solution.py:32
  30.8 2.5 %collective-permute-done.3.sums_ref = f32[1,64,64]{2,1,0:T(8,128)S(1)} collective-permute-done((f32[1,64,64]{2,1,0:T(8,128)S(1)}, f32[1,64,64]{2,1,0:T(8,128)S(1)}, u32[]{:S(2)}, u32[]{:S(2)}) %collective-permute-start.3) | collective-permute-done | bytes 16416 | tf_op jit(solution)/shard_map/ppermute | solution.py:32
  33.3 2.5 %collective-permute-start.4 = (f32[32,4096]{1,0:T(8,128)}, f32[32,4096]{1,0:T(8,128)}, u32[]{:S(2)}, u32[]{:S(2)}) collective-permute-start(f32[32,4096]{1,0:T(8,128)} %get-tuple-element.44), channel_id=1, source_target_pairs={{0,1},{1,2},{2,3},{3,4},{4,5},{5,6},{6,7},{7,8},{8,9},{9,10},{10,1... | collective-permute-start | bytes 1572872 | tf_op jit(solution)/shard_map/ppermute | solution.py:27
  39.3 4.7 %collective-permute-start.10 = (bf16[16,32,128]{2,1,0:T(8,128)(2,1)}, bf16[16,32,128]{2,1,0:T(8,128)(2,1)S(1)}, u32[]{:S(2)}, u32[]{:S(2)}) collective-permute-start(bf16[16,32,128]{2,1,0:T(8,128)(2,1)} %get-tuple-element.18), channel_id=1, source_target_pairs={{0,2},{1,3},{2,4},{3,5},{4,6},{5,7},{6,8},{7,9},{8,10},{9,11},{10,... | collective-permute-start | bytes 393224 | tf_op jit(solution)/shard_map/ppermute | solution.py:27
  44.0 8.5 %collective-permute-done.10.rest_6_ = bf16[16,32,128]{2,1,0:T(8,128)(2,1)S(1)} collective-permute-done((bf16[16,32,128]{2,1,0:T(8,128)(2,1)}, bf16[16,32,128]{2,1,0:T(8,128)(2,1)S(1)}, u32[]{:S(2)}, u32[]{:S(2)}) %collective-permute-start.10) | collective-permute-done | bytes 131104 | tf_op jit(solution)/shard_map/ppermute | solution.py:27
  52.5 12.0 %collective-permute-start.9 = (bf16[16,32,128]{2,1,0:T(8,128)(2,1)}, bf16[16,32,128]{2,1,0:T(8,128)(2,1)}, u32[]{:S(2)}, u32[]{:S(2)}) collective-permute-start(bf16[16,32,128]{2,1,0:T(8,128)(2,1)} %get-tuple-element.18), channel_id=1, source_target_pairs={{0,3},{1,4},{2,5},{3,6},{4,7},{5,8},{6,9},{7,10},{8,11},{9,12},{10... | collective-permute-start | bytes 393224 | tf_op jit(solution)/shard_map/ppermute | solution.py:27
  66.6 4.4 %reshape.43 = bf16[16,8,64,2,32]{4,3,2,1,0:T(2,128)(2,1)} reshape(bf16[16,8,4096]{2,1,0:T(8,128)(2,1)S(1)} %copy-done.3) | data formatting | bytes 2097152 | tf_op jit(solution)/shard_map/reshape | solution.py:331
  71.0 9.7 %copy.23 = bf16[16,2,64,8,32]{2,1,4,3,0:T(2,128)(2,1)S(1)} copy(bf16[16,2,64,8,32]{4,1,2,3,0:T(2,128)(2,1)} %bitcast.12) | data formatting | bytes 2097152 | tf_op jit(solution)/shard_map/transpose | solution.py:332
  83.1 2.4 %collective-permute-start.8 = (bf16[16,32,128]{2,1,0:T(8,128)(2,1)}, bf16[16,32,128]{2,1,0:T(8,128)(2,1)S(1)}, u32[]{:S(2)}, u32[]{:S(2)}) collective-permute-start(bf16[16,32,128]{2,1,0:T(8,128)(2,1)} %get-tuple-element.18), channel_id=1, source_target_pairs={{0,4},{1,5},{2,6},{3,7},{4,8},{5,9},{6,10},{7,11},{8,12},{9,13},{1... | collective-permute-start | bytes 393224 | tf_op jit(solution)/shard_map/ppermute | solution.py:27
  85.5 8.2 %self_tiles.1.tself_ref = bf16[16,512,512]{2,1,0:T(8,128)(2,1)} custom-call(f32[32,8192]{1,0:T(8,128)} %eo_ref.1), custom_call_target="tpu_custom_call" | custom-call | flops 2147483648 | bytes 8388608 | tf_op jit(solution)/shard_map/self_tiles/pallas_call | solution.py:372
  94.4 31.3 %first_product.1 = (bf16[16,2,512,512]{3,2,1,0:T(8,128)(2,1)}, f32[64,8192]{1,0:T(8,128)}, bf16[64,4096]{1,0:T(8,128)(2,1)}, bf16[64,4096]{1,0:T(8,128)(2,1)}, b...) custom-call(s32[16,3]{1,0:T(8,128)} %copy.27.near_ref, s32[16,8]{1,0:T(8,128)} %copy.28.far_ref, ...), custom_call_target="tpu_custom_call" | custom-call | tf_op jit(solution)/shard_map/first_product/pallas_call | solution.py:392
  131.9 3.0 %collective-permute-start.16 = (f32[64,64]{1,0:T(8,128)S(1)}, f32[64,64]{1,0:T(8,128)S(1)}, u32[]{:S(2)}, u32[]{:S(2)}) collective-permute-start(f32[64,64]{1,0:T(8,128)S(1)} %add.67), channel_id=1, source_target_pairs={{0,4},{1,5},{2,6},{3,7},{4,0},{5,1},{6,2},{7,3},{8,12},{9,13},{10,... | collective-permute-start | bytes 49160 | tf_op jit(solution)/shard_map/ppermute | solution.py:32
  134.8 9.6 %collective-permute-done.16 = f32[64,64]{1,0:T(8,128)S(1)} collective-permute-done((f32[64,64]{1,0:T(8,128)S(1)}, f32[64,64]{1,0:T(8,128)S(1)}, u32[]{:S(2)}, u32[]{:S(2)}) %collective-permute-start.16) | collective-permute-done | bytes 16416 | tf_op jit(solution)/shard_map/ppermute | solution.py:32
  147.0 2.6 %collective-permute-done.17.sums_ref = f32[1,64,64]{2,1,0:T(8,128)S(1)} collective-permute-done((f32[1,64,64]{2,1,0:T(8,128)S(1)}, f32[1,64,64]{2,1,0:T(8,128)S(1)}, u32[]{:S(2)}, u32[]{:S(2)}) %collective-permute-start.17) | collective-permute-done | bytes 16416 | tf_op jit(solution)/shard_map/ppermute | solution.py:32
  151.5 4.0 %collective-permute-start.22 = (bf16[16,32,128]{2,1,0:T(8,128)(2,1)}, bf16[16,32,128]{2,1,0:T(8,128)(2,1)S(1)}, u32[]{:S(2)}, u32[]{:S(2)}) collective-permute-start(bf16[16,32,128]{2,1,0:T(8,128)(2,1)} %get-tuple-element.25), channel_id=1, source_target_pairs={{0,2},{1,3},{2,4},{3,5},{4,6},{5,7},{6,8},{7,9},{8,10},{9,11},{10,... | collective-permute-start | bytes 393224 | tf_op jit(solution)/shard_map/ppermute | solution.py:27
  157.6 4.5 %collective-permute-start.20 = (bf16[16,32,128]{2,1,0:T(8,128)(2,1)}, bf16[16,32,128]{2,1,0:T(8,128)(2,1)S(1)}, u32[]{:S(2)}, u32[]{:S(2)}) collective-permute-start(bf16[16,32,128]{2,1,0:T(8,128)(2,1)} %get-tuple-element.25), channel_id=1, source_target_pairs={{0,4},{1,5},{2,6},{3,7},{4,8},{5,9},{6,10},{7,11},{8,12},{9,13},{1... | collective-permute-start | bytes 393224 | tf_op jit(solution)/shard_map/ppermute | solution.py:27
  162.2 2.8 %collective-permute-done.20.rest_4_ = bf16[16,32,128]{2,1,0:T(8,128)(2,1)S(1)} collective-permute-done((bf16[16,32,128]{2,1,0:T(8,128)(2,1)}, bf16[16,32,128]{2,1,0:T(8,128)(2,1)S(1)}, u32[]{:S(2)}, u32[]{:S(2)}) %collective-permute-start.20) | collective-permute-done | bytes 131104 | tf_op jit(solution)/shard_map/ppermute | solution.py:27
  165.9 19.5 %second_product.1 = (f32[64,8192]{1,0:T(8,128)}, f32[64,128]{1,0:T(8,128)}) custom-call(s32[16,3]{1,0:T(8,128)} %copy.27.near_ref, s32[16,8]{1,0:T(8,128)} %copy.28.far_ref, s32[1]{0:T(128)} %bitcast.pos_ref, bf16[16,512,512]{2,1,0:T(8,128)(2,1)} %self_tiles.1.tself_ref, bf16[16,2,512,512]{3,2,1,0:T(8,128)(2,1)} %get-tuple-element.19.tile_ref, ...), custom_call_target="tpu_custom_call" | custom-call | tf_op jit(solution)/shard_map/second_product/pallas_call | solution.py:426
  189.1 2.6 %collective-permute-done.27 = f32[64,128]{1,0:T(8,128)S(1)} collective-permute-done((f32[64,128]{1,0:T(8,128)S(1)}, f32[64,128]{1,0:T(8,128)S(1)}, u32[]{:S(2)}, u32[]{:S(2)}) %collective-permute-start.27) | collective-permute-done | bytes 32800 | tf_op jit(solution)/shard_map/ppermute | solution.py:32
  191.6 2.3 %collective-permute-start.28 = (f32[64,128]{1,0:T(8,128)S(1)}, f32[64,128]{1,0:T(8,128)S(1)}, u32[]{:S(2)}, u32[]{:S(2)}) collective-permute-start(f32[64,128]{1,0:T(8,128)S(1)} %add.70), channel_id=1, source_target_pairs={{0,4},{1,5},{2,6},{3,7},{4,0},{5,1},{6,2},{7,3},{8,12},{9,13},{10,... | collective-permute-start | bytes 98312 | tf_op jit(solution)/shard_map/ppermute | solution.py:32
  195.9 3.4 %collective-permute-start.29 = (f32[64,128]{1,0:T(8,128)S(1)}, f32[64,128]{1,0:T(8,128)S(1)}, u32[]{:S(2)}, u32[]{:S(2)}) collective-permute-start(f32[64,128]{1,0:T(8,128)S(1)} %add.71), channel_id=1, source_target_pairs={{0,8},{1,9},{2,10},{3,11},{4,12},{5,13},{6,14},{7,15},{8,0},{9,1},... | collective-permute-start | bytes 98312 | tf_op jit(solution)/shard_map/ppermute | solution.py:32
  201.5 4.2 %multiply_add_fusion = (f32[64,8192]{1,0:T(8,128)}, f32[64,8192]{1,0:T(8,128)}) fusion(f32[64,8192]{1,0:T(8,128)} %get-tuple-element.27, f32[64,8192]{1,0:T(8,128)S(1)} %copy-done, f32[64,8192]{1,0:T(8,128)S(1)} %copy-done.2, f32[64]{0:T(128)S(1)} %get-tuple-element.40, f32[64]{0:T(128)S(1)} %get-tuple-element.39, f32[8192]{0:T(1024)S(1)} %copy-done.6), kind=kLoop, calls=%fused_computation | loop fusion | flops 4194304 | bytes 10519040 | tf_op jit(solution)/shard_map/add | solution.py:461
  (108 shorter events, 44.4 us)
Async XLA Ops:
  11.4 4.7 %collective-permute-start.1 = (f32[64,64]{1,0:T(8,128)S(1)}, f32[64,64]{1,0:T(8,128)S(1)}, u32[]{:S(2)}, u32[]{:S(2)}) collective-permute-start(f32[64,64]{1,0:T(8,128)S(1)} %add.63), channel_id=1, source_target_pairs={{0,2},{1,3},{2,0},{3,1},{4,6},{5,7},{6,4},{7,5},{8,10},{9,11},{10,... | collective-permute-start | bytes 49160 | tf_op jit(solution)/shard_map/ppermute | solution.py:32
  16.1 6.0 %collective-permute-start.2 = (f32[64,64]{1,0:T(8,128)S(1)}, f32[64,64]{1,0:T(8,128)S(1)}, u32[]{:S(2)}, u32[]{:S(2)}) collective-permute-start(f32[64,64]{1,0:T(8,128)S(1)} %add.64), channel_id=1, source_target_pairs={{0,4},{1,5},{2,6},{3,7},{4,0},{5,1},{6,2},{7,3},{8,12},{9,13},{10,... | collective-permute-start | bytes 49160 | tf_op jit(solution)/shard_map/ppermute | solution.py:32
  18.2 17.6 %collective-permute-start.13 = (bf16[16,32,128]{2,1,0:T(8,128)(2,1)}, bf16[16,32,128]{2,1,0:T(8,128)(2,1)S(1)}, u32[]{:S(2)}, u32[]{:S(2)}) collective-permute-start(bf16[16,32,128]{2,1,0:T(8,128)(2,1)} %get-tuple-element.18), channel_id=1, source_target_pairs={{4,0},{5,1},{6,2},{7,3},{8,4},{9,5},{10,6},{11,7},{12,8},{13,9},{1... | collective-permute-start | bytes 393224 | tf_op jit(solution)/shard_map/ppermute | solution.py:27
  19.5 18.5 %collective-permute-start.12 = (bf16[16,32,128]{2,1,0:T(8,128)(2,1)}, bf16[16,32,128]{2,1,0:T(8,128)(2,1)S(1)}, u32[]{:S(2)}, u32[]{:S(2)}) collective-permute-start(bf16[16,32,128]{2,1,0:T(8,128)(2,1)} %get-tuple-element.18), channel_id=1, source_target_pairs={{3,0},{4,1},{5,2},{6,3},{7,4},{8,5},{9,6},{10,7},{11,8},{12,9},{13... | collective-permute-start | bytes 393224 | tf_op jit(solution)/shard_map/ppermute | solution.py:27
  20.8 18.5 %collective-permute-start.11 = (bf16[16,32,128]{2,1,0:T(8,128)(2,1)}, bf16[16,32,128]{2,1,0:T(8,128)(2,1)S(1)}, u32[]{:S(2)}, u32[]{:S(2)}) collective-permute-start(bf16[16,32,128]{2,1,0:T(8,128)(2,1)} %get-tuple-element.18), channel_id=1, source_target_pairs={{2,0},{3,1},{4,2},{5,3},{6,4},{7,5},{8,6},{9,7},{10,8},{11,9},{12,... | collective-permute-start | bytes 393224 | tf_op jit(solution)/shard_map/ppermute | solution.py:27
  22.1 11.2 %collective-permute-start.3 = (f32[1,64,64]{2,1,0:T(8,128)S(1)}, f32[1,64,64]{2,1,0:T(8,128)S(1)}, u32[]{:S(2)}, u32[]{:S(2)}) collective-permute-start(f32[1,64,64]{2,1,0:T(8,128)S(1)} %add_bitcast_fusion.1), channel_id=1, source_target_pairs={{0,8},{1,9},{2,10},{3,11},{4,12},{5,13},{6,14},{7,15},{8,0},{9,1},... | collective-permute-start | bytes 49160 | tf_op jit(solution)/shard_map/ppermute | solution.py:32
  29.5 64.2 %collective-permute-start.5 = (f32[32,4096]{1,0:T(8,128)}, f32[32,4096]{1,0:T(8,128)}, u32[]{:S(2)}, u32[]{:S(2)}) collective-permute-start(f32[32,4096]{1,0:T(8,128)} %get-tuple-element.43), channel_id=1, source_target_pairs={{1,0},{2,1},{3,2},{4,3},{5,4},{6,5},{7,6},{8,7},{9,8},{10,9},{11,1... | collective-permute-start | bytes 1572872 | tf_op jit(solution)/shard_map/ppermute | solution.py:27
  33.3 60.5 %collective-permute-start.4 = (f32[32,4096]{1,0:T(8,128)}, f32[32,4096]{1,0:T(8,128)}, u32[]{:S(2)}, u32[]{:S(2)}) collective-permute-start(f32[32,4096]{1,0:T(8,128)} %get-tuple-element.44), channel_id=1, source_target_pairs={{0,1},{1,2},{2,3},{3,4},{4,5},{5,6},{6,7},{7,8},{8,9},{9,10},{10,1... | collective-permute-start | bytes 1572872 | tf_op jit(solution)/shard_map/ppermute | solution.py:27
  35.8 58.0 %collective-permute-start.6 = (bf16[64,4096]{1,0:T(8,128)(2,1)}, bf16[64,4096]{1,0:T(8,128)(2,1)}, u32[]{:S(2)}, u32[]{:S(2)}) collective-permute-start(bf16[64,4096]{1,0:T(8,128)(2,1)} %get-tuple-element.16.rest_2_), channel_id=1, source_target_pairs={{0,1},{1,2},{2,3},{3,4},{4,5},{5,6},{6,7},{7,8},{8,9},{9,10},{10,1... | collective-permute-start | bytes 1572872 | tf_op jit(solution)/shard_map/ppermute | solution.py:27
  37.9 55.8 %collective-permute-start.7 = (bf16[64,4096]{1,0:T(8,128)(2,1)}, bf16[64,4096]{1,0:T(8,128)(2,1)}, u32[]{:S(2)}, u32[]{:S(2)}) collective-permute-start(bf16[64,4096]{1,0:T(8,128)(2,1)} %get-tuple-element.17.rest_1_), channel_id=1, source_target_pairs={{1,0},{2,1},{3,2},{4,3},{5,4},{6,5},{7,6},{8,7},{9,8},{10,9},{11,1... | collective-permute-start | bytes 1572872 | tf_op jit(solution)/shard_map/ppermute | solution.py:27
  39.3 13.3 %collective-permute-start.10 = (bf16[16,32,128]{2,1,0:T(8,128)(2,1)}, bf16[16,32,128]{2,1,0:T(8,128)(2,1)S(1)}, u32[]{:S(2)}, u32[]{:S(2)}) collective-permute-start(bf16[16,32,128]{2,1,0:T(8,128)(2,1)} %get-tuple-element.18), channel_id=1, source_target_pairs={{0,2},{1,3},{2,4},{3,5},{4,6},{5,7},{6,8},{7,9},{8,10},{9,11},{10,... | collective-permute-start | bytes 393224 | tf_op jit(solution)/shard_map/ppermute | solution.py:27
  52.5 30.5 %collective-permute-start.9 = (bf16[16,32,128]{2,1,0:T(8,128)(2,1)}, bf16[16,32,128]{2,1,0:T(8,128)(2,1)}, u32[]{:S(2)}, u32[]{:S(2)}) collective-permute-start(bf16[16,32,128]{2,1,0:T(8,128)(2,1)} %get-tuple-element.18), channel_id=1, source_target_pairs={{0,3},{1,4},{2,5},{3,6},{4,7},{5,8},{6,9},{7,10},{8,11},{9,12},{10... | collective-permute-start | bytes 393224 | tf_op jit(solution)/shard_map/ppermute | solution.py:27
  83.1 10.6 %collective-permute-start.8 = (bf16[16,32,128]{2,1,0:T(8,128)(2,1)}, bf16[16,32,128]{2,1,0:T(8,128)(2,1)S(1)}, u32[]{:S(2)}, u32[]{:S(2)}) collective-permute-start(bf16[16,32,128]{2,1,0:T(8,128)(2,1)} %get-tuple-element.18), channel_id=1, source_target_pairs={{0,4},{1,5},{2,6},{3,7},{4,8},{5,9},{6,10},{7,11},{8,12},{9,13},{1... | collective-permute-start | bytes 393224 | tf_op jit(solution)/shard_map/ppermute | solution.py:27
  127.9 37.0 %collective-permute-start.18 = (bf16[64,4096]{1,0:T(8,128)(2,1)}, bf16[64,4096]{1,0:T(8,128)(2,1)S(1)}, u32[]{:S(2)}, u32[]{:S(2)}) collective-permute-start(bf16[64,4096]{1,0:T(8,128)(2,1)} %get-tuple-element.23.rest_2_), channel_id=1, source_target_pairs={{0,1},{1,2},{2,3},{3,4},{4,5},{5,6},{6,7},{7,8},{8,9},{9,10},{10,1... | collective-permute-start | bytes 1572872 | tf_op jit(solution)/shard_map/ppermute | solution.py:27
  130.0 34.9 %collective-permute-start.19 = (bf16[64,4096]{1,0:T(8,128)(2,1)}, bf16[64,4096]{1,0:T(8,128)(2,1)S(1)}, u32[]{:S(2)}, u32[]{:S(2)}) collective-permute-start(bf16[64,4096]{1,0:T(8,128)(2,1)} %get-tuple-element.24.rest_1_), channel_id=1, source_target_pairs={{1,0},{2,1},{3,2},{4,3},{5,4},{6,5},{7,6},{8,7},{9,8},{10,9},{11,1... | collective-permute-start | bytes 1572872 | tf_op jit(solution)/shard_map/ppermute | solution.py:27
  131.9 12.5 %collective-permute-start.16 = (f32[64,64]{1,0:T(8,128)S(1)}, f32[64,64]{1,0:T(8,128)S(1)}, u32[]{:S(2)}, u32[]{:S(2)}) collective-permute-start(f32[64,64]{1,0:T(8,128)S(1)} %add.67), channel_id=1, source_target_pairs={{0,4},{1,5},{2,6},{3,7},{4,0},{5,1},{6,2},{7,3},{8,12},{9,13},{10,... | collective-permute-start | bytes 49160 | tf_op jit(solution)/shard_map/ppermute | solution.py:32
  144.4 5.2 %collective-permute-start.17 = (f32[1,64,64]{2,1,0:T(8,128)S(1)}, f32[1,64,64]{2,1,0:T(8,128)S(1)}, u32[]{:S(2)}, u32[]{:S(2)}) collective-permute-start(f32[1,64,64]{2,1,0:T(8,128)S(1)} %add_bitcast_fusion), channel_id=1, source_target_pairs={{0,8},{1,9},{2,10},{3,11},{4,12},{5,13},{6,14},{7,15},{8,0},{9,1},... | collective-permute-start | bytes 49160 | tf_op jit(solution)/shard_map/ppermute | solution.py:32
  144.4 7.1 %collective-permute-start.25 = (bf16[16,32,128]{2,1,0:T(8,128)(2,1)}, bf16[16,32,128]{2,1,0:T(8,128)(2,1)S(1)}, u32[]{:S(2)}, u32[]{:S(2)}) collective-permute-start(bf16[16,32,128]{2,1,0:T(8,128)(2,1)} %get-tuple-element.25), channel_id=1, source_target_pairs={{4,0},{5,1},{6,2},{7,3},{8,4},{9,5},{10,6},{11,7},{12,8},{13,9},{1... | collective-permute-start | bytes 393224 | tf_op jit(solution)/shard_map/ppermute | solution.py:27
  145.7 9.7 %collective-permute-start.24 = (bf16[16,32,128]{2,1,0:T(8,128)(2,1)}, bf16[16,32,128]{2,1,0:T(8,128)(2,1)S(1)}, u32[]{:S(2)}, u32[]{:S(2)}) collective-permute-start(bf16[16,32,128]{2,1,0:T(8,128)(2,1)} %get-tuple-element.25), channel_id=1, source_target_pairs={{3,0},{4,1},{5,2},{6,3},{7,4},{8,5},{9,6},{10,7},{11,8},{12,9},{13... | collective-permute-start | bytes 393224 | tf_op jit(solution)/shard_map/ppermute | solution.py:27
  149.6 8.0 %collective-permute-start.23 = (bf16[16,32,128]{2,1,0:T(8,128)(2,1)}, bf16[16,32,128]{2,1,0:T(8,128)(2,1)S(1)}, u32[]{:S(2)}, u32[]{:S(2)}) collective-permute-start(bf16[16,32,128]{2,1,0:T(8,128)(2,1)} %get-tuple-element.25), channel_id=1, source_target_pairs={{2,0},{3,1},{4,2},{5,3},{6,4},{7,5},{8,6},{9,7},{10,8},{11,9},{12,... | collective-permute-start | bytes 393224 | tf_op jit(solution)/shard_map/ppermute | solution.py:27
  151.5 10.6 %collective-permute-start.22 = (bf16[16,32,128]{2,1,0:T(8,128)(2,1)}, bf16[16,32,128]{2,1,0:T(8,128)(2,1)S(1)}, u32[]{:S(2)}, u32[]{:S(2)}) collective-permute-start(bf16[16,32,128]{2,1,0:T(8,128)(2,1)} %get-tuple-element.25), channel_id=1, source_target_pairs={{0,2},{1,3},{2,4},{3,5},{4,6},{5,7},{6,8},{7,9},{8,10},{9,11},{10,... | collective-permute-start | bytes 393224 | tf_op jit(solution)/shard_map/ppermute | solution.py:27
  155.5 6.7 %collective-permute-start.21 = (bf16[16,32,128]{2,1,0:T(8,128)(2,1)}, bf16[16,32,128]{2,1,0:T(8,128)(2,1)S(1)}, u32[]{:S(2)}, u32[]{:S(2)}) collective-permute-start(bf16[16,32,128]{2,1,0:T(8,128)(2,1)} %get-tuple-element.25), channel_id=1, source_target_pairs={{0,3},{1,4},{2,5},{3,6},{4,7},{5,8},{6,9},{7,10},{8,11},{9,12},{10... | collective-permute-start | bytes 393224 | tf_op jit(solution)/shard_map/ppermute | solution.py:27
  157.6 7.4 %collective-permute-start.20 = (bf16[16,32,128]{2,1,0:T(8,128)(2,1)}, bf16[16,32,128]{2,1,0:T(8,128)(2,1)S(1)}, u32[]{:S(2)}, u32[]{:S(2)}) collective-permute-start(bf16[16,32,128]{2,1,0:T(8,128)(2,1)} %get-tuple-element.25), channel_id=1, source_target_pairs={{0,4},{1,5},{2,6},{3,7},{4,8},{5,9},{6,10},{7,11},{8,12},{9,13},{1... | collective-permute-start | bytes 393224 | tf_op jit(solution)/shard_map/ppermute | solution.py:27
  195.9 5.3 %collective-permute-start.29 = (f32[64,128]{1,0:T(8,128)S(1)}, f32[64,128]{1,0:T(8,128)S(1)}, u32[]{:S(2)}, u32[]{:S(2)}) collective-permute-start(f32[64,128]{1,0:T(8,128)S(1)} %add.71), channel_id=1, source_target_pairs={{0,8},{1,9},{2,10},{3,11},{4,12},{5,13},{6,14},{7,15},{8,0},{9,1},... | collective-permute-start | bytes 98312 | tf_op jit(solution)/shard_map/ppermute | solution.py:32
  (29 other events, 562.9 us)

commit v2 on v0

v2 whole, which is shorter than its diff:
```python
import math

import jax
import jax.numpy as jnp
from jax import lax
from jax.experimental import pallas as pl
from jax.experimental.pallas import tpu as pltpu
from jax.sharding import PartitionSpec as P

FARDEV = 4
CDEV = 8
KERNEL_SCALE = 0.0625
RIDGE_TERM = 1.0
EPSILON = 1e-06
F32 = jnp.float32
BF16 = jnp.bfloat16
HALF_SCALE = math.sqrt(2.0 * KERNEL_SCALE * math.log2(math.e))
UNROLL = 2
VMEM_LIMIT = 12 * 1024 * 1024
WHOLE = pl.BlockSpec(memory_space=pltpu.VMEM)
SCALAR = pl.BlockSpec(memory_space=pltpu.SMEM)


def involution(value, partner):
    count = lax.axis_size("leaf")
    pairs = [(i, partner(i)) for i in range(count) if 0 <= partner(i) < count]
    return lax.ppermute(value, "leaf", pairs)


def sibling(value):
    return involution(value, lambda i: i ^ 1)


def beside(value):
    return involution(value, lambda i: i + 1 if i % 2 else i - 1)


def two_chips(value):
    return involution(value, lambda i: i + 3 if i % 2 else i - 3)


def dot(a, b, ca, cb):
    return lax.dot_general(a, b, (((ca,), (cb,)), ((), ())), preferred_element_type=F32)


def split3(value):
    high = value.astype(BF16)
    rest = value - high.astype(F32)
    mid = rest.astype(BF16)
    low = (rest - mid.astype(F32)).astype(BF16)
    return high, mid, low


def point_pieces(points):
    scaled = points * HALF_SCALE
    high, mid, low = split3(scaled)
    square = 0.5 * jnp.sum(scaled * scaled, axis=0, keepdims=True)
    s_high, s_mid, s_low = split3(square)
    return high, mid, low, s_high.astype(F32), s_mid.astype(F32), s_low.astype(F32)


def norm_rows(first, second, third, width, swap, sign):
    row = lax.broadcasted_iota(jnp.int32, (16, width), 0)
    base = 3 if swap else 0
    ones = 0 if swap else 3
    out = jnp.where((row >= ones) & (row < ones + 3), sign, 0.0)
    for at, piece in enumerate((first, second, third)):
        out = jnp.where(row == base + at, sign * piece, out)
    return out.astype(BF16)


def own_rows(points):
    high, mid, low, a, b, c = point_pieces(points)
    norms = norm_rows(a, b, c, points.shape[1], False, 1.0)
    return jnp.concatenate([high, mid, high, mid, low, high, norms], axis=0)


def other_rows(points):
    high, mid, low, a, b, c = point_pieces(points)
    norms = norm_rows(a, b, c, points.shape[1], True, -1.0)
    return jnp.concatenate([high, high, mid, mid, high, low, norms], axis=0)


def tile_of(other, own):
    return jnp.exp2(dot(other, own, 0, 0)).astype(BF16)


def pack_pair(block):
    half = block.shape[0] // 2
    return jnp.concatenate([block[:half], block[half:]], axis=1)


def leaf_coefficients(basis, rounded, trans):
    coef = dot(basis, rounded, 1, 1).astype(BF16)
    return pack_pair(coef), dot(trans, coef, 0, 0)


def columns_of(ref, at, width):
    return ref[:, pl.ds(pl.multiple_of(at * width, width), width)]


def leaf_loop(count, unroll, fn):
    def trip(i, carry):
        for u in range(unroll):
            fn(i * unroll + u)
        return carry

    lax.fori_loop(0, count // unroll, trip, 0)


def send_margins(v_ref, mx_ref, mo_ref, odd):
    half = mx_ref.shape[0]
    mx_ref[...] = v_ref[pl.ds(half * (1 - odd), half)]
    mo_ref[...] = v_ref[pl.ds(half * odd, half)]


def store_share(total, part_ref, cp_ref, rows):
    packed = pack_pair(total)
    part_ref[...] = packed
    size = packed.shape[0]
    for at, piece in enumerate(split3(packed)):
        cp_ref[rows + at * size : rows + (at + 1) * size] = piece


def prep_kernel(pos_ref, rs_ref, sc_ref, basis_ref, trans_ref, v_ref, mx_ref, mo_ref, cp_ref, part_ref, acc):
    per, rank, leaf = basis_ref.shape
    size = rank // 2
    acc[...] = jnp.zeros_like(acc)

    def one(at):
        rounded = (columns_of(rs_ref, at, leaf) * columns_of(sc_ref, at, leaf)).astype(BF16)
        packed, share = leaf_coefficients(basis_ref[at], rounded, trans_ref[at])
        v_ref[at] = rounded
        cp_ref[pl.ds(pl.multiple_of(at * size, size), size)] = packed
        acc[...] += share

    leaf_loop(per, UNROLL, one)
    store_share(acc[...], part_ref, cp_ref, per * size)
    send_margins(v_ref, mx_ref, mo_ref, pos_ref[0] % 2)


def pair_kernel(pos_ref, own_ref, got_ref, part_ref, pair_ref, sum_ref):
    odd = pos_ref[0] % 2
    rows = pair_ref.shape[1]
    size = part_ref.shape[0]
    pair_ref[odd] = own_ref[:rows]
    pair_ref[1 - odd] = got_ref[:rows]
    total = part_ref[...]
    for at in range(3):
        total += got_ref[rows + at * size : rows + (at + 1) * size].astype(F32)
    sum_ref[...] = total


def list_entries(near_ref, list_ref, pos, half, want_own):
    slots = near_ref.shape[1] - 1
    total = near_ref.shape[0] * slots
    base = pos * 2 * half - half

    def put(at, n):
        m = near_ref[at // slots, 1 + at % slots] - base
        own = (m >= half) & (m < 3 * half)
        list_ref[n] = at
        return n + jnp.where(own == want_own, 1, 0)

    n = lax.fori_loop(0, total, put, 0)
    list_ref[n] = total
    return n


def near_entry(near_ref, list_ref, at, pos, half, own):
    slots = near_ref.shape[1] - 1
    per = near_ref.shape[0]
    entry = list_ref[at]
    spare = entry == per * slots
    leaf_at = entry // slots
    row = jnp.minimum(leaf_at, per - 1)
    m = near_ref[row, 1 + entry % slots] - (pos * 2 * half - half)
    if own:
        place = jnp.clip(m - half, 0, per - 1)
    else:
        place = jnp.clip(jnp.where(m < half, m, m - 2 * half), 0, 2 * half - 1)
    return entry, leaf_at, row, place


def load_halves(target, from_sibling, from_beside, odd):
    half = from_sibling.shape[0]
    target[pl.ds(half * (1 - odd), half)] = from_sibling[...]
    target[pl.ds(half * odd, half)] = from_beside[...]


def own_kernel(pos_ref, near_ref, e_ref, v_ref, tile_ref, near_out, list_ref):
    per, _, leaf = v_ref.shape
    half = per // 2
    pos = pos_ref[0]

    def one(at):
        points = columns_of(e_ref, at, leaf)
        tile = tile_of(other_rows(points), own_rows(points))
        tile_ref[at] = tile
        near_out[at] = dot(v_ref[at], tile, 1, 0)

    leaf_loop(per, UNROLL, one)
    n = list_entries(near_ref, list_ref, pos, half, True)

    def trip(i, carry):
        for u in range(UNROLL):
            entry, leaf_at, row, place = near_entry(near_ref, list_ref, i * UNROLL + u, pos, half, True)
            tile = tile_of(other_rows(columns_of(e_ref, place, leaf)), own_rows(columns_of(e_ref, row, leaf)))
            tile_ref[per + entry] = tile
            near_out[leaf_at] += dot(v_ref[place], tile, 1, 0)
        return carry

    lax.fori_loop(0, (n + UNROLL - 1) // UNROLL, trip, 0)


def own_again_kernel(pos_ref, near_ref, v_ref, tile_ref, near_out, list_ref):
    per, _, leaf = v_ref.shape
    half = per // 2
    pos = pos_ref[0]

    def one(at):
        near_out[at] = dot(v_ref[at], tile_ref[at], 1, 0)

    leaf_loop(per, UNROLL, one)
    n = list_entries(near_ref, list_ref, pos, half, True)

    def trip(i, carry):
        for u in range(UNROLL):
            entry, leaf_at, _, place = near_entry(near_ref, list_ref, i * UNROLL + u, pos, half, True)
            near_out[leaf_at] += dot(v_ref[place], tile_ref[per + entry], 1, 0)
        return carry

    lax.fori_loop(0, (n + UNROLL - 1) // UNROLL, trip, 0)


def load_coefficients(cw, sources):
    rows = sources[0].shape[1]
    per = rows // cw.shape[1]
    for slot, source in enumerate(sources):
        for core in range(2):
            for at in range(per):
                cw[(slot * 2 + core) * per + at] = source[core, at * cw.shape[1] : (at + 1) * cw.shape[1]]


def coarse_rows(coarse_ref, sum_refs, fc):
    rank = coarse_ref.shape[1]
    acc = jnp.zeros((rank, rank), F32)
    for at in range(coarse_ref.shape[0]):
        packed = sum_refs[0][at]
        for ref in sum_refs[1:]:
            packed += ref[at]
        total = jnp.concatenate([packed[:, :rank], packed[:, rank:]], axis=0)
        for piece in split3(total):
            acc += dot(coarse_ref[at], piece, 1, 0)
    fc[...] = jnp.concatenate(split3(acc), axis=1)


def far_columns(l, pos, far_ref, cw, coup_ref, trans_ref, fc, basis_ref):
    per, rank, _ = basis_ref.shape
    odd = pos % 2
    picks = []
    for s in range(far_ref.shape[1]):
        leaf_id = far_ref[l, s]
        device = leaf_id // per
        gap = device // 2 - pos // 2
        direct = (gap < 0) == (odd == 0)
        slot = jnp.where(direct, 0, 2) + jnp.where(jnp.abs(gap) == 2, 1, 0)
        picks.append(cw[(slot * 2 + device % 2) * per + leaf_id % per])
    wide = dot(coup_ref[l], jnp.concatenate(picks, axis=0), 1, 0)
    coupled = wide[:rank, :rank] + wide[rank:, rank:]
    moved = dot(trans_ref[l], fc[...], 1, 0)
    combined = coupled + moved[:, :rank] + moved[:, rank : 2 * rank] + moved[:, 2 * rank :]
    return dot(combined.astype(BF16), basis_ref[l], 0, 0)


def rest_kernel(
    pos_ref, near_ref, far_ref, e_ref, ex_ref, eo_ref, rs_ref, sc_ref, basis_ref, coup_ref, trans_ref,
    coarse_ref, sum_a, sum_b, vx_ref, vo_ref, c0, c1, c2, c3, tile_in, near_in,
    tile_ref, near_ref_out, u_ref, q_ref, mx_ref, mo_ref, cp_ref, part_ref, msg_ref,
    list_ref, vw, cw, fc, acc, acc_uu, acc_ru,
):
    per, rank, leaf = basis_ref.shape
    half = per // 2
    size = rank // 2
    pos = pos_ref[0]
    odd = pos % 2
    load_halves(vw, vx_ref, vo_ref, odd)
    load_coefficients(cw, (c0, c1, c2, c3))
    coarse_rows(coarse_ref, (sum_a, sum_b), fc)
    n = list_entries(near_ref, list_ref, pos, half, False)

    def trip(i, carry):
        for u in range(UNROLL):
            entry, leaf_at, row, place = near_entry(near_ref, list_ref, i * UNROLL + u, pos, half, False)
            beneath = place < half
            from_x = beneath == (odd == 1)
            within = jnp.where(beneath, place, place - half)
            far_x = columns_of(ex_ref, within, leaf)
            far_o = columns_of(eo_ref, within, leaf)
            points = jnp.where(from_x, far_x, far_o)
            tile = tile_of(other_rows(points), own_rows(columns_of(e_ref, row, leaf)))
            tile_ref[per + entry] = tile
            near_ref_out[leaf_at] += dot(vw[place], tile, 1, 0)
        return carry

    lax.fori_loop(0, (n + UNROLL - 1) // UNROLL, trip, 0)
    acc[...] = jnp.zeros_like(acc)
    acc_uu[...] = jnp.zeros_like(acc_uu)
    acc_ru[...] = jnp.zeros_like(acc_ru)

    def one(l):
        far = far_columns(l, pos, far_ref, cw, coup_ref, trans_ref, fc, basis_ref)
        right = columns_of(rs_ref, l, leaf)
        scale = columns_of(sc_ref, l, leaf)
        image = RIDGE_TERM * (right * scale) + (near_ref_out[l] + far)
        u_ref[:, pl.ds(pl.multiple_of(l * leaf, leaf), leaf)] = image
        acc_uu[...] += image * image
        acc_ru[...] += right * image
        rounded = (image * scale).astype(BF16)
        packed, share = leaf_coefficients(basis_ref[l], rounded, trans_ref[l])
        q_ref[l] = rounded
        cp_ref[pl.ds(pl.multiple_of(l * size, size), size)] = packed
        acc[...] += share

    leaf_loop(per, UNROLL, one)
    store_share(acc[...], part_ref, cp_ref, per * size)
    send_margins(q_ref, mx_ref, mo_ref, odd)
    lane = lax.broadcasted_iota(jnp.int32, msg_ref.shape, 1)
    out = jnp.where(lane == 0, jnp.sum(acc_uu[...], axis=1, keepdims=True), 0.0)
    out = jnp.where(lane == 1, jnp.sum(acc_ru[...], axis=1, keepdims=True), out)
    msg_ref[...] = out


def rest_again_kernel(
    pos_ref, near_ref, far_ref, rs_ref, sc_ref, u_ref, basis_ref, coup_ref, trans_ref,
    coarse_ref, sum_a, sum_b, vx_ref, vo_ref, c0, c1, c2, c3, tile_ref, near_in, prev_ref,
    near_out, w_ref, msg_ref,
    list_ref, vw, cw, fc, acc_uw, acc_ww, acc_rw,
):
    per, rank, leaf = basis_ref.shape
    half = per // 2
    pos = pos_ref[0]
    load_halves(vw, vx_ref, vo_ref, pos % 2)
    load_coefficients(cw, (c0, c1, c2, c3))
    coarse_rows(coarse_ref, (sum_a, sum_b), fc)
    n = list_entries(near_ref, list_ref, pos, half, False)

    def trip(i, carry):
        for u in range(UNROLL):
            entry, leaf_at, _, place = near_entry(near_ref, list_ref, i * UNROLL + u, pos, half, False)
            near_out[leaf_at] += dot(vw[place], tile_ref[per + entry], 1, 0)
        return carry

    lax.fori_loop(0, (n + UNROLL - 1) // UNROLL, trip, 0)
    for acc in (acc_uw, acc_ww, acc_rw):
        acc[...] = jnp.zeros_like(acc)

    def one(l):
        far = far_columns(l, pos, far_ref, cw, coup_ref, trans_ref, fc, basis_ref)
        image = columns_of(u_ref, l, leaf)
        second = RIDGE_TERM * (image * columns_of(sc_ref, l, leaf)) + (near_out[l] + far)
        w_ref[:, pl.ds(pl.multiple_of(l * leaf, leaf), leaf)] = second
        acc_uw[...] += image * second
        acc_ww[...] += second * second
        acc_rw[...] += columns_of(rs_ref, l, leaf) * second

    leaf_loop(per, UNROLL, one)
    lane = lax.broadcasted_iota(jnp.int32, msg_ref.shape, 1)
    out = prev_ref[...]
    for at, acc in enumerate((acc_uw, acc_ww, acc_rw)):
        out = jnp.where(lane == 2 + at, jnp.sum(acc[...], axis=1, keepdims=True), out)
    msg_ref[...] = out


def call(kernel, name, in_specs, out_shape, scratch, args, aliases=None, flops=0):
    return pl.pallas_call(
        kernel,
        in_specs=in_specs,
        out_specs=[WHOLE] * len(out_shape),
        out_shape=out_shape,
        scratch_shapes=scratch,
        input_output_aliases=aliases or {},
        compiler_params=pltpu.CompilerParams(vmem_limit_bytes=VMEM_LIMIT),
        cost_estimate=pl.CostEstimate(flops=flops, bytes_accessed=0, transcendentals=0),
        name=name,
    )(*args)


def cluster_sums(pair_sum):
    count = lax.axis_size("leaf")
    if count == 2 * CDEV and CDEV == 8:
        first = involution(pair_sum, lambda i: i ^ (8 + 2 * (i % 2)))
        second = involution(pair_sum, lambda i: i ^ (12 + 2 * (i % 2)))
        mine = (first + second)[None]
        return mine, sibling(mine)
    mask = 2
    while mask < CDEV:
        pair_sum = pair_sum + involution(pair_sum, lambda i: i ^ mask)
        mask *= 2
    sums = pair_sum[None]
    while mask < count:
        sums = jnp.concatenate([sums, involution(sums, lambda i: i ^ mask)], axis=0)
        mask *= 2
    return sums[1:], jnp.zeros_like(sums[1:])


def exchange(position, cp, part, mx, mo):
    rows = cp.shape[0] - 3 * part.shape[0]
    got = sibling(cp)
    pair, pair_sum = call(
        pair_kernel, "pair", [SCALAR] + [WHOLE] * 3,
        [pltpu.VMEM((2, rows, cp.shape[1]), BF16), jax.ShapeDtypeStruct(part.shape, F32)],
        [], (position, cp, got, part),
    )
    near_pair = beside(pair)
    far_pair = two_chips(pair)
    sums = cluster_sums(pair_sum)
    vx = sibling(mx)
    vo = beside(mo)
    return vx, vo, (near_pair, far_pair, sibling(near_pair), sibling(far_pair)), sums


def body(
    right_side, scaling, embeddings, near_leaves, far_leaves, leaf_basis, leaf_coupling,
    transfer, coarse_coupling,
):
    columns, local_points = right_side.shape
    per, rank, leaf = leaf_basis.shape
    features = embeddings.shape[0]
    slots = near_leaves.shape[1] - 1
    far_count = far_leaves.shape[1]
    half = per // 2
    margin = half * leaf
    size = rank // 2
    count = lax.axis_size("leaf")
    pos = lax.axis_index("leaf")
    odd = pos % 2
    position = pos.reshape(1).astype(jnp.int32)
    cluster = pos // CDEV
    coarse_count = count // CDEV

    e_sibling = sibling(lax.dynamic_slice_in_dim(embeddings, (1 - odd) * margin, margin, 1))
    e_beside = beside(lax.dynamic_slice_in_dim(embeddings, odd * margin, margin, 1))

    scale_row = scaling.reshape(1, local_points)
    trans = transfer.reshape(per, rank, rank)
    coup = leaf_coupling.reshape(per, far_count, rank, 2, rank // 2)
    coup = coup.transpose(0, 3, 2, 1, 4).reshape(per, 2 * rank, far_count * rank // 2)
    row = lax.dynamic_index_in_dim(coarse_coupling, cluster, 0, keepdims=False)
    order = jnp.arange(1, coarse_count, dtype=jnp.int32) ^ cluster
    coarse = jnp.take(row, order, axis=0).reshape(coarse_count - 1, rank, rank)

    leaf_shape = pltpu.VMEM((per, columns, leaf), BF16)
    half_shape = pltpu.VMEM((half, columns, leaf), BF16)
    cp_shape = pltpu.VMEM((per * size + 3 * size, 2 * columns), BF16)
    part_shape = pltpu.VMEM((size, 2 * columns), F32)
    tile_shape = pltpu.VMEM((per * (1 + slots) + 1, leaf, leaf), BF16)
    near_shape = pltpu.VMEM((per + 1, columns, leaf), F32)
    wide_shape = pltpu.VMEM((columns, local_points), F32)
    msg_shape = pltpu.VMEM((columns, 128), F32)
    share_acc = pltpu.VMEM((rank, columns), F32)
    acc_shape = pltpu.VMEM((columns, leaf), F32)
    list_shape = pltpu.SMEM((per * slots + UNROLL,), jnp.int32)
    window = [
        pltpu.VMEM((2 * half, columns, leaf), BF16),
        pltpu.VMEM((8 * per, size, 2 * columns), BF16),
        pltpu.VMEM((rank, 3 * columns), BF16),
    ]

    v, mx, mo, cp, part = call(
        prep_kernel, "prep", [SCALAR] + [WHOLE] * 4,
        [leaf_shape, half_shape, half_shape, cp_shape, part_shape], [share_acc],
        (position, right_side, scale_row, leaf_basis, trans),
    )
    vx, vo, coefs, sums = exchange(position, cp, part, mx, mo)
    tiles, near = call(
        own_kernel, "own_tiles", [SCALAR] * 2 + [WHOLE] * 2, [tile_shape, near_shape], [list_shape],
        (position, near_leaves, embeddings, v), flops=2 * 32 * leaf * leaf * 320,
    )
    tiles, _, image, q, mx, mo, cp, part, msg = call(
        rest_kernel, "first_product", [SCALAR] * 3 + [WHOLE] * 19,
        [tile_shape, near_shape, wide_shape, leaf_shape, half_shape, half_shape, cp_shape, part_shape, msg_shape],
        [list_shape] + window + [share_acc, acc_shape, acc_shape],
        (position, near_leaves, far_leaves, embeddings, e_sibling, e_beside, right_side, scale_row,
         leaf_basis, coup, trans, coarse, *sums, vx, vo, *coefs, tiles, near),
        aliases={20: 0, 21: 1}, flops=2 * 16 * leaf * leaf * 320,
    )
    vx, vo, coefs, sums = exchange(position, cp, part, mx, mo)
    (near,) = call(
        own_again_kernel, "own_again", [SCALAR] * 2 + [WHOLE] * 2, [near_shape], [list_shape],
        (position, near_leaves, q, tiles), flops=2 * 32 * leaf * leaf * 64,
    )
    _, second, msg = call(
        rest_again_kernel, "second_product", [SCALAR] * 3 + [WHOLE] * 18,
        [near_shape, wide_shape, msg_shape],
        [list_shape] + window + [acc_shape] * 3,
        (position, near_leaves, far_leaves, right_side, scale_row, image, leaf_basis, coup, trans,
         coarse, *sums, vx, vo, *coefs, tiles, near, msg),
        aliases={19: 0}, flops=2 * 16 * leaf * leaf * 64,
    )

    mask = 1
    while mask < count:
        msg = msg + involution(msg, lambda i: i ^ mask)
        mask *= 2
    uu, ru, uw, ww, rw = [msg[:, k : k + 1] for k in range(5)]
    step_one = ru / (uu + EPSILON)
    beta = -(uu - step_one * uw) / (uu + EPSILON)
    lead = 1.0 + beta
    curvature = lead * lead * uu - 2.0 * lead * step_one * uw + step_one * step_one * ww
    aligned = lead * (ru - step_one * uu) - step_one * (rw - step_one * uw)
    step_two = aligned / (curvature + EPSILON)
    first_weight = step_one + step_two * lead
    second_weight = step_two * step_one
    solution = scale_row * (first_weight * right_side - second_weight * image)
    residual = right_side - first_weight * image + second_weight * second
    return (solution, residual)


def solution(mesh):
    return jax.shard_map(
        body,
        mesh=mesh,
        in_specs=(
            P(None, ("groups", "leaf")),
            P(("groups", "leaf")),
            P(None, ("groups", "leaf")),
            P(("groups", "leaf"), None),
            P(("groups", "leaf"), None),
            P(("groups", "leaf"), None, None),
            P(("groups", "leaf"), None, None),
            P(("groups", "leaf"), None),
            P("groups", None, None),
        ),
        out_specs=(P(None, ("groups", "leaf")), P(None, ("groups", "leaf"))),
        check_vma=False,
    )
```

time: 393 us -> 200 us (0.51)
  blocking collectives: 143 us -> 0 us
  matrix products: 100 us -> 0 us
  Pallas kernels: 0 us -> 57.9 us
  waiting for transfers between devices: 0.07 us -> 29.6 us
  starting transfers between devices: 61.1 us -> 32.8 us
  other arithmetic: 27.1 us -> 3.13 us
  local copies, waits for them, and re-layouts: 57.6 us -> 74.6 us
    dot_general x15 -> x0, matrix products: 100 us -> none  [the longest x1 54.2 us: body(): jnp.einsum('dip,disq->ispq', own_points, chosen_points, precision=HIGHEST...]
    psum x3 -> x0, blocking collectives: 94.8 us -> none  [the longest x1 33.6 us: body(): lax.psum(jnp.sum(product_now * direction_image, axis=1), 'leaf')]
    pallas_call x0 -> x7, Pallas kernels: none -> 57.9 us  [call(): pl.pallas_call(kernel, in_specs=in_specs, out_specs=[WHOLE] * len(out_sha...]
    all_gather x2 -> x0, blocking collectives: 48.6 us -> none  [body(): gathered = lax.all_gather(partial_value[None], 'leaf', axis=0, tiled=True)]
    ppermute x22 -> x26, waiting for transfers between devices: 0.07 us -> 29.6 us  [involution(): return lax.ppermute(value, 'leaf', pairs)]
    ppermute x22 -> x26, starting transfers between devices: 61.1 us -> 32.8 us  [involution(): return lax.ppermute(value, 'leaf', pairs)]
    unnamed x69 -> x46, local copies, waits for them, and re-layouts: 24.5 us -> 50 us
    gather x5 -> x0, local copies, waits for them, and re-layouts: 17.1 us -> none  [the longest x2 8.25 us: body(): jnp.take(padded.reshape(columns, window_leaves, leaf_size), near_index, a...]
  transfers between devices with their start and end apart: 22 -> 26, of which waited for: 0 -> 10; matrix products, arithmetic and copies ran while one was open for 15% -> 11% of each run, Pallas kernels for 0% -> 15%
where the time goes in v2:
time: 200 us; the launch traced here: 199 us
  local copies, waits for them, and re-layouts  74.6 us (37%)
  Pallas kernels  57.9 us (29%)
  starting transfers between devices  32.8 us (16%)
  waiting for transfers between devices  29.6 us (15%)
  other arithmetic  3.13 us (2%)
    pallas_call x7, Pallas kernels, call(): pl.pallas_call(kernel, in_specs=in_specs, out_specs=[WHOLE] * len(out_sha...  57.9 us
    unnamed x46, local copies, waits for them, and re-layouts  50 us
    ppermute x26, starting transfers between devices, involution(): return lax.ppermute(value, 'leaf', pairs)  32.8 us
    ppermute x26, waiting for transfers between devices, involution(): return lax.ppermute(value, 'leaf', pairs)  29.6 us
    transpose x1, local copies, waits for them, and re-layouts, body(): coup.transpose(0, 3, 2, 1, 4).reshape(per, 2 * rank, far_count * rank // 2)  11.2 us
    reshape x2, local copies, waits for them, and re-layouts, body(): coup.transpose(0, 3, 2, 1, 4).reshape(per, 2 * rank, far_count * rank // 2)  6.22 us
    reshape x1, local copies, waits for them, and re-layouts, body(): coup = leaf_coupling.reshape(per, far_count, rank, 2, rank // 2)  4.39 us
  transfers between devices with their start and end apart: 26, of which 10 were waited for; matrix products, arithmetic and copies ran while one was open for 11% of the time, Pallas kernels for 15%

profile of v2, /device:TPU:0, one launch (start us, length us, event | category | flops | bytes accessed | tf_op | source)
XLA Modules:
  0.0 199.0 jit_solution(16515606532635887733)
XLA Ops:
  6.2 4.7 %prep.1 = (bf16[16,64,512]{2,1,0:T(8,128)(2,1)S(1)}, bf16[8,64,512]{2,1,0:T(8,128)(2,1)}, bf16[8,64,512]{2,1,0:T(8,128)(2,1)}, bf16[608,128]{1,0:T(8,128)(2,1)S(1)}, f32[32,128]{1,0:T(8,128)S(1)}) custom-call(s32[1]{0:T(128)} %bitcast.pos_ref, f32[64,8192]{1,0:T(8,128)S(1)} %copy-done.5, f32[1,8192]{1,0:T(1,128)S(1)} %bitcast.12, ...), custom_call_target="tpu_custom_call" | custom-call | tf_op jit(solution)/shard_map/prep/pallas_call | solution.py:376
  11.9 3.5 %collective-permute-start.2 = (bf16[608,128]{1,0:T(8,128)(2,1)S(1)}, bf16[608,128]{1,0:T(8,128)(2,1)S(1)}, u32[]{:S(2)}, u32[]{:S(2)}) collective-permute-start(bf16[608,128]{1,0:T(8,128)(2,1)S(1)} %get-tuple-element.23.own_ref), channel_id=1, source_target_pairs={{0,1},{1,0},{2,3},{3,2},{4,5},{5,4},{6,7},{7,6},{8,9},{9,8},{10,11... | collective-permute-start | bytes 466952 | tf_op jit(solution)/shard_map/ppermute | solution.py:27
  18.5 4.6 %collective-permute-start.4 = (f32[32,128]{1,0:T(8,128)S(1)}, f32[32,128]{1,0:T(8,128)S(1)}, u32[]{:S(2)}, u32[]{:S(2)}) collective-permute-start(f32[32,128]{1,0:T(8,128)S(1)} %get-tuple-element.25), channel_id=1, source_target_pairs={{0,12},{1,15},{2,14},{3,13},{4,8},{5,11},{6,10},{7,9},{8,4},{9,7},... | collective-permute-start | bytes 49160 | tf_op jit(solution)/shard_map/ppermute | solution.py:27
  24.5 3.6 %collective-permute-done.4 = f32[32,128]{1,0:T(8,128)S(1)} collective-permute-done((f32[32,128]{1,0:T(8,128)S(1)}, f32[32,128]{1,0:T(8,128)S(1)}, u32[]{:S(2)}, u32[]{:S(2)}) %collective-permute-start.4) | collective-permute-done | bytes 16416 | tf_op jit(solution)/shard_map/ppermute | solution.py:27
  31.4 4.4 %reshape.43 = bf16[16,8,64,2,32]{4,3,2,1,0:T(2,128)(2,1)} reshape(bf16[16,8,4096]{2,1,0:T(8,128)(2,1)S(1)} %copy-done.17) | data formatting | bytes 2097152 | tf_op jit(solution)/shard_map/reshape | solution.py:447
  35.8 11.2 %copy.30 = bf16[16,2,64,8,32]{2,1,4,3,0:T(2,128)(2,1)} copy(bf16[16,2,64,8,32]{4,1,2,3,0:T(2,128)(2,1)} %bitcast.15) | data formatting | bytes 2097152 | tf_op jit(solution)/shard_map/transpose | solution.py:448
  47.0 4.7 %reshape.44 = bf16[16,128,256]{1,2,0:T(8,128)(2,1)} reshape(bf16[16,2,64,8,32]{2,1,4,3,0:T(2,128)(2,1)} %copy.30) | data formatting | bytes 2097152 | tf_op jit(solution)/shard_map/reshape | solution.py:448
  57.9 17.2 %own_tiles.1 = (bf16[49,512,512]{2,1,0:T(8,128)(2,1)S(1)}, f32[17,64,512]{2,1,0:T(8,128)S(1)}) custom-call(s32[1]{0:T(128)} %bitcast.pos_ref, s32[16,3]{1,0:T(8,128)S(1)} %copy.36.near_ref, f32[32,8192]{1,0:T(8,128)S(1)} %copy-done.8, bf16[16,64,512]{2,1,0:T(8,128)(2,1)S(1)} %copy-done.16), custom_call_target="tpu_custom_call" | custom-call | flops 5368709120 | tf_op jit(solution)/shard_map/own_tiles/pallas_call | solution.py:376
  75.2 8.5 %copy-done = bf16[49,512,512]{2,1,0:T(8,128)(2,1)} copy-done((bf16[49,512,512]{2,1,0:T(8,128)(2,1)}, bf16[49,512,512]{2,1,0:T(8,128)(2,1)S(1)}, u32[]{:S(2)}) %copy-start) | copy-done | bytes 25690136
  85.1 8.3 %copy-done.1 = bf16[49,512,512]{2,1,0:T(8,128)(2,1)S(1)} copy-done((bf16[49,512,512]{2,1,0:T(8,128)(2,1)S(1)}, bf16[49,512,512]{2,1,0:T(8,128)(2,1)}, u32[]{:S(2)}) %copy-start.1) | copy-done | bytes 25690136
  95.3 18.3 %first_product.1 = (bf16[49,512,512]{2,1,0:T(8,128)(2,1)S(1)}, f32[17,64,512]{2,1,0:T(8,128)S(1)}, f32[64,8192]{1,0:T(8,128)S(1)}, bf16[16,64,512]{2,1,0:T(8,128...) custom-call(s32[1]{0:T(128)} %bitcast.pos_ref, ...), custom_call_target="tpu_custom_call", output_to_operand_aliasing={{0}: (20, {}), {1}: (21, {})} | custom-call | flops 2684354560 | tf_op jit(solution)/shard_map/first_product/pallas_call | solution.py:376
  113.6 8.5 %copy-done.2 = bf16[49,512,512]{2,1,0:T(8,128)(2,1)} copy-done((bf16[49,512,512]{2,1,0:T(8,128)(2,1)}, bf16[49,512,512]{2,1,0:T(8,128)(2,1)S(1)}, u32[]{:S(2)}) %copy-start.2) | copy-done | bytes 25690136
  125.0 4.9 %collective-permute-start.16 = (bf16[8,64,512]{2,1,0:T(8,128)(2,1)S(1)}, bf16[8,64,512]{2,1,0:T(8,128)(2,1)S(1)}, u32[]{:S(2)}, u32[]{:S(2)}) collective-permute-start(bf16[8,64,512]{2,1,0:T(8,128)(2,1)S(1)} %get-tuple-element.36), channel_id=1, source_target_pairs={{0,1},{1,0},{2,3},{3,2},{4,5},{5,4},{6,7},{7,6},{8,9},{9,8},{10,11... | collective-permute-start | bytes 1572872 | tf_op jit(solution)/shard_map/ppermute | solution.py:27
  130.6 5.4 %collective-permute-start.14 = (f32[32,128]{1,0:T(8,128)S(1)}, f32[32,128]{1,0:T(8,128)S(1)}, u32[]{:S(2)}, u32[]{:S(2)}) collective-permute-start(f32[32,128]{1,0:T(8,128)S(1)} %get-tuple-element.35), channel_id=1, source_target_pairs={{0,12},{1,15},{2,14},{3,13},{4,8},{5,11},{6,10},{7,9},{8,4},{9,7},... | collective-permute-start | bytes 49160 | tf_op jit(solution)/shard_map/ppermute | solution.py:27
  136.0 7.6 %collective-permute-done.14 = f32[32,128]{1,0:T(8,128)S(1)} collective-permute-done((f32[32,128]{1,0:T(8,128)S(1)}, f32[32,128]{1,0:T(8,128)S(1)}, u32[]{:S(2)}, u32[]{:S(2)}) %collective-permute-start.14) | collective-permute-done | bytes 16416 | tf_op jit(solution)/shard_map/ppermute | solution.py:27
  144.1 4.1 %collective-permute-done.13 = f32[32,128]{1,0:T(8,128)S(1)} collective-permute-done((f32[32,128]{1,0:T(8,128)S(1)}, f32[32,128]{1,0:T(8,128)S(1)}, u32[]{:S(2)}, u32[]{:S(2)}) %collective-permute-start.13) | collective-permute-done | bytes 16416 | tf_op jit(solution)/shard_map/ppermute | solution.py:27
  148.2 8.3 %copy-done.3 = bf16[49,512,512]{2,1,0:T(8,128)(2,1)S(1)} copy-done((bf16[49,512,512]{2,1,0:T(8,128)(2,1)S(1)}, bf16[49,512,512]{2,1,0:T(8,128)(2,1)}, u32[]{:S(2)}) %copy-start.3) | copy-done | bytes 25690136
  156.5 6.9 %own_again.1.near_in = f32[17,64,512]{2,1,0:T(8,128)S(1)} custom-call(s32[1]{0:T(128)} %bitcast.pos_ref, s32[16,3]{1,0:T(8,128)S(1)} %copy.36.near_ref, bf16[16,64,512]{2,1,0:T(8,128)(2,1)S(1)} %get-tuple-element.40.v_ref, bf16[49,512,512]{2,1,0:T(8,128)(2,1)S(1)} %copy-done.3), custom_call_target="tpu_custom_call" | custom-call | flops 1073741824 | tf_op jit(solution)/shard_map/own_again/pallas_call | solution.py:376
  163.5 8.3 %copy-done.4 = bf16[49,512,512]{2,1,0:T(8,128)(2,1)S(1)} copy-done((bf16[49,512,512]{2,1,0:T(8,128)(2,1)S(1)}, bf16[49,512,512]{2,1,0:T(8,128)(2,1)}, u32[]{:S(2)}) %copy-start.4) | copy-done | bytes 25690136
  171.8 10.1 %second_product.1 = (f32[17,64,512]{2,1,0:T(8,128)S(1)}, f32[64,8192]{1,0:T(8,128)S(1)}, f32[64,128]{1,0:T(8,128)S(1)}) custom-call(s32[1]{0:T(128)} %bitcast.pos_ref, s32[16,3]{1,0:T(8,128)S(1)} %copy.36.near_ref, s32[16,8]{1,0:T(8,128)S(1)} %copy.37.far_ref, f32[64,8192]{1,0:T(8,128)S(1)} %copy-done.5, ...), custom_call_target="tpu_custom_call", output_to_operand_aliasing={{0}: (19, {})} | custom-call | flops 536870912 | tf_op jit(solution)/shard_map/second_product/pallas_call | solution.py:376
  183.3 3.9 %collective-permute-done.23 = f32[64,128]{1,0:T(8,128)S(1)} collective-permute-done((f32[64,128]{1,0:T(8,128)S(1)}, f32[64,128]{1,0:T(8,128)S(1)}, u32[]{:S(2)}, u32[]{:S(2)}) %collective-permute-start.23) | collective-permute-done | bytes 32800 | tf_op jit(solution)/shard_map/ppermute | solution.py:27
  188.3 2.9 %collective-permute-done.24 = f32[64,128]{1,0:T(8,128)S(1)} collective-permute-done((f32[64,128]{1,0:T(8,128)S(1)}, f32[64,128]{1,0:T(8,128)S(1)}, u32[]{:S(2)}, u32[]{:S(2)}) %collective-permute-start.24) | collective-permute-done | bytes 32800 | tf_op jit(solution)/shard_map/ppermute | solution.py:27
  192.1 3.9 %collective-permute-done.25 = f32[64,128]{1,0:T(8,128)S(1)} collective-permute-done((f32[64,128]{1,0:T(8,128)S(1)}, f32[64,128]{1,0:T(8,128)S(1)}, u32[]{:S(2)}, u32[]{:S(2)}) %collective-permute-start.25) | collective-permute-done | bytes 32800 | tf_op jit(solution)/shard_map/ppermute | solution.py:27
  196.2 2.8 %multiply_add_fusion = (f32[64,8192]{1,0:T(8,128)}, f32[64,8192]{1,0:T(8,128)}) fusion(f32[64,8192]{1,0:T(8,128)S(1)} %get-tuple-element.43, f32[64,8192]{1,0:T(8,128)S(1)} %copy-done.5, f32[64,8192]{1,0:T(8,128)S(1)} %get-tuple-element.32.u_ref, f32[64]{0:T(128)S(1)} %get-tuple-element.56, f32[64]{0:T(128)S(1)} %get-tuple-element.55, f32[8192]{0:T(1024)S(1)} %copy-done.10), kind=kLoop, calls=%fused_computation | loop fusion | flops 4194304 | bytes 10519040 | tf_op jit(solution)/shard_map/add | solution.py:516
  (97 shorter events, 31.5 us)
Async XLA Ops:
  3.1 52.3 %collective-permute-start.1 = (f32[32,4096]{1,0:T(8,128)}, f32[32,4096]{1,0:T(8,128)}, u32[]{:S(2)}, u32[]{:S(2)}) collective-permute-start(f32[32,4096]{1,0:T(8,128)} %get-tuple-element.59), channel_id=1, source_target_pairs={{1,2},{2,1},{3,4},{4,3},{5,6},{6,5},{7,8},{8,7},{9,10},{10,9},{11,... | collective-permute-start | bytes 1572872 | tf_op jit(solution)/shard_map/ppermute | solution.py:27
  11.9 4.5 %collective-permute-start.2 = (bf16[608,128]{1,0:T(8,128)(2,1)S(1)}, bf16[608,128]{1,0:T(8,128)(2,1)S(1)}, u32[]{:S(2)}, u32[]{:S(2)}) collective-permute-start(bf16[608,128]{1,0:T(8,128)(2,1)S(1)} %get-tuple-element.23.own_ref), channel_id=1, source_target_pairs={{0,1},{1,0},{2,3},{3,2},{4,5},{5,4},{6,7},{7,6},{8,9},{9,8},{10,11... | collective-permute-start | bytes 466952 | tf_op jit(solution)/shard_map/ppermute | solution.py:27
  17.2 12.4 %collective-permute-start.9 = (bf16[2,512,128]{2,1,0:T(8,128)(2,1)}, bf16[2,512,128]{2,1,0:T(8,128)(2,1)}, u32[]{:S(2)}, u32[]{:S(2)}) collective-permute-start(bf16[2,512,128]{2,1,0:T(8,128)(2,1)} %get-tuple-element.28), channel_id=1, source_target_pairs={{1,4},{3,6},{4,1},{5,8},{6,3},{7,10},{8,5},{9,12},{10,7},{11,14},{... | collective-permute-start | bytes 786440 | tf_op jit(solution)/shard_map/ppermute | solution.py:27
  18.5 9.6 %collective-permute-start.4 = (f32[32,128]{1,0:T(8,128)S(1)}, f32[32,128]{1,0:T(8,128)S(1)}, u32[]{:S(2)}, u32[]{:S(2)}) collective-permute-start(f32[32,128]{1,0:T(8,128)S(1)} %get-tuple-element.25), channel_id=1, source_target_pairs={{0,12},{1,15},{2,14},{3,13},{4,8},{5,11},{6,10},{7,9},{8,4},{9,7},... | collective-permute-start | bytes 49160 | tf_op jit(solution)/shard_map/ppermute | solution.py:27
  23.2 5.0 %collective-permute-start.3 = (f32[32,128]{1,0:T(8,128)S(1)}, f32[32,128]{1,0:T(8,128)S(1)}, u32[]{:S(2)}, u32[]{:S(2)}) collective-permute-start(f32[32,128]{1,0:T(8,128)S(1)} %get-tuple-element.25), channel_id=1, source_target_pairs={{0,8},{1,11},{2,10},{3,9},{4,12},{5,15},{6,14},{7,13},{8,0},{9,3},... | collective-permute-start | bytes 49160 | tf_op jit(solution)/shard_map/ppermute | solution.py:27
  23.2 30.1 %collective-permute-start.8 = (bf16[2,512,128]{2,1,0:T(8,128)(2,1)}, bf16[2,512,128]{2,1,0:T(8,128)(2,1)}, u32[]{:S(2)}, u32[]{:S(2)}) collective-permute-start(bf16[2,512,128]{2,1,0:T(8,128)(2,1)} %get-tuple-element.28), channel_id=1, source_target_pairs={{1,2},{2,1},{3,4},{4,3},{5,6},{6,5},{7,8},{8,7},{9,10},{10,9},{11,... | collective-permute-start | bytes 786440 | tf_op jit(solution)/shard_map/ppermute | solution.py:27
  28.2 55.4 %collective-permute-start = (f32[32,4096]{1,0:T(8,128)}, f32[32,4096]{1,0:T(8,128)}, u32[]{:S(2)}, u32[]{:S(2)}) collective-permute-start(f32[32,4096]{1,0:T(8,128)} %get-tuple-element.60), channel_id=1, source_target_pairs={{0,1},{1,0},{2,3},{3,2},{4,5},{5,4},{6,7},{7,6},{8,9},{9,8},{10,11... | collective-permute-start | bytes 1572872 | tf_op jit(solution)/shard_map/ppermute | solution.py:27
  29.4 54.3 %collective-permute-start.6 = (bf16[8,64,512]{2,1,0:T(8,128)(2,1)}, bf16[8,64,512]{2,1,0:T(8,128)(2,1)}, u32[]{:S(2)}, u32[]{:S(2)}) collective-permute-start(bf16[8,64,512]{2,1,0:T(8,128)(2,1)} %get-tuple-element.26), channel_id=1, source_target_pairs={{0,1},{1,0},{2,3},{3,2},{4,5},{5,4},{6,7},{7,6},{8,9},{9,8},{10,11... | collective-permute-start | bytes 1572872 | tf_op jit(solution)/shard_map/ppermute | solution.py:27
  29.6 54.1 %collective-permute-start.7 = (bf16[8,64,512]{2,1,0:T(8,128)(2,1)}, bf16[8,64,512]{2,1,0:T(8,128)(2,1)}, u32[]{:S(2)}, u32[]{:S(2)}) collective-permute-start(bf16[8,64,512]{2,1,0:T(8,128)(2,1)} %get-tuple-element.27), channel_id=1, source_target_pairs={{1,2},{2,1},{3,4},{4,3},{5,6},{6,5},{7,8},{8,7},{9,10},{10,9},{11,... | collective-permute-start | bytes 1572872 | tf_op jit(solution)/shard_map/ppermute | solution.py:27
  53.2 30.4 %collective-permute-start.11 = (bf16[2,512,128]{2,1,0:T(8,128)(2,1)}, bf16[2,512,128]{2,1,0:T(8,128)(2,1)S(1)}, u32[]{:S(2)}, u32[]{:S(2)}) collective-permute-start(bf16[2,512,128]{2,1,0:T(8,128)(2,1)} %collective-permute-done.9.c1), channel_id=1, source_target_pairs={{0,1},{1,0},{2,3},{3,2},{4,5},{5,4},{6,7},{7,6},{8,9},{9,8},{10,11... | collective-permute-start | bytes 786440 | tf_op jit(solution)/shard_map/ppermute | solution.py:27
  55.4 29.0 %collective-permute-start.10 = (bf16[2,512,128]{2,1,0:T(8,128)(2,1)}, bf16[2,512,128]{2,1,0:T(8,128)(2,1)S(1)}, u32[]{:S(2)}, u32[]{:S(2)}) collective-permute-start(bf16[2,512,128]{2,1,0:T(8,128)(2,1)} %collective-permute-done.8.c0), channel_id=1, source_target_pairs={{0,1},{1,0},{2,3},{3,2},{4,5},{5,4},{6,7},{7,6},{8,9},{9,8},{10,11... | collective-permute-start | bytes 786440 | tf_op jit(solution)/shard_map/ppermute | solution.py:27
  122.1 1.5 collective-permute-start.12
  123.6 19.9 %collective-permute-start.19 = (bf16[2,512,128]{2,1,0:T(8,128)(2,1)S(1)}, bf16[2,512,128]{2,1,0:T(8,128)(2,1)S(1)}, u32[]{:S(2)}, u32[]{:S(2)}) collective-permute-start(bf16[2,512,128]{2,1,0:T(8,128)(2,1)S(1)} %get-tuple-element.38), channel_id=1, source_target_pairs={{1,4},{3,6},{4,1},{5,8},{6,3},{7,10},{8,5},{9,12},{10,7},{11,14},{... | collective-permute-start | bytes 786440 | tf_op jit(solution)/shard_map/ppermute | solution.py:27
  124.3 19.3 %collective-permute-start.18 = (bf16[2,512,128]{2,1,0:T(8,128)(2,1)S(1)}, bf16[2,512,128]{2,1,0:T(8,128)(2,1)S(1)}, u32[]{:S(2)}, u32[]{:S(2)}) collective-permute-start(bf16[2,512,128]{2,1,0:T(8,128)(2,1)S(1)} %get-tuple-element.38), channel_id=1, source_target_pairs={{1,2},{2,1},{3,4},{4,3},{5,6},{6,5},{7,8},{8,7},{9,10},{10,9},{11,... | collective-permute-start | bytes 786440 | tf_op jit(solution)/shard_map/ppermute | solution.py:27
  125.0 38.4 %collective-permute-start.16 = (bf16[8,64,512]{2,1,0:T(8,128)(2,1)S(1)}, bf16[8,64,512]{2,1,0:T(8,128)(2,1)S(1)}, u32[]{:S(2)}, u32[]{:S(2)}) collective-permute-start(bf16[8,64,512]{2,1,0:T(8,128)(2,1)S(1)} %get-tuple-element.36), channel_id=1, source_target_pairs={{0,1},{1,0},{2,3},{3,2},{4,5},{5,4},{6,7},{7,6},{8,9},{9,8},{10,11... | collective-permute-start | bytes 1572872 | tf_op jit(solution)/shard_map/ppermute | solution.py:27
  129.9 33.6 %collective-permute-start.17 = (bf16[8,64,512]{2,1,0:T(8,128)(2,1)S(1)}, bf16[8,64,512]{2,1,0:T(8,128)(2,1)S(1)}, u32[]{:S(2)}, u32[]{:S(2)}) collective-permute-start(bf16[8,64,512]{2,1,0:T(8,128)(2,1)S(1)} %get-tuple-element.37), channel_id=1, source_target_pairs={{1,2},{2,1},{3,4},{4,3},{5,6},{6,5},{7,8},{8,7},{9,10},{10,9},{11,... | collective-permute-start | bytes 1572872 | tf_op jit(solution)/shard_map/ppermute | solution.py:27
  130.6 13.0 %collective-permute-start.14 = (f32[32,128]{1,0:T(8,128)S(1)}, f32[32,128]{1,0:T(8,128)S(1)}, u32[]{:S(2)}, u32[]{:S(2)}) collective-permute-start(f32[32,128]{1,0:T(8,128)S(1)} %get-tuple-element.35), channel_id=1, source_target_pairs={{0,12},{1,15},{2,14},{3,13},{4,8},{5,11},{6,10},{7,9},{8,4},{9,7},... | collective-permute-start | bytes 49160 | tf_op jit(solution)/shard_map/ppermute | solution.py:27
  143.5 4.6 %collective-permute-start.13 = (f32[32,128]{1,0:T(8,128)S(1)}, f32[32,128]{1,0:T(8,128)S(1)}, u32[]{:S(2)}, u32[]{:S(2)}) collective-permute-start(f32[32,128]{1,0:T(8,128)S(1)} %get-tuple-element.35), channel_id=1, source_target_pairs={{0,8},{1,11},{2,10},{3,9},{4,12},{5,15},{6,14},{7,13},{8,0},{9,3},... | collective-permute-start | bytes 49160 | tf_op jit(solution)/shard_map/ppermute | solution.py:27
  143.5 19.9 %collective-permute-start.21 = (bf16[2,512,128]{2,1,0:T(8,128)(2,1)S(1)}, bf16[2,512,128]{2,1,0:T(8,128)(2,1)S(1)}, u32[]{:S(2)}, u32[]{:S(2)}) collective-permute-start(bf16[2,512,128]{2,1,0:T(8,128)(2,1)S(1)} %collective-permute-done.19.c1), channel_id=1, source_target_pairs={{0,1},{1,0},{2,3},{3,2},{4,5},{5,4},{6,7},{7,6},{8,9},{9,8},{10,11... | collective-permute-start | bytes 786440 | tf_op jit(solution)/shard_map/ppermute | solution.py:27
  143.6 19.9 %collective-permute-start.20 = (bf16[2,512,128]{2,1,0:T(8,128)(2,1)S(1)}, bf16[2,512,128]{2,1,0:T(8,128)(2,1)S(1)}, u32[]{:S(2)}, u32[]{:S(2)}) collective-permute-start(bf16[2,512,128]{2,1,0:T(8,128)(2,1)S(1)} %collective-permute-done.18.c0), channel_id=1, source_target_pairs={{0,1},{1,0},{2,3},{3,2},{4,5},{5,4},{6,7},{7,6},{8,9},{9,8},{10,11... | collective-permute-start | bytes 786440 | tf_op jit(solution)/shard_map/ppermute | solution.py:27
  148.2 15.2 %collective-permute-start.15 = (f32[1,32,128]{2,1,0:T(8,128)S(1)}, f32[1,32,128]{2,1,0:T(8,128)S(1)}, u32[]{:S(2)}, u32[]{:S(2)}) collective-permute-start(f32[1,32,128]{2,1,0:T(8,128)S(1)} %add_bitcast_fusion.sum_a), channel_id=1, source_target_pairs={{0,1},{1,0},{2,3},{3,2},{4,5},{5,4},{6,7},{7,6},{8,9},{9,8},{10,11... | collective-permute-start | bytes 49160 | tf_op jit(solution)/shard_map/ppermute | solution.py:27
  183.3 3.9 %collective-permute-start.23 = (f32[64,128]{1,0:T(8,128)S(1)}, f32[64,128]{1,0:T(8,128)S(1)}, u32[]{:S(2)}, u32[]{:S(2)}) collective-permute-start(f32[64,128]{1,0:T(8,128)S(1)} %add.66), channel_id=1, source_target_pairs={{0,2},{1,3},{2,0},{3,1},{4,6},{5,7},{6,4},{7,5},{8,10},{9,11},{10,... | collective-permute-start | bytes 98312 | tf_op jit(solution)/shard_map/ppermute | solution.py:27
  187.3 3.9 %collective-permute-start.24 = (f32[64,128]{1,0:T(8,128)S(1)}, f32[64,128]{1,0:T(8,128)S(1)}, u32[]{:S(2)}, u32[]{:S(2)}) collective-permute-start(f32[64,128]{1,0:T(8,128)S(1)} %add.67), channel_id=1, source_target_pairs={{0,4},{1,5},{2,6},{3,7},{4,0},{5,1},{6,2},{7,3},{8,12},{9,13},{10,... | collective-permute-start | bytes 98312 | tf_op jit(solution)/shard_map/ppermute | solution.py:27
  191.2 4.8 %collective-permute-start.25 = (f32[64,128]{1,0:T(8,128)S(1)}, f32[64,128]{1,0:T(8,128)S(1)}, u32[]{:S(2)}, u32[]{:S(2)}) collective-permute-start(f32[64,128]{1,0:T(8,128)S(1)} %add.68), channel_id=1, source_target_pairs={{0,8},{1,9},{2,10},{3,11},{4,12},{5,13},{6,14},{7,15},{8,0},{9,1},... | collective-permute-start | bytes 98312 | tf_op jit(solution)/shard_map/ppermute | solution.py:27
  (24 other events, 229.1 us)

commit v3 on v2

--- a/solution.py
+++ b/solution.py
@@ -15,9 +15,10 @@
 F32 = jnp.float32
 BF16 = jnp.bfloat16
 HALF_SCALE = math.sqrt(2.0 * KERNEL_SCALE * math.log2(math.e))
-UNROLL = 2
-VMEM_LIMIT = 12 * 1024 * 1024
+UNROLL = 4
+VMEM_LIMIT = 8 * 1024 * 1024
 WHOLE = pl.BlockSpec(memory_space=pltpu.VMEM)
+ANYWHERE = pl.BlockSpec(memory_space=pl.ANY)
 SCALAR = pl.BlockSpec(memory_space=pltpu.SMEM)
 
 
@@ -90,9 +91,12 @@
     return jnp.concatenate([block[:half], block[half:]], axis=1)
 
 
-def leaf_coefficients(basis, rounded, trans):
+def store_coefficients(basis, rounded, at, cp_ref, coefs):
     coef = dot(basis, rounded, 1, 1).astype(BF16)
-    return pack_pair(coef), dot(trans, coef, 0, 0)
+    rank = coef.shape[0]
+    coefs[pl.ds(pl.multiple_of(at * rank, rank), rank)] = coef
+    size = rank // 2
+    cp_ref[pl.ds(pl.multiple_of(at * size, size), size)] = pack_pair(coef)
 
 
 def columns_of(ref, at, width):
@@ -108,35 +112,79 @@
     lax.fori_loop(0, count // unroll, trip, 0)
 
 
-def send_margins(v_ref, mx_ref, mo_ref, odd):
+def store_share(trans_ref, coefs, part_ref, cp_ref):
+    per, rank, _ = trans_ref.shape
+    packed = pack_pair(dot(trans_ref[...].reshape(per * rank, rank), coefs[...], 0, 0))
+    part_ref[...] = packed
+    size = packed.shape[0]
+    rows = per * size
+    for at, piece in enumerate(split3(packed)):
+        cp_ref[rows + at * size : rows + (at + 1) * size] = piece
+
+
+def relayout_kernel(coup_ref, out_ref, by_slot, by_row):
+    per, slots, flat = coup_ref.shape
+    rank = out_ref.shape[1] // 2
+    quarter = rank // 2
+    pairs = flat // 128
+    lane = lax.broadcasted_iota(jnp.int32, (pairs, 128), 1) // quarter
+
+    def one(l, carry):
+        wide = coup_ref[l].astype(F32)
+        for k in range(pairs):
+            by_slot[k * slots : (k + 1) * slots] = wide[:, k * 128 : (k + 1) * 128]
+        rows = [by_slot[pl.ds(s, pairs, stride=slots)] for s in range(slots)]
+        turned = [[rows[s] if t == 0 else pltpu.roll(rows[s], t * quarter, 1) for t in range(4)] for s in range(slots)]
+        for half in range(2):
+            for parity in range(2):
+                chunk = 2 * parity + half
+                for group in range(slots // 4):
+                    out = turned[4 * group][(0 - chunk) % 4]
+                    for r in range(1, 4):
+                        out = jnp.where(lane == r, turned[4 * group + r][(r - chunk) % 4], out)
+                    by_row[half, group, pl.ds(parity, pairs, stride=2)] = out
+        for half in range(2):
+            for group in range(slots // 4):
+                out_ref[l, half * rank : (half + 1) * rank, group * 128 : (group + 1) * 128] = by_row[half, group].astype(BF16)
+        return carry
+
+    lax.fori_loop(0, per, one, 0)
+
+
+def margins_kernel(pos_ref, e_ref, ex_ref, eo_ref, sems):
+    odd = pos_ref[0] % 2
+    width = ex_ref.shape[1]
+    first = pltpu.make_async_copy(
+        e_ref.at[:, pl.ds(pl.multiple_of((1 - odd) * width, width), width)], ex_ref, sems.at[0]
+    )
+    second = pltpu.make_async_copy(
+        e_ref.at[:, pl.ds(pl.multiple_of(odd * width, width), width)], eo_ref, sems.at[1]
+    )
+    first.start()
+    second.start()
+    first.wait()
+    second.wait()
+
+
+def prep_kernel(rs_ref, sc_ref, basis_ref, trans_ref, ex_ref, eo_ref, v_ref, cp_ref, part_ref, coefs):
+    per, rank, leaf = basis_ref.shape
+
+    def one(at):
+        rounded = (columns_of(rs_ref, at, leaf) * columns_of(sc_ref, at, leaf)).astype(BF16)
+        v_ref[at] = rounded
+        store_coefficients(basis_ref[at], rounded, at, cp_ref, coefs)
+
+    leaf_loop(per, UNROLL, one)
+    store_share(trans_ref, coefs, part_ref, cp_ref)
+
+
+def send_kernel(pos_ref, v_ref, a_ref, b_ref, *rest):
+    mx_ref, mo_ref, sum_ref = rest[-3:]
+    odd = pos_ref[0] % 2
     half = mx_ref.shape[0]
     mx_ref[...] = v_ref[pl.ds(half * (1 - odd), half)]
     mo_ref[...] = v_ref[pl.ds(half * odd, half)]
-
-
-def store_share(total, part_ref, cp_ref, rows):
-    packed = pack_pair(total)
-    part_ref[...] = packed
-    size = packed.shape[0]
-    for at, piece in enumerate(split3(packed)):
-        cp_ref[rows + at * size : rows + (at + 1) * size] = piece
-
-
-def prep_kernel(pos_ref, rs_ref, sc_ref, basis_ref, trans_ref, v_ref, mx_ref, mo_ref, cp_ref, part_ref, acc):
-    per, rank, leaf = basis_ref.shape
-    size = rank // 2
-    acc[...] = jnp.zeros_like(acc)
-
-    def one(at):
-        rounded = (columns_of(rs_ref, at, leaf) * columns_of(sc_ref, at, leaf)).astype(BF16)
-        packed, share = leaf_coefficients(basis_ref[at], rounded, trans_ref[at])
-        v_ref[at] = rounded
-        cp_ref[pl.ds(pl.multiple_of(at * size, size), size)] = packed
-        acc[...] += share
-
-    leaf_loop(per, UNROLL, one)
-    store_share(acc[...], part_ref, cp_ref, per * size)
-    send_margins(v_ref, mx_ref, mo_ref, pos_ref[0] % 2)
+    sum_ref[...] = a_ref[...] + b_ref[...]
 
 
 def pair_kernel(pos_ref, own_ref, got_ref, part_ref, pair_ref, sum_ref):
@@ -163,7 +211,8 @@
         return n + jnp.where(own == want_own, 1, 0)
 
     n = lax.fori_loop(0, total, put, 0)
-    list_ref[n] = total
+    for u in range(UNROLL):
+        list_ref[n + u] = total
     return n
 
 
@@ -188,46 +237,51 @@
     target[pl.ds(half * odd, half)] = from_beside[...]
 
 
-def own_kernel(pos_ref, near_ref, e_ref, v_ref, tile_ref, near_out, list_ref):
+def self_kernel(e_ref, v_ref, self_ref, near_out):
+    per, _, leaf = v_ref.shape
+
+    def one(at):
+        points = columns_of(e_ref, at, leaf)
+        tile = tile_of(other_rows(points), own_rows(points))
+        self_ref[at] = tile
+        near_out[at] = dot(v_ref[at], tile, 1, 0)
+
+    leaf_loop(per, UNROLL, one)
+
+
+def own_kernel(pos_ref, near_ref, e_ref, v_ref, near_in, tile_ref, near_out, list_ref):
     per, _, leaf = v_ref.shape
     half = per // 2
     pos = pos_ref[0]
-
-    def one(at):
-        points = columns_of(e_ref, at, leaf)
-        tile = tile_of(other_rows(points), own_rows(points))
-        tile_ref[at] = tile
-        near_out[at] = dot(v_ref[at], tile, 1, 0)
-
-    leaf_loop(per, UNROLL, one)
     n = list_entries(near_ref, list_ref, pos, half, True)
 
     def trip(i, carry):
         for u in range(UNROLL):
             entry, leaf_at, row, place = near_entry(near_ref, list_ref, i * UNROLL + u, pos, half, True)
             tile = tile_of(other_rows(columns_of(e_ref, place, leaf)), own_rows(columns_of(e_ref, row, leaf)))
-            tile_ref[per + entry] = tile
+            tile_ref[entry] = tile
             near_out[leaf_at] += dot(v_ref[place], tile, 1, 0)
         return carry
 
     lax.fori_loop(0, (n + UNROLL - 1) // UNROLL, trip, 0)
 
 
-def own_again_kernel(pos_ref, near_ref, v_ref, tile_ref, near_out, list_ref):
-    per, _, leaf = v_ref.shape
-    half = per // 2
+def self_again_kernel(v_ref, self_ref, near_out):
+    def one(at):
+        near_out[at] = dot(v_ref[at], self_ref[at], 1, 0)
+
+    leaf_loop(v_ref.shape[0], UNROLL, one)
+
+
+def own_again_kernel(pos_ref, near_ref, v_ref, tile_ref, near_in, near_out, list_ref):
+    half = v_ref.shape[0] // 2
     pos = pos_ref[0]
-
-    def one(at):
-        near_out[at] = dot(v_ref[at], tile_ref[at], 1, 0)
-
-    leaf_loop(per, UNROLL, one)
     n = list_entries(near_ref, list_ref, pos, half, True)
 
     def trip(i, carry):
         for u in range(UNROLL):
             entry, leaf_at, _, place = near_entry(near_ref, list_ref, i * UNROLL + u, pos, half, True)
-            near_out[leaf_at] += dot(v_ref[place], tile_ref[per + entry], 1, 0)
+            near_out[leaf_at] += dot(v_ref[place], tile_ref[entry], 1, 0)
         return carry
 
     lax.fori_loop(0, (n + UNROLL - 1) // UNROLL, trip, 0)
@@ -276,12 +330,11 @@
 def rest_kernel(
     pos_ref, near_ref, far_ref, e_ref, ex_ref, eo_ref, rs_ref, sc_ref, basis_ref, coup_ref, trans_ref,
     coarse_ref, sum_a, sum_b, vx_ref, vo_ref, c0, c1, c2, c3, tile_in, near_in,
-    tile_ref, near_ref_out, u_ref, q_ref, mx_ref, mo_ref, cp_ref, part_ref, msg_ref,
-    list_ref, vw, cw, fc, acc, acc_uu, acc_ru,
+    tile_ref, near_ref_out, u_ref, q_ref, cp_ref, part_ref, msg_ref,
+    list_ref, vw, cw, fc, coefs, acc_uu, acc_ru,
 ):
     per, rank, leaf = basis_ref.shape
     half = per // 2
-    size = rank // 2
     pos = pos_ref[0]
     odd = pos % 2
     load_halves(vw, vx_ref, vo_ref, odd)
@@ -299,12 +352,11 @@
             far_o = columns_of(eo_ref, within, leaf)
             points = jnp.where(from_x, far_x, far_o)
             tile = tile_of(other_rows(points), own_rows(columns_of(e_ref, row, leaf)))
-            tile_ref[per + entry] = tile
+            tile_ref[entry] = tile
             near_ref_out[leaf_at] += dot(vw[place], tile, 1, 0)
         return carry
 
     lax.fori_loop(0, (n + UNROLL - 1) // UNROLL, trip, 0)
-    acc[...] = jnp.zeros_like(acc)
     acc_uu[...] = jnp.zeros_like(acc_uu)
     acc_ru[...] = jnp.zeros_like(acc_ru)
 
@@ -317,14 +369,11 @@
         acc_uu[...] += image * image
         acc_ru[...] += right * image
         rounded = (image * scale).astype(BF16)
-        packed, share = leaf_coefficients(basis_ref[l], rounded, trans_ref[l])
         q_ref[l] = rounded
-        cp_ref[pl.ds(pl.multiple_of(l * size, size), size)] = packed
-        acc[...] += share
+        store_coefficients(basis_ref[l], rounded, l, cp_ref, coefs)
 
     leaf_loop(per, UNROLL, one)
-    store_share(acc[...], part_ref, cp_ref, per * size)
-    send_margins(q_ref, mx_ref, mo_ref, odd)
+    store_share(trans_ref, coefs, part_ref, cp_ref)
     lane = lax.broadcasted_iota(jnp.int32, msg_ref.shape, 1)
     out = jnp.where(lane == 0, jnp.sum(acc_uu[...], axis=1, keepdims=True), 0.0)
     out = jnp.where(lane == 1, jnp.sum(acc_ru[...], axis=1, keepdims=True), out)
@@ -348,7 +397,7 @@
     def trip(i, carry):
         for u in range(UNROLL):
             entry, leaf_at, _, place = near_entry(near_ref, list_ref, i * UNROLL + u, pos, half, False)
-            near_out[leaf_at] += dot(vw[place], tile_ref[per + entry], 1, 0)
+            near_out[leaf_at] += dot(vw[place], tile_ref[entry], 1, 0)
         return carry
 
     lax.fori_loop(0, (n + UNROLL - 1) // UNROLL, trip, 0)
@@ -386,13 +435,16 @@
     )(*args)
 
 
-def cluster_sums(pair_sum):
+def two_clusters():
+    return CDEV == 8 and lax.axis_size("leaf") == 2 * CDEV
+
+
+def cluster_addends(pair_sum):
     count = lax.axis_size("leaf")
-    if count == 2 * CDEV and CDEV == 8:
+    if two_clusters():
         first = involution(pair_sum, lambda i: i ^ (8 + 2 * (i % 2)))
         second = involution(pair_sum, lambda i: i ^ (12 + 2 * (i % 2)))
-        mine = (first + second)[None]
-        return mine, sibling(mine)
+        return first[None], second[None]
     mask = 2
     while mask < CDEV:
         pair_sum = pair_sum + involution(pair_sum, lambda i: i ^ mask)
@@ -404,20 +456,28 @@
     return sums[1:], jnp.zeros_like(sums[1:])
 
 
-def exchange(position, cp, part, mx, mo):
+def exchange(position, cp, part, v, meanwhile):
+    per, columns, leaf = v.shape
     rows = cp.shape[0] - 3 * part.shape[0]
     got = sibling(cp)
     pair, pair_sum = call(
         pair_kernel, "pair", [SCALAR] + [WHOLE] * 3,
-        [pltpu.VMEM((2, rows, cp.shape[1]), BF16), jax.ShapeDtypeStruct(part.shape, F32)],
+        [pltpu.VMEM((2, rows, cp.shape[1]), BF16), pltpu.VMEM(part.shape, F32)],
         [], (position, cp, got, part),
     )
     near_pair = beside(pair)
     far_pair = two_chips(pair)
-    sums = cluster_sums(pair_sum)
-    vx = sibling(mx)
-    vo = beside(mo)
-    return vx, vo, (near_pair, far_pair, sibling(near_pair), sibling(far_pair)), sums
+    first, second = cluster_addends(pair_sum)
+    near = meanwhile()
+    half_shape = pltpu.VMEM((per // 2, columns, leaf), BF16)
+    mx, mo, mine = call(
+        send_kernel, "send", [SCALAR] + [WHOLE] * 3 + [ANYWHERE] * 3,
+        [half_shape, half_shape, pltpu.VMEM(first.shape, F32)],
+        [], (position, v, first, second, near_pair, far_pair, near),
+    )
+    other = sibling(mine) if two_clusters() else jnp.zeros_like(mine)
+    coefs = (near_pair, far_pair, sibling(near_pair), sibling(far_pair))
+    return sibling(mx), beside(mo), coefs, (mine, other), near
 
 
 def body(
@@ -434,31 +494,39 @@
     size = rank // 2
     count = lax.axis_size("leaf")
     pos = lax.axis_index("leaf")
-    odd = pos % 2
     position = pos.reshape(1).astype(jnp.int32)
     cluster = pos // CDEV
     coarse_count = count // CDEV
 
-    e_sibling = sibling(lax.dynamic_slice_in_dim(embeddings, (1 - odd) * margin, margin, 1))
-    e_beside = beside(lax.dynamic_slice_in_dim(embeddings, odd * margin, margin, 1))
+    margin_shape = pltpu.VMEM((features, margin), F32)
+    ex, eo = call(
+        margins_kernel, "margins", [SCALAR, ANYWHERE], [margin_shape] * 2,
+        [pltpu.SemaphoreType.DMA((2,))], (position, embeddings),
+    )
+    e_sibling = sibling(ex)
+    e_beside = beside(eo)
 
     scale_row = scaling.reshape(1, local_points)
     trans = transfer.reshape(per, rank, rank)
-    coup = leaf_coupling.reshape(per, far_count, rank, 2, rank // 2)
-    coup = coup.transpose(0, 3, 2, 1, 4).reshape(per, 2 * rank, far_count * rank // 2)
+    (coup,) = call(
+        relayout_kernel, "relayout", [WHOLE],
+        [pltpu.VMEM((per, 2 * rank, far_count * size), BF16)],
+        [pltpu.VMEM((far_count * rank * rank // 128, 128), F32), pltpu.VMEM((2, far_count // 4, rank, 128), F32)],
+        (leaf_coupling,),
+    )
     row = lax.dynamic_index_in_dim(coarse_coupling, cluster, 0, keepdims=False)
     order = jnp.arange(1, coarse_count, dtype=jnp.int32) ^ cluster
     coarse = jnp.take(row, order, axis=0).reshape(coarse_count - 1, rank, rank)
 
     leaf_shape = pltpu.VMEM((per, columns, leaf), BF16)
-    half_shape = pltpu.VMEM((half, columns, leaf), BF16)
     cp_shape = pltpu.VMEM((per * size + 3 * size, 2 * columns), BF16)
     part_shape = pltpu.VMEM((size, 2 * columns), F32)
-    tile_shape = pltpu.VMEM((per * (1 + slots) + 1, leaf, leaf), BF16)
+    self_shape = pltpu.VMEM((per, leaf, leaf), BF16)
+    tile_shape = pltpu.VMEM((per * slots + 1, leaf, leaf), BF16)
     near_shape = pltpu.VMEM((per + 1, columns, leaf), F32)
     wide_shape = pltpu.VMEM((columns, local_points), F32)
     msg_shape = pltpu.VMEM((columns, 128), F32)
-    share_acc = pltpu.VMEM((rank, columns), F32)
+    coefs_shape = pltpu.VMEM((per * rank, columns), BF16)
     acc_shape = pltpu.VMEM((columns, leaf), F32)
     list_shape = pltpu.SMEM((per * slots + UNROLL,), jnp.int32)
     window = [
@@ -467,28 +535,46 @@
         pltpu.VMEM((rank, 3 * columns), BF16),
     ]
 
-    v, mx, mo, cp, part = call(
-        prep_kernel, "prep", [SCALAR] + [WHOLE] * 4,
-        [leaf_shape, half_shape, half_shape, cp_shape, part_shape], [share_acc],
-        (position, right_side, scale_row, leaf_basis, trans),
-    )
-    vx, vo, coefs, sums = exchange(position, cp, part, mx, mo)
+    v, cp, part = call(
+        prep_kernel, "prep", [WHOLE] * 4 + [ANYWHERE] * 2, [leaf_shape, cp_shape, part_shape], [coefs_shape],
+        (right_side, scale_row, leaf_basis, trans, ex, eo),
+    )
+    kept = []
+
+    def self_tiles():
+        tself, near = call(
+            self_kernel, "self_tiles", [WHOLE] * 2, [self_shape, near_shape], [], (embeddings, v),
+            flops=2 * per * leaf * leaf * 320,
+        )
+        kept.append(tself)
+        return near
+
+    vx, vo, coefs, sums, near = exchange(position, cp, part, v, self_tiles)
+    (tself,) = kept
     tiles, near = call(
-        own_kernel, "own_tiles", [SCALAR] * 2 + [WHOLE] * 2, [tile_shape, near_shape], [list_shape],
-        (position, near_leaves, embeddings, v), flops=2 * 32 * leaf * leaf * 320,
-    )
-    tiles, _, image, q, mx, mo, cp, part, msg = call(
+        own_kernel, "own_tiles", [SCALAR] * 2 + [WHOLE] * 3, [tile_shape, near_shape], [list_shape],
+        (position, near_leaves, embeddings, v, near), aliases={4: 1}, flops=2 * per * leaf * leaf * 320,
+    )
+    tiles, _, image, q, cp, part, msg = call(
         rest_kernel, "first_product", [SCALAR] * 3 + [WHOLE] * 19,
-        [tile_shape, near_shape, wide_shape, leaf_shape, half_shape, half_shape, cp_shape, part_shape, msg_shape],
-        [list_shape] + window + [share_acc, acc_shape, acc_shape],
+        [tile_shape, near_shape, wide_shape, leaf_shape, cp_shape, part_shape, msg_shape],
+        [list_shape] + window + [coefs_shape, acc_shape, acc_shape],
         (position, near_leaves, far_leaves, embeddings, e_sibling, e_beside, right_side, scale_row,
          leaf_basis, coup, trans, coarse, *sums, vx, vo, *coefs, tiles, near),
-        aliases={20: 0, 21: 1}, flops=2 * 16 * leaf * leaf * 320,
-    )
-    vx, vo, coefs, sums = exchange(position, cp, part, mx, mo)
+        aliases={20: 0, 21: 1}, flops=2 * per * leaf * leaf * 320,
+    )
+
+    def self_products():
+        (near,) = call(
+            self_again_kernel, "self_again", [WHOLE] * 2, [near_shape], [], (q, tself),
+            flops=2 * per * leaf * leaf * 64,
+        )
+        return near
+
+    vx, vo, coefs, sums, near = exchange(position, cp, part, q, self_products)
     (near,) = call(
-        own_again_kernel, "own_again", [SCALAR] * 2 + [WHOLE] * 2, [near_shape], [list_shape],
-        (position, near_leaves, q, tiles), flops=2 * 32 * leaf * leaf * 64,
+        own_again_kernel, "own_again", [SCALAR] * 2 + [WHOLE] * 3, [near_shape], [list_shape],
+        (position, near_leaves, q, tiles, near), aliases={4: 0}, flops=2 * per * leaf * leaf * 64,
     )
     _, second, msg = call(
         rest_again_kernel, "second_product", [SCALAR] * 3 + [WHOLE] * 18,
@@ -496,7 +582,7 @@
         [list_shape] + window + [acc_shape] * 3,
         (position, near_leaves, far_leaves, right_side, scale_row, image, leaf_basis, coup, trans,
          coarse, *sums, vx, vo, *coefs, tiles, near, msg),
-        aliases={19: 0}, flops=2 * 16 * leaf * leaf * 64,
+        aliases={19: 0}, flops=2 * per * leaf * leaf * 64,
     )
 
     mask = 1

time: 200 us -> 136 us (0.68)
  local copies, waits for them, and re-layouts: 74.6 us -> 14.9 us
  waiting for transfers between devices: 29.6 us -> 12.1 us
  starting transfers between devices: 32.8 us -> 48.8 us
  Pallas kernels: 57.9 us -> 54.2 us
    unnamed x46 -> x50, local copies, waits for them, and re-layouts: 50 us -> 12.9 us
    ppermute x26, waiting for transfers between devices: 29.6 us -> 12.1 us  [involution(): return lax.ppermute(value, 'leaf', pairs)]
    ppermute x26, starting transfers between devices: 32.8 us -> 48.8 us  [involution(): return lax.ppermute(value, 'leaf', pairs)]
    transpose x1 -> x0, local copies, waits for them, and re-layouts: 11.2 us -> none  [body(): coup.transpose(0, 3, 2, 1, 4).reshape(per, 2 * rank, far_count * rank // 2)]
    reshape x3 -> x0, local copies, waits for them, and re-layouts: 10.6 us -> none  [the longest x2 6.22 us: body(): coup.transpose(0, 3, 2, 1, 4).reshape(per, 2 * rank, far_count * rank // 2)]
    pallas_call x7 -> x13, Pallas kernels: 57.9 us -> 54.2 us  [call(): pl.pallas_call(kernel, in_specs=in_specs, out_specs=[WHOLE] * len(out_sha...]
    dynamic_slice x1 -> x0, local copies, waits for them, and re-layouts: 2.45 us -> none  [body(): lax.dynamic_slice_in_dim(embeddings, odd * margin, margin, 1)]
  transfers between devices with their start and end apart: 26 -> 26, of which waited for: 10 -> 9; matrix products, arithmetic and copies ran while one was open for 11% -> 3% of each run, Pallas kernels for 15% -> 16%
where the time goes in v3:
time: 136 us
  Pallas kernels  54.2 us (40%)
  starting transfers between devices  48.8 us (36%)
  local copies, waits for them, and re-layouts  14.9 us (11%)
  waiting for transfers between devices  12.1 us (9%)
  other arithmetic  4.53 us (3%)
    pallas_call x13, Pallas kernels, call(): pl.pallas_call(kernel, in_specs=in_specs, out_specs=[WHOLE] * len(out_sha...  54.2 us
    ppermute x26, starting transfers between devices, involution(): return lax.ppermute(value, 'leaf', pairs)  48.8 us
    unnamed x50, local copies, waits for them, and re-layouts  12.9 us
    ppermute x26, waiting for transfers between devices, involution(): return lax.ppermute(value, 'leaf', pairs)  12.1 us
    add x1, other arithmetic, body(): residual = right_side - first_weight * image + second_weight * second  2.92 us
  transfers between devices with their start and end apart: 26, of which 9 were waited for; matrix products, arithmetic and copies ran while one was open for 3% of the time, Pallas kernels for 16%

profile of v3, /device:TPU:0, one launch (start us, length us, event | category | flops | bytes accessed | tf_op | source)
XLA Modules:
  0.0 135.6 jit_solution(7485711789568081707)
XLA Ops:
  12.2 4.2 %collective-permute-start = (f32[32,4096]{1,0:T(8,128)S(1)}, f32[32,4096]{1,0:T(8,128)S(1)}, u32[]{:S(2)}, u32[]{:S(2)}) collective-permute-start(f32[32,4096]{1,0:T(8,128)S(1)} %get-tuple-element.29.ex_ref), channel_id=1, source_target_pairs={{0,1},{1,0},{2,3},{3,2},{4,5},{5,4},{6,7},{7,6},{8,9},{9,8},{10,11... | collective-permute-start | bytes 1572872 | tf_op jit(solution)/shard_map/ppermute | solution.py:28
  16.4 4.6 %collective-permute-start.4 = (f32[32,128]{1,0:T(8,128)S(1)}, f32[32,128]{1,0:T(8,128)S(1)}, u32[]{:S(2)}, u32[]{:S(2)}) collective-permute-start(f32[32,128]{1,0:T(8,128)S(1)} %get-tuple-element.34), channel_id=1, source_target_pairs={{0,12},{1,15},{2,14},{3,13},{4,8},{5,11},{6,10},{7,9},{8,4},{9,7},... | collective-permute-start | bytes 49160 | tf_op jit(solution)/shard_map/ppermute | solution.py:28
  21.1 5.9 %self_tiles.1 = (bf16[16,512,512]{2,1,0:T(8,128)(2,1)S(1)}, f32[17,64,512]{2,1,0:T(8,128)S(1)}) custom-call(f32[32,8192]{1,0:T(8,128)S(1)} %copy-done.5, bf16[16,64,512]{2,1,0:T(8,128)(2,1)S(1)} %get-tuple-element.31.v_ref), custom_call_target="tpu_custom_call" | custom-call | flops 2684354560 | tf_op jit(solution)/shard_map/self_tiles/pallas_call | solution.py:425
  27.0 3.3 %copy-done.3 = bf16[16,512,512]{2,1,0:T(8,128)(2,1)} copy-done((bf16[16,512,512]{2,1,0:T(8,128)(2,1)}, bf16[16,512,512]{2,1,0:T(8,128)(2,1)S(1)}, u32[]{:S(2)}) %copy-start.3) | copy-done | bytes 8388632
  30.3 1.6 %collective-permute-start.1 = (f32[32,4096]{1,0:T(8,128)}, f32[32,4096]{1,0:T(8,128)}, u32[]{:S(2)}, u32[]{:S(2)}) collective-permute-start(f32[32,4096]{1,0:T(8,128)} %get-tuple-element.30.eo_ref), channel_id=1, source_target_pairs={{1,2},{2,1},{3,4},{4,3},{5,6},{6,5},{7,8},{8,7},{9,10},{10,9},{11,... | collective-permute-start | bytes 1572872 | tf_op jit(solution)/shard_map/ppermute | solution.py:28
  35.2 2.6 %collective-permute-start.7 = (f32[1,32,128]{2,1,0:T(8,128)S(1)}, f32[1,32,128]{2,1,0:T(8,128)S(1)}, u32[]{:S(2)}, u32[]{:S(2)}) collective-permute-start(f32[1,32,128]{2,1,0:T(8,128)S(1)} %get-tuple-element.37.sum_a), channel_id=1, source_target_pairs={{0,1},{1,0},{2,3},{3,2},{4,5},{5,4},{6,7},{7,6},{8,9},{9,8},{10,11... | collective-permute-start | bytes 49160 | tf_op jit(solution)/shard_map/ppermute | solution.py:28
  45.9 3.2 %relayout.1.coup_ref = bf16[16,128,256]{2,1,0:T(8,128)(2,1)S(1)} custom-call(bf16[16,8,4096]{2,1,0:T(8,128)(2,1)S(1)} %copy-done.7), custom_call_target="tpu_custom_call" | custom-call | tf_op jit(solution)/shard_map/relayout/pallas_call | solution.py:425
  49.8 7.3 %own_tiles.1 = (bf16[33,512,512]{2,1,0:T(8,128)(2,1)S(1)}, f32[17,64,512]{2,1,0:T(8,128)S(1)}) custom-call(s32[1]{0:T(128)} %bitcast.pos_ref, s32[16,3]{1,0:T(8,128)S(1)} %copy-done.14, f32[32,8192]{1,0:T(8,128)S(1)} %copy-done.6, bf16[16,64,512]{2,1,0:T(8,128)(2,1)S(1)} %copy-done.9, ...), custom_call_target="tpu_custom_call", output_to_operand_aliasing={{1}: (4, {})} | custom-call | flops 2684354560 | tf_op jit(solution)/shard_map/own_tiles/pallas_call | solution.py:425
  57.3 19.1 %first_product.1 = (bf16[33,512,512]{2,1,0:T(8,128)(2,1)S(1)}, f32[17,64,512]{2,1,0:T(8,128)S(1)}, f32[64,8192]{1,0:T(8,128)S(1)}, bf16[16,64,512]{2,1,0:T(8,128...) custom-call(s32[1]{0:T(128)} %bitcast.pos_ref, ...), custom_call_target="tpu_custom_call", output_to_operand_aliasing={{0}: (20, {}), {1}: (21, {})} | custom-call | flops 2684354560 | tf_op jit(solution)/shard_map/first_product/pallas_call | solution.py:425
  79.3 7.1 %collective-permute-start.14 = (f32[32,128]{1,0:T(8,128)S(1)}, f32[32,128]{1,0:T(8,128)S(1)}, u32[]{:S(2)}, u32[]{:S(2)}) collective-permute-start(f32[32,128]{1,0:T(8,128)S(1)} %get-tuple-element.46), channel_id=1, source_target_pairs={{0,12},{1,15},{2,14},{3,13},{4,8},{5,11},{6,10},{7,9},{8,4},{9,7},... | collective-permute-start | bytes 49160 | tf_op jit(solution)/shard_map/ppermute | solution.py:28
  86.3 1.6 %collective-permute-start.13 = (f32[32,128]{1,0:T(8,128)S(1)}, f32[32,128]{1,0:T(8,128)S(1)}, u32[]{:S(2)}, u32[]{:S(2)}) collective-permute-start(f32[32,128]{1,0:T(8,128)S(1)} %get-tuple-element.46), channel_id=1, source_target_pairs={{0,8},{1,11},{2,10},{3,9},{4,12},{5,15},{6,14},{7,13},{8,0},{9,3},... | collective-permute-start | bytes 49160 | tf_op jit(solution)/shard_map/ppermute | solution.py:28
  88.0 1.9 %self_again.1.rest_2_.near_in = f32[17,64,512]{2,1,0:T(8,128)S(1)} custom-call(bf16[16,64,512]{2,1,0:T(8,128)(2,1)S(1)} %get-tuple-element.43.v_ref, bf16[16,512,512]{2,1,0:T(8,128)(2,1)S(1)} %bitcast.10), custom_call_target="tpu_custom_call" | custom-call | flops 536870912 | tf_op jit(solution)/shard_map/self_again/pallas_call | solution.py:425
  89.9 2.1 %collective-permute-done.14 = f32[32,128]{1,0:T(8,128)S(1)} collective-permute-done((f32[32,128]{1,0:T(8,128)S(1)}, f32[32,128]{1,0:T(8,128)S(1)}, u32[]{:S(2)}, u32[]{:S(2)}) %collective-permute-start.14) | collective-permute-done | bytes 16416 | tf_op jit(solution)/shard_map/ppermute | solution.py:28
  93.5 2.2 %collective-permute-start.21 = (bf16[2,512,128]{2,1,0:T(8,128)(2,1)S(1)}, bf16[2,512,128]{2,1,0:T(8,128)(2,1)S(1)}, u32[]{:S(2)}, u32[]{:S(2)}) collective-permute-start(bf16[2,512,128]{2,1,0:T(8,128)(2,1)S(1)} %collective-permute-done.16.rest_1_.c1), channel_id=1, source_target_pairs={{0,1},{1,0},{2,3},{3,2},{4,5},{5,4},{6,7},{7,6},{8,9},{9,8},{10,11... | collective-permute-start | bytes 786440 | tf_op jit(solution)/shard_map/ppermute | solution.py:28
  96.3 3.1 %own_again.1.near_in = f32[17,64,512]{2,1,0:T(8,128)S(1)} custom-call(s32[1]{0:T(128)} %bitcast.pos_ref, s32[16,3]{1,0:T(8,128)S(1)} %copy-done.15, bf16[16,64,512]{2,1,0:T(8,128)(2,1)S(1)} %get-tuple-element.43.v_ref, bf16[33,512,512]{2,1,0:T(8,128)(2,1)S(1)} %get-tuple-element.52.tile_ref, ...), custom_call_target="tpu_custom_call", output_to_operand_aliasing={{}: (4, {})} | custom-call | flops 536870912 | tf_op jit(solution)/shard_map/own_again/pallas_call | solution.py:425
  99.5 10.2 %second_product.1 = (f32[17,64,512]{2,1,0:T(8,128)S(1)}, f32[64,8192]{1,0:T(8,128)S(1)}, f32[64,128]{1,0:T(8,128)S(1)}) custom-call(s32[1]{0:T(128)} %bitcast.pos_ref, s32[16,3]{1,0:T(8,128)S(1)} %copy-done.15, s32[16,8]{1,0:T(8,128)S(1)} %copy-done.16, f32[64,8192]{1,0:T(8,128)S(1)} %copy-done.1, ...), custom_call_target="tpu_custom_call", output_to_operand_aliasing={{0}: (19, {})} | custom-call | flops 536870912 | tf_op jit(solution)/shard_map/second_product/pallas_call | solution.py:425
  109.6 8.5 %collective-permute-start.22 = (f32[64,128]{1,0:T(8,128)S(1)}, f32[64,128]{1,0:T(8,128)S(1)}, u32[]{:S(2)}, u32[]{:S(2)}) collective-permute-start(f32[64,128]{1,0:T(8,128)S(1)} %get-tuple-element.54), channel_id=1, source_target_pairs={{0,1},{1,0},{2,3},{3,2},{4,5},{5,4},{6,7},{7,6},{8,9},{9,8},{10,11... | collective-permute-start | bytes 98312 | tf_op jit(solution)/shard_map/ppermute | solution.py:28
  119.0 1.8 %collective-permute-start.23 = (f32[64,128]{1,0:T(8,128)S(1)}, f32[64,128]{1,0:T(8,128)S(1)}, u32[]{:S(2)}, u32[]{:S(2)}) collective-permute-start(f32[64,128]{1,0:T(8,128)S(1)} %add.45), channel_id=1, source_target_pairs={{0,2},{1,3},{2,0},{3,1},{4,6},{5,7},{6,4},{7,5},{8,10},{9,11},{10,... | collective-permute-start | bytes 98312 | tf_op jit(solution)/shard_map/ppermute | solution.py:28
  120.7 2.2 %collective-permute-done.23 = f32[64,128]{1,0:T(8,128)S(1)} collective-permute-done((f32[64,128]{1,0:T(8,128)S(1)}, f32[64,128]{1,0:T(8,128)S(1)}, u32[]{:S(2)}, u32[]{:S(2)}) %collective-permute-start.23) | collective-permute-done | bytes 32800 | tf_op jit(solution)/shard_map/ppermute | solution.py:28
  122.9 2.8 %collective-permute-start.24 = (f32[64,128]{1,0:T(8,128)S(1)}, f32[64,128]{1,0:T(8,128)S(1)}, u32[]{:S(2)}, u32[]{:S(2)}) collective-permute-start(f32[64,128]{1,0:T(8,128)S(1)} %add.46), channel_id=1, source_target_pairs={{0,4},{1,5},{2,6},{3,7},{4,0},{5,1},{6,2},{7,3},{8,12},{9,13},{10,... | collective-permute-start | bytes 98312 | tf_op jit(solution)/shard_map/ppermute | solution.py:28
  125.7 1.9 %collective-permute-done.24 = f32[64,128]{1,0:T(8,128)S(1)} collective-permute-done((f32[64,128]{1,0:T(8,128)S(1)}, f32[64,128]{1,0:T(8,128)S(1)}, u32[]{:S(2)}, u32[]{:S(2)}) %collective-permute-start.24) | collective-permute-done | bytes 32800 | tf_op jit(solution)/shard_map/ppermute | solution.py:28
  127.6 2.8 %collective-permute-start.25 = (f32[64,128]{1,0:T(8,128)S(1)}, f32[64,128]{1,0:T(8,128)S(1)}, u32[]{:S(2)}, u32[]{:S(2)}) collective-permute-start(f32[64,128]{1,0:T(8,128)S(1)} %add.47), channel_id=1, source_target_pairs={{0,8},{1,9},{2,10},{3,11},{4,12},{5,13},{6,14},{7,15},{8,0},{9,1},... | collective-permute-start | bytes 98312 | tf_op jit(solution)/shard_map/ppermute | solution.py:28
  130.4 2.1 %collective-permute-done.25 = f32[64,128]{1,0:T(8,128)S(1)} collective-permute-done((f32[64,128]{1,0:T(8,128)S(1)}, f32[64,128]{1,0:T(8,128)S(1)}, u32[]{:S(2)}, u32[]{:S(2)}) %collective-permute-start.25) | collective-permute-done | bytes 32800 | tf_op jit(solution)/shard_map/ppermute | solution.py:28
  132.6 2.9 %multiply_add_fusion = (f32[64,8192]{1,0:T(8,128)}, f32[64,8192]{1,0:T(8,128)}) fusion(f32[64,8192]{1,0:T(8,128)S(1)} %get-tuple-element.55, f32[64,8192]{1,0:T(8,128)S(1)} %copy-done.1, f32[64,8192]{1,0:T(8,128)S(1)} %get-tuple-element.42.u_ref, f32[64]{0:T(128)S(1)} %get-tuple-element.68, f32[64]{0:T(128)S(1)} %get-tuple-element.67, f32[8192]{0:T(1024)S(1)} %copy-done.13), kind=kLoop, calls=%fused_computation | loop fusion | flops 4194304 | bytes 10519040 | tf_op jit(solution)/shard_map/add | solution.py:602
  (101 shorter events, 29.6 us)
Async XLA Ops:
  9.5 22.4 %collective-permute-start.6 = (bf16[2,512,128]{2,1,0:T(8,128)(2,1)S(1)}, bf16[2,512,128]{2,1,0:T(8,128)(2,1)}, u32[]{:S(2)}, u32[]{:S(2)}) collective-permute-start(bf16[2,512,128]{2,1,0:T(8,128)(2,1)S(1)} %get-tuple-element.35), channel_id=1, source_target_pairs={{1,4},{3,6},{4,1},{5,8},{6,3},{7,10},{8,5},{9,12},{10,7},{11,14},{... | collective-permute-start | bytes 786440 | tf_op jit(solution)/shard_map/ppermute | solution.py:28
  10.8 21.1 %collective-permute-start.5 = (bf16[2,512,128]{2,1,0:T(8,128)(2,1)S(1)}, bf16[2,512,128]{2,1,0:T(8,128)(2,1)}, u32[]{:S(2)}, u32[]{:S(2)}) collective-permute-start(bf16[2,512,128]{2,1,0:T(8,128)(2,1)S(1)} %get-tuple-element.35), channel_id=1, source_target_pairs={{1,2},{2,1},{3,4},{4,3},{5,6},{6,5},{7,8},{8,7},{9,10},{10,9},{11,... | collective-permute-start | bytes 786440 | tf_op jit(solution)/shard_map/ppermute | solution.py:28
  12.2 27.3 %collective-permute-start = (f32[32,4096]{1,0:T(8,128)S(1)}, f32[32,4096]{1,0:T(8,128)S(1)}, u32[]{:S(2)}, u32[]{:S(2)}) collective-permute-start(f32[32,4096]{1,0:T(8,128)S(1)} %get-tuple-element.29.ex_ref), channel_id=1, source_target_pairs={{0,1},{1,0},{2,3},{3,2},{4,5},{5,4},{6,7},{7,6},{8,9},{9,8},{10,11... | collective-permute-start | bytes 1572872 | tf_op jit(solution)/shard_map/ppermute | solution.py:28
  16.4 13.9 %collective-permute-start.4 = (f32[32,128]{1,0:T(8,128)S(1)}, f32[32,128]{1,0:T(8,128)S(1)}, u32[]{:S(2)}, u32[]{:S(2)}) collective-permute-start(f32[32,128]{1,0:T(8,128)S(1)} %get-tuple-element.34), channel_id=1, source_target_pairs={{0,12},{1,15},{2,14},{3,13},{4,8},{5,11},{6,10},{7,9},{8,4},{9,7},... | collective-permute-start | bytes 49160 | tf_op jit(solution)/shard_map/ppermute | solution.py:28
  21.1 10.8 %collective-permute-start.3 = (f32[32,128]{1,0:T(8,128)S(1)}, f32[32,128]{1,0:T(8,128)S(1)}, u32[]{:S(2)}, u32[]{:S(2)}) collective-permute-start(f32[32,128]{1,0:T(8,128)S(1)} %get-tuple-element.34), channel_id=1, source_target_pairs={{0,8},{1,11},{2,10},{3,9},{4,12},{5,15},{6,14},{7,13},{8,0},{9,3},... | collective-permute-start | bytes 49160 | tf_op jit(solution)/shard_map/ppermute | solution.py:28
  30.3 26.8 %collective-permute-start.1 = (f32[32,4096]{1,0:T(8,128)}, f32[32,4096]{1,0:T(8,128)}, u32[]{:S(2)}, u32[]{:S(2)}) collective-permute-start(f32[32,4096]{1,0:T(8,128)} %get-tuple-element.30.eo_ref), channel_id=1, source_target_pairs={{1,2},{2,1},{3,4},{4,3},{5,6},{6,5},{7,8},{8,7},{9,10},{10,9},{11,... | collective-permute-start | bytes 1572872 | tf_op jit(solution)/shard_map/ppermute | solution.py:28
  33.0 24.2 %collective-permute-start.8 = (bf16[8,64,512]{2,1,0:T(8,128)(2,1)}, bf16[8,64,512]{2,1,0:T(8,128)(2,1)}, u32[]{:S(2)}, u32[]{:S(2)}) collective-permute-start(bf16[8,64,512]{2,1,0:T(8,128)(2,1)} %get-tuple-element.38), channel_id=1, source_target_pairs={{0,1},{1,0},{2,3},{3,2},{4,5},{5,4},{6,7},{7,6},{8,9},{9,8},{10,11... | collective-permute-start | bytes 1572872 | tf_op jit(solution)/shard_map/ppermute | solution.py:28
  33.7 23.5 %collective-permute-start.9 = (bf16[8,64,512]{2,1,0:T(8,128)(2,1)}, bf16[8,64,512]{2,1,0:T(8,128)(2,1)}, u32[]{:S(2)}, u32[]{:S(2)}) collective-permute-start(bf16[8,64,512]{2,1,0:T(8,128)(2,1)} %get-tuple-element.39), channel_id=1, source_target_pairs={{1,2},{2,1},{3,4},{4,3},{5,6},{6,5},{7,8},{8,7},{9,10},{10,9},{11,... | collective-permute-start | bytes 1572872 | tf_op jit(solution)/shard_map/ppermute | solution.py:28
  35.2 3.4 %collective-permute-start.7 = (f32[1,32,128]{2,1,0:T(8,128)S(1)}, f32[1,32,128]{2,1,0:T(8,128)S(1)}, u32[]{:S(2)}, u32[]{:S(2)}) collective-permute-start(f32[1,32,128]{2,1,0:T(8,128)S(1)} %get-tuple-element.37.sum_a), channel_id=1, source_target_pairs={{0,1},{1,0},{2,3},{3,2},{4,5},{5,4},{6,7},{7,6},{8,9},{9,8},{10,11... | collective-permute-start | bytes 49160 | tf_op jit(solution)/shard_map/ppermute | solution.py:28
  39.2 18.0 %collective-permute-start.11 = (bf16[2,512,128]{2,1,0:T(8,128)(2,1)}, bf16[2,512,128]{2,1,0:T(8,128)(2,1)}, u32[]{:S(2)}, u32[]{:S(2)}) collective-permute-start(bf16[2,512,128]{2,1,0:T(8,128)(2,1)} %collective-permute-done.6.rest_1_.c1), channel_id=1, source_target_pairs={{0,1},{1,0},{2,3},{3,2},{4,5},{5,4},{6,7},{7,6},{8,9},{9,8},{10,11... | collective-permute-start | bytes 786440 | tf_op jit(solution)/shard_map/ppermute | solution.py:28
  40.3 16.8 %collective-permute-start.10 = (bf16[2,512,128]{2,1,0:T(8,128)(2,1)}, bf16[2,512,128]{2,1,0:T(8,128)(2,1)}, u32[]{:S(2)}, u32[]{:S(2)}) collective-permute-start(bf16[2,512,128]{2,1,0:T(8,128)(2,1)} %collective-permute-done.5.rest_0_.c0), channel_id=1, source_target_pairs={{0,1},{1,0},{2,3},{3,2},{4,5},{5,4},{6,7},{7,6},{8,9},{9,8},{10,11... | collective-permute-start | bytes 786440 | tf_op jit(solution)/shard_map/ppermute | solution.py:28
  77.9 14.8 %collective-permute-start.16 = (bf16[2,512,128]{2,1,0:T(8,128)(2,1)S(1)}, bf16[2,512,128]{2,1,0:T(8,128)(2,1)S(1)}, u32[]{:S(2)}, u32[]{:S(2)}) collective-permute-start(bf16[2,512,128]{2,1,0:T(8,128)(2,1)S(1)} %get-tuple-element.47), channel_id=1, source_target_pairs={{1,4},{3,6},{4,1},{5,8},{6,3},{7,10},{8,5},{9,12},{10,7},{11,14},{... | collective-permute-start | bytes 786440 | tf_op jit(solution)/shard_map/ppermute | solution.py:28
  78.6 14.1 %collective-permute-start.15 = (bf16[2,512,128]{2,1,0:T(8,128)(2,1)S(1)}, bf16[2,512,128]{2,1,0:T(8,128)(2,1)S(1)}, u32[]{:S(2)}, u32[]{:S(2)}) collective-permute-start(bf16[2,512,128]{2,1,0:T(8,128)(2,1)S(1)} %get-tuple-element.47), channel_id=1, source_target_pairs={{1,2},{2,1},{3,4},{4,3},{5,6},{6,5},{7,8},{8,7},{9,10},{10,9},{11,... | collective-permute-start | bytes 786440 | tf_op jit(solution)/shard_map/ppermute | solution.py:28
  79.3 12.7 %collective-permute-start.14 = (f32[32,128]{1,0:T(8,128)S(1)}, f32[32,128]{1,0:T(8,128)S(1)}, u32[]{:S(2)}, u32[]{:S(2)}) collective-permute-start(f32[32,128]{1,0:T(8,128)S(1)} %get-tuple-element.46), channel_id=1, source_target_pairs={{0,12},{1,15},{2,14},{3,13},{4,8},{5,11},{6,10},{7,9},{8,4},{9,7},... | collective-permute-start | bytes 49160 | tf_op jit(solution)/shard_map/ppermute | solution.py:28
  86.3 6.3 %collective-permute-start.13 = (f32[32,128]{1,0:T(8,128)S(1)}, f32[32,128]{1,0:T(8,128)S(1)}, u32[]{:S(2)}, u32[]{:S(2)}) collective-permute-start(f32[32,128]{1,0:T(8,128)S(1)} %get-tuple-element.46), channel_id=1, source_target_pairs={{0,8},{1,11},{2,10},{3,9},{4,12},{5,15},{6,14},{7,13},{8,0},{9,3},... | collective-permute-start | bytes 49160 | tf_op jit(solution)/shard_map/ppermute | solution.py:28
  92.8 6.7 %collective-permute-start.18 = (bf16[8,64,512]{2,1,0:T(8,128)(2,1)S(1)}, bf16[8,64,512]{2,1,0:T(8,128)(2,1)S(1)}, u32[]{:S(2)}, u32[]{:S(2)}) collective-permute-start(bf16[8,64,512]{2,1,0:T(8,128)(2,1)S(1)} %get-tuple-element.50), channel_id=1, source_target_pairs={{0,1},{1,0},{2,3},{3,2},{4,5},{5,4},{6,7},{7,6},{8,9},{9,8},{10,11... | collective-permute-start | bytes 1572872 | tf_op jit(solution)/shard_map/ppermute | solution.py:28
  92.8 6.6 %collective-permute-start.19 = (bf16[8,64,512]{2,1,0:T(8,128)(2,1)S(1)}, bf16[8,64,512]{2,1,0:T(8,128)(2,1)S(1)}, u32[]{:S(2)}, u32[]{:S(2)}) collective-permute-start(bf16[8,64,512]{2,1,0:T(8,128)(2,1)S(1)} %get-tuple-element.51), channel_id=1, source_target_pairs={{1,2},{2,1},{3,4},{4,3},{5,6},{6,5},{7,8},{8,7},{9,10},{10,9},{11,... | collective-permute-start | bytes 1572872 | tf_op jit(solution)/shard_map/ppermute | solution.py:28
  93.5 5.9 %collective-permute-start.21 = (bf16[2,512,128]{2,1,0:T(8,128)(2,1)S(1)}, bf16[2,512,128]{2,1,0:T(8,128)(2,1)S(1)}, u32[]{:S(2)}, u32[]{:S(2)}) collective-permute-start(bf16[2,512,128]{2,1,0:T(8,128)(2,1)S(1)} %collective-permute-done.16.rest_1_.c1), channel_id=1, source_target_pairs={{0,1},{1,0},{2,3},{3,2},{4,5},{5,4},{6,7},{7,6},{8,9},{9,8},{10,11... | collective-permute-start | bytes 786440 | tf_op jit(solution)/shard_map/ppermute | solution.py:28
  95.8 3.7 %collective-permute-start.20 = (bf16[2,512,128]{2,1,0:T(8,128)(2,1)S(1)}, bf16[2,512,128]{2,1,0:T(8,128)(2,1)S(1)}, u32[]{:S(2)}, u32[]{:S(2)}) collective-permute-start(bf16[2,512,128]{2,1,0:T(8,128)(2,1)S(1)} %collective-permute-done.15.rest_0_.c0), channel_id=1, source_target_pairs={{0,1},{1,0},{2,3},{3,2},{4,5},{5,4},{6,7},{7,6},{8,9},{9,8},{10,11... | collective-permute-start | bytes 786440 | tf_op jit(solution)/shard_map/ppermute | solution.py:28
  95.9 3.6 %collective-permute-start.17 = (f32[1,32,128]{2,1,0:T(8,128)S(1)}, f32[1,32,128]{2,1,0:T(8,128)S(1)}, u32[]{:S(2)}, u32[]{:S(2)}) collective-permute-start(f32[1,32,128]{2,1,0:T(8,128)S(1)} %get-tuple-element.49.sum_a), channel_id=1, source_target_pairs={{0,1},{1,0},{2,3},{3,2},{4,5},{5,4},{6,7},{7,6},{8,9},{9,8},{10,11... | collective-permute-start | bytes 49160 | tf_op jit(solution)/shard_map/ppermute | solution.py:28
  109.6 9.4 %collective-permute-start.22 = (f32[64,128]{1,0:T(8,128)S(1)}, f32[64,128]{1,0:T(8,128)S(1)}, u32[]{:S(2)}, u32[]{:S(2)}) collective-permute-start(f32[64,128]{1,0:T(8,128)S(1)} %get-tuple-element.54), channel_id=1, source_target_pairs={{0,1},{1,0},{2,3},{3,2},{4,5},{5,4},{6,7},{7,6},{8,9},{9,8},{10,11... | collective-permute-start | bytes 98312 | tf_op jit(solution)/shard_map/ppermute | solution.py:28
  119.0 3.9 %collective-permute-start.23 = (f32[64,128]{1,0:T(8,128)S(1)}, f32[64,128]{1,0:T(8,128)S(1)}, u32[]{:S(2)}, u32[]{:S(2)}) collective-permute-start(f32[64,128]{1,0:T(8,128)S(1)} %add.45), channel_id=1, source_target_pairs={{0,2},{1,3},{2,0},{3,1},{4,6},{5,7},{6,4},{7,5},{8,10},{9,11},{10,... | collective-permute-start | bytes 98312 | tf_op jit(solution)/shard_map/ppermute | solution.py:28
  122.9 4.7 %collective-permute-start.24 = (f32[64,128]{1,0:T(8,128)S(1)}, f32[64,128]{1,0:T(8,128)S(1)}, u32[]{:S(2)}, u32[]{:S(2)}) collective-permute-start(f32[64,128]{1,0:T(8,128)S(1)} %add.46), channel_id=1, source_target_pairs={{0,4},{1,5},{2,6},{3,7},{4,0},{5,1},{6,2},{7,3},{8,12},{9,13},{10,... | collective-permute-start | bytes 98312 | tf_op jit(solution)/shard_map/ppermute | solution.py:28
  127.6 4.8 %collective-permute-start.25 = (f32[64,128]{1,0:T(8,128)S(1)}, f32[64,128]{1,0:T(8,128)S(1)}, u32[]{:S(2)}, u32[]{:S(2)}) collective-permute-start(f32[64,128]{1,0:T(8,128)S(1)} %add.47), channel_id=1, source_target_pairs={{0,8},{1,9},{2,10},{3,11},{4,12},{5,13},{6,14},{7,15},{8,0},{9,1},... | collective-permute-start | bytes 98312 | tf_op jit(solution)/shard_map/ppermute | solution.py:28
  (26 other events, 186.0 us)

commit v4 on v3

v4 whole, which is shorter than its diff:
```python
import functools
import math

import jax
import jax.numpy as jnp
from jax import lax
from jax.experimental import pallas as pl
from jax.experimental.pallas import tpu as pltpu
from jax.sharding import PartitionSpec as P

FARDEV = 4
CDEV = 8
KERNEL_SCALE = 0.0625
RIDGE_TERM = 1.0
EPSILON = 1e-06
F32 = jnp.float32
BF16 = jnp.bfloat16
HALF_SCALE = math.sqrt(2.0 * KERNEL_SCALE * math.log2(math.e))
UNROLL = 4
FAR_UNROLL = 8
VMEM_LIMIT = 12 * 1024 * 1024
WIDE_LIMIT = 54 * 1024 * 1024
SELF_LIMIT = 28 * 1024 * 1024
WHOLE = pl.BlockSpec(memory_space=pltpu.VMEM)
ANYWHERE = pl.BlockSpec(memory_space=pl.ANY)
OUTSIDE = pl.BlockSpec(memory_space=pltpu.HBM)
SCALAR = pl.BlockSpec(memory_space=pltpu.SMEM)


def involution(value, partner):
    count = lax.axis_size("leaf")
    pairs = [(i, partner(i)) for i in range(count) if 0 <= partner(i) < count]
    return lax.ppermute(value, "leaf", pairs)


def sibling(value):
    return involution(value, lambda i: i ^ 1)


def beside(value):
    return involution(value, lambda i: i + 1 if i % 2 else i - 1)


def across(value):
    return involution(value, lambda i: i ^ 2)


def two_chips(value):
    return involution(value, lambda i: i + 3 if i % 2 else i - 3)


def dot(a, b, ca, cb):
    return lax.dot_general(a, b, (((ca,), (cb,)), ((), ())), preferred_element_type=F32)


def split3(value):
    high = value.astype(BF16)
    rest = value - high.astype(F32)
    mid = rest.astype(BF16)
    low = (rest - mid.astype(F32)).astype(BF16)
    return high, mid, low


def point_pieces(points):
    scaled = points * HALF_SCALE
    high, mid, low = split3(scaled)
    square = 0.5 * jnp.sum(scaled * scaled, axis=0, keepdims=True)
    s_high, s_mid, s_low = split3(square)
    return high, mid, low, s_high.astype(F32), s_mid.astype(F32), s_low.astype(F32)


def norm_rows(first, second, third, width, swap, sign):
    row = lax.broadcasted_iota(jnp.int32, (16, width), 0)
    base = 3 if swap else 0
    ones = 0 if swap else 3
    out = jnp.where((row >= ones) & (row < ones + 3), sign, 0.0)
    for at, piece in enumerate((first, second, third)):
        out = jnp.where(row == base + at, sign * piece, out)
    return out.astype(BF16)


def own_rows(points):
    high, mid, low, a, b, c = point_pieces(points)
    norms = norm_rows(a, b, c, points.shape[1], False, 1.0)
    return jnp.concatenate([high, mid, high, mid, low, high, norms], axis=0)


def other_rows(points):
    high, mid, low, a, b, c = point_pieces(points)
    norms = norm_rows(a, b, c, points.shape[1], True, -1.0)
    return jnp.concatenate([high, high, mid, mid, high, low, norms], axis=0)


def tile_of(other, own):
    return jnp.exp2(dot(other, own, 0, 0)).astype(BF16)


def pack_pair(block):
    half = block.shape[0] // 2
    return jnp.concatenate([block[:half], block[half:]], axis=1)


def lane_groups(value):
    total = value[:, :128]
    for at in range(128, value.shape[1], 128):
        total += value[:, at : at + 128]
    return total


def leaf_coefficients(basis, rounded):
    return dot(basis, rounded, 1, 1).astype(BF16)


def share_of(trans, coefs):
    count, rank, _ = trans.shape
    return dot(trans.reshape(count * rank, rank), coefs, 0, 0)


def columns_of(ref, at, width):
    return ref[:, pl.ds(pl.multiple_of(at * width, width), width)]


def leaf_loop(count, unroll, fn):
    def trip(i, carry):
        for u in range(unroll):
            fn(i * unroll + u)
        return carry

    lax.fori_loop(0, count // unroll, trip, 0)


def store_share(total, part_ref, cp_ref):
    packed = pack_pair(total)
    part_ref[...] = packed
    size = packed.shape[0]
    rows = cp_ref.shape[0] - 3 * size
    for at, piece in enumerate(split3(packed)):
        cp_ref[rows + at * size : rows + (at + 1) * size] = piece


def store_square(flat, target):
    pairs = flat.shape[0]
    target[pl.ds(0, pairs, stride=2)] = flat
    target[pl.ds(1, pairs, stride=2)] = pltpu.roll(flat, 64, 1)


def relayout_kernel(pos_ref, coup_ref, coarse_ref, wait_ref, out_ref, coarse_out, by_slot, by_row, flat, square):
    per, slots, entries = coup_ref.shape
    rank = out_ref.shape[1] // 2
    quarter = rank // 2
    pairs = entries // 128
    lane = lax.broadcasted_iota(jnp.int32, (pairs, 128), 1) // quarter

    def one(l, carry):
        wide = coup_ref[l].astype(F32)
        for k in range(pairs):
            by_slot[k * slots : (k + 1) * slots] = wide[:, k * 128 : (k + 1) * 128]
        rows = [by_slot[pl.ds(s, pairs, stride=slots)] for s in range(slots)]
        turned = [[rows[s] if t == 0 else pltpu.roll(rows[s], t * quarter, 1) for t in range(4)] for s in range(slots)]
        for half in range(2):
            for parity in range(2):
                chunk = 2 * parity + half
                for group in range(slots // 4):
                    out = turned[4 * group][(0 - chunk) % 4]
                    for r in range(1, 4):
                        out = jnp.where(lane == r, turned[4 * group + r][(r - chunk) % 4], out)
                    by_row[half, group, pl.ds(parity, pairs, stride=2)] = out
        for half in range(2):
            for group in range(slots // 4):
                out_ref[l, half * rank : (half + 1) * rank, group * 128 : (group + 1) * 128] = by_row[half, group].astype(BF16)
        return carry

    lax.fori_loop(0, per, one, 0)
    cluster = pos_ref[0] // CDEV
    wide = coarse_ref[cluster].astype(F32)
    number = lax.broadcasted_iota(jnp.int32, wide.shape, 0)
    for at in range(coarse_out.shape[0]):
        row = jnp.sum(jnp.where(number == (cluster ^ (at + 1)), wide, 0.0), axis=0, keepdims=True)
        for k in range(pairs):
            flat[k : k + 1] = row[:, k * 128 : (k + 1) * 128]
        store_square(flat[...], square)
        coarse_out[at] = square[:, :rank].astype(BF16)


def margins_kernel(pos_ref, e_ref, ex_ref, eo_ref, sems):
    odd = pos_ref[0] % 2
    width = ex_ref.shape[1]
    first = pltpu.make_async_copy(
        e_ref.at[:, pl.ds(pl.multiple_of((1 - odd) * width, width), width)], ex_ref, sems.at[0]
    )
    second = pltpu.make_async_copy(
        e_ref.at[:, pl.ds(pl.multiple_of(odd * width, width), width)], eo_ref, sems.at[1]
    )
    first.start()
    second.start()
    first.wait()
    second.wait()


def prep_kernel(
    pos_ref, rs_hbm, sc_hbm, basis_hbm, transfer_hbm, v_ref, cp_ref, part_ref, trans_ref, mx_ref, mo_ref,
    rs_ref, sc_ref, basis_ref, transfer_ref, coefs, by_leaf, squares, sems,
):
    per, rank, leaf = basis_ref.shape
    copies = [
        pltpu.make_async_copy(source, target, sems.at[at])
        for at, (source, target) in enumerate(
            ((transfer_hbm, transfer_ref), (sc_hbm, sc_ref), (rs_hbm, rs_ref), (basis_hbm, basis_ref))
        )
    ]
    for copy in copies:
        copy.start()
    copies[0].wait()
    size = rank // 2
    wide = transfer_ref[...].astype(F32)
    for k in range(rank * rank // 128):
        by_leaf[k * per : (k + 1) * per] = wide[:, k * 128 : (k + 1) * 128]
    for at in range(per):
        store_square(by_leaf[pl.ds(at, rank * rank // 128, stride=per)], squares.at[at])
    trans_ref[...] = squares[:, :, :rank].astype(BF16)
    for copy in copies[1:]:
        copy.wait()

    def one(at):
        rounded = (columns_of(rs_ref, at, leaf) * columns_of(sc_ref, at, leaf)).astype(BF16)
        v_ref[at] = rounded
        coef = leaf_coefficients(basis_ref[at], rounded)
        coefs[pl.ds(pl.multiple_of(at * rank, rank), rank)] = coef
        cp_ref[pl.ds(pl.multiple_of(at * size, size), size)] = pack_pair(coef)

    leaf_loop(per, UNROLL, one)
    store_share(share_of(trans_ref[...], coefs[...]), part_ref, cp_ref)
    odd = pos_ref[0] % 2
    mx_ref[...] = v_ref[pl.ds(per // 2 * (1 - odd), per // 2)]
    mo_ref[...] = v_ref[pl.ds(per // 2 * odd, per // 2)]


def quad_kernel(pos_ref, own_ref, sib_ref, across_ref, both_ref, part_ref, *rest):
    quad_ref, sum_ref = rest[-2:]
    place = pos_ref[0] % 4
    rows = quad_ref.shape[1]
    size = part_ref.shape[0]
    quad_ref[place] = own_ref[:rows]
    total = part_ref[...]
    for flip, ref in ((1, sib_ref), (2, across_ref), (3, both_ref)):
        quad_ref[place ^ flip] = ref[:rows]
        for at in range(3):
            total += ref[rows + at * size : rows + (at + 1) * size].astype(F32)
    sum_ref[...] = total[None]


def list_entries(near_ref, list_ref, pos, half, want_own, first, rows):
    slots = near_ref.shape[0] - 1
    base = pos * 2 * half - half

    def put(at, n):
        entry = first * slots + at
        m = near_ref[1 + entry % slots, entry // slots] - base
        own = (m >= half) & (m < 3 * half)
        list_ref[n] = entry
        return n + jnp.where(own == want_own, 1, 0)

    n = lax.fori_loop(0, rows * slots, put, 0)
    for u in range(UNROLL):
        list_ref[n + u] = near_ref.shape[1] * slots
    return n


def near_entry(near_ref, list_ref, at, pos, half, own):
    slots = near_ref.shape[0] - 1
    per = near_ref.shape[1]
    entry = list_ref[at]
    leaf_at = entry // slots
    row = jnp.minimum(leaf_at, per - 1)
    m = near_ref[1 + entry % slots, row] - (pos * 2 * half - half)
    if own:
        place = jnp.clip(m - half, 0, per - 1)
    else:
        place = jnp.clip(jnp.where(m < half, m, m - 2 * half), 0, 2 * half - 1)
    return entry, leaf_at, row, place


def load_halves(target, from_sibling, from_beside, odd):
    half = from_sibling.shape[0]
    target[pl.ds(half * (1 - odd), half)] = from_sibling[...]
    target[pl.ds(half * odd, half)] = from_beside[...]


def self_kernel(e_ref, v_ref, cp_in, self_ref, near_out, cp_out, buffer, sems):
    per, _, leaf = v_ref.shape

    def copy_out(slot, at):
        return pltpu.make_async_copy(buffer.at[slot], self_ref.at[at], sems.at[slot])

    def trip(i, carry):
        for u in range(UNROLL):
            at = i * UNROLL + u
            slot = (i % 2) * UNROLL + u

            @pl.when(i >= 2)
            def _():
                copy_out(slot, at - 2 * UNROLL).wait()

        for u in range(UNROLL):
            at = i * UNROLL + u
            points = columns_of(e_ref, at, leaf)
            tile = tile_of(other_rows(points), own_rows(points))
            buffer[(i % 2) * UNROLL + u] = tile
            near_out[at] = dot(v_ref[at], tile, 1, 0)
        for u in range(UNROLL):
            copy_out((i % 2) * UNROLL + u, i * UNROLL + u).start()
        return carry

    trips = per // UNROLL
    lax.fori_loop(0, trips, trip, 0)
    for i in range(max(trips - 2, 0), trips):
        for u in range(UNROLL):
            copy_out((i % 2) * UNROLL + u, i * UNROLL + u).wait()


def own_kernel(pos_ref, near_ref, e_ref, v_ref, near_in, *rest):
    tile_ref, near_out, list_ref = rest[-3:]
    per, _, leaf = v_ref.shape
    half = per // 2
    pos = pos_ref[0]
    n = list_entries(near_ref, list_ref, pos, half, True, 0, 2 * half)

    def trip(i, carry):
        for u in range(UNROLL):
            entry, leaf_at, row, place = near_entry(near_ref, list_ref, i * UNROLL + u, pos, half, True)
            tile = tile_of(other_rows(columns_of(e_ref, place, leaf)), own_rows(columns_of(e_ref, row, leaf)))
            tile_ref[entry] = tile
            near_out[leaf_at] += dot(v_ref[place], tile, 1, 0)
        return carry

    lax.fori_loop(0, (n + UNROLL - 1) // UNROLL, trip, 0)


def own_again_kernel(pos_ref, near_ref, v_ref, tile_ref, self_hbm, near_out, list_ref, self_ref, sems):
    per = v_ref.shape[0]
    half = per // 2
    pos = pos_ref[0]
    copies = [
        pltpu.make_async_copy(self_hbm.at[pl.ds(at, UNROLL)], self_ref.at[pl.ds(at, UNROLL)], sems.at[at // UNROLL])
        for at in range(0, per, UNROLL)
    ]
    for copy in copies:
        copy.start()
    near_out[...] = jnp.zeros_like(near_out)
    n = list_entries(near_ref, list_ref, pos, half, True, 0, 2 * half)

    def trip(i, carry):
        for u in range(UNROLL):
            entry, leaf_at, _, place = near_entry(near_ref, list_ref, i * UNROLL + u, pos, half, True)
            near_out[leaf_at] += dot(v_ref[place], tile_ref[entry], 1, 0)
        return carry

    lax.fori_loop(0, (n + UNROLL - 1) // UNROLL, trip, 0)
    for i, copy in enumerate(copies):
        copy.wait()
        for u in range(UNROLL):
            at = i * UNROLL + u
            near_out[at] += dot(v_ref[at], self_ref[at], 1, 0)


def load_coefficients(cw, sources):
    devices, rows, _ = sources[0].shape
    per = rows // cw.shape[1]
    for slot, source in enumerate(sources):
        for device in range(devices):
            for at in range(per):
                cw[(slot * devices + device) * per + at] = source[device, at * cw.shape[1] : (at + 1) * cw.shape[1]]


def coarse_rows(coarse_ref, sum_refs, fc):
    rank = coarse_ref.shape[1]
    acc = jnp.zeros((rank, rank), F32)
    for at in range(coarse_ref.shape[0]):
        packed = sum_refs[0][at]
        for ref in sum_refs[1:]:
            packed += ref[at]
        total = jnp.concatenate([packed[:, :rank], packed[:, rank:]], axis=0)
        for piece in split3(total):
            acc += dot(coarse_ref[at], piece, 1, 0)
    fc[...] = jnp.concatenate(split3(acc), axis=1)


def far_sum(l, pos, far_ref, cw, coup_ref, moved, basis_ref):
    per, rank, _ = basis_ref.shape
    odd = pos % 2
    picks = []
    for s in range(far_ref.shape[0]):
        leaf_id = far_ref[s, l]
        device = leaf_id // per
        gap = device // 4 - pos // 4
        slot = jnp.where(gap == 0, 0, jnp.where((gap < 0) == (odd == 0), 1, 2))
        picks.append(cw[(slot * 4 + device % 4) * per + leaf_id % per])
    wide = dot(coup_ref[l], jnp.concatenate(picks, axis=0), 1, 0)
    combined = wide[:rank, :rank] + wide[rank:, rank:] + moved
    return dot(combined.astype(BF16), basis_ref[l], 0, 0)


def store_moved(trans, fc, mv):
    count, rank, _ = trans.shape
    wide = dot(trans.reshape(count * rank, rank), fc[...], 1, 0)
    mv[...] = wide[:, :rank] + wide[:, rank : 2 * rank] + wide[:, 2 * rank :]


def foreign_kernel(
    pos_ref, near_ref, e_ref, ex_ref, eo_ref, vx_ref, vo_ref, tile_in, near_in, tile_ref, near_out, list_ref, vw,
):
    half, _, leaf = vx_ref.shape
    pos = pos_ref[0]
    odd = pos % 2
    load_halves(vw, vx_ref, vo_ref, odd)
    n = list_entries(near_ref, list_ref, pos, half, False, 0, 2 * half)

    def trip(i, carry):
        for u in range(UNROLL):
            entry, leaf_at, row, place = near_entry(near_ref, list_ref, i * UNROLL + u, pos, half, False)
            beneath = place < half
            from_x = beneath == (odd == 1)
            within = jnp.where(beneath, place, place - half)
            points = jnp.where(from_x, columns_of(ex_ref, within, leaf), columns_of(eo_ref, within, leaf))
            tile = tile_of(other_rows(points), own_rows(columns_of(e_ref, row, leaf)))
            tile_ref[entry] = tile
            near_out[leaf_at] += dot(vw[place], tile, 1, 0)
        return carry

    lax.fori_loop(0, (n + UNROLL - 1) // UNROLL, trip, 0)


def far_first_kernel(
    last, pos_ref, far_ref, rs_ref, sc_ref, basis_ref, coup_ref, trans_ref, near_ref, *rest,
):
    per, rank, leaf = basis_ref.shape
    half = per // 2
    size = rank // 2
    pos = pos_ref[0]
    odd = pos % 2
    first = half * ((1 - odd) if last else odd)
    if last:
        cw, mv, u_in, q_before, cp_before, share_before, msg_before = rest[:7]
        u_ref, mx_ref, q_ref, cp_ref, part_ref, msg_ref, coefs, acc_uu, acc_ru = rest[7:]
    else:
        coarse_ref, sum_a, sum_b, c0, c1, c2 = rest[:6]
        cw, mv, u_ref, mx_ref, cp_ref, share_ref, msg_ref, fc, coefs, acc_uu, acc_ru = rest[6:]
        load_coefficients(cw, (c0, c1, c2))
        coarse_rows(coarse_ref, (sum_a, sum_b), fc)
        store_moved(trans_ref[...], fc, mv)
    acc_uu[...] = jnp.zeros_like(acc_uu)
    acc_ru[...] = jnp.zeros_like(acc_ru)
    cp_first = first * size if last else 0

    def one(j):
        l = first + j
        far = far_sum(l, pos, far_ref, cw, coup_ref, mv[pl.ds(pl.multiple_of(l * rank, rank), rank)], basis_ref)
        right = columns_of(rs_ref, l, leaf)
        scale = columns_of(sc_ref, l, leaf)
        image = RIDGE_TERM * (right * scale) + (near_ref[l] + far)
        u_ref[:, pl.ds(pl.multiple_of(l * leaf, leaf), leaf)] = image
        acc_uu[...] += lane_groups(image * image)
        acc_ru[...] += lane_groups(right * image)
        rounded = (image * scale).astype(BF16)
        mx_ref[j] = rounded
        coef = leaf_coefficients(basis_ref[l], rounded)
        coefs[pl.ds(pl.multiple_of(j * rank, rank), rank)] = coef
        cp_ref[pl.ds(pl.multiple_of(cp_first + j * size, size), size)] = pack_pair(coef)

    leaf_loop(half, FAR_UNROLL, one)
    share = share_of(trans_ref[pl.ds(first, half)], coefs[...])
    lane = lax.broadcasted_iota(jnp.int32, msg_ref.shape, 1)
    out = jnp.where(lane == 0, jnp.sum(acc_uu[...], axis=1, keepdims=True), 0.0)
    out = jnp.where(lane == 1, jnp.sum(acc_ru[...], axis=1, keepdims=True), out)
    if last:
        other = half - first
        cp_ref[pl.ds(pl.multiple_of(other * size, size), half * size)] = cp_before[...]
        q_ref[pl.ds(other, half)] = q_before[...]
        q_ref[pl.ds(first, half)] = mx_ref[...]
        store_share(share + share_before[...], part_ref, cp_ref)
        msg_ref[...] = out + msg_before[...]
    else:
        share_ref[...] = share
        msg_ref[...] = out


def near_again_kernel(pos_ref, near_ref, vx_ref, vo_ref, tile_ref, near_in, near_out, list_ref, vw):
    half = vx_ref.shape[0]
    pos = pos_ref[0]
    load_halves(vw, vx_ref, vo_ref, pos % 2)
    n = list_entries(near_ref, list_ref, pos, half, False, 0, 2 * half)

    def trip(i, carry):
        for u in range(UNROLL):
            entry, leaf_at, _, place = near_entry(near_ref, list_ref, i * UNROLL + u, pos, half, False)
            near_out[leaf_at] += dot(vw[place], tile_ref[entry], 1, 0)
        return carry

    lax.fori_loop(0, (n + UNROLL - 1) // UNROLL, trip, 0)


def far_again_kernel(
    pos_ref, far_ref, rs_ref, sc_ref, u_ref, basis_ref, coup_ref, trans_ref,
    coarse_ref, sum_a, sum_b, c0, c1, c2, near_ref, prev_ref, w_ref, msg_ref,
    cw, fc, mv, acc_uw, acc_ww, acc_rw,
):
    per, rank, leaf = basis_ref.shape
    pos = pos_ref[0]
    load_coefficients(cw, (c0, c1, c2))
    coarse_rows(coarse_ref, (sum_a, sum_b), fc)
    store_moved(trans_ref[...], fc, mv)
    for acc in (acc_uw, acc_ww, acc_rw):
        acc[...] = jnp.zeros_like(acc)

    def one(l):
        far = far_sum(l, pos, far_ref, cw, coup_ref, mv[pl.ds(pl.multiple_of(l * rank, rank), rank)], basis_ref)
        image = columns_of(u_ref, l, leaf)
        second = RIDGE_TERM * (image * columns_of(sc_ref, l, leaf)) + (near_ref[l] + far)
        w_ref[:, pl.ds(pl.multiple_of(l * leaf, leaf), leaf)] = second
        acc_uw[...] += lane_groups(image * second)
        acc_ww[...] += lane_groups(second * second)
        acc_rw[...] += lane_groups(columns_of(rs_ref, l, leaf) * second)

    leaf_loop(per, FAR_UNROLL, one)
    lane = lax.broadcasted_iota(jnp.int32, msg_ref.shape, 1)
    out = prev_ref[...]
    for at, acc in enumerate((acc_uw, acc_ww, acc_rw)):
        out = jnp.where(lane == 2 + at, jnp.sum(acc[...], axis=1, keepdims=True), out)
    msg_ref[...] = out


def call(kernel, name, in_specs, out_shape, scratch, args, aliases=None, flops=0, out_specs=None, limit=VMEM_LIMIT):
    return pl.pallas_call(
        kernel,
        in_specs=in_specs,
        out_specs=out_specs or [WHOLE] * len(out_shape),
        out_shape=out_shape,
        scratch_shapes=scratch,
        input_output_aliases=aliases or {},
        compiler_params=pltpu.CompilerParams(vmem_limit_bytes=limit),
        cost_estimate=pl.CostEstimate(flops=flops, bytes_accessed=0, transcendentals=0),
        name=name,
    )(*args)


def two_clusters():
    return CDEV == 8 and lax.axis_size("leaf") == 2 * CDEV


def other_clusters(plane_sum):
    count = lax.axis_size("leaf")
    if two_clusters():
        return involution(plane_sum, lambda i: i ^ (12 if i % 2 else 8))
    mask = 4
    while mask < CDEV:
        plane_sum = plane_sum + involution(plane_sum, lambda i: i ^ mask)
        mask *= 2
    sums = plane_sum
    while mask < count:
        sums = jnp.concatenate([sums, involution(sums, lambda i: i ^ mask)], axis=0)
        mask *= 2
    return sums[1:]


def pass_kernel(*refs):
    pass


def after(values, *before):
    return call(
        pass_kernel, "after", [WHOLE] * len(values) + [ANYWHERE] * len(before),
        [pltpu.VMEM(value.shape, value.dtype) for value in values], [], (*values, *before),
        aliases={at: at for at in range(len(values))},
    )


def first_messages(cp):
    return sibling(cp), across(cp)


def second_messages(position, cp, got, part, *before):
    rows = cp.shape[0] - 3 * part.shape[0]
    got = (*got, sibling(got[1]))
    quad, plane_sum = call(
        quad_kernel, "quad", [SCALAR] + [WHOLE] * 5 + [ANYWHERE] * len(before),
        [pltpu.VMEM((4, rows, cp.shape[1]), BF16), pltpu.VMEM((1,) + part.shape, F32)],
        [], (position, cp, *got, part, *before),
    )
    return quad, two_chips(quad), other_clusters(plane_sum)


def last_messages(quad, mine):
    other = sibling(mine) if two_clusters() else jnp.zeros_like(mine)
    return (quad, sibling(quad)), (mine, other)


def body(
    right_side, scaling, embeddings, near_leaves, far_leaves, leaf_basis, leaf_coupling,
    transfer, coarse_coupling,
):
    columns, local_points = right_side.shape
    per, rank, leaf = leaf_basis.shape
    features = embeddings.shape[0]
    slots = near_leaves.shape[1] - 1
    far_count = far_leaves.shape[1]
    half = per // 2
    margin = half * leaf
    size = rank // 2
    count = lax.axis_size("leaf")
    pos = lax.axis_index("leaf")
    position = pos.reshape(1).astype(jnp.int32)
    near_rows = near_leaves.T
    far_rows = far_leaves.T
    coarse_count = count // CDEV

    margin_shape = pltpu.VMEM((features, margin), F32)
    ex, eo = call(
        margins_kernel, "margins", [SCALAR, ANYWHERE], [margin_shape] * 2,
        [pltpu.SemaphoreType.DMA((2,))], (position, embeddings), limit=WIDE_LIMIT,
    )
    e_sibling = sibling(ex)
    e_beside = beside(eo)

    scale_row = scaling.reshape(1, local_points)
    leaf_shape = pltpu.VMEM((per, columns, leaf), BF16)
    cp_shape = pltpu.VMEM((per * size + 3 * size, 2 * columns), BF16)
    part_shape = pltpu.VMEM((size, 2 * columns), F32)
    self_shape = pltpu.HBM((4 * per, leaf, leaf), BF16)
    trans_shape = pltpu.VMEM((per, rank, rank), BF16)
    half_shape = pltpu.VMEM((half, columns, leaf), BF16)
    share_shape = pltpu.VMEM((rank, columns), F32)
    cp_half_shape = pltpu.VMEM((half * size, 2 * columns), BF16)
    half_coefs_shape = pltpu.VMEM((half * rank, columns), BF16)
    moved_shape = pltpu.VMEM((per * rank, columns), F32)
    tile_shape = pltpu.VMEM((per * slots + 1, leaf, leaf), BF16)
    near_shape = pltpu.VMEM((per + 1, columns, leaf), F32)
    wide_shape = pltpu.VMEM((columns, local_points), F32)
    msg_shape = pltpu.VMEM((columns, 128), F32)
    coefs_shape = pltpu.VMEM((per * rank, columns), BF16)
    acc_shape = pltpu.VMEM((columns, 128), F32)
    list_shape = pltpu.SMEM((per * slots + UNROLL,), jnp.int32)
    window = [
        pltpu.VMEM((2 * half, columns, leaf), BF16),
        pltpu.VMEM((12 * per, size, 2 * columns), BF16),
        pltpu.VMEM((rank, 3 * columns), BF16),
    ]

    v, cp, part, trans, mx, mo = call(
        prep_kernel, "prep", [SCALAR] + [OUTSIDE] * 4,
        [leaf_shape, cp_shape, part_shape, trans_shape, half_shape, half_shape],
        [pltpu.VMEM(right_side.shape, F32), pltpu.VMEM(scale_row.shape, F32), pltpu.VMEM(leaf_basis.shape, BF16),
         pltpu.VMEM(transfer.shape, BF16), coefs_shape, pltpu.VMEM((per * rank * rank // 128, 128), F32), pltpu.VMEM((per, rank, 128), F32), pltpu.SemaphoreType.DMA((4,))],
        (position, right_side, scale_row, leaf_basis, transfer), limit=WIDE_LIMIT,
    )
    tself, near, cp = call(
        self_kernel, "self_tiles", [WHOLE] * 3, [self_shape, near_shape, cp_shape],
        [pltpu.VMEM((2 * UNROLL, leaf, leaf), BF16), pltpu.SemaphoreType.DMA((2 * UNROLL,))],
        (embeddings, v, cp), out_specs=[OUTSIDE, WHOLE, WHOLE], aliases={2: 2},
    )
    got = first_messages(cp)
    vo = beside(mo)
    coup, coarse = call(
        relayout_kernel, "relayout", [SCALAR] + [WHOLE] * 2 + [ANYWHERE],
        [pltpu.VMEM((per, 2 * rank, far_count * size), BF16), pltpu.VMEM((coarse_count - 1, rank, rank), BF16)],
        [
            pltpu.VMEM((far_count * rank * rank // 128, 128), F32),
            pltpu.VMEM((2, far_count // 4, rank, 128), F32),
            pltpu.VMEM((size, 128), F32), pltpu.VMEM((rank, 128), F32),
        ],
        (position, leaf_coupling, coarse_coupling, cp),
    )
    tiles, near = call(
        own_kernel, "own_tiles", [SCALAR] * 2 + [WHOLE] * 3 + [ANYWHERE] * 2, [tile_shape, near_shape], [list_shape],
        (position, near_rows, embeddings, v, near, coup, e_beside), aliases={4: 1}, flops=2 * per * leaf * leaf * 320,
    )
    got = (got[0], *after(got[1:], near))
    quad, far_quad, mine = second_messages(position, cp, got, part, vo)
    vx = sibling(mx)
    tiles, near = call(
        foreign_kernel, "foreign_tiles", [SCALAR] * 2 + [WHOLE] * 7, [tile_shape, near_shape],
        [list_shape, window[0]],
        (position, near_rows, embeddings, e_sibling, e_beside, vx, vo, tiles, near),
        aliases={7: 0, 8: 1}, flops=2 * per * leaf * leaf * 320,
    )
    coefs, sums = last_messages(*after((far_quad, mine), near))
    common = (position, far_rows, right_side, scale_row, leaf_basis, coup, trans, near)
    cw, mv, image, mo, cp_half, share, msg = call(
        functools.partial(far_first_kernel, False), "far_half", [SCALAR] * 2 + [WHOLE] * 12,
        [window[1], moved_shape, wide_shape, half_shape, cp_half_shape, share_shape, msg_shape],
        [window[2], half_coefs_shape, acc_shape, acc_shape],
        (*common, coarse, *sums, quad, *coefs), flops=per * leaf * leaf * 32,
    )
    vo = beside(mo)
    image, mx, q, cp, part, msg = call(
        functools.partial(far_first_kernel, True), "other_half", [SCALAR] * 2 + [WHOLE] * 13,
        [wide_shape, half_shape, leaf_shape, cp_shape, part_shape, msg_shape],
        [half_coefs_shape, acc_shape, acc_shape],
        (*common, cw, mv, image, mo, cp_half, share, msg), aliases={10: 0}, flops=per * leaf * leaf * 32,
    )
    got = first_messages(cp)
    (near,) = call(
        own_again_kernel, "own_again", [SCALAR] * 2 + [WHOLE] * 2 + [OUTSIDE], [near_shape],
        [list_shape, pltpu.VMEM((per, leaf, leaf), BF16), pltpu.SemaphoreType.DMA((per // UNROLL,))],
        (position, near_rows, q, tiles, tself), flops=2 * per * leaf * leaf * 64,
    )
    got = (got[0], *after(got[1:], near))
    quad, far_quad, mine = second_messages(position, cp, got, part, vo)
    vx = sibling(mx)
    (near,) = call(
        near_again_kernel, "near_again", [SCALAR] * 2 + [WHOLE] * 4, [near_shape], [list_shape, window[0]],
        (position, near_rows, vx, vo, tiles, near), aliases={5: 0}, flops=2 * per * leaf * leaf * 64,
    )
    coefs, sums = last_messages(*after((far_quad, mine), near))
    second, msg = call(
        far_again_kernel, "far_again", [SCALAR] * 2 + [WHOLE] * 14, [wide_shape, msg_shape],
        window[1:] + [moved_shape] + [acc_shape] * 3,
        (position, far_rows, right_side, scale_row, image, leaf_basis, coup, trans,
         coarse, *sums, quad, *coefs, near, msg), flops=per * leaf * leaf * 64,
    )

    mask = 1
    while mask < count:
        msg = msg + involution(msg, lambda i: i ^ mask)
        mask *= 2
    uu, ru, uw, ww, rw = [msg[:, k : k + 1] for k in range(5)]
    step_one = ru / (uu + EPSILON)
    beta = -(uu - step_one * uw) / (uu + EPSILON)
    lead = 1.0 + beta
    curvature = lead * lead * uu - 2.0 * lead * step_one * uw + step_one * step_one * ww
    aligned = lead * (ru - step_one * uu) - step_one * (rw - step_one * uw)
    step_two = aligned / (curvature + EPSILON)
    first_weight = step_one + step_two * lead
    second_weight = step_two * step_one
    solution = scale_row * (first_weight * right_side - second_weight * image)
    residual = right_side - first_weight * image + second_weight * second
    return (solution, residual)


def solution(mesh):
    return jax.shard_map(
        body,
        mesh=mesh,
        in_specs=(
            P(None, ("groups", "leaf")),
            P(("groups", "leaf")),
            P(None, ("groups", "leaf")),
            P(("groups", "leaf"), None),
            P(("groups", "leaf"), None),
            P(("groups", "leaf"), None, None),
            P(("groups", "leaf"), None, None),
            P(("groups", "leaf"), None),
            P("groups", None, None),
        ),
        out_specs=(P(None, ("groups", "leaf")), P(None, ("groups", "leaf"))),
        check_vma=False,
    )
```

time: 136 us -> 114 us (0.84)
  starting transfers between devices: 48.8 us -> 33.7 us
  local copies, waits for them, and re-layouts: 14.9 us -> 0.04 us
  waiting for transfers between devices: 12.1 us -> 25.3 us
  Pallas kernels: 54.2 us -> 51.2 us
  other arithmetic: 4.53 us -> 2.87 us
    ppermute x26 -> x24, starting transfers between devices: 48.8 us -> 33.7 us  [involution(): return lax.ppermute(value, 'leaf', pairs)]
    ppermute x26 -> x24, waiting for transfers between devices: 12.1 us -> 25.3 us  [involution(): return lax.ppermute(value, 'leaf', pairs)]
    unnamed x50 -> x16, local copies, waits for them, and re-layouts: 12.9 us -> 0.04 us
    pallas_call x13 -> x17, Pallas kernels: 54.2 us -> 51.2 us  [call(): pl.pallas_call(kernel, in_specs=in_specs, out_specs=out_specs or [WHOLE]...]
    select_n x1 -> x0, other arithmetic: 1.37 us -> none  [body(): coarse = jnp.take(row, order, axis=0).reshape(coarse_count - 1, rank, rank)]
  transfers between devices with their start and end apart: 26 -> 24, of which waited for: 9 -> 10; matrix products, arithmetic and copies ran while one was open for 3% -> 0% of each run, Pallas kernels for 16% -> 36%
where the time goes in v4:
time: 114 us
  Pallas kernels  51.2 us (45%)
  starting transfers between devices  33.7 us (30%)
  waiting for transfers between devices  25.3 us (22%)
  other arithmetic  2.87 us (3%)
    pallas_call x17, Pallas kernels, call(): pl.pallas_call(kernel, in_specs=in_specs, out_specs=out_specs or [WHOLE]...  51.2 us
    ppermute x24, starting transfers between devices, involution(): return lax.ppermute(value, 'leaf', pairs)  33.7 us
    ppermute x24, waiting for transfers between devices, involution(): return lax.ppermute(value, 'leaf', pairs)  25.3 us
    add x1, other arithmetic, body(): residual = right_side - first_weight * image + second_weight * second  2.64 us
  transfers between devices with their start and end apart: 24, of which 10 were waited for; matrix products, arithmetic and copies ran while one was open for 0% of the time, Pallas kernels for 36%

profile of v4, /device:TPU:0, one launch (start us, length us, event | category | flops | bytes accessed | tf_op | source)
XLA Modules:
  0.0 114.0 jit_solution(18219287270413673118)
XLA Ops:
  2.7 3.6 %prep.1 = (bf16[16,64,512]{2,1,0:T(8,128)(2,1)S(1)}, bf16[608,128]{1,0:T(8,128)(2,1)S(1)}, f32[32,128]{1,0:T(8,128)S(1)}, bf16[16,64,64]{2,1,0:T(8,128)(2,1)S(1)...) custom-call(s32[1]{0:T(128)} %bitcast.pos_ref, f32[64,8192]{1,0:T(8,128)} %rs_ref.5, ...), custom_call_target="tpu_custom_call" | custom-call | tf_op jit(solution)/shard_map/prep/pallas_call | solution.py:533
  7.0 7.2 %self_tiles.1 = (bf16[64,512,512]{2,1,0:T(8,128)(2,1)}, f32[17,64,512]{2,1,0:T(8,128)S(1)}, bf16[608,128]{1,0:T(8,128)(2,1)S(1)}) custom-call(f32[32,8192]{1,0:T(8,128)S(1)} %copy-done.2, bf16[16,64,512]{2,1,0:T(8,128)(2,1)S(1)} %get-tuple-element.42.v_ref, bf16[608,128]{1,0:T(8,128)(2,1)S(1)} %get-tuple-element.43.cp_in), custom_call_target="tpu_custom_call", output_to_operand_aliasing={{2}: (2, {})} | custom-call | tf_op jit(solution)/shard_map/self_tiles/pallas_call | solution.py:533
  14.2 7.2 %collective-permute-start.5 = (bf16[608,128]{1,0:T(8,128)(2,1)S(1)}, bf16[608,128]{1,0:T(8,128)(2,1)S(1)}, u32[]{:S(2)}, u32[]{:S(2)}) collective-permute-start(bf16[608,128]{1,0:T(8,128)(2,1)S(1)} %get-tuple-element.44.wait_ref.own_ref), channel_id=1, source_target_pairs={{0,2},{1,3},{2,0},{3,1},{4,6},{5,7},{6,4},{7,5},{8,10},{9,11},{10,... | collective-permute-start | bytes 466952 | tf_op jit(solution)/shard_map/ppermute | solution.py:33
  21.9 3.3 %relayout.1 = (bf16[16,128,256]{2,1,0:T(8,128)(2,1)S(1)}, bf16[1,64,64]{2,1,0:T(8,128)(2,1)S(1)}) custom-call(s32[1]{0:T(128)} %bitcast.pos_ref, bf16[16,8,4096]{2,1,0:T(8,128)(2,1)S(1)} %copy-done.3, bf16[2,2,4096]{2,1,0:T(2,128)(2,1)S(1)} %copy-done.6, bf16[608,128]{1,0:T(8,128)(2,1)S(1)} %get-tuple-element.44.wait_ref.own_ref), custom_call_target="tpu_custom_call" | custom-call | tf_op jit(solution)/shard_map/relayout/pallas_call | solution.py:533
  25.9 8.8 %own_tiles.1 = (bf16[33,512,512]{2,1,0:T(8,128)(2,1)S(1)}, f32[17,64,512]{2,1,0:T(8,128)S(1)}) custom-call(s32[1]{0:T(128)} %bitcast.pos_ref, s32[3,16]{1,0:T(4,128)S(1)} %bitcast.11, f32[32,8192]{1,0:T(8,128)S(1)} %copy-done.2, bf16[16,64,512]{2,1,0:T(8,128)(2,1)S(1)} %get-tuple-element.42.v_ref, ...), custom_call_target="tpu_custom_call", output_to_operand_aliasing={{1}: (4, {})} | custom-call | flops 2684354560 | tf_op jit(solution)/shard_map/own_tiles/pallas_call | solution.py:533
  36.9 4.7 %collective-permute-start.8 = (f32[1,32,128]{2,1,0:T(8,128)S(1)}, f32[1,32,128]{2,1,0:T(8,128)S(1)}, u32[]{:S(2)}, u32[]{:S(2)}) collective-permute-start(f32[1,32,128]{2,1,0:T(8,128)S(1)} %get-tuple-element.58), channel_id=1, source_target_pairs={{0,8},{1,13},{2,10},{3,15},{4,12},{5,9},{6,14},{7,11},{8,0},{9,5},... | collective-permute-start | bytes 49160 | tf_op jit(solution)/shard_map/ppermute | solution.py:33
  41.6 5.8 %foreign_tiles.1 = (bf16[33,512,512]{2,1,0:T(8,128)(2,1)S(1)}, f32[17,64,512]{2,1,0:T(8,128)S(1)}) custom-call(s32[1]{0:T(128)} %bitcast.pos_ref, s32[3,16]{1,0:T(4,128)S(1)} %bitcast.12, f32[32,8192]{1,0:T(8,128)S(1)} %copy-done.2, f32[32,4096]{1,0:T(8,128)S(1)} %collective-permute-done.ex_ref, ...), custom_call_target="tpu_custom_call", output_to_operand_aliasing={{0}: (7, {}), {1}: (8, {})} | custom-call | flops 2684354560 | tf_op jit(solution)/shard_map/foreign_tiles/pallas_call | solution.py:533
  47.5 1.7 %collective-permute-done.8.refs_1_ = f32[1,32,128]{2,1,0:T(8,128)S(1)} collective-permute-done((f32[1,32,128]{2,1,0:T(8,128)S(1)}, f32[1,32,128]{2,1,0:T(8,128)S(1)}, u32[]{:S(2)}, u32[]{:S(2)}) %collective-permute-start.8) | collective-permute-done | bytes 16416 | tf_op jit(solution)/shard_map/ppermute | solution.py:33
  49.7 1.4 %collective-permute-done.9.rest_2_ = f32[1,32,128]{2,1,0:T(8,128)S(1)} collective-permute-done((f32[1,32,128]{2,1,0:T(8,128)S(1)}, f32[1,32,128]{2,1,0:T(8,128)S(1)}, u32[]{:S(2)}, u32[]{:S(2)}) %collective-permute-start.9) | collective-permute-done | bytes 16416 | tf_op jit(solution)/shard_map/ppermute | solution.py:33
  51.2 4.3 %far_half.1 = (bf16[192,32,128]{2,1,0:T(8,128)(2,1)S(1)}, f32[1024,64]{1,0:T(8,128)S(1)}, f32[64,8192]{1,0:T(8,128)S(1)}, bf16[8,64,512]{2,1,0:T(8,128)(2,1)S(1)...) custom-call(s32[1]{0:T(128)} %bitcast.pos_ref, s32[8,16]{1,0:T(8,128)S(1)} %bitcast.8, ...), custom_call_target="tpu_custom_call" | custom-call | flops 134217728 | tf_op jit(solution)/shard_map/far_half/pallas_call | solution.py:533
  56.2 3.6 %other_half.1 = (f32[64,8192]{1,0:T(8,128)S(1)}, bf16[8,64,512]{2,1,0:T(8,128)(2,1)S(1)}, bf16[16,64,512]{2,1,0:T(8,128)(2,1)S(1)}, bf16[608,128]{1,0:T(8,128)(2...) custom-call(s32[1]{0:T(128)} %bitcast.pos_ref, s32[8,16]{1,0:T(8,128)S(1)} %bitcast.9, ...), custom_call_target="tpu_custom_call", output_to_operand_aliasing={{0}: (10, {})} | custom-call | flops 134217728 | tf_op jit(solution)/shard_map/other_half/pallas_call | solution.py:533
  59.8 3.9 %collective-permute-start.12 = (bf16[608,128]{1,0:T(8,128)(2,1)S(1)}, bf16[608,128]{1,0:T(8,128)(2,1)S(1)}, u32[]{:S(2)}, u32[]{:S(2)}) collective-permute-start(bf16[608,128]{1,0:T(8,128)(2,1)S(1)} %get-tuple-element.69.own_ref), channel_id=1, source_target_pairs={{0,2},{1,3},{2,0},{3,1},{4,6},{5,7},{6,4},{7,5},{8,10},{9,11},{10,... | collective-permute-start | bytes 466952 | tf_op jit(solution)/shard_map/ppermute | solution.py:33
  63.7 1.7 %collective-permute-start.11 = (bf16[608,128]{1,0:T(8,128)(2,1)S(1)}, bf16[608,128]{1,0:T(8,128)(2,1)S(1)}, u32[]{:S(2)}, u32[]{:S(2)}) collective-permute-start(bf16[608,128]{1,0:T(8,128)(2,1)S(1)} %get-tuple-element.69.own_ref), channel_id=1, source_target_pairs={{0,1},{1,0},{2,3},{3,2},{4,5},{5,4},{6,7},{7,6},{8,9},{9,8},{10,11... | collective-permute-start | bytes 466952 | tf_op jit(solution)/shard_map/ppermute | solution.py:33
  65.4 5.6 %own_again.1.refs_1_.near_in = f32[17,64,512]{2,1,0:T(8,128)S(1)} custom-call(s32[1]{0:T(128)} %bitcast.pos_ref, s32[3,16]{1,0:T(4,128)S(1)} %bitcast.13, bf16[16,64,512]{2,1,0:T(8,128)(2,1)S(1)} %get-tuple-element.70.v_ref, bf16[33,512,512]{2,1,0:T(8,128)(2,1)S(1)} %get-tuple-element.71.tile_ref, bf16[64,512,512]{2,1,0:T(8,128)(2,1)} %get-tuple-element.72.self_hbm), custom_call_target="tpu_custom_call" | custom-call | flops 536870912 | tf_op jit(solution)/shard_map/own_again/pallas_call | solution.py:533
  71.0 4.1 %collective-permute-start.13 = (bf16[608,128]{1,0:T(8,128)(2,1)S(1)}, bf16[608,128]{1,0:T(8,128)(2,1)S(1)}, u32[]{:S(2)}, u32[]{:S(2)}) collective-permute-start(bf16[608,128]{1,0:T(8,128)(2,1)S(1)} %after.6.across_ref), channel_id=1, source_target_pairs={{0,1},{1,0},{2,3},{3,2},{4,5},{5,4},{6,7},{7,6},{8,9},{9,8},{10,11... | collective-permute-start | bytes 466952 | tf_op jit(solution)/shard_map/ppermute | solution.py:33
  76.9 6.0 %collective-permute-start.16 = (f32[1,32,128]{2,1,0:T(8,128)S(1)}, f32[1,32,128]{2,1,0:T(8,128)S(1)}, u32[]{:S(2)}, u32[]{:S(2)}) collective-permute-start(f32[1,32,128]{2,1,0:T(8,128)S(1)} %get-tuple-element.75), channel_id=1, source_target_pairs={{0,8},{1,13},{2,10},{3,15},{4,12},{5,9},{6,14},{7,11},{8,0},{9,5},... | collective-permute-start | bytes 49160 | tf_op jit(solution)/shard_map/ppermute | solution.py:33
  82.9 2.8 %near_again.1.refs_2_.near_ref = f32[17,64,512]{2,1,0:T(8,128)S(1)} custom-call(s32[1]{0:T(128)} %bitcast.pos_ref, s32[3,16]{1,0:T(4,128)S(1)} %bitcast.14, bf16[8,64,512]{2,1,0:T(8,128)(2,1)S(1)} %collective-permute-done.17.vx_ref, bf16[8,64,512]{2,1,0:T(8,128)(2,1)S(1)} %collective-permute-done.14.rest_0_.vo_ref, ...), custom_call_target="tpu_custom_call", output_to_operand_aliasing={{}: (5, {})} | custom-call | flops 536870912 | tf_op jit(solution)/shard_map/near_again/pallas_call | solution.py:533
  85.7 4.8 %collective-permute-done.16.refs_1_ = f32[1,32,128]{2,1,0:T(8,128)S(1)} collective-permute-done((f32[1,32,128]{2,1,0:T(8,128)S(1)}, f32[1,32,128]{2,1,0:T(8,128)S(1)}, u32[]{:S(2)}, u32[]{:S(2)}) %collective-permute-start.16) | collective-permute-done | bytes 16416 | tf_op jit(solution)/shard_map/ppermute | solution.py:33
  91.1 1.4 %collective-permute-done.18.sum_b = f32[1,32,128]{2,1,0:T(8,128)S(1)} collective-permute-done((f32[1,32,128]{2,1,0:T(8,128)S(1)}, f32[1,32,128]{2,1,0:T(8,128)S(1)}, u32[]{:S(2)}, u32[]{:S(2)}) %collective-permute-start.18) | collective-permute-done | bytes 16416 | tf_op jit(solution)/shard_map/ppermute | solution.py:33
  92.5 4.7 %far_again.1 = (f32[64,8192]{1,0:T(8,128)S(1)}, f32[64,128]{1,0:T(8,128)S(1)}) custom-call(s32[1]{0:T(128)} %bitcast.pos_ref, s32[8,16]{1,0:T(8,128)S(1)} %bitcast.10, f32[64,8192]{1,0:T(8,128)S(1)} %copy-done, f32[1,8192]{1,0:T(1,128)S(1)} %bitcast.7, f32[64,8192]{1,0:T(8,128)S(1)} %get-tuple-element.68.u_ref, bf16[16,64,512]{2,1,0:T(8,128)(2,1)S(1)} %copy-done.1, ...), custom_call_target="tpu_custom_call" | custom-call | flops 268435456 | tf_op jit(solution)/shard_map/far_again/pallas_call | solution.py:533
  98.5 3.9 %collective-permute-done.21 = f32[64,128]{1,0:T(8,128)S(1)} collective-permute-done((f32[64,128]{1,0:T(8,128)S(1)}, f32[64,128]{1,0:T(8,128)S(1)}, u32[]{:S(2)}, u32[]{:S(2)}) %collective-permute-start.21) | collective-permute-done | bytes 32800 | tf_op jit(solution)/shard_map/ppermute | solution.py:33
  102.6 3.7 %collective-permute-done.22 = f32[64,128]{1,0:T(8,128)S(1)} collective-permute-done((f32[64,128]{1,0:T(8,128)S(1)}, f32[64,128]{1,0:T(8,128)S(1)}, u32[]{:S(2)}, u32[]{:S(2)}) %collective-permute-start.22) | collective-permute-done | bytes 32800 | tf_op jit(solution)/shard_map/ppermute | solution.py:33
  106.3 4.8 %collective-permute-done.23 = f32[64,128]{1,0:T(8,128)S(1)} collective-permute-done((f32[64,128]{1,0:T(8,128)S(1)}, f32[64,128]{1,0:T(8,128)S(1)}, u32[]{:S(2)}, u32[]{:S(2)}) %collective-permute-start.23) | collective-permute-done | bytes 32800 | tf_op jit(solution)/shard_map/ppermute | solution.py:33
  111.4 2.6 %multiply_add_fusion = (f32[64,8192]{1,0:T(8,128)}, f32[64,8192]{1,0:T(8,128)}) fusion(f32[64,8192]{1,0:T(8,128)S(1)} %get-tuple-element.81, f32[64,8192]{1,0:T(8,128)S(1)} %copy-done, f32[64,8192]{1,0:T(8,128)S(1)} %get-tuple-element.68.u_ref, f32[64]{0:T(128)S(1)} %get-tuple-element.83, f32[64]{0:T(128)S(1)} %get-tuple-element.82, f32[8192]{0:T(1024)S(1)} %copy-done.4), kind=kLoop, calls=%fused_computation | loop fusion | flops 4194304 | bytes 10519040 | tf_op jit(solution)/shard_map/add | solution.py:735
  (63 shorter events, 11.3 us)
Async XLA Ops:
  2.0 23.3 %collective-permute-start.1 = (f32[32,4096]{1,0:T(8,128)S(1)}, f32[32,4096]{1,0:T(8,128)S(1)}, u32[]{:S(2)}, u32[]{:S(2)}) collective-permute-start(f32[32,4096]{1,0:T(8,128)S(1)} %get-tuple-element.48), channel_id=1, source_target_pairs={{1,2},{2,1},{3,4},{4,3},{5,6},{6,5},{7,8},{8,7},{9,10},{10,9},{11,... | collective-permute-start | bytes 1572872 | tf_op jit(solution)/shard_map/ppermute | solution.py:33
  6.3 28.5 %collective-permute-start.3 = (bf16[8,64,512]{2,1,0:T(8,128)(2,1)S(1)}, bf16[8,64,512]{2,1,0:T(8,128)(2,1)S(1)}, u32[]{:S(2)}, u32[]{:S(2)}) collective-permute-start(bf16[8,64,512]{2,1,0:T(8,128)(2,1)S(1)} %get-tuple-element.50), channel_id=1, source_target_pairs={{1,2},{2,1},{3,4},{4,3},{5,6},{6,5},{7,8},{8,7},{9,10},{10,9},{11,... | collective-permute-start | bytes 1572872 | tf_op jit(solution)/shard_map/ppermute | solution.py:33
  14.2 20.4 %collective-permute-start.5 = (bf16[608,128]{1,0:T(8,128)(2,1)S(1)}, bf16[608,128]{1,0:T(8,128)(2,1)S(1)}, u32[]{:S(2)}, u32[]{:S(2)}) collective-permute-start(bf16[608,128]{1,0:T(8,128)(2,1)S(1)} %get-tuple-element.44.wait_ref.own_ref), channel_id=1, source_target_pairs={{0,2},{1,3},{2,0},{3,1},{4,6},{5,7},{6,4},{7,5},{8,10},{9,11},{10,... | collective-permute-start | bytes 466952 | tf_op jit(solution)/shard_map/ppermute | solution.py:33
  21.4 13.3 %collective-permute-start.4 = (bf16[608,128]{1,0:T(8,128)(2,1)S(1)}, bf16[608,128]{1,0:T(8,128)(2,1)S(1)}, u32[]{:S(2)}, u32[]{:S(2)}) collective-permute-start(bf16[608,128]{1,0:T(8,128)(2,1)S(1)} %get-tuple-element.44.wait_ref.own_ref), channel_id=1, source_target_pairs={{0,1},{1,0},{2,3},{3,2},{4,5},{5,4},{6,7},{7,6},{8,9},{9,8},{10,11... | collective-permute-start | bytes 466952 | tf_op jit(solution)/shard_map/ppermute | solution.py:33
  21.9 19.7 %collective-permute-start = (f32[32,4096]{1,0:T(8,128)S(1)}, f32[32,4096]{1,0:T(8,128)S(1)}, u32[]{:S(2)}, u32[]{:S(2)}) collective-permute-start(f32[32,4096]{1,0:T(8,128)S(1)} %get-tuple-element.47), channel_id=1, source_target_pairs={{0,1},{1,0},{2,3},{3,2},{4,5},{5,4},{6,7},{7,6},{8,9},{9,8},{10,11... | collective-permute-start | bytes 1572872 | tf_op jit(solution)/shard_map/ppermute | solution.py:33
  25.2 16.4 %collective-permute-start.2 = (bf16[8,64,512]{2,1,0:T(8,128)(2,1)S(1)}, bf16[8,64,512]{2,1,0:T(8,128)(2,1)S(1)}, u32[]{:S(2)}, u32[]{:S(2)}) collective-permute-start(bf16[8,64,512]{2,1,0:T(8,128)(2,1)S(1)} %get-tuple-element.49), channel_id=1, source_target_pairs={{0,1},{1,0},{2,3},{3,2},{4,5},{5,4},{6,7},{7,6},{8,9},{9,8},{10,11... | collective-permute-start | bytes 1572872 | tf_op jit(solution)/shard_map/ppermute | solution.py:33
  34.7 1.4 %collective-permute-start.6 = (bf16[608,128]{1,0:T(8,128)(2,1)S(1)}, bf16[608,128]{1,0:T(8,128)(2,1)S(1)}, u32[]{:S(2)}, u32[]{:S(2)}) collective-permute-start(bf16[608,128]{1,0:T(8,128)(2,1)S(1)} %after.4.across_ref), channel_id=1, source_target_pairs={{0,1},{1,0},{2,3},{3,2},{4,5},{5,4},{6,7},{7,6},{8,9},{9,8},{10,11... | collective-permute-start | bytes 466952 | tf_op jit(solution)/shard_map/ppermute | solution.py:33
  36.2 13.0 %collective-permute-start.7 = (bf16[4,512,128]{2,1,0:T(8,128)(2,1)S(1)}, bf16[4,512,128]{2,1,0:T(8,128)(2,1)S(1)}, u32[]{:S(2)}, u32[]{:S(2)}) collective-permute-start(bf16[4,512,128]{2,1,0:T(8,128)(2,1)S(1)} %get-tuple-element.57.rest_3_), channel_id=1, source_target_pairs={{1,4},{3,6},{4,1},{5,8},{6,3},{7,10},{8,5},{9,12},{10,7},{11,14},{... | collective-permute-start | bytes 1572872 | tf_op jit(solution)/shard_map/ppermute | solution.py:33
  36.9 12.3 %collective-permute-start.8 = (f32[1,32,128]{2,1,0:T(8,128)S(1)}, f32[1,32,128]{2,1,0:T(8,128)S(1)}, u32[]{:S(2)}, u32[]{:S(2)}) collective-permute-start(f32[1,32,128]{2,1,0:T(8,128)S(1)} %get-tuple-element.58), channel_id=1, source_target_pairs={{0,8},{1,13},{2,10},{3,15},{4,12},{5,9},{6,14},{7,11},{8,0},{9,5},... | collective-permute-start | bytes 49160 | tf_op jit(solution)/shard_map/ppermute | solution.py:33
  49.2 1.9 %collective-permute-start.10 = (bf16[4,512,128]{2,1,0:T(8,128)(2,1)S(1)}, bf16[4,512,128]{2,1,0:T(8,128)(2,1)S(1)}, u32[]{:S(2)}, u32[]{:S(2)}) collective-permute-start(bf16[4,512,128]{2,1,0:T(8,128)(2,1)S(1)} %get-tuple-element.60.rest_4_), channel_id=1, source_target_pairs={{0,1},{1,0},{2,3},{3,2},{4,5},{5,4},{6,7},{7,6},{8,9},{9,8},{10,11... | collective-permute-start | bytes 1572872 | tf_op jit(solution)/shard_map/ppermute | solution.py:33
  49.2 1.9 %collective-permute-start.9 = (f32[1,32,128]{2,1,0:T(8,128)S(1)}, f32[1,32,128]{2,1,0:T(8,128)S(1)}, u32[]{:S(2)}, u32[]{:S(2)}) collective-permute-start(f32[1,32,128]{2,1,0:T(8,128)S(1)} %get-tuple-element.59.rest_1_), channel_id=1, source_target_pairs={{0,1},{1,0},{2,3},{3,2},{4,5},{5,4},{6,7},{7,6},{8,9},{9,8},{10,11... | collective-permute-start | bytes 49160 | tf_op jit(solution)/shard_map/ppermute | solution.py:33
  55.5 20.7 %collective-permute-start.14 = (bf16[8,64,512]{2,1,0:T(8,128)(2,1)S(1)}, bf16[8,64,512]{2,1,0:T(8,128)(2,1)S(1)}, u32[]{:S(2)}, u32[]{:S(2)}) collective-permute-start(bf16[8,64,512]{2,1,0:T(8,128)(2,1)S(1)} %get-tuple-element.64.rest_3_), channel_id=1, source_target_pairs={{1,2},{2,1},{3,4},{4,3},{5,6},{6,5},{7,8},{8,7},{9,10},{10,9},{11,... | collective-permute-start | bytes 1572872 | tf_op jit(solution)/shard_map/ppermute | solution.py:33
  59.8 11.2 %collective-permute-start.12 = (bf16[608,128]{1,0:T(8,128)(2,1)S(1)}, bf16[608,128]{1,0:T(8,128)(2,1)S(1)}, u32[]{:S(2)}, u32[]{:S(2)}) collective-permute-start(bf16[608,128]{1,0:T(8,128)(2,1)S(1)} %get-tuple-element.69.own_ref), channel_id=1, source_target_pairs={{0,2},{1,3},{2,0},{3,1},{4,6},{5,7},{6,4},{7,5},{8,10},{9,11},{10,... | collective-permute-start | bytes 466952 | tf_op jit(solution)/shard_map/ppermute | solution.py:33
  63.7 11.5 %collective-permute-start.11 = (bf16[608,128]{1,0:T(8,128)(2,1)S(1)}, bf16[608,128]{1,0:T(8,128)(2,1)S(1)}, u32[]{:S(2)}, u32[]{:S(2)}) collective-permute-start(bf16[608,128]{1,0:T(8,128)(2,1)S(1)} %get-tuple-element.69.own_ref), channel_id=1, source_target_pairs={{0,1},{1,0},{2,3},{3,2},{4,5},{5,4},{6,7},{7,6},{8,9},{9,8},{10,11... | collective-permute-start | bytes 466952 | tf_op jit(solution)/shard_map/ppermute | solution.py:33
  71.0 5.1 %collective-permute-start.13 = (bf16[608,128]{1,0:T(8,128)(2,1)S(1)}, bf16[608,128]{1,0:T(8,128)(2,1)S(1)}, u32[]{:S(2)}, u32[]{:S(2)}) collective-permute-start(bf16[608,128]{1,0:T(8,128)(2,1)S(1)} %after.6.across_ref), channel_id=1, source_target_pairs={{0,1},{1,0},{2,3},{3,2},{4,5},{5,4},{6,7},{7,6},{8,9},{9,8},{10,11... | collective-permute-start | bytes 466952 | tf_op jit(solution)/shard_map/ppermute | solution.py:33
  75.2 7.7 %collective-permute-start.17 = (bf16[8,64,512]{2,1,0:T(8,128)(2,1)S(1)}, bf16[8,64,512]{2,1,0:T(8,128)(2,1)S(1)}, u32[]{:S(2)}, u32[]{:S(2)}) collective-permute-start(bf16[8,64,512]{2,1,0:T(8,128)(2,1)S(1)} %get-tuple-element.76), channel_id=1, source_target_pairs={{0,1},{1,0},{2,3},{3,2},{4,5},{5,4},{6,7},{7,6},{8,9},{9,8},{10,11... | collective-permute-start | bytes 1572872 | tf_op jit(solution)/shard_map/ppermute | solution.py:33
  76.2 14.3 %collective-permute-start.15 = (bf16[4,512,128]{2,1,0:T(8,128)(2,1)S(1)}, bf16[4,512,128]{2,1,0:T(8,128)(2,1)S(1)}, u32[]{:S(2)}, u32[]{:S(2)}) collective-permute-start(bf16[4,512,128]{2,1,0:T(8,128)(2,1)S(1)} %get-tuple-element.74.c0), channel_id=1, source_target_pairs={{1,4},{3,6},{4,1},{5,8},{6,3},{7,10},{8,5},{9,12},{10,7},{11,14},{... | collective-permute-start | bytes 1572872 | tf_op jit(solution)/shard_map/ppermute | solution.py:33
  76.9 13.6 %collective-permute-start.16 = (f32[1,32,128]{2,1,0:T(8,128)S(1)}, f32[1,32,128]{2,1,0:T(8,128)S(1)}, u32[]{:S(2)}, u32[]{:S(2)}) collective-permute-start(f32[1,32,128]{2,1,0:T(8,128)S(1)} %get-tuple-element.75), channel_id=1, source_target_pairs={{0,8},{1,13},{2,10},{3,15},{4,12},{5,9},{6,14},{7,11},{8,0},{9,5},... | collective-permute-start | bytes 49160 | tf_op jit(solution)/shard_map/ppermute | solution.py:33
  90.5 1.9 %collective-permute-start.19 = (bf16[4,512,128]{2,1,0:T(8,128)(2,1)S(1)}, bf16[4,512,128]{2,1,0:T(8,128)(2,1)S(1)}, u32[]{:S(2)}, u32[]{:S(2)}) collective-permute-start(bf16[4,512,128]{2,1,0:T(8,128)(2,1)S(1)} %get-tuple-element.78.c1), channel_id=1, source_target_pairs={{0,1},{1,0},{2,3},{3,2},{4,5},{5,4},{6,7},{7,6},{8,9},{9,8},{10,11... | collective-permute-start | bytes 1572872 | tf_op jit(solution)/shard_map/ppermute | solution.py:33
  90.5 1.9 %collective-permute-start.18 = (f32[1,32,128]{2,1,0:T(8,128)S(1)}, f32[1,32,128]{2,1,0:T(8,128)S(1)}, u32[]{:S(2)}, u32[]{:S(2)}) collective-permute-start(f32[1,32,128]{2,1,0:T(8,128)S(1)} %get-tuple-element.77.sum_a), channel_id=1, source_target_pairs={{0,1},{1,0},{2,3},{3,2},{4,5},{5,4},{6,7},{7,6},{8,9},{9,8},{10,11... | collective-permute-start | bytes 49160 | tf_op jit(solution)/shard_map/ppermute | solution.py:33
  97.2 1.3 %collective-permute-start.20 = (f32[64,128]{1,0:T(8,128)S(1)}, f32[64,128]{1,0:T(8,128)S(1)}, u32[]{:S(2)}, u32[]{:S(2)}) collective-permute-start(f32[64,128]{1,0:T(8,128)S(1)} %get-tuple-element.80), channel_id=1, source_target_pairs={{0,1},{1,0},{2,3},{3,2},{4,5},{5,4},{6,7},{7,6},{8,9},{9,8},{10,11... | collective-permute-start | bytes 98312 | tf_op jit(solution)/shard_map/ppermute | solution.py:33
  98.5 3.9 %collective-permute-start.21 = (f32[64,128]{1,0:T(8,128)S(1)}, f32[64,128]{1,0:T(8,128)S(1)}, u32[]{:S(2)}, u32[]{:S(2)}) collective-permute-start(f32[64,128]{1,0:T(8,128)S(1)} %add.34), channel_id=1, source_target_pairs={{0,2},{1,3},{2,0},{3,1},{4,6},{5,7},{6,4},{7,5},{8,10},{9,11},{10,... | collective-permute-start | bytes 98312 | tf_op jit(solution)/shard_map/ppermute | solution.py:33
  102.4 3.9 %collective-permute-start.22 = (f32[64,128]{1,0:T(8,128)S(1)}, f32[64,128]{1,0:T(8,128)S(1)}, u32[]{:S(2)}, u32[]{:S(2)}) collective-permute-start(f32[64,128]{1,0:T(8,128)S(1)} %add.35), channel_id=1, source_target_pairs={{0,4},{1,5},{2,6},{3,7},{4,0},{5,1},{6,2},{7,3},{8,12},{9,13},{10,... | collective-permute-start | bytes 98312 | tf_op jit(solution)/shard_map/ppermute | solution.py:33
  106.3 4.9 %collective-permute-start.23 = (f32[64,128]{1,0:T(8,128)S(1)}, f32[64,128]{1,0:T(8,128)S(1)}, u32[]{:S(2)}, u32[]{:S(2)}) collective-permute-start(f32[64,128]{1,0:T(8,128)S(1)} %add.36), channel_id=1, source_target_pairs={{0,8},{1,9},{2,10},{3,11},{4,12},{5,13},{6,14},{7,15},{8,0},{9,1},... | collective-permute-start | bytes 98312 | tf_op jit(solution)/shard_map/ppermute | solution.py:33
  (8 other events, 85.1 us)

commit v5 on v4

--- a/solution.py
+++ b/solution.py
@@ -1,4 +1,3 @@
-import functools
 import math
 
 import jax
@@ -18,6 +17,7 @@
 HALF_SCALE = math.sqrt(2.0 * KERNEL_SCALE * math.log2(math.e))
 UNROLL = 4
 FAR_UNROLL = 8
+RELAY_UNROLL = 4
 VMEM_LIMIT = 12 * 1024 * 1024
 WIDE_LIMIT = 54 * 1024 * 1024
 SELF_LIMIT = 28 * 1024 * 1024
@@ -144,14 +144,14 @@
     target[pl.ds(1, pairs, stride=2)] = pltpu.roll(flat, 64, 1)
 
 
-def relayout_kernel(pos_ref, coup_ref, coarse_ref, wait_ref, out_ref, coarse_out, by_slot, by_row, flat, square):
+def relayout_kernel(pos_ref, coup_ref, coarse_ref, wait_ref, out_ref, coarse_out, by_slots, by_rows, flat, square):
     per, slots, entries = coup_ref.shape
     rank = out_ref.shape[1] // 2
     quarter = rank // 2
     pairs = entries // 128
     lane = lax.broadcasted_iota(jnp.int32, (pairs, 128), 1) // quarter
 
-    def one(l, carry):
+    def one(l, by_slot, by_row):
         wide = coup_ref[l].astype(F32)
         for k in range(pairs):
             by_slot[k * slots : (k + 1) * slots] = wide[:, k * 128 : (k + 1) * 128]
@@ -168,9 +168,13 @@
         for half in range(2):
             for group in range(slots // 4):
                 out_ref[l, half * rank : (half + 1) * rank, group * 128 : (group + 1) * 128] = by_row[half, group].astype(BF16)
+
+    def trip(i, carry):
+        for u in range(by_slots.shape[0]):
+            one(i * by_slots.shape[0] + u, by_slots.at[u], by_rows.at[u])
         return carry
 
-    lax.fori_loop(0, per, one, 0)
+    lax.fori_loop(0, per // by_slots.shape[0], trip, 0)
     cluster = pos_ref[0] // CDEV
     wide = coarse_ref[cluster].astype(F32)
     number = lax.broadcasted_iota(jnp.int32, wide.shape, 0)
@@ -182,36 +186,22 @@
         coarse_out[at] = square[:, :rank].astype(BF16)
 
 
-def margins_kernel(pos_ref, e_ref, ex_ref, eo_ref, sems):
-    odd = pos_ref[0] % 2
-    width = ex_ref.shape[1]
-    first = pltpu.make_async_copy(
-        e_ref.at[:, pl.ds(pl.multiple_of((1 - odd) * width, width), width)], ex_ref, sems.at[0]
-    )
-    second = pltpu.make_async_copy(
-        e_ref.at[:, pl.ds(pl.multiple_of(odd * width, width), width)], eo_ref, sems.at[1]
-    )
-    first.start()
-    second.start()
-    first.wait()
-    second.wait()
-
-
 def prep_kernel(
-    pos_ref, rs_hbm, sc_hbm, basis_hbm, transfer_hbm, v_ref, cp_ref, part_ref, trans_ref, mx_ref, mo_ref,
-    rs_ref, sc_ref, basis_ref, transfer_ref, coefs, by_leaf, squares, sems,
+    pos_ref, rs_hbm, sc_hbm, basis_hbm, transfer_hbm, e_hbm, v_ref, cp_ref, part_ref, trans_ref, mx_ref, mo_ref,
+    rs_ref, sc_ref, basis_ref, transfer_ref, e_ref, points, coefs, by_leaf, squares, sems,
 ):
     per, rank, leaf = basis_ref.shape
+    columns, features = rs_ref.shape[0], e_ref.shape[0]
+    size = rank // 2
     copies = [
         pltpu.make_async_copy(source, target, sems.at[at])
         for at, (source, target) in enumerate(
-            ((transfer_hbm, transfer_ref), (sc_hbm, sc_ref), (rs_hbm, rs_ref), (basis_hbm, basis_ref))
+            ((transfer_hbm, transfer_ref), (sc_hbm, sc_ref), (rs_hbm, rs_ref), (basis_hbm, basis_ref), (e_hbm, e_ref))
         )
     ]
     for copy in copies:
         copy.start()
     copies[0].wait()
-    size = rank // 2
     wide = transfer_ref[...].astype(F32)
     for k in range(rank * rank // 128):
         by_leaf[k * per : (k + 1) * per] = wide[:, k * 128 : (k + 1) * 128]
@@ -224,6 +214,10 @@
     def one(at):
         rounded = (columns_of(rs_ref, at, leaf) * columns_of(sc_ref, at, leaf)).astype(BF16)
         v_ref[at] = rounded
+        here = columns_of(e_ref, at, leaf)
+        high = here.astype(BF16)
+        points[at, :features] = high
+        points[at, features:] = (here - high.astype(F32)).astype(BF16)
         coef = leaf_coefficients(basis_ref[at], rounded)
         coefs[pl.ds(pl.multiple_of(at * rank, rank), rank)] = coef
         cp_ref[pl.ds(pl.multiple_of(at * size, size), size)] = pack_pair(coef)
@@ -231,8 +225,10 @@
     leaf_loop(per, UNROLL, one)
     store_share(share_of(trans_ref[...], coefs[...]), part_ref, cp_ref)
     odd = pos_ref[0] % 2
-    mx_ref[...] = v_ref[pl.ds(per // 2 * (1 - odd), per // 2)]
-    mo_ref[...] = v_ref[pl.ds(per // 2 * odd, per // 2)]
+    half = per // 2
+    for ref, first in ((mx_ref, half * (1 - odd)), (mo_ref, half * odd)):
+        ref[:, :columns] = v_ref[pl.ds(first, half)]
+        ref[:, columns:] = points[pl.ds(first, half)]
 
 
 def quad_kernel(pos_ref, own_ref, sib_ref, across_ref, both_ref, part_ref, *rest):
@@ -249,44 +245,43 @@
     sum_ref[...] = total[None]
 
 
-def list_entries(near_ref, list_ref, pos, half, want_own, first, rows):
+def list_entries(near_ref, list_ref, pos, half, own_part):
     slots = near_ref.shape[0] - 1
+    total = near_ref.shape[1] * slots
     base = pos * 2 * half - half
 
-    def put(at, n):
-        entry = first * slots + at
+    def put(entry, carry):
+        n, seen = carry
         m = near_ref[1 + entry % slots, entry // slots] - base
         own = (m >= half) & (m < 3 * half)
+        early = own & (seen < 2 * half)
         list_ref[n] = entry
-        return n + jnp.where(own == want_own, 1, 0)
-
-    n = lax.fori_loop(0, rows * slots, put, 0)
+        return n + jnp.where(early == own_part, 1, 0), seen + jnp.where(own, 1, 0)
+
+    n, _ = lax.fori_loop(0, total, put, (0, 0))
     for u in range(UNROLL):
-        list_ref[n + u] = near_ref.shape[1] * slots
+        list_ref[n + u] = total
     return n
 
 
-def near_entry(near_ref, list_ref, at, pos, half, own):
+def near_entry(near_ref, list_ref, at, pos, half):
     slots = near_ref.shape[0] - 1
-    per = near_ref.shape[1]
     entry = list_ref[at]
     leaf_at = entry // slots
-    row = jnp.minimum(leaf_at, per - 1)
+    row = jnp.minimum(leaf_at, near_ref.shape[1] - 1)
     m = near_ref[1 + entry % slots, row] - (pos * 2 * half - half)
-    if own:
-        place = jnp.clip(m - half, 0, per - 1)
-    else:
-        place = jnp.clip(jnp.where(m < half, m, m - 2 * half), 0, 2 * half - 1)
-    return entry, leaf_at, row, place
-
-
-def load_halves(target, from_sibling, from_beside, odd):
+    return entry, leaf_at, row, jnp.clip(m, 0, 4 * half - 1)
+
+
+def load_window(target, own, from_sibling, from_beside, odd):
     half = from_sibling.shape[0]
-    target[pl.ds(half * (1 - odd), half)] = from_sibling[...]
-    target[pl.ds(half * odd, half)] = from_beside[...]
-
-
-def self_kernel(e_ref, v_ref, cp_in, self_ref, near_out, cp_out, buffer, sems):
+    rows = target.shape[1]
+    target[pl.ds(half, 2 * half)] = own[...]
+    target[pl.ds(3 * half * (1 - odd), half)] = from_sibling[:, :rows]
+    target[pl.ds(3 * half * odd, half)] = from_beside[:, :rows]
+
+
+def self_kernel(e_ref, v_ref, wait_ref, self_ref, near_out, buffer, sems):
     per, _, leaf = v_ref.shape
 
     def copy_out(slot, at):
@@ -323,11 +318,12 @@
     per, _, leaf = v_ref.shape
     half = per // 2
     pos = pos_ref[0]
-    n = list_entries(near_ref, list_ref, pos, half, True, 0, 2 * half)
+    n = list_entries(near_ref, list_ref, pos, half, True)
 
     def trip(i, carry):
         for u in range(UNROLL):
-            entry, leaf_at, row, place = near_entry(near_ref, list_ref, i * UNROLL + u, pos, half, True)
+            entry, leaf_at, row, m = near_entry(near_ref, list_ref, i * UNROLL + u, pos, half)
+            place = jnp.clip(m - half, 0, 2 * half - 1)
             tile = tile_of(other_rows(columns_of(e_ref, place, leaf)), own_rows(columns_of(e_ref, row, leaf)))
             tile_ref[entry] = tile
             near_out[leaf_at] += dot(v_ref[place], tile, 1, 0)
@@ -336,26 +332,30 @@
     lax.fori_loop(0, (n + UNROLL - 1) // UNROLL, trip, 0)
 
 
-def own_again_kernel(pos_ref, near_ref, v_ref, tile_ref, self_hbm, near_out, list_ref, self_ref, sems):
+def own_again_kernel(pos_ref, near_ref, v_ref, tile_ref, near_out, list_ref):
+    half = v_ref.shape[0] // 2
+    pos = pos_ref[0]
+    near_out[...] = jnp.zeros_like(near_out)
+    n = list_entries(near_ref, list_ref, pos, half, True)
+
+    def trip(i, carry):
+        for u in range(UNROLL):
+            entry, leaf_at, _, m = near_entry(near_ref, list_ref, i * UNROLL + u, pos, half)
+            place = jnp.clip(m - half, 0, 2 * half - 1)
+            near_out[leaf_at] += dot(v_ref[place], tile_ref[entry], 1, 0)
+        return carry
+
+    lax.fori_loop(0, (n + UNROLL - 1) // UNROLL, trip, 0)
+
+
+def self_again_kernel(v_ref, self_hbm, near_in, wait_ref, near_out, self_ref, sems):
     per = v_ref.shape[0]
-    half = per // 2
-    pos = pos_ref[0]
     copies = [
         pltpu.make_async_copy(self_hbm.at[pl.ds(at, UNROLL)], self_ref.at[pl.ds(at, UNROLL)], sems.at[at // UNROLL])
         for at in range(0, per, UNROLL)
     ]
     for copy in copies:
         copy.start()
-    near_out[...] = jnp.zeros_like(near_out)
-    n = list_entries(near_ref, list_ref, pos, half, True, 0, 2 * half)
-
-    def trip(i, carry):
-        for u in range(UNROLL):
-            entry, leaf_at, _, place = near_entry(near_ref, list_ref, i * UNROLL + u, pos, half, True)
-            near_out[leaf_at] += dot(v_ref[place], tile_ref[entry], 1, 0)
-        return carry
-
-    lax.fori_loop(0, (n + UNROLL - 1) // UNROLL, trip, 0)
     for i, copy in enumerate(copies):
         copy.wait()
         for u in range(UNROLL):
@@ -407,54 +407,54 @@
 
 
 def foreign_kernel(
-    pos_ref, near_ref, e_ref, ex_ref, eo_ref, vx_ref, vo_ref, tile_in, near_in, tile_ref, near_out, list_ref, vw,
+    pos_ref, near_ref, e_ref, v_ref, vx_ref, vo_ref, tile_in, near_in, tile_ref, near_out, list_ref, vw,
 ):
     half, _, leaf = vx_ref.shape
+    _, columns, _ = v_ref.shape
+    features = e_ref.shape[0]
     pos = pos_ref[0]
     odd = pos % 2
-    load_halves(vw, vx_ref, vo_ref, odd)
-    n = list_entries(near_ref, list_ref, pos, half, False, 0, 2 * half)
+    load_window(vw, v_ref, vx_ref, vo_ref, odd)
+    n = list_entries(near_ref, list_ref, pos, half, False)
+
+    def points_of(ref, at):
+        high = ref[at, columns : columns + features].astype(F32)
+        return high + ref[at, columns + features :].astype(F32)
 
     def trip(i, carry):
         for u in range(UNROLL):
-            entry, leaf_at, row, place = near_entry(near_ref, list_ref, i * UNROLL + u, pos, half, False)
-            beneath = place < half
-            from_x = beneath == (odd == 1)
-            within = jnp.where(beneath, place, place - half)
-            points = jnp.where(from_x, columns_of(ex_ref, within, leaf), columns_of(eo_ref, within, leaf))
+            entry, leaf_at, row, m = near_entry(near_ref, list_ref, i * UNROLL + u, pos, half)
+            own = (m >= half) & (m < 3 * half)
+            from_x = (m < half) == (odd == 1)
+            within = m % half
+            points = jnp.where(from_x, points_of(vx_ref, within), points_of(vo_ref, within))
+            points = jnp.where(own, columns_of(e_ref, jnp.clip(m - half, 0, 2 * half - 1), leaf), points)
             tile = tile_of(other_rows(points), own_rows(columns_of(e_ref, row, leaf)))
             tile_ref[entry] = tile
-            near_out[leaf_at] += dot(vw[place], tile, 1, 0)
+            near_out[leaf_at] += dot(vw[m], tile, 1, 0)
         return carry
 
     lax.fori_loop(0, (n + UNROLL - 1) // UNROLL, trip, 0)
 
 
 def far_first_kernel(
-    last, pos_ref, far_ref, rs_ref, sc_ref, basis_ref, coup_ref, trans_ref, near_ref, *rest,
+    pos_ref, far_ref, rs_ref, sc_ref, basis_ref, coup_ref, trans_ref, near_ref, coarse_ref, sum_a, sum_b, c0, c1, c2,
+    u_ref, q_ref, cp_ref, part_ref, msg_ref, mx_ref, mo_ref, cw, fc, mv, coefs, acc_uu, acc_ru,
 ):
     per, rank, leaf = basis_ref.shape
     half = per // 2
     size = rank // 2
     pos = pos_ref[0]
     odd = pos % 2
-    first = half * ((1 - odd) if last else odd)
-    if last:
-        cw, mv, u_in, q_before, cp_before, share_before, msg_before = rest[:7]
-        u_ref, mx_ref, q_ref, cp_ref, part_ref, msg_ref, coefs, acc_uu, acc_ru = rest[7:]
-    else:
-        coarse_ref, sum_a, sum_b, c0, c1, c2 = rest[:6]
-        cw, mv, u_ref, mx_ref, cp_ref, share_ref, msg_ref, fc, coefs, acc_uu, acc_ru = rest[6:]
-        load_coefficients(cw, (c0, c1, c2))
-        coarse_rows(coarse_ref, (sum_a, sum_b), fc)
-        store_moved(trans_ref[...], fc, mv)
+    load_coefficients(cw, (c0, c1, c2))
+    coarse_rows(coarse_ref, (sum_a, sum_b), fc)
+    store_moved(trans_ref[...], fc, mv)
     acc_uu[...] = jnp.zeros_like(acc_uu)
     acc_ru[...] = jnp.zeros_like(acc_ru)
-    cp_first = first * size if last else 0
-
-    def one(j):
-        l = first + j
-        far = far_sum(l, pos, far_ref, cw, coup_ref, mv[pl.ds(pl.multiple_of(l * rank, rank), rank)], basis_ref)
+
+    def one(l):
+        rows = pl.ds(pl.multiple_of(l * rank, rank), rank)
+        far = far_sum(l, pos, far_ref, cw, coup_ref, mv[rows], basis_ref)
         right = columns_of(rs_ref, l, leaf)
         scale = columns_of(sc_ref, l, leaf)
         image = RIDGE_TERM * (right * scale) + (near_ref[l] + far)
@@ -462,38 +462,30 @@
         acc_uu[...] += lane_groups(image * image)
         acc_ru[...] += lane_groups(right * image)
         rounded = (image * scale).astype(BF16)
-        mx_ref[j] = rounded
+        q_ref[l] = rounded
         coef = leaf_coefficients(basis_ref[l], rounded)
-        coefs[pl.ds(pl.multiple_of(j * rank, rank), rank)] = coef
-        cp_ref[pl.ds(pl.multiple_of(cp_first + j * size, size), size)] = pack_pair(coef)
-
-    leaf_loop(half, FAR_UNROLL, one)
-    share = share_of(trans_ref[pl.ds(first, half)], coefs[...])
+        coefs[rows] = coef
+        cp_ref[pl.ds(pl.multiple_of(l * size, size), size)] = pack_pair(coef)
+
+    leaf_loop(per, FAR_UNROLL, one)
+    store_share(share_of(trans_ref[...], coefs[...]), part_ref, cp_ref)
+    mx_ref[...] = q_ref[pl.ds(half * (1 - odd), half)]
+    mo_ref[...] = q_ref[pl.ds(half * odd, half)]
     lane = lax.broadcasted_iota(jnp.int32, msg_ref.shape, 1)
     out = jnp.where(lane == 0, jnp.sum(acc_uu[...], axis=1, keepdims=True), 0.0)
-    out = jnp.where(lane == 1, jnp.sum(acc_ru[...], axis=1, keepdims=True), out)
-    if last:
-        other = half - first
-        cp_ref[pl.ds(pl.multiple_of(other * size, size), half * size)] = cp_before[...]
-        q_ref[pl.ds(other, half)] = q_before[...]
-        q_ref[pl.ds(first, half)] = mx_ref[...]
-        store_share(share + share_before[...], part_ref, cp_ref)
-        msg_ref[...] = out + msg_before[...]
-    else:
-        share_ref[...] = share
-        msg_ref[...] = out
-
-
-def near_again_kernel(pos_ref, near_ref, vx_ref, vo_ref, tile_ref, near_in, near_out, list_ref, vw):
+    msg_ref[...] = jnp.where(lane == 1, jnp.sum(acc_ru[...], axis=1, keepdims=True), out)
+
+
+def near_again_kernel(pos_ref, near_ref, q_ref, vx_ref, vo_ref, tile_ref, near_in, near_out, list_ref, vw):
     half = vx_ref.shape[0]
     pos = pos_ref[0]
-    load_halves(vw, vx_ref, vo_ref, pos % 2)
-    n = list_entries(near_ref, list_ref, pos, half, False, 0, 2 * half)
+    load_window(vw, q_ref, vx_ref, vo_ref, pos % 2)
+    n = list_entries(near_ref, list_ref, pos, half, False)
 
     def trip(i, carry):
         for u in range(UNROLL):
-            entry, leaf_at, _, place = near_entry(near_ref, list_ref, i * UNROLL + u, pos, half, False)
-            near_out[leaf_at] += dot(vw[place], tile_ref[entry], 1, 0)
+            entry, leaf_at, _, m = near_entry(near_ref, list_ref, i * UNROLL + u, pos, half)
+            near_out[leaf_at] += dot(vw[m], tile_ref[entry], 1, 0)
         return carry
 
     lax.fori_loop(0, (n + UNROLL - 1) // UNROLL, trip, 0)
@@ -604,7 +596,6 @@
     slots = near_leaves.shape[1] - 1
     far_count = far_leaves.shape[1]
     half = per // 2
-    margin = half * leaf
     size = rank // 2
     count = lax.axis_size("leaf")
     pos = lax.axis_index("leaf")
@@ -613,24 +604,13 @@
     far_rows = far_leaves.T
     coarse_count = count // CDEV
 
-    margin_shape = pltpu.VMEM((features, margin), F32)
-    ex, eo = call(
-        margins_kernel, "margins", [SCALAR, ANYWHERE], [margin_shape] * 2,
-        [pltpu.SemaphoreType.DMA((2,))], (position, embeddings), limit=WIDE_LIMIT,
-    )
-    e_sibling = sibling(ex)
-    e_beside = beside(eo)
-
     scale_row = scaling.reshape(1, local_points)
     leaf_shape = pltpu.VMEM((per, columns, leaf), BF16)
     cp_shape = pltpu.VMEM((per * size + 3 * size, 2 * columns), BF16)
     part_shape = pltpu.VMEM((size, 2 * columns), F32)
-    self_shape = pltpu.HBM((4 * per, leaf, leaf), BF16)
+    self_shape = pltpu.HBM((8 * per, leaf, leaf), BF16)
     trans_shape = pltpu.VMEM((per, rank, rank), BF16)
     half_shape = pltpu.VMEM((half, columns, leaf), BF16)
-    share_shape = pltpu.VMEM((rank, columns), F32)
-    cp_half_shape = pltpu.VMEM((half * size, 2 * columns), BF16)
-    half_coefs_shape = pltpu.VMEM((half * rank, columns), BF16)
     moved_shape = pltpu.VMEM((per * rank, columns), F32)
     tile_shape = pltpu.VMEM((per * slots + 1, leaf, leaf), BF16)
     near_shape = pltpu.VMEM((per + 1, columns, leaf), F32)
@@ -640,82 +620,84 @@
     acc_shape = pltpu.VMEM((columns, 128), F32)
     list_shape = pltpu.SMEM((per * slots + UNROLL,), jnp.int32)
     window = [
-        pltpu.VMEM((2 * half, columns, leaf), BF16),
+        pltpu.VMEM((4 * half, columns, leaf), BF16),
         pltpu.VMEM((12 * per, size, 2 * columns), BF16),
         pltpu.VMEM((rank, 3 * columns), BF16),
     ]
 
+    both_shape = pltpu.VMEM((half, columns + 2 * features, leaf), BF16)
     v, cp, part, trans, mx, mo = call(
-        prep_kernel, "prep", [SCALAR] + [OUTSIDE] * 4,
-        [leaf_shape, cp_shape, part_shape, trans_shape, half_shape, half_shape],
+        prep_kernel, "prep", [SCALAR] + [OUTSIDE] * 5,
+        [leaf_shape, cp_shape, part_shape, trans_shape, both_shape, both_shape],
         [pltpu.VMEM(right_side.shape, F32), pltpu.VMEM(scale_row.shape, F32), pltpu.VMEM(leaf_basis.shape, BF16),
-         pltpu.VMEM(transfer.shape, BF16), coefs_shape, pltpu.VMEM((per * rank * rank // 128, 128), F32), pltpu.VMEM((per, rank, 128), F32), pltpu.SemaphoreType.DMA((4,))],
-        (position, right_side, scale_row, leaf_basis, transfer), limit=WIDE_LIMIT,
-    )
-    tself, near, cp = call(
-        self_kernel, "self_tiles", [WHOLE] * 3, [self_shape, near_shape, cp_shape],
-        [pltpu.VMEM((2 * UNROLL, leaf, leaf), BF16), pltpu.SemaphoreType.DMA((2 * UNROLL,))],
-        (embeddings, v, cp), out_specs=[OUTSIDE, WHOLE, WHOLE], aliases={2: 2},
+         pltpu.VMEM(transfer.shape, BF16), pltpu.VMEM(embeddings.shape, F32),
+         pltpu.VMEM((per, 2 * features, leaf), BF16), coefs_shape, pltpu.VMEM((per * rank * rank // 128, 128), F32), pltpu.VMEM((per, rank, 128), F32), pltpu.SemaphoreType.DMA((5,))],
+        (position, right_side, scale_row, leaf_basis, transfer, embeddings), limit=WIDE_LIMIT,
     )
     got = first_messages(cp)
-    vo = beside(mo)
     coup, coarse = call(
         relayout_kernel, "relayout", [SCALAR] + [WHOLE] * 2 + [ANYWHERE],
         [pltpu.VMEM((per, 2 * rank, far_count * size), BF16), pltpu.VMEM((coarse_count - 1, rank, rank), BF16)],
         [
-            pltpu.VMEM((far_count * rank * rank // 128, 128), F32),
-            pltpu.VMEM((2, far_count // 4, rank, 128), F32),
+            pltpu.VMEM((RELAY_UNROLL, far_count * rank * rank // 128, 128), F32),
+            pltpu.VMEM((RELAY_UNROLL, 2, far_count // 4, rank, 128), F32),
             pltpu.VMEM((size, 128), F32), pltpu.VMEM((rank, 128), F32),
         ],
         (position, leaf_coupling, coarse_coupling, cp),
     )
-    tiles, near = call(
-        own_kernel, "own_tiles", [SCALAR] * 2 + [WHOLE] * 3 + [ANYWHERE] * 2, [tile_shape, near_shape], [list_shape],
-        (position, near_rows, embeddings, v, near, coup, e_beside), aliases={4: 1}, flops=2 * per * leaf * leaf * 320,
-    )
-    got = (got[0], *after(got[1:], near))
-    quad, far_quad, mine = second_messages(position, cp, got, part, vo)
+    across_cp, mo = after((got[1], mo), coup)
+    got = (got[0], across_cp)
+    vo = beside(mo)
+    tself, near = call(
+        self_kernel, "self_tiles", [WHOLE] * 2 + [ANYWHERE], [self_shape, near_shape],
+        [pltpu.VMEM((2 * UNROLL, leaf, leaf), BF16), pltpu.SemaphoreType.DMA((2 * UNROLL,))],
+        (embeddings, v, mo), out_specs=[OUTSIDE, WHOLE],
+    )
+    quad, far_quad, mine = second_messages(position, cp, got, part, near)
+    (mx,) = after((mx,), quad)
     vx = sibling(mx)
     tiles, near = call(
-        foreign_kernel, "foreign_tiles", [SCALAR] * 2 + [WHOLE] * 7, [tile_shape, near_shape],
+        own_kernel, "own_tiles", [SCALAR] * 2 + [WHOLE] * 3 + [ANYWHERE], [tile_shape, near_shape], [list_shape],
+        (position, near_rows, embeddings, v, near, quad), aliases={4: 1},
+    )
+    tiles, near = call(
+        foreign_kernel, "foreign_tiles", [SCALAR] * 2 + [WHOLE] * 6, [tile_shape, near_shape],
         [list_shape, window[0]],
-        (position, near_rows, embeddings, e_sibling, e_beside, vx, vo, tiles, near),
-        aliases={7: 0, 8: 1}, flops=2 * per * leaf * leaf * 320,
+        (position, near_rows, embeddings, v, vx, vo, tiles, near), aliases={6: 0, 7: 1},
     )
     coefs, sums = last_messages(*after((far_quad, mine), near))
-    common = (position, far_rows, right_side, scale_row, leaf_basis, coup, trans, near)
-    cw, mv, image, mo, cp_half, share, msg = call(
-        functools.partial(far_first_kernel, False), "far_half", [SCALAR] * 2 + [WHOLE] * 12,
-        [window[1], moved_shape, wide_shape, half_shape, cp_half_shape, share_shape, msg_shape],
-        [window[2], half_coefs_shape, acc_shape, acc_shape],
-        (*common, coarse, *sums, quad, *coefs), flops=per * leaf * leaf * 32,
-    )
-    vo = beside(mo)
-    image, mx, q, cp, part, msg = call(
-        functools.partial(far_first_kernel, True), "other_half", [SCALAR] * 2 + [WHOLE] * 13,
-        [wide_shape, half_shape, leaf_shape, cp_shape, part_shape, msg_shape],
-        [half_coefs_shape, acc_shape, acc_shape],
-        (*common, cw, mv, image, mo, cp_half, share, msg), aliases={10: 0}, flops=per * leaf * leaf * 32,
+    image, q, cp, part, msg, mx, mo = call(
+        far_first_kernel, "far_first", [SCALAR] * 2 + [WHOLE] * 12,
+        [wide_shape, leaf_shape, cp_shape, part_shape, msg_shape, half_shape, half_shape],
+        [*window[1:], moved_shape, coefs_shape, acc_shape, acc_shape],
+        (position, far_rows, right_side, scale_row, leaf_basis, coup, trans, near, coarse, *sums, quad, *coefs),
     )
     got = first_messages(cp)
     (near,) = call(
-        own_again_kernel, "own_again", [SCALAR] * 2 + [WHOLE] * 2 + [OUTSIDE], [near_shape],
-        [list_shape, pltpu.VMEM((per, leaf, leaf), BF16), pltpu.SemaphoreType.DMA((per // UNROLL,))],
-        (position, near_rows, q, tiles, tself), flops=2 * per * leaf * leaf * 64,
-    )
-    got = (got[0], *after(got[1:], near))
-    quad, far_quad, mine = second_messages(position, cp, got, part, vo)
+        own_again_kernel, "own_again", [SCALAR] * 2 + [WHOLE] * 2, [near_shape], [list_shape],
+        (position, near_rows, q, tiles),
+    )
+    across_cp, mo = after((got[1], mo), near)
+    got = (got[0], across_cp)
+    vo = beside(mo)
+    quad, far_quad, mine = second_messages(position, cp, got, part)
+    (mx,) = after((mx,), quad)
     vx = sibling(mx)
     (near,) = call(
-        near_again_kernel, "near_again", [SCALAR] * 2 + [WHOLE] * 4, [near_shape], [list_shape, window[0]],
-        (position, near_rows, vx, vo, tiles, near), aliases={5: 0}, flops=2 * per * leaf * leaf * 64,
+        self_again_kernel, "self_again", [WHOLE, OUTSIDE, WHOLE, ANYWHERE], [near_shape],
+        [pltpu.VMEM((per, leaf, leaf), BF16), pltpu.SemaphoreType.DMA((per // UNROLL,))],
+        (q, tself, near, quad), aliases={2: 0},
+    )
+    (near,) = call(
+        near_again_kernel, "near_again", [SCALAR] * 2 + [WHOLE] * 5, [near_shape], [list_shape, window[0]],
+        (position, near_rows, q, vx, vo, tiles, near), aliases={6: 0},
     )
     coefs, sums = last_messages(*after((far_quad, mine), near))
     second, msg = call(
         far_again_kernel, "far_again", [SCALAR] * 2 + [WHOLE] * 14, [wide_shape, msg_shape],
         window[1:] + [moved_shape] + [acc_shape] * 3,
         (position, far_rows, right_side, scale_row, image, leaf_basis, coup, trans,
-         coarse, *sums, quad, *coefs, near, msg), flops=per * leaf * leaf * 64,
+         coarse, *sums, quad, *coefs, near, msg),
     )
 
     mask = 1

time: 114 us -> 109 us (0.956)
  waiting for transfers between devices: 25.3 us -> 17 us
  starting transfers between devices: 33.7 us -> 37.3 us
    ppermute x24 -> x22, waiting for transfers between devices: 25.3 us -> 17 us  [involution(): return lax.ppermute(value, 'leaf', pairs)]
    ppermute x24 -> x22, starting transfers between devices: 33.7 us -> 37.3 us  [involution(): return lax.ppermute(value, 'leaf', pairs)]
    pallas_call x17 -> x18, Pallas kernels: 51.2 us -> 50.7 us  [call(): pl.pallas_call(kernel, in_specs=in_specs, out_specs=out_specs or [WHOLE]...]
  transfers between devices with their start and end apart: 24 -> 22, of which waited for: 10 -> 10; matrix products, arithmetic and copies ran while one was open for 0% -> 0% of each run, Pallas kernels for 36% -> 32%
where the time goes in v5:
time: 109 us
  Pallas kernels  50.7 us (47%)
  starting transfers between devices  37.3 us (34%)
  waiting for transfers between devices  17 us (16%)
  other arithmetic  2.94 us (3%)
    pallas_call x18, Pallas kernels, call(): pl.pallas_call(kernel, in_specs=in_specs, out_specs=out_specs or [WHOLE]...  50.7 us
    ppermute x22, starting transfers between devices, involution(): return lax.ppermute(value, 'leaf', pairs)  37.3 us
    ppermute x22, waiting for transfers between devices, involution(): return lax.ppermute(value, 'leaf', pairs)  17 us
    add x1, other arithmetic, body(): residual = right_side - first_weight * image + second_weight * second  2.71 us
  transfers between devices with their start and end apart: 22, of which 10 were waited for; matrix products, arithmetic and copies ran while one was open for 0% of the time, Pallas kernels for 32%

profile of v5, /device:TPU:0, one launch (start us, length us, event | category | flops | bytes accessed | tf_op | source)
XLA Modules:
  0.0 109.0 jit_solution(14657641700547041956)
XLA Ops:
  0.7 4.0 %prep.1 = (bf16[16,64,512]{2,1,0:T(8,128)(2,1)S(1)}, bf16[608,128]{1,0:T(8,128)(2,1)S(1)}, f32[32,128]{1,0:T(8,128)S(1)}, bf16[16,64,64]{2,1,0:T(8,128)(2,1)S(1)...) custom-call(s32[1]{0:T(128)} %bitcast.pos_ref, f32[64,8192]{1,0:T(8,128)} %rs_ref.3, ...), custom_call_target="tpu_custom_call" | custom-call | tf_op jit(solution)/shard_map/prep/pallas_call | solution.py:525
  4.7 3.0 %collective-permute-start.1 = (bf16[608,128]{1,0:T(8,128)(2,1)S(1)}, bf16[608,128]{1,0:T(8,128)(2,1)S(1)}, u32[]{:S(2)}, u32[]{:S(2)}) collective-permute-start(bf16[608,128]{1,0:T(8,128)(2,1)S(1)} %get-tuple-element.37.wait_ref.own_ref), channel_id=1, source_target_pairs={{0,2},{1,3},{2,0},{3,1},{4,6},{5,7},{6,4},{7,5},{8,10},{9,11},{10,... | collective-permute-start | bytes 466952 | tf_op jit(solution)/shard_map/ppermute | solution.py:33
  7.7 2.3 %relayout.1 = (bf16[16,128,256]{2,1,0:T(8,128)(2,1)S(1)}, bf16[1,64,64]{2,1,0:T(8,128)(2,1)S(1)}) custom-call(s32[1]{0:T(128)} %bitcast.pos_ref, bf16[16,8,4096]{2,1,0:T(8,128)(2,1)S(1)} %copy-done.3, bf16[2,2,4096]{2,1,0:T(2,128)(2,1)S(1)} %copy-done.5, bf16[608,128]{1,0:T(8,128)(2,1)S(1)} %get-tuple-element.37.wait_ref.own_ref), custom_call_target="tpu_custom_call" | custom-call | tf_op jit(solution)/shard_map/relayout/pallas_call | solution.py:525
  12.4 7.2 %self_tiles.1 = (bf16[128,512,512]{2,1,0:T(8,128)(2,1)}, f32[17,64,512]{2,1,0:T(8,128)S(1)}) custom-call(f32[32,8192]{1,0:T(8,128)S(1)} %copy-done.1, bf16[16,64,512]{2,1,0:T(8,128)(2,1)S(1)} %get-tuple-element.40.v_ref, bf16[8,128,512]{2,1,0:T(8,128)(2,1)S(1)} %get-tuple-element.45.wait_ref), custom_call_target="tpu_custom_call" | custom-call | tf_op jit(solution)/shard_map/self_tiles/pallas_call | solution.py:525
  19.8 3.1 %collective-permute-start.3 = (bf16[8,128,512]{2,1,0:T(8,128)(2,1)S(1)}, bf16[8,128,512]{2,1,0:T(8,128)(2,1)S(1)}, u32[]{:S(2)}, u32[]{:S(2)}) collective-permute-start(bf16[8,128,512]{2,1,0:T(8,128)(2,1)S(1)} %after.7), channel_id=1, source_target_pairs={{0,1},{1,0},{2,3},{3,2},{4,5},{5,4},{6,7},{7,6},{8,9},{9,8},{10,11... | collective-permute-start | bytes 3145736 | tf_op jit(solution)/shard_map/ppermute | solution.py:33
  23.6 4.3 %collective-permute-start.6 = (f32[1,32,128]{2,1,0:T(8,128)S(1)}, f32[1,32,128]{2,1,0:T(8,128)S(1)}, u32[]{:S(2)}, u32[]{:S(2)}) collective-permute-start(f32[1,32,128]{2,1,0:T(8,128)S(1)} %get-tuple-element.52), channel_id=1, source_target_pairs={{0,8},{1,13},{2,10},{3,15},{4,12},{5,9},{6,14},{7,11},{8,0},{9,5},... | collective-permute-start | bytes 49160 | tf_op jit(solution)/shard_map/ppermute | solution.py:33
  27.9 7.3 %own_tiles.1 = (bf16[33,512,512]{2,1,0:T(8,128)(2,1)S(1)}, f32[17,64,512]{2,1,0:T(8,128)S(1)}) custom-call(s32[1]{0:T(128)} %bitcast.pos_ref, s32[3,16]{1,0:T(4,128)S(1)} %bitcast.7, f32[32,8192]{1,0:T(8,128)S(1)} %copy-done.1, bf16[16,64,512]{2,1,0:T(8,128)(2,1)S(1)} %get-tuple-element.40.v_ref, ...), custom_call_target="tpu_custom_call", output_to_operand_aliasing={{1}: (4, {})} | custom-call | tf_op jit(solution)/shard_map/own_tiles/pallas_call | solution.py:525
  35.2 7.4 %foreign_tiles.1 = (bf16[33,512,512]{2,1,0:T(8,128)(2,1)S(1)}, f32[17,64,512]{2,1,0:T(8,128)S(1)}) custom-call(s32[1]{0:T(128)} %bitcast.pos_ref, s32[3,16]{1,0:T(4,128)S(1)} %bitcast.8, f32[32,8192]{1,0:T(8,128)S(1)} %copy-done.1, bf16[16,64,512]{2,1,0:T(8,128)(2,1)S(1)} %get-tuple-element.40.v_ref, ...), custom_call_target="tpu_custom_call", output_to_operand_aliasing={{0}: (6, {}), {1}: (7, {})} | custom-call | tf_op jit(solution)/shard_map/foreign_tiles/pallas_call | solution.py:525
  42.6 3.3 %collective-permute-start.8 = (bf16[4,512,128]{2,1,0:T(8,128)(2,1)S(1)}, bf16[4,512,128]{2,1,0:T(8,128)(2,1)S(1)}, u32[]{:S(2)}, u32[]{:S(2)}) collective-permute-start(bf16[4,512,128]{2,1,0:T(8,128)(2,1)S(1)} %get-tuple-element.54.c1), channel_id=1, source_target_pairs={{0,1},{1,0},{2,3},{3,2},{4,5},{5,4},{6,7},{7,6},{8,9},{9,8},{10,11... | collective-permute-start | bytes 1572872 | tf_op jit(solution)/shard_map/ppermute | solution.py:33
  47.5 7.2 %far_first.1 = (f32[64,8192]{1,0:T(8,128)S(1)}, bf16[16,64,512]{2,1,0:T(8,128)(2,1)S(1)}, bf16[608,128]{1,0:T(8,128)(2,1)S(1)}, f32[32,128]{1,0:T(8,128)S(1)}, f...) custom-call(s32[1]{0:T(128)} %bitcast.pos_ref, s32[8,16]{1,0:T(8,128)S(1)} %bitcast.11, ...), custom_call_target="tpu_custom_call" | custom-call | tf_op jit(solution)/shard_map/far_first/pallas_call | solution.py:525
  54.7 5.8 %collective-permute-start.10 = (bf16[608,128]{1,0:T(8,128)(2,1)S(1)}, bf16[608,128]{1,0:T(8,128)(2,1)S(1)}, u32[]{:S(2)}, u32[]{:S(2)}) collective-permute-start(bf16[608,128]{1,0:T(8,128)(2,1)S(1)} %get-tuple-element.56.own_ref), channel_id=1, source_target_pairs={{0,2},{1,3},{2,0},{3,1},{4,6},{5,7},{6,4},{7,5},{8,10},{9,11},{10,... | collective-permute-start | bytes 466952 | tf_op jit(solution)/shard_map/ppermute | solution.py:33
  60.6 3.2 %own_again.1.refs_2_.near_in = f32[17,64,512]{2,1,0:T(8,128)S(1)} custom-call(s32[1]{0:T(128)} %bitcast.pos_ref, s32[3,16]{1,0:T(4,128)S(1)} %bitcast.9, bf16[16,64,512]{2,1,0:T(8,128)(2,1)S(1)} %get-tuple-element.58.v_ref.q_ref, bf16[33,512,512]{2,1,0:T(8,128)(2,1)S(1)} %get-tuple-element.59.tile_ref), custom_call_target="tpu_custom_call" | custom-call | tf_op jit(solution)/shard_map/own_again/pallas_call | solution.py:525
  66.3 2.5 %collective-permute-start.14 = (bf16[8,64,512]{2,1,0:T(8,128)(2,1)S(1)}, bf16[8,64,512]{2,1,0:T(8,128)(2,1)S(1)}, u32[]{:S(2)}, u32[]{:S(2)}) collective-permute-start(bf16[8,64,512]{2,1,0:T(8,128)(2,1)S(1)} %after.10), channel_id=1, source_target_pairs={{0,1},{1,0},{2,3},{3,2},{4,5},{5,4},{6,7},{7,6},{8,9},{9,8},{10,11... | collective-permute-start | bytes 1572872 | tf_op jit(solution)/shard_map/ppermute | solution.py:33
  69.5 4.3 %collective-permute-start.13 = (f32[1,32,128]{2,1,0:T(8,128)S(1)}, f32[1,32,128]{2,1,0:T(8,128)S(1)}, u32[]{:S(2)}, u32[]{:S(2)}) collective-permute-start(f32[1,32,128]{2,1,0:T(8,128)S(1)} %get-tuple-element.63), channel_id=1, source_target_pairs={{0,8},{1,13},{2,10},{3,15},{4,12},{5,9},{6,14},{7,11},{8,0},{9,5},... | collective-permute-start | bytes 49160 | tf_op jit(solution)/shard_map/ppermute | solution.py:33
  73.8 4.0 %self_again.1.near_in = f32[17,64,512]{2,1,0:T(8,128)S(1)} custom-call(bf16[16,64,512]{2,1,0:T(8,128)(2,1)S(1)} %get-tuple-element.58.v_ref.q_ref, bf16[128,512,512]{2,1,0:T(8,128)(2,1)} %get-tuple-element.66.self_hbm, f32[17,64,512]{2,1,0:T(8,128)S(1)} %own_again.1.refs_2_.near_in, ...), custom_call_target="tpu_custom_call", output_to_operand_aliasing={{}: (2, {})} | custom-call | tf_op jit(solution)/shard_map/self_again/pallas_call | solution.py:525
  77.8 3.4 %near_again.1.refs_2_.near_ref = f32[17,64,512]{2,1,0:T(8,128)S(1)} custom-call(s32[1]{0:T(128)} %bitcast.pos_ref, s32[3,16]{1,0:T(4,128)S(1)} %bitcast.10, bf16[16,64,512]{2,1,0:T(8,128)(2,1)S(1)} %get-tuple-element.58.v_ref.q_ref, bf16[8,64,512]{2,1,0:T(8,128)(2,1)S(1)} %collective-permute-done.14.vx_ref, ...), custom_call_target="tpu_custom_call", output_to_operand_aliasing={{}: (6, {})} | custom-call | tf_op jit(solution)/shard_map/near_again/pallas_call | solution.py:525
  81.2 3.4 %collective-permute-done.13.refs_1_ = f32[1,32,128]{2,1,0:T(8,128)S(1)} collective-permute-done((f32[1,32,128]{2,1,0:T(8,128)S(1)}, f32[1,32,128]{2,1,0:T(8,128)S(1)}, u32[]{:S(2)}, u32[]{:S(2)}) %collective-permute-start.13) | collective-permute-done | bytes 16416 | tf_op jit(solution)/shard_map/ppermute | solution.py:33
  86.6 4.7 %far_again.1 = (f32[64,8192]{1,0:T(8,128)S(1)}, f32[64,128]{1,0:T(8,128)S(1)}) custom-call(s32[1]{0:T(128)} %bitcast.pos_ref, s32[8,16]{1,0:T(8,128)S(1)} %bitcast.12, f32[64,8192]{1,0:T(8,128)S(1)} %copy-done, f32[1,8192]{1,0:T(1,128)S(1)} %bitcast.6, f32[64,8192]{1,0:T(8,128)S(1)} %get-tuple-element.55.u_ref, bf16[16,64,512]{2,1,0:T(8,128)(2,1)S(1)} %copy-done.2, ...), custom_call_target="tpu_custom_call" | custom-call | tf_op jit(solution)/shard_map/far_again/pallas_call | solution.py:525
  92.5 2.6 %collective-permute-start.19 = (f32[64,128]{1,0:T(8,128)S(1)}, f32[64,128]{1,0:T(8,128)S(1)}, u32[]{:S(2)}, u32[]{:S(2)}) collective-permute-start(f32[64,128]{1,0:T(8,128)S(1)} %add.34), channel_id=1, source_target_pairs={{0,2},{1,3},{2,0},{3,1},{4,6},{5,7},{6,4},{7,5},{8,10},{9,11},{10,... | collective-permute-start | bytes 98312 | tf_op jit(solution)/shard_map/ppermute | solution.py:33
  95.1 1.9 %collective-permute-done.19 = f32[64,128]{1,0:T(8,128)S(1)} collective-permute-done((f32[64,128]{1,0:T(8,128)S(1)}, f32[64,128]{1,0:T(8,128)S(1)}, u32[]{:S(2)}, u32[]{:S(2)}) %collective-permute-start.19) | collective-permute-done | bytes 32800 | tf_op jit(solution)/shard_map/ppermute | solution.py:33
  98.6 2.3 %collective-permute-done.20 = f32[64,128]{1,0:T(8,128)S(1)} collective-permute-done((f32[64,128]{1,0:T(8,128)S(1)}, f32[64,128]{1,0:T(8,128)S(1)}, u32[]{:S(2)}, u32[]{:S(2)}) %collective-permute-start.20) | collective-permute-done | bytes 32800 | tf_op jit(solution)/shard_map/ppermute | solution.py:33
  100.9 3.2 %collective-permute-start.21 = (f32[64,128]{1,0:T(8,128)S(1)}, f32[64,128]{1,0:T(8,128)S(1)}, u32[]{:S(2)}, u32[]{:S(2)}) collective-permute-start(f32[64,128]{1,0:T(8,128)S(1)} %add.36), channel_id=1, source_target_pairs={{0,8},{1,9},{2,10},{3,11},{4,12},{5,13},{6,14},{7,15},{8,0},{9,1},... | collective-permute-start | bytes 98312 | tf_op jit(solution)/shard_map/ppermute | solution.py:33
  104.1 1.9 %collective-permute-done.21 = f32[64,128]{1,0:T(8,128)S(1)} collective-permute-done((f32[64,128]{1,0:T(8,128)S(1)}, f32[64,128]{1,0:T(8,128)S(1)}, u32[]{:S(2)}, u32[]{:S(2)}) %collective-permute-start.21) | collective-permute-done | bytes 32800 | tf_op jit(solution)/shard_map/ppermute | solution.py:33
  106.3 2.7 %multiply_add_fusion = (f32[64,8192]{1,0:T(8,128)}, f32[64,8192]{1,0:T(8,128)}) fusion(f32[64,8192]{1,0:T(8,128)S(1)} %get-tuple-element.71, f32[64,8192]{1,0:T(8,128)S(1)} %copy-done, f32[64,8192]{1,0:T(8,128)S(1)} %get-tuple-element.55.u_ref, f32[64]{0:T(128)S(1)} %get-tuple-element.73, f32[64]{0:T(128)S(1)} %get-tuple-element.72, f32[8192]{0:T(1024)S(1)} %copy-done.4), kind=kLoop, calls=%fused_computation | loop fusion | flops 4194304 | bytes 10519040 | tf_op jit(solution)/shard_map/add | solution.py:717
  (60 shorter events, 13.1 us)
Async XLA Ops:
  4.7 7.0 %collective-permute-start.1 = (bf16[608,128]{1,0:T(8,128)(2,1)S(1)}, bf16[608,128]{1,0:T(8,128)(2,1)S(1)}, u32[]{:S(2)}, u32[]{:S(2)}) collective-permute-start(bf16[608,128]{1,0:T(8,128)(2,1)S(1)} %get-tuple-element.37.wait_ref.own_ref), channel_id=1, source_target_pairs={{0,2},{1,3},{2,0},{3,1},{4,6},{5,7},{6,4},{7,5},{8,10},{9,11},{10,... | collective-permute-start | bytes 466952 | tf_op jit(solution)/shard_map/ppermute | solution.py:33
  7.7 12.0 %collective-permute-start = (bf16[608,128]{1,0:T(8,128)(2,1)S(1)}, bf16[608,128]{1,0:T(8,128)(2,1)S(1)}, u32[]{:S(2)}, u32[]{:S(2)}) collective-permute-start(bf16[608,128]{1,0:T(8,128)(2,1)S(1)} %get-tuple-element.37.wait_ref.own_ref), channel_id=1, source_target_pairs={{0,1},{1,0},{2,3},{3,2},{4,5},{5,4},{6,7},{7,6},{8,9},{9,8},{10,11... | collective-permute-start | bytes 466952 | tf_op jit(solution)/shard_map/ppermute | solution.py:33
  11.7 8.0 %collective-permute-start.2 = (bf16[608,128]{1,0:T(8,128)(2,1)S(1)}, bf16[608,128]{1,0:T(8,128)(2,1)S(1)}, u32[]{:S(2)}, u32[]{:S(2)}) collective-permute-start(bf16[608,128]{1,0:T(8,128)(2,1)S(1)} %get-tuple-element.43.across_ref), channel_id=1, source_target_pairs={{0,1},{1,0},{2,3},{3,2},{4,5},{5,4},{6,7},{7,6},{8,9},{9,8},{10,11... | collective-permute-start | bytes 466952 | tf_op jit(solution)/shard_map/ppermute | solution.py:33
  11.7 23.5 %collective-permute-start.4 = (bf16[8,128,512]{2,1,0:T(8,128)(2,1)S(1)}, bf16[8,128,512]{2,1,0:T(8,128)(2,1)S(1)}, u32[]{:S(2)}, u32[]{:S(2)}) collective-permute-start(bf16[8,128,512]{2,1,0:T(8,128)(2,1)S(1)} %get-tuple-element.45.wait_ref), channel_id=1, source_target_pairs={{1,2},{2,1},{3,4},{4,3},{5,6},{6,5},{7,8},{8,7},{9,10},{10,9},{11,... | collective-permute-start | bytes 3145736 | tf_op jit(solution)/shard_map/ppermute | solution.py:33
  19.7 8.2 %copy-start.6 = (s32[16,3]{0,1:T(4,128)S(1)}, s32[16,3]{0,1:T(4,128)}, u32[]{:S(2)}) copy-start(s32[16,3]{0,1:T(4,128)} %param.12) | copy-start | bytes 580
  19.8 15.4 %collective-permute-start.3 = (bf16[8,128,512]{2,1,0:T(8,128)(2,1)S(1)}, bf16[8,128,512]{2,1,0:T(8,128)(2,1)S(1)}, u32[]{:S(2)}, u32[]{:S(2)}) collective-permute-start(bf16[8,128,512]{2,1,0:T(8,128)(2,1)S(1)} %after.7), channel_id=1, source_target_pairs={{0,1},{1,0},{2,3},{3,2},{4,5},{5,4},{6,7},{7,6},{8,9},{9,8},{10,11... | collective-permute-start | bytes 3145736 | tf_op jit(solution)/shard_map/ppermute | solution.py:33
  22.9 19.7 %collective-permute-start.5 = (bf16[4,512,128]{2,1,0:T(8,128)(2,1)S(1)}, bf16[4,512,128]{2,1,0:T(8,128)(2,1)S(1)}, u32[]{:S(2)}, u32[]{:S(2)}) collective-permute-start(bf16[4,512,128]{2,1,0:T(8,128)(2,1)S(1)} %get-tuple-element.47.refs_1_.rest_0_.c0), channel_id=1, source_target_pairs={{1,4},{3,6},{4,1},{5,8},{6,3},{7,10},{8,5},{9,12},{10,7},{11,14},{... | collective-permute-start | bytes 1572872 | tf_op jit(solution)/shard_map/ppermute | solution.py:33
  23.6 19.0 %collective-permute-start.6 = (f32[1,32,128]{2,1,0:T(8,128)S(1)}, f32[1,32,128]{2,1,0:T(8,128)S(1)}, u32[]{:S(2)}, u32[]{:S(2)}) collective-permute-start(f32[1,32,128]{2,1,0:T(8,128)S(1)} %get-tuple-element.52), channel_id=1, source_target_pairs={{0,8},{1,13},{2,10},{3,15},{4,12},{5,9},{6,14},{7,11},{8,0},{9,5},... | collective-permute-start | bytes 49160 | tf_op jit(solution)/shard_map/ppermute | solution.py:33
  35.2 12.3 %copy-start.2 = (bf16[16,64,512]{2,1,0:T(8,128)(2,1)S(1)}, bf16[16,64,512]{2,1,0:T(8,128)(2,1)}, u32[]{:S(2)}) copy-start(bf16[16,64,512]{2,1,0:T(8,128)(2,1)} %basis_ref.3) | copy-start | bytes 3145732
  42.6 4.9 %collective-permute-start.8 = (bf16[4,512,128]{2,1,0:T(8,128)(2,1)S(1)}, bf16[4,512,128]{2,1,0:T(8,128)(2,1)S(1)}, u32[]{:S(2)}, u32[]{:S(2)}) collective-permute-start(bf16[4,512,128]{2,1,0:T(8,128)(2,1)S(1)} %get-tuple-element.54.c1), channel_id=1, source_target_pairs={{0,1},{1,0},{2,3},{3,2},{4,5},{5,4},{6,7},{7,6},{8,9},{9,8},{10,11... | collective-permute-start | bytes 1572872 | tf_op jit(solution)/shard_map/ppermute | solution.py:33
  45.9 1.6 %collective-permute-start.7 = (f32[1,32,128]{2,1,0:T(8,128)S(1)}, f32[1,32,128]{2,1,0:T(8,128)S(1)}, u32[]{:S(2)}, u32[]{:S(2)}) collective-permute-start(f32[1,32,128]{2,1,0:T(8,128)S(1)} %get-tuple-element.53.sum_a), channel_id=1, source_target_pairs={{0,1},{1,0},{2,3},{3,2},{4,5},{5,4},{6,7},{7,6},{8,9},{9,8},{10,11... | collective-permute-start | bytes 49160 | tf_op jit(solution)/shard_map/ppermute | solution.py:33
  54.7 10.2 %collective-permute-start.10 = (bf16[608,128]{1,0:T(8,128)(2,1)S(1)}, bf16[608,128]{1,0:T(8,128)(2,1)S(1)}, u32[]{:S(2)}, u32[]{:S(2)}) collective-permute-start(bf16[608,128]{1,0:T(8,128)(2,1)S(1)} %get-tuple-element.56.own_ref), channel_id=1, source_target_pairs={{0,2},{1,3},{2,0},{3,1},{4,6},{5,7},{6,4},{7,5},{8,10},{9,11},{10,... | collective-permute-start | bytes 466952 | tf_op jit(solution)/shard_map/ppermute | solution.py:33
  60.6 5.0 %collective-permute-start.9 = (bf16[608,128]{1,0:T(8,128)(2,1)S(1)}, bf16[608,128]{1,0:T(8,128)(2,1)S(1)}, u32[]{:S(2)}, u32[]{:S(2)}) collective-permute-start(bf16[608,128]{1,0:T(8,128)(2,1)S(1)} %get-tuple-element.56.own_ref), channel_id=1, source_target_pairs={{0,1},{1,0},{2,3},{3,2},{4,5},{5,4},{6,7},{7,6},{8,9},{9,8},{10,11... | collective-permute-start | bytes 466952 | tf_op jit(solution)/shard_map/ppermute | solution.py:33
  64.9 1.4 %collective-permute-start.11 = (bf16[608,128]{1,0:T(8,128)(2,1)S(1)}, bf16[608,128]{1,0:T(8,128)(2,1)S(1)}, u32[]{:S(2)}, u32[]{:S(2)}) collective-permute-start(bf16[608,128]{1,0:T(8,128)(2,1)S(1)} %get-tuple-element.60.across_ref), channel_id=1, source_target_pairs={{0,1},{1,0},{2,3},{3,2},{4,5},{5,4},{6,7},{7,6},{8,9},{9,8},{10,11... | collective-permute-start | bytes 466952 | tf_op jit(solution)/shard_map/ppermute | solution.py:33
  64.9 12.9 %collective-permute-start.15 = (bf16[8,64,512]{2,1,0:T(8,128)(2,1)S(1)}, bf16[8,64,512]{2,1,0:T(8,128)(2,1)S(1)}, u32[]{:S(2)}, u32[]{:S(2)}) collective-permute-start(bf16[8,64,512]{2,1,0:T(8,128)(2,1)S(1)} %get-tuple-element.65), channel_id=1, source_target_pairs={{1,2},{2,1},{3,4},{4,3},{5,6},{6,5},{7,8},{8,7},{9,10},{10,9},{11,... | collective-permute-start | bytes 1572872 | tf_op jit(solution)/shard_map/ppermute | solution.py:33
  66.3 11.5 %collective-permute-start.14 = (bf16[8,64,512]{2,1,0:T(8,128)(2,1)S(1)}, bf16[8,64,512]{2,1,0:T(8,128)(2,1)S(1)}, u32[]{:S(2)}, u32[]{:S(2)}) collective-permute-start(bf16[8,64,512]{2,1,0:T(8,128)(2,1)S(1)} %after.10), channel_id=1, source_target_pairs={{0,1},{1,0},{2,3},{3,2},{4,5},{5,4},{6,7},{7,6},{8,9},{9,8},{10,11... | collective-permute-start | bytes 1572872 | tf_op jit(solution)/shard_map/ppermute | solution.py:33
  68.8 15.8 %collective-permute-start.12 = (bf16[4,512,128]{2,1,0:T(8,128)(2,1)S(1)}, bf16[4,512,128]{2,1,0:T(8,128)(2,1)S(1)}, u32[]{:S(2)}, u32[]{:S(2)}) collective-permute-start(bf16[4,512,128]{2,1,0:T(8,128)(2,1)S(1)} %get-tuple-element.62.refs_1_.wait_ref.c0), channel_id=1, source_target_pairs={{1,4},{3,6},{4,1},{5,8},{6,3},{7,10},{8,5},{9,12},{10,7},{11,14},{... | collective-permute-start | bytes 1572872 | tf_op jit(solution)/shard_map/ppermute | solution.py:33
  69.5 15.1 %collective-permute-start.13 = (f32[1,32,128]{2,1,0:T(8,128)S(1)}, f32[1,32,128]{2,1,0:T(8,128)S(1)}, u32[]{:S(2)}, u32[]{:S(2)}) collective-permute-start(f32[1,32,128]{2,1,0:T(8,128)S(1)} %get-tuple-element.63), channel_id=1, source_target_pairs={{0,8},{1,13},{2,10},{3,15},{4,12},{5,9},{6,14},{7,11},{8,0},{9,5},... | collective-permute-start | bytes 49160 | tf_op jit(solution)/shard_map/ppermute | solution.py:33
  84.6 1.9 %collective-permute-start.17 = (bf16[4,512,128]{2,1,0:T(8,128)(2,1)S(1)}, bf16[4,512,128]{2,1,0:T(8,128)(2,1)S(1)}, u32[]{:S(2)}, u32[]{:S(2)}) collective-permute-start(bf16[4,512,128]{2,1,0:T(8,128)(2,1)S(1)} %get-tuple-element.68.c1), channel_id=1, source_target_pairs={{0,1},{1,0},{2,3},{3,2},{4,5},{5,4},{6,7},{7,6},{8,9},{9,8},{10,11... | collective-permute-start | bytes 1572872 | tf_op jit(solution)/shard_map/ppermute | solution.py:33
  84.6 1.9 %collective-permute-start.16 = (f32[1,32,128]{2,1,0:T(8,128)S(1)}, f32[1,32,128]{2,1,0:T(8,128)S(1)}, u32[]{:S(2)}, u32[]{:S(2)}) collective-permute-start(f32[1,32,128]{2,1,0:T(8,128)S(1)} %get-tuple-element.67.sum_a), channel_id=1, source_target_pairs={{0,1},{1,0},{2,3},{3,2},{4,5},{5,4},{6,7},{7,6},{8,9},{9,8},{10,11... | collective-permute-start | bytes 49160 | tf_op jit(solution)/shard_map/ppermute | solution.py:33
  91.3 1.3 %collective-permute-start.18 = (f32[64,128]{1,0:T(8,128)S(1)}, f32[64,128]{1,0:T(8,128)S(1)}, u32[]{:S(2)}, u32[]{:S(2)}) collective-permute-start(f32[64,128]{1,0:T(8,128)S(1)} %get-tuple-element.70), channel_id=1, source_target_pairs={{0,1},{1,0},{2,3},{3,2},{4,5},{5,4},{6,7},{7,6},{8,9},{9,8},{10,11... | collective-permute-start | bytes 98312 | tf_op jit(solution)/shard_map/ppermute | solution.py:33
  92.5 4.5 %collective-permute-start.19 = (f32[64,128]{1,0:T(8,128)S(1)}, f32[64,128]{1,0:T(8,128)S(1)}, u32[]{:S(2)}, u32[]{:S(2)}) collective-permute-start(f32[64,128]{1,0:T(8,128)S(1)} %add.34), channel_id=1, source_target_pairs={{0,2},{1,3},{2,0},{3,1},{4,6},{5,7},{6,4},{7,5},{8,10},{9,11},{10,... | collective-permute-start | bytes 98312 | tf_op jit(solution)/shard_map/ppermute | solution.py:33
  97.0 3.9 %collective-permute-start.20 = (f32[64,128]{1,0:T(8,128)S(1)}, f32[64,128]{1,0:T(8,128)S(1)}, u32[]{:S(2)}, u32[]{:S(2)}) collective-permute-start(f32[64,128]{1,0:T(8,128)S(1)} %add.35), channel_id=1, source_target_pairs={{0,4},{1,5},{2,6},{3,7},{4,0},{5,1},{6,2},{7,3},{8,12},{9,13},{10,... | collective-permute-start | bytes 98312 | tf_op jit(solution)/shard_map/ppermute | solution.py:33
  100.9 5.1 %collective-permute-start.21 = (f32[64,128]{1,0:T(8,128)S(1)}, f32[64,128]{1,0:T(8,128)S(1)}, u32[]{:S(2)}, u32[]{:S(2)}) collective-permute-start(f32[64,128]{1,0:T(8,128)S(1)} %add.36), channel_id=1, source_target_pairs={{0,8},{1,9},{2,10},{3,11},{4,12},{5,13},{6,14},{7,15},{8,0},{9,1},... | collective-permute-start | bytes 98312 | tf_op jit(solution)/shard_map/ppermute | solution.py:33
  (6 other events, 36.6 us)

commit v6 on v5

--- a/solution.py
+++ b/solution.py
@@ -144,7 +144,9 @@
     target[pl.ds(1, pairs, stride=2)] = pltpu.roll(flat, 64, 1)
 
 
-def relayout_kernel(pos_ref, coup_ref, coarse_ref, wait_ref, out_ref, coarse_out, by_slots, by_rows, flat, square):
+def relayout_kernel(
+    pos_ref, near_ref, coup_ref, coarse_ref, wait_ref, out_ref, coarse_out, lists, by_slots, by_rows, flat, square
+):
     per, slots, entries = coup_ref.shape
     rank = out_ref.shape[1] // 2
     quarter = rank // 2
@@ -175,6 +177,7 @@
         return carry
 
     lax.fori_loop(0, per // by_slots.shape[0], trip, 0)
+    build_lists(near_ref, lists, pos_ref[0], per // 2)
     cluster = pos_ref[0] // CDEV
     wide = coarse_ref[cluster].astype(F32)
     number = lax.broadcasted_iota(jnp.int32, wide.shape, 0)
@@ -245,40 +248,33 @@
     sum_ref[...] = total[None]
 
 
-def list_entries(near_ref, list_ref, pos, half, own_part):
+def build_lists(near_ref, lists, pos, half):
     slots = near_ref.shape[0] - 1
     total = near_ref.shape[1] * slots
     base = pos * 2 * half - half
 
-    def put(entry, carry):
-        n, seen = carry
+    def put(entry, counts):
         m = near_ref[1 + entry % slots, entry // slots] - base
         own = (m >= half) & (m < 3 * half)
-        early = own & (seen < 2 * half)
-        list_ref[n] = entry
-        return n + jnp.where(early == own_part, 1, 0), seen + jnp.where(own, 1, 0)
-
-    n, _ = lax.fori_loop(0, total, put, (0, 0))
-    for u in range(UNROLL):
-        list_ref[n + u] = total
-    return n
-
-
-def near_entry(near_ref, list_ref, at, pos, half):
-    slots = near_ref.shape[0] - 1
-    entry = list_ref[at]
+        low = (m < half) == (pos % 2 == 1)
+        takes = (own, ~own & low, ~own & ~low, own | low)
+        for kind, count in enumerate(counts):
+            lists[kind, count] = entry * 4 * half + m
+        return tuple(count + jnp.where(take, 1, 0) for count, take in zip(counts, takes))
+
+    counts = lax.fori_loop(0, total, put, (0, 0, 0, 0))
+    for kind, count in enumerate(counts):
+        for u in range(UNROLL):
+            lists[kind, count + u] = total * 4 * half + half
+        lists[kind, lists.shape[1] - 1] = count
+
+
+def near_entry(lists, kind, at, tile_ref, half):
+    slots = (tile_ref.shape[0] - 1) // (2 * half)
+    value = lists[kind, at]
+    entry = value // (4 * half)
     leaf_at = entry // slots
-    row = jnp.minimum(leaf_at, near_ref.shape[1] - 1)
-    m = near_ref[1 + entry % slots, row] - (pos * 2 * half - half)
-    return entry, leaf_at, row, jnp.clip(m, 0, 4 * half - 1)
-
-
-def load_window(target, own, from_sibling, from_beside, odd):
-    half = from_sibling.shape[0]
-    rows = target.shape[1]
-    target[pl.ds(half, 2 * half)] = own[...]
-    target[pl.ds(3 * half * (1 - odd), half)] = from_sibling[:, :rows]
-    target[pl.ds(3 * half * odd, half)] = from_beside[:, :rows]
+    return entry, leaf_at, jnp.minimum(leaf_at, 2 * half - 1), value % (4 * half)
 
 
 def self_kernel(e_ref, v_ref, wait_ref, self_ref, near_out, buffer, sems):
@@ -313,34 +309,42 @@
             copy_out((i % 2) * UNROLL + u, i * UNROLL + u).wait()
 
 
-def own_kernel(pos_ref, near_ref, e_ref, v_ref, near_in, *rest):
-    tile_ref, near_out, list_ref = rest[-3:]
-    per, _, leaf = v_ref.shape
+def points_of(ref, at, columns, features):
+    high = ref[at, columns : columns + features].astype(F32)
+    return high + ref[at, columns + features :].astype(F32)
+
+
+def own_kernel(pos_ref, lists, e_ref, v_ref, vx_ref, near_in, wait_ref, tile_ref, near_out, vw):
+    per, columns, leaf = v_ref.shape
     half = per // 2
-    pos = pos_ref[0]
-    n = list_entries(near_ref, list_ref, pos, half, True)
+    vw[:per] = v_ref[...]
+    vw[per:] = vx_ref[:, :columns]
+    n = lists[3, lists.shape[1] - 1]
 
     def trip(i, carry):
         for u in range(UNROLL):
-            entry, leaf_at, row, m = near_entry(near_ref, list_ref, i * UNROLL + u, pos, half)
-            place = jnp.clip(m - half, 0, 2 * half - 1)
-            tile = tile_of(other_rows(columns_of(e_ref, place, leaf)), own_rows(columns_of(e_ref, row, leaf)))
+            entry, leaf_at, row, m = near_entry(lists, 3, i * UNROLL + u, tile_ref, half)
+            own = (m >= half) & (m < 3 * half)
+            place = jnp.clip(m - half, 0, per - 1)
+            points = jnp.where(
+                own, columns_of(e_ref, place, leaf), points_of(vx_ref, m % half, columns, e_ref.shape[0])
+            )
+            tile = tile_of(other_rows(points), own_rows(columns_of(e_ref, row, leaf)))
             tile_ref[entry] = tile
-            near_out[leaf_at] += dot(v_ref[place], tile, 1, 0)
+            near_out[leaf_at] += dot(vw[jnp.where(own, place, per + m % half)], tile, 1, 0)
         return carry
 
     lax.fori_loop(0, (n + UNROLL - 1) // UNROLL, trip, 0)
 
 
-def own_again_kernel(pos_ref, near_ref, v_ref, tile_ref, near_out, list_ref):
+def own_again_kernel(pos_ref, lists, v_ref, tile_ref, near_out):
     half = v_ref.shape[0] // 2
-    pos = pos_ref[0]
     near_out[...] = jnp.zeros_like(near_out)
-    n = list_entries(near_ref, list_ref, pos, half, True)
+    n = lists[0, lists.shape[1] - 1]
 
     def trip(i, carry):
         for u in range(UNROLL):
-            entry, leaf_at, _, m = near_entry(near_ref, list_ref, i * UNROLL + u, pos, half)
+            entry, leaf_at, _, m = near_entry(lists, 0, i * UNROLL + u, tile_ref, half)
             place = jnp.clip(m - half, 0, 2 * half - 1)
             near_out[leaf_at] += dot(v_ref[place], tile_ref[entry], 1, 0)
         return carry
@@ -348,14 +352,26 @@
     lax.fori_loop(0, (n + UNROLL - 1) // UNROLL, trip, 0)
 
 
-def self_again_kernel(v_ref, self_hbm, near_in, wait_ref, near_out, self_ref, sems):
+def self_again_kernel(
+    pos_ref, lists, v_ref, vx_ref, tile_ref, self_hbm, near_in, wait_ref, near_out, self_ref, sems,
+):
     per = v_ref.shape[0]
+    half = per // 2
     copies = [
         pltpu.make_async_copy(self_hbm.at[pl.ds(at, UNROLL)], self_ref.at[pl.ds(at, UNROLL)], sems.at[at // UNROLL])
         for at in range(0, per, UNROLL)
     ]
     for copy in copies:
         copy.start()
+    n = lists[1, lists.shape[1] - 1]
+
+    def trip(i, carry):
+        for u in range(UNROLL):
+            entry, leaf_at, _, m = near_entry(lists, 1, i * UNROLL + u, tile_ref, half)
+            near_out[leaf_at] += dot(vx_ref[m % half], tile_ref[entry], 1, 0)
+        return carry
+
+    lax.fori_loop(0, (n + UNROLL - 1) // UNROLL, trip, 0)
     for i, copy in enumerate(copies):
         copy.wait()
         for u in range(UNROLL):
@@ -406,32 +422,19 @@
     mv[...] = wide[:, :rank] + wide[:, rank : 2 * rank] + wide[:, 2 * rank :]
 
 
-def foreign_kernel(
-    pos_ref, near_ref, e_ref, v_ref, vx_ref, vo_ref, tile_in, near_in, tile_ref, near_out, list_ref, vw,
-):
-    half, _, leaf = vx_ref.shape
-    _, columns, _ = v_ref.shape
+def foreign_kernel(pos_ref, lists, e_ref, vo_ref, tile_in, near_in, tile_ref, near_out):
+    half, _, leaf = vo_ref.shape
     features = e_ref.shape[0]
-    pos = pos_ref[0]
-    odd = pos % 2
-    load_window(vw, v_ref, vx_ref, vo_ref, odd)
-    n = list_entries(near_ref, list_ref, pos, half, False)
-
-    def points_of(ref, at):
-        high = ref[at, columns : columns + features].astype(F32)
-        return high + ref[at, columns + features :].astype(F32)
+    columns = vo_ref.shape[1] - 2 * features
+    n = lists[2, lists.shape[1] - 1]
 
     def trip(i, carry):
         for u in range(UNROLL):
-            entry, leaf_at, row, m = near_entry(near_ref, list_ref, i * UNROLL + u, pos, half)
-            own = (m >= half) & (m < 3 * half)
-            from_x = (m < half) == (odd == 1)
-            within = m % half
-            points = jnp.where(from_x, points_of(vx_ref, within), points_of(vo_ref, within))
-            points = jnp.where(own, columns_of(e_ref, jnp.clip(m - half, 0, 2 * half - 1), leaf), points)
+            entry, leaf_at, row, m = near_entry(lists, 2, i * UNROLL + u, tile_ref, half)
+            points = points_of(vo_ref, m % half, columns, features)
             tile = tile_of(other_rows(points), own_rows(columns_of(e_ref, row, leaf)))
             tile_ref[entry] = tile
-            near_out[leaf_at] += dot(vw[m], tile, 1, 0)
+            near_out[leaf_at] += dot(vo_ref[m % half, :columns], tile, 1, 0)
         return carry
 
     lax.fori_loop(0, (n + UNROLL - 1) // UNROLL, trip, 0)
@@ -476,16 +479,14 @@
     msg_ref[...] = jnp.where(lane == 1, jnp.sum(acc_ru[...], axis=1, keepdims=True), out)
 
 
-def near_again_kernel(pos_ref, near_ref, q_ref, vx_ref, vo_ref, tile_ref, near_in, near_out, list_ref, vw):
-    half = vx_ref.shape[0]
-    pos = pos_ref[0]
-    load_window(vw, q_ref, vx_ref, vo_ref, pos % 2)
-    n = list_entries(near_ref, list_ref, pos, half, False)
+def near_again_kernel(pos_ref, lists, vo_ref, tile_ref, near_in, near_out):
+    half = vo_ref.shape[0]
+    n = lists[2, lists.shape[1] - 1]
 
     def trip(i, carry):
         for u in range(UNROLL):
-            entry, leaf_at, _, m = near_entry(near_ref, list_ref, i * UNROLL + u, pos, half)
-            near_out[leaf_at] += dot(vw[m], tile_ref[entry], 1, 0)
+            entry, leaf_at, _, m = near_entry(lists, 2, i * UNROLL + u, tile_ref, half)
+            near_out[leaf_at] += dot(vo_ref[m % half], tile_ref[entry], 1, 0)
         return carry
 
     lax.fori_loop(0, (n + UNROLL - 1) // UNROLL, trip, 0)
@@ -618,9 +619,7 @@
     msg_shape = pltpu.VMEM((columns, 128), F32)
     coefs_shape = pltpu.VMEM((per * rank, columns), BF16)
     acc_shape = pltpu.VMEM((columns, 128), F32)
-    list_shape = pltpu.SMEM((per * slots + UNROLL,), jnp.int32)
     window = [
-        pltpu.VMEM((4 * half, columns, leaf), BF16),
         pltpu.VMEM((12 * per, size, 2 * columns), BF16),
         pltpu.VMEM((rank, 3 * columns), BF16),
     ]
@@ -635,67 +634,66 @@
         (position, right_side, scale_row, leaf_basis, transfer, embeddings), limit=WIDE_LIMIT,
     )
     got = first_messages(cp)
-    coup, coarse = call(
-        relayout_kernel, "relayout", [SCALAR] + [WHOLE] * 2 + [ANYWHERE],
-        [pltpu.VMEM((per, 2 * rank, far_count * size), BF16), pltpu.VMEM((coarse_count - 1, rank, rank), BF16)],
+    coup, coarse, lists = call(
+        relayout_kernel, "relayout", [SCALAR] * 2 + [WHOLE] * 2 + [ANYWHERE],
+        [pltpu.VMEM((per, 2 * rank, far_count * size), BF16), pltpu.VMEM((coarse_count - 1, rank, rank), BF16),
+         jax.ShapeDtypeStruct((4, per * slots + 2 * UNROLL), jnp.int32)],
         [
             pltpu.VMEM((RELAY_UNROLL, far_count * rank * rank // 128, 128), F32),
             pltpu.VMEM((RELAY_UNROLL, 2, far_count // 4, rank, 128), F32),
             pltpu.VMEM((size, 128), F32), pltpu.VMEM((rank, 128), F32),
         ],
-        (position, leaf_coupling, coarse_coupling, cp),
-    )
-    across_cp, mo = after((got[1], mo), coup)
+        (position, near_rows, leaf_coupling, coarse_coupling, cp), out_specs=[WHOLE, WHOLE, SCALAR],
+    )
+    across_cp, mo, mx = after((got[1], mo, mx), coup)
     got = (got[0], across_cp)
     vo = beside(mo)
+    vx = sibling(mx)
     tself, near = call(
         self_kernel, "self_tiles", [WHOLE] * 2 + [ANYWHERE], [self_shape, near_shape],
         [pltpu.VMEM((2 * UNROLL, leaf, leaf), BF16), pltpu.SemaphoreType.DMA((2 * UNROLL,))],
         (embeddings, v, mo), out_specs=[OUTSIDE, WHOLE],
     )
     quad, far_quad, mine = second_messages(position, cp, got, part, near)
-    (mx,) = after((mx,), quad)
-    vx = sibling(mx)
     tiles, near = call(
-        own_kernel, "own_tiles", [SCALAR] * 2 + [WHOLE] * 3 + [ANYWHERE], [tile_shape, near_shape], [list_shape],
-        (position, near_rows, embeddings, v, near, quad), aliases={4: 1},
-    )
+        own_kernel, "own_tiles", [SCALAR] * 2 + [WHOLE] * 4 + [ANYWHERE], [tile_shape, near_shape],
+        [pltpu.VMEM((per + half, columns, leaf), BF16)],
+        (position, lists, embeddings, v, vx, near, quad), aliases={5: 1},
+    )
+    coefs, sums = last_messages(*after((far_quad, mine), near))
     tiles, near = call(
-        foreign_kernel, "foreign_tiles", [SCALAR] * 2 + [WHOLE] * 6, [tile_shape, near_shape],
-        [list_shape, window[0]],
-        (position, near_rows, embeddings, v, vx, vo, tiles, near), aliases={6: 0, 7: 1},
-    )
-    coefs, sums = last_messages(*after((far_quad, mine), near))
+        foreign_kernel, "foreign_tiles", [SCALAR] * 2 + [WHOLE] * 4, [tile_shape, near_shape], [],
+        (position, lists, embeddings, vo, tiles, near), aliases={4: 0, 5: 1},
+    )
     image, q, cp, part, msg, mx, mo = call(
         far_first_kernel, "far_first", [SCALAR] * 2 + [WHOLE] * 12,
         [wide_shape, leaf_shape, cp_shape, part_shape, msg_shape, half_shape, half_shape],
-        [*window[1:], moved_shape, coefs_shape, acc_shape, acc_shape],
+        [*window, moved_shape, coefs_shape, acc_shape, acc_shape],
         (position, far_rows, right_side, scale_row, leaf_basis, coup, trans, near, coarse, *sums, quad, *coefs),
     )
     got = first_messages(cp)
     (near,) = call(
-        own_again_kernel, "own_again", [SCALAR] * 2 + [WHOLE] * 2, [near_shape], [list_shape],
-        (position, near_rows, q, tiles),
+        own_again_kernel, "own_again", [SCALAR] * 2 + [WHOLE] * 2, [near_shape], [],
+        (position, lists, q, tiles),
     )
     across_cp, mo = after((got[1], mo), near)
     got = (got[0], across_cp)
     vo = beside(mo)
     quad, far_quad, mine = second_messages(position, cp, got, part)
-    (mx,) = after((mx,), quad)
     vx = sibling(mx)
     (near,) = call(
-        self_again_kernel, "self_again", [WHOLE, OUTSIDE, WHOLE, ANYWHERE], [near_shape],
+        self_again_kernel, "self_again", [SCALAR] * 2 + [WHOLE] * 3 + [OUTSIDE, WHOLE, ANYWHERE], [near_shape],
         [pltpu.VMEM((per, leaf, leaf), BF16), pltpu.SemaphoreType.DMA((per // UNROLL,))],
-        (q, tself, near, quad), aliases={2: 0},
-    )
+        (position, lists, q, vx, tiles, tself, near, quad), aliases={6: 0},
+    )
+    coefs, sums = last_messages(*after((far_quad, mine), near, vo))
     (near,) = call(
-        near_again_kernel, "near_again", [SCALAR] * 2 + [WHOLE] * 5, [near_shape], [list_shape, window[0]],
-        (position, near_rows, q, vx, vo, tiles, near), aliases={6: 0},
-    )
-    coefs, sums = last_messages(*after((far_quad, mine), near))
+        near_again_kernel, "near_again", [SCALAR] * 2 + [WHOLE] * 3, [near_shape], [],
+        (position, lists, vo, tiles, near), aliases={4: 0},
+    )
     second, msg = call(
         far_again_kernel, "far_again", [SCALAR] * 2 + [WHOLE] * 14, [wide_shape, msg_shape],
-        window[1:] + [moved_shape] + [acc_shape] * 3,
+        window + [moved_shape] + [acc_shape] * 3,
         (position, far_rows, right_side, scale_row, image, leaf_basis, coup, trans,
          coarse, *sums, quad, *coefs, near, msg),
     )

time: 109 us -> 101 us (0.927)
  starting transfers between devices: 37.3 us -> 27.6 us
  waiting for transfers between devices: 17 us -> 19.6 us
    ppermute x22, starting transfers between devices: 37.3 us -> 27.6 us  [involution(): return lax.ppermute(value, 'leaf', pairs)]
    ppermute x22, waiting for transfers between devices: 17 us -> 19.6 us  [involution(): return lax.ppermute(value, 'leaf', pairs)]
    pallas_call x18 -> x16, Pallas kernels: 50.7 us -> 49.8 us  [call(): pl.pallas_call(kernel, in_specs=in_specs, out_specs=out_specs or [WHOLE]...]
  transfers between devices with their start and end apart: 22 -> 22, of which waited for: 10 -> 8; matrix products, arithmetic and copies ran while one was open for 0% -> 0% of each run, Pallas kernels for 32% -> 34%
where the time goes in v6:
time: 101 us
  Pallas kernels  49.8 us (49%)
  starting transfers between devices  27.6 us (27%)
  waiting for transfers between devices  19.6 us (19%)
  other arithmetic  2.87 us (3%)
    pallas_call x16, Pallas kernels, call(): pl.pallas_call(kernel, in_specs=in_specs, out_specs=out_specs or [WHOLE]...  49.8 us
    ppermute x22, starting transfers between devices, involution(): return lax.ppermute(value, 'leaf', pairs)  27.6 us
    ppermute x22, waiting for transfers between devices, involution(): return lax.ppermute(value, 'leaf', pairs)  19.6 us
    add x1, other arithmetic, body(): residual = right_side - first_weight * image + second_weight * second  2.64 us
  transfers between devices with their start and end apart: 22, of which 8 were waited for; matrix products, arithmetic and copies ran while one was open for 0% of the time, Pallas kernels for 34%

profile of v6, /device:TPU:0, one launch (start us, length us, event | category | flops | bytes accessed | tf_op | source)
XLA Modules:
  0.0 101.3 jit_solution(14468306100209963570)
XLA Ops:
  0.7 4.0 %prep.1 = (bf16[16,64,512]{2,1,0:T(8,128)(2,1)S(1)}, bf16[608,128]{1,0:T(8,128)(2,1)S(1)}, f32[32,128]{1,0:T(8,128)S(1)}, bf16[16,64,64]{2,1,0:T(8,128)(2,1)S(1)...) custom-call(s32[1]{0:T(128)} %bitcast.pos_ref, f32[64,8192]{1,0:T(8,128)} %rs_ref.3, ...), custom_call_target="tpu_custom_call" | custom-call | tf_op jit(solution)/shard_map/prep/pallas_call | solution.py:526
  4.7 3.0 %collective-permute-start = (bf16[608,128]{1,0:T(8,128)(2,1)S(1)}, bf16[608,128]{1,0:T(8,128)(2,1)S(1)}, u32[]{:S(2)}, u32[]{:S(2)}) collective-permute-start(bf16[608,128]{1,0:T(8,128)(2,1)S(1)} %get-tuple-element.39.wait_ref.own_ref), channel_id=1, source_target_pairs={{0,2},{1,3},{2,0},{3,1},{4,6},{5,7},{6,4},{7,5},{8,10},{9,11},{10,... | collective-permute-start | bytes 466952 | tf_op jit(solution)/shard_map/ppermute | solution.py:33
  7.7 4.3 %relayout.1 = (bf16[16,128,256]{2,1,0:T(8,128)(2,1)S(1)}, bf16[1,64,64]{2,1,0:T(8,128)(2,1)S(1)}, s32[4,40]{1,0:T(4,128)S(1)}) custom-call(s32[1]{0:T(128)} %bitcast.pos_ref, s32[3,16]{1,0:T(4,128)S(1)} %bitcast.9, bf16[16,8,4096]{2,1,0:T(8,128)(2,1)S(1)} %copy-done.3, bf16[2,2,4096]{2,1,0:T(2,128)(2,1)S(1)} %copy-done.5, ...), custom_call_target="tpu_custom_call" | custom-call | tf_op jit(solution)/shard_map/relayout/pallas_call | solution.py:526
  12.7 0.7 collective-permute-start.1
  13.4 7.2 %self_tiles.1 = (bf16[128,512,512]{2,1,0:T(8,128)(2,1)}, f32[17,64,512]{2,1,0:T(8,128)S(1)}) custom-call(f32[32,8192]{1,0:T(8,128)S(1)} %copy-done.1, bf16[16,64,512]{2,1,0:T(8,128)(2,1)S(1)} %get-tuple-element.46.v_ref, bf16[8,128,512]{2,1,0:T(8,128)(2,1)S(1)} %get-tuple-element.45.wait_ref), custom_call_target="tpu_custom_call" | custom-call | tf_op jit(solution)/shard_map/self_tiles/pallas_call | solution.py:526
  21.4 6.5 %collective-permute-start.6 = (f32[1,32,128]{2,1,0:T(8,128)S(1)}, f32[1,32,128]{2,1,0:T(8,128)S(1)}, u32[]{:S(2)}, u32[]{:S(2)}) collective-permute-start(f32[1,32,128]{2,1,0:T(8,128)S(1)} %get-tuple-element.56), channel_id=1, source_target_pairs={{0,8},{1,13},{2,10},{3,15},{4,12},{5,9},{6,14},{7,11},{8,0},{9,5},... | collective-permute-start | bytes 49160 | tf_op jit(solution)/shard_map/ppermute | solution.py:33
  27.9 12.8 %own_tiles.1 = (bf16[33,512,512]{2,1,0:T(8,128)(2,1)S(1)}, f32[17,64,512]{2,1,0:T(8,128)S(1)}) custom-call(s32[1]{0:T(128)} %bitcast.pos_ref, s32[4,40]{1,0:T(4,128)S(1)} %get-tuple-element.42.lists, f32[32,8192]{1,0:T(8,128)S(1)} %copy-done.1, bf16[16,64,512]{2,1,0:T(8,128)(2,1)S(1)} %get-tuple-element.46.v_ref, ...), custom_call_target="tpu_custom_call", output_to_operand_aliasing={{1}: (5, {})} | custom-call | tf_op jit(solution)/shard_map/own_tiles/pallas_call | solution.py:526
  42.0 0.8 collective-permute-done.7.sum_b
  43.2 7.2 %far_first.1 = (f32[64,8192]{1,0:T(8,128)S(1)}, bf16[16,64,512]{2,1,0:T(8,128)(2,1)S(1)}, bf16[608,128]{1,0:T(8,128)(2,1)S(1)}, f32[32,128]{1,0:T(8,128)S(1)}, f...) custom-call(s32[1]{0:T(128)} %bitcast.pos_ref, s32[8,16]{1,0:T(8,128)S(1)} %bitcast.7, ...), custom_call_target="tpu_custom_call" | custom-call | tf_op jit(solution)/shard_map/far_first/pallas_call | solution.py:526
  50.4 3.4 %collective-permute-start.10 = (bf16[608,128]{1,0:T(8,128)(2,1)S(1)}, bf16[608,128]{1,0:T(8,128)(2,1)S(1)}, u32[]{:S(2)}, u32[]{:S(2)}) collective-permute-start(bf16[608,128]{1,0:T(8,128)(2,1)S(1)} %get-tuple-element.60.own_ref), channel_id=1, source_target_pairs={{0,2},{1,3},{2,0},{3,1},{4,6},{5,7},{6,4},{7,5},{8,10},{9,11},{10,... | collective-permute-start | bytes 466952 | tf_op jit(solution)/shard_map/ppermute | solution.py:33
  54.0 3.6 %own_again.1.refs_2_.near_in = f32[17,64,512]{2,1,0:T(8,128)S(1)} custom-call(s32[1]{0:T(128)} %bitcast.pos_ref, s32[4,40]{1,0:T(4,128)S(1)} %get-tuple-element.42.lists, bf16[16,64,512]{2,1,0:T(8,128)(2,1)S(1)} %get-tuple-element.62.v_ref, bf16[33,512,512]{2,1,0:T(8,128)(2,1)S(1)} %get-tuple-element.63.tile_ref), custom_call_target="tpu_custom_call" | custom-call | tf_op jit(solution)/shard_map/own_again/pallas_call | solution.py:526
  57.6 0.8 collective-permute-start.11
  60.2 6.0 %collective-permute-start.13 = (f32[1,32,128]{2,1,0:T(8,128)S(1)}, f32[1,32,128]{2,1,0:T(8,128)S(1)}, u32[]{:S(2)}, u32[]{:S(2)}) collective-permute-start(f32[1,32,128]{2,1,0:T(8,128)S(1)} %get-tuple-element.67), channel_id=1, source_target_pairs={{0,8},{1,13},{2,10},{3,15},{4,12},{5,9},{6,14},{7,11},{8,0},{9,5},... | collective-permute-start | bytes 49160 | tf_op jit(solution)/shard_map/ppermute | solution.py:33
  66.2 4.6 %self_again.1.refs_2_.near_in = f32[17,64,512]{2,1,0:T(8,128)S(1)} custom-call(s32[1]{0:T(128)} %bitcast.pos_ref, s32[4,40]{1,0:T(4,128)S(1)} %get-tuple-element.42.lists, bf16[16,64,512]{2,1,0:T(8,128)(2,1)S(1)} %get-tuple-element.62.v_ref, bf16[8,64,512]{2,1,0:T(8,128)(2,1)S(1)} %collective-permute-done.14.vx_ref, ...), custom_call_target="tpu_custom_call", output_to_operand_aliasing={{}: (6, {})} | custom-call | tf_op jit(solution)/shard_map/self_again/pallas_call | solution.py:526
  70.8 6.5 %collective-permute-done.13.refs_1_ = f32[1,32,128]{2,1,0:T(8,128)S(1)} collective-permute-done((f32[1,32,128]{2,1,0:T(8,128)S(1)}, f32[1,32,128]{2,1,0:T(8,128)S(1)}, u32[]{:S(2)}, u32[]{:S(2)}) %collective-permute-start.13) | collective-permute-done | bytes 16416 | tf_op jit(solution)/shard_map/ppermute | solution.py:33
  77.8 0.8 near_again.1.near_ref
  79.3 4.7 %far_again.1 = (f32[64,8192]{1,0:T(8,128)S(1)}, f32[64,128]{1,0:T(8,128)S(1)}) custom-call(s32[1]{0:T(128)} %bitcast.pos_ref, s32[8,16]{1,0:T(8,128)S(1)} %bitcast.8, f32[64,8192]{1,0:T(8,128)S(1)} %copy-done, f32[1,8192]{1,0:T(1,128)S(1)} %bitcast.6, f32[64,8192]{1,0:T(8,128)S(1)} %get-tuple-element.59.u_ref, bf16[16,64,512]{2,1,0:T(8,128)(2,1)S(1)} %copy-done.2, ...), custom_call_target="tpu_custom_call" | custom-call | tf_op jit(solution)/shard_map/far_again/pallas_call | solution.py:526
  83.9 1.0 collective-permute-start.18
  84.9 0.9 collective-permute-done.18
  85.8 3.9 %collective-permute-done.19 = f32[64,128]{1,0:T(8,128)S(1)} collective-permute-done((f32[64,128]{1,0:T(8,128)S(1)}, f32[64,128]{1,0:T(8,128)S(1)}, u32[]{:S(2)}, u32[]{:S(2)}) %collective-permute-start.19) | collective-permute-done | bytes 32800 | tf_op jit(solution)/shard_map/ppermute | solution.py:33
  89.7 1.6 %collective-permute-start.20 = (f32[64,128]{1,0:T(8,128)S(1)}, f32[64,128]{1,0:T(8,128)S(1)}, u32[]{:S(2)}, u32[]{:S(2)}) collective-permute-start(f32[64,128]{1,0:T(8,128)S(1)} %add.35), channel_id=1, source_target_pairs={{0,4},{1,5},{2,6},{3,7},{4,0},{5,1},{6,2},{7,3},{8,12},{9,13},{10,... | collective-permute-start | bytes 98312 | tf_op jit(solution)/shard_map/ppermute | solution.py:33
  91.3 2.3 %collective-permute-done.20 = f32[64,128]{1,0:T(8,128)S(1)} collective-permute-done((f32[64,128]{1,0:T(8,128)S(1)}, f32[64,128]{1,0:T(8,128)S(1)}, u32[]{:S(2)}, u32[]{:S(2)}) %collective-permute-start.20) | collective-permute-done | bytes 32800 | tf_op jit(solution)/shard_map/ppermute | solution.py:33
  94.2 4.2 %collective-permute-done.21 = f32[64,128]{1,0:T(8,128)S(1)} collective-permute-done((f32[64,128]{1,0:T(8,128)S(1)}, f32[64,128]{1,0:T(8,128)S(1)}, u32[]{:S(2)}, u32[]{:S(2)}) %collective-permute-start.21) | collective-permute-done | bytes 32800 | tf_op jit(solution)/shard_map/ppermute | solution.py:33
  98.7 2.6 %multiply_add_fusion = (f32[64,8192]{1,0:T(8,128)}, f32[64,8192]{1,0:T(8,128)}) fusion(f32[64,8192]{1,0:T(8,128)S(1)} %get-tuple-element.75, f32[64,8192]{1,0:T(8,128)S(1)} %copy-done, f32[64,8192]{1,0:T(8,128)S(1)} %get-tuple-element.59.u_ref, f32[64]{0:T(128)S(1)} %get-tuple-element.77, f32[64]{0:T(128)S(1)} %get-tuple-element.76, f32[8192]{0:T(1024)S(1)} %copy-done.4), kind=kLoop, calls=%fused_computation | loop fusion | flops 4194304 | bytes 10519040 | tf_op jit(solution)/shard_map/add | solution.py:715
  (58 shorter events, 7.1 us)
Async XLA Ops:
  0.6 7.0 %copy-start.3 = (bf16[16,8,4096]{2,1,0:T(8,128)(2,1)S(1)}, bf16[16,8,4096]{2,1,0:T(8,128)(2,1)}, u32[]{:S(2)}) copy-start(bf16[16,8,4096]{2,1,0:T(8,128)(2,1)} %coup_ref.1) | copy-start | bytes 3145732
  0.6 7.0 %copy-start.5 = (bf16[2,2,4096]{2,1,0:T(2,128)(2,1)S(1)}, bf16[2,2,4096]{2,1,0:T(2,128)(2,1)}, u32[]{:S(2)}) copy-start(bf16[2,2,4096]{2,1,0:T(2,128)(2,1)} %coarse_ref.1) | copy-start | bytes 98308
  4.7 7.3 %collective-permute-start = (bf16[608,128]{1,0:T(8,128)(2,1)S(1)}, bf16[608,128]{1,0:T(8,128)(2,1)S(1)}, u32[]{:S(2)}, u32[]{:S(2)}) collective-permute-start(bf16[608,128]{1,0:T(8,128)(2,1)S(1)} %get-tuple-element.39.wait_ref.own_ref), channel_id=1, source_target_pairs={{0,2},{1,3},{2,0},{3,1},{4,6},{5,7},{6,4},{7,5},{8,10},{9,11},{10,... | collective-permute-start | bytes 466952 | tf_op jit(solution)/shard_map/ppermute | solution.py:33
  12.0 15.9 %collective-permute-start.2 = (bf16[8,128,512]{2,1,0:T(8,128)(2,1)S(1)}, bf16[8,128,512]{2,1,0:T(8,128)(2,1)S(1)}, u32[]{:S(2)}, u32[]{:S(2)}) collective-permute-start(bf16[8,128,512]{2,1,0:T(8,128)(2,1)S(1)} %get-tuple-element.47), channel_id=1, source_target_pairs={{0,1},{1,0},{2,3},{3,2},{4,5},{5,4},{6,7},{7,6},{8,9},{9,8},{10,11... | collective-permute-start | bytes 3145736 | tf_op jit(solution)/shard_map/ppermute | solution.py:33
  12.1 8.6 %collective-permute-start.3 = (bf16[608,128]{1,0:T(8,128)(2,1)S(1)}, bf16[608,128]{1,0:T(8,128)(2,1)S(1)}, u32[]{:S(2)}, u32[]{:S(2)}) collective-permute-start(bf16[608,128]{1,0:T(8,128)(2,1)S(1)} %get-tuple-element.39.wait_ref.own_ref), channel_id=1, source_target_pairs={{0,1},{1,0},{2,3},{3,2},{4,5},{5,4},{6,7},{7,6},{8,9},{9,8},{10,11... | collective-permute-start | bytes 466952 | tf_op jit(solution)/shard_map/ppermute | solution.py:33
  12.6 8.1 %collective-permute-start.4 = (bf16[608,128]{1,0:T(8,128)(2,1)S(1)}, bf16[608,128]{1,0:T(8,128)(2,1)S(1)}, u32[]{:S(2)}, u32[]{:S(2)}) collective-permute-start(bf16[608,128]{1,0:T(8,128)(2,1)S(1)} %get-tuple-element.49.across_ref), channel_id=1, source_target_pairs={{0,1},{1,0},{2,3},{3,2},{4,5},{5,4},{6,7},{7,6},{8,9},{9,8},{10,11... | collective-permute-start | bytes 466952 | tf_op jit(solution)/shard_map/ppermute | solution.py:33
  12.7 28.7 %collective-permute-start.1 = (bf16[8,128,512]{2,1,0:T(8,128)(2,1)S(1)}, bf16[8,128,512]{2,1,0:T(8,128)(2,1)S(1)}, u32[]{:S(2)}, u32[]{:S(2)}) collective-permute-start(bf16[8,128,512]{2,1,0:T(8,128)(2,1)S(1)} %get-tuple-element.45.wait_ref), channel_id=1, source_target_pairs={{1,2},{2,1},{3,4},{4,3},{5,6},{6,5},{7,8},{8,7},{9,10},{10,9},{11,... | collective-permute-start | bytes 3145736 | tf_op jit(solution)/shard_map/ppermute | solution.py:33
  20.7 20.0 %collective-permute-start.5 = (bf16[4,512,128]{2,1,0:T(8,128)(2,1)S(1)}, bf16[4,512,128]{2,1,0:T(8,128)(2,1)S(1)}, u32[]{:S(2)}, u32[]{:S(2)}) collective-permute-start(bf16[4,512,128]{2,1,0:T(8,128)(2,1)S(1)} %get-tuple-element.51.wait_ref.c0), channel_id=1, source_target_pairs={{1,4},{3,6},{4,1},{5,8},{6,3},{7,10},{8,5},{9,12},{10,7},{11,14},{... | collective-permute-start | bytes 1572872 | tf_op jit(solution)/shard_map/ppermute | solution.py:33
  21.4 19.3 %collective-permute-start.6 = (f32[1,32,128]{2,1,0:T(8,128)S(1)}, f32[1,32,128]{2,1,0:T(8,128)S(1)}, u32[]{:S(2)}, u32[]{:S(2)}) collective-permute-start(f32[1,32,128]{2,1,0:T(8,128)S(1)} %get-tuple-element.56), channel_id=1, source_target_pairs={{0,8},{1,13},{2,10},{3,15},{4,12},{5,9},{6,14},{7,11},{8,0},{9,5},... | collective-permute-start | bytes 49160 | tf_op jit(solution)/shard_map/ppermute | solution.py:33
  40.8 2.0 %collective-permute-start.8 = (bf16[4,512,128]{2,1,0:T(8,128)(2,1)S(1)}, bf16[4,512,128]{2,1,0:T(8,128)(2,1)S(1)}, u32[]{:S(2)}, u32[]{:S(2)}) collective-permute-start(bf16[4,512,128]{2,1,0:T(8,128)(2,1)S(1)} %get-tuple-element.58.c1), channel_id=1, source_target_pairs={{0,1},{1,0},{2,3},{3,2},{4,5},{5,4},{6,7},{7,6},{8,9},{9,8},{10,11... | collective-permute-start | bytes 1572872 | tf_op jit(solution)/shard_map/ppermute | solution.py:33
  40.9 1.9 %collective-permute-start.7 = (f32[1,32,128]{2,1,0:T(8,128)S(1)}, f32[1,32,128]{2,1,0:T(8,128)S(1)}, u32[]{:S(2)}, u32[]{:S(2)}) collective-permute-start(f32[1,32,128]{2,1,0:T(8,128)S(1)} %get-tuple-element.57.sum_a), channel_id=1, source_target_pairs={{0,1},{1,0},{2,3},{3,2},{4,5},{5,4},{6,7},{7,6},{8,9},{9,8},{10,11... | collective-permute-start | bytes 49160 | tf_op jit(solution)/shard_map/ppermute | solution.py:33
  50.4 7.2 %collective-permute-start.10 = (bf16[608,128]{1,0:T(8,128)(2,1)S(1)}, bf16[608,128]{1,0:T(8,128)(2,1)S(1)}, u32[]{:S(2)}, u32[]{:S(2)}) collective-permute-start(bf16[608,128]{1,0:T(8,128)(2,1)S(1)} %get-tuple-element.60.own_ref), channel_id=1, source_target_pairs={{0,2},{1,3},{2,0},{3,1},{4,6},{5,7},{6,4},{7,5},{8,10},{9,11},{10,... | collective-permute-start | bytes 466952 | tf_op jit(solution)/shard_map/ppermute | solution.py:33
  53.7 5.4 %collective-permute-start.9 = (bf16[608,128]{1,0:T(8,128)(2,1)S(1)}, bf16[608,128]{1,0:T(8,128)(2,1)S(1)}, u32[]{:S(2)}, u32[]{:S(2)}) collective-permute-start(bf16[608,128]{1,0:T(8,128)(2,1)S(1)} %get-tuple-element.60.own_ref), channel_id=1, source_target_pairs={{0,1},{1,0},{2,3},{3,2},{4,5},{5,4},{6,7},{7,6},{8,9},{9,8},{10,11... | collective-permute-start | bytes 466952 | tf_op jit(solution)/shard_map/ppermute | solution.py:33
  57.6 1.8 %collective-permute-start.11 = (bf16[608,128]{1,0:T(8,128)(2,1)S(1)}, bf16[608,128]{1,0:T(8,128)(2,1)S(1)}, u32[]{:S(2)}, u32[]{:S(2)}) collective-permute-start(bf16[608,128]{1,0:T(8,128)(2,1)S(1)} %get-tuple-element.64.across_ref), channel_id=1, source_target_pairs={{0,1},{1,0},{2,3},{3,2},{4,5},{5,4},{6,7},{7,6},{8,9},{9,8},{10,11... | collective-permute-start | bytes 466952 | tf_op jit(solution)/shard_map/ppermute | solution.py:33
  58.4 7.8 %collective-permute-start.14 = (bf16[8,64,512]{2,1,0:T(8,128)(2,1)S(1)}, bf16[8,64,512]{2,1,0:T(8,128)(2,1)S(1)}, u32[]{:S(2)}, u32[]{:S(2)}) collective-permute-start(bf16[8,64,512]{2,1,0:T(8,128)(2,1)S(1)} %get-tuple-element.68), channel_id=1, source_target_pairs={{0,1},{1,0},{2,3},{3,2},{4,5},{5,4},{6,7},{7,6},{8,9},{9,8},{10,11... | collective-permute-start | bytes 1572872 | tf_op jit(solution)/shard_map/ppermute | solution.py:33
  58.4 18.8 %collective-permute-start.15 = (bf16[8,64,512]{2,1,0:T(8,128)(2,1)S(1)}, bf16[8,64,512]{2,1,0:T(8,128)(2,1)S(1)}, u32[]{:S(2)}, u32[]{:S(2)}) collective-permute-start(bf16[8,64,512]{2,1,0:T(8,128)(2,1)S(1)} %get-tuple-element.70), channel_id=1, source_target_pairs={{1,2},{2,1},{3,4},{4,3},{5,6},{6,5},{7,8},{8,7},{9,10},{10,9},{11,... | collective-permute-start | bytes 1572872 | tf_op jit(solution)/shard_map/ppermute | solution.py:33
  59.5 17.7 %collective-permute-start.12 = (bf16[4,512,128]{2,1,0:T(8,128)(2,1)S(1)}, bf16[4,512,128]{2,1,0:T(8,128)(2,1)S(1)}, u32[]{:S(2)}, u32[]{:S(2)}) collective-permute-start(bf16[4,512,128]{2,1,0:T(8,128)(2,1)S(1)} %get-tuple-element.66.wait_ref.c0), channel_id=1, source_target_pairs={{1,4},{3,6},{4,1},{5,8},{6,3},{7,10},{8,5},{9,12},{10,7},{11,14},{... | collective-permute-start | bytes 1572872 | tf_op jit(solution)/shard_map/ppermute | solution.py:33
  60.2 17.0 %collective-permute-start.13 = (f32[1,32,128]{2,1,0:T(8,128)S(1)}, f32[1,32,128]{2,1,0:T(8,128)S(1)}, u32[]{:S(2)}, u32[]{:S(2)}) collective-permute-start(f32[1,32,128]{2,1,0:T(8,128)S(1)} %get-tuple-element.67), channel_id=1, source_target_pairs={{0,8},{1,13},{2,10},{3,15},{4,12},{5,9},{6,14},{7,11},{8,0},{9,5},... | collective-permute-start | bytes 49160 | tf_op jit(solution)/shard_map/ppermute | solution.py:33
  77.3 2.0 %collective-permute-start.17 = (bf16[4,512,128]{2,1,0:T(8,128)(2,1)S(1)}, bf16[4,512,128]{2,1,0:T(8,128)(2,1)S(1)}, u32[]{:S(2)}, u32[]{:S(2)}) collective-permute-start(bf16[4,512,128]{2,1,0:T(8,128)(2,1)S(1)} %get-tuple-element.72.c1), channel_id=1, source_target_pairs={{0,1},{1,0},{2,3},{3,2},{4,5},{5,4},{6,7},{7,6},{8,9},{9,8},{10,11... | collective-permute-start | bytes 1572872 | tf_op jit(solution)/shard_map/ppermute | solution.py:33
  77.3 1.9 %collective-permute-start.16 = (f32[1,32,128]{2,1,0:T(8,128)S(1)}, f32[1,32,128]{2,1,0:T(8,128)S(1)}, u32[]{:S(2)}, u32[]{:S(2)}) collective-permute-start(f32[1,32,128]{2,1,0:T(8,128)S(1)} %get-tuple-element.71.sum_a), channel_id=1, source_target_pairs={{0,1},{1,0},{2,3},{3,2},{4,5},{5,4},{6,7},{7,6},{8,9},{9,8},{10,11... | collective-permute-start | bytes 49160 | tf_op jit(solution)/shard_map/ppermute | solution.py:33
  83.9 1.8 %collective-permute-start.18 = (f32[64,128]{1,0:T(8,128)S(1)}, f32[64,128]{1,0:T(8,128)S(1)}, u32[]{:S(2)}, u32[]{:S(2)}) collective-permute-start(f32[64,128]{1,0:T(8,128)S(1)} %get-tuple-element.74), channel_id=1, source_target_pairs={{0,1},{1,0},{2,3},{3,2},{4,5},{5,4},{6,7},{7,6},{8,9},{9,8},{10,11... | collective-permute-start | bytes 98312 | tf_op jit(solution)/shard_map/ppermute | solution.py:33
  85.8 3.9 %collective-permute-start.19 = (f32[64,128]{1,0:T(8,128)S(1)}, f32[64,128]{1,0:T(8,128)S(1)}, u32[]{:S(2)}, u32[]{:S(2)}) collective-permute-start(f32[64,128]{1,0:T(8,128)S(1)} %add.34), channel_id=1, source_target_pairs={{0,2},{1,3},{2,0},{3,1},{4,6},{5,7},{6,4},{7,5},{8,10},{9,11},{10,... | collective-permute-start | bytes 98312 | tf_op jit(solution)/shard_map/ppermute | solution.py:33
  89.7 3.9 %collective-permute-start.20 = (f32[64,128]{1,0:T(8,128)S(1)}, f32[64,128]{1,0:T(8,128)S(1)}, u32[]{:S(2)}, u32[]{:S(2)}) collective-permute-start(f32[64,128]{1,0:T(8,128)S(1)} %add.35), channel_id=1, source_target_pairs={{0,4},{1,5},{2,6},{3,7},{4,0},{5,1},{6,2},{7,3},{8,12},{9,13},{10,... | collective-permute-start | bytes 98312 | tf_op jit(solution)/shard_map/ppermute | solution.py:33
  93.6 4.8 %collective-permute-start.21 = (f32[64,128]{1,0:T(8,128)S(1)}, f32[64,128]{1,0:T(8,128)S(1)}, u32[]{:S(2)}, u32[]{:S(2)}) collective-permute-start(f32[64,128]{1,0:T(8,128)S(1)} %add.36), channel_id=1, source_target_pairs={{0,8},{1,9},{2,10},{3,11},{4,12},{5,13},{6,14},{7,15},{8,0},{9,1},... | collective-permute-start | bytes 98312 | tf_op jit(solution)/shard_map/ppermute | solution.py:33
  (6 other events, 19.9 us)

commit v7 on v6

--- a/solution.py
+++ b/solution.py
@@ -16,9 +16,9 @@
 BF16 = jnp.bfloat16
 HALF_SCALE = math.sqrt(2.0 * KERNEL_SCALE * math.log2(math.e))
 UNROLL = 4
-FAR_UNROLL = 8
+FAR_UNROLL = 16
 RELAY_UNROLL = 4
-VMEM_LIMIT = 12 * 1024 * 1024
+VMEM_LIMIT = 13 * 1024 * 1024
 WIDE_LIMIT = 54 * 1024 * 1024
 SELF_LIMIT = 28 * 1024 * 1024
 WHOLE = pl.BlockSpec(memory_space=pltpu.VMEM)
@@ -196,36 +196,47 @@
     per, rank, leaf = basis_ref.shape
     columns, features = rs_ref.shape[0], e_ref.shape[0]
     size = rank // 2
-    copies = [
-        pltpu.make_async_copy(source, target, sems.at[at])
-        for at, (source, target) in enumerate(
-            ((transfer_hbm, transfer_ref), (sc_hbm, sc_ref), (rs_hbm, rs_ref), (basis_hbm, basis_ref), (e_hbm, e_ref))
-        )
+    groups = per // UNROLL
+    width = UNROLL * leaf
+    small = [
+        pltpu.make_async_copy(transfer_hbm, transfer_ref, sems.at[0, 0]),
+        pltpu.make_async_copy(sc_hbm, sc_ref, sems.at[0, 1]),
     ]
-    for copy in copies:
+    copies = []
+    for group in range(groups):
+        cols, rows = pl.ds(group * width, width), pl.ds(group * UNROLL, UNROLL)
+        copies.append([
+            pltpu.make_async_copy(rs_hbm.at[:, cols], rs_ref.at[:, cols], sems.at[group + 1, 0]),
+            pltpu.make_async_copy(basis_hbm.at[rows], basis_ref.at[rows], sems.at[group + 1, 1]),
+            pltpu.make_async_copy(e_hbm.at[:, cols], e_ref.at[:, cols], sems.at[group + 1, 2]),
+        ])
+    for copy in small + sum(copies, []):
         copy.start()
-    copies[0].wait()
+    small[0].wait()
     wide = transfer_ref[...].astype(F32)
     for k in range(rank * rank // 128):
         by_leaf[k * per : (k + 1) * per] = wide[:, k * 128 : (k + 1) * 128]
     for at in range(per):
         store_square(by_leaf[pl.ds(at, rank * rank // 128, stride=per)], squares.at[at])
     trans_ref[...] = squares[:, :, :rank].astype(BF16)
-    for copy in copies[1:]:
-        copy.wait()
+    small[1].wait()
 
     def one(at):
-        rounded = (columns_of(rs_ref, at, leaf) * columns_of(sc_ref, at, leaf)).astype(BF16)
+        rounded = (rs_ref[:, at * leaf : (at + 1) * leaf] * sc_ref[:, at * leaf : (at + 1) * leaf]).astype(BF16)
         v_ref[at] = rounded
-        here = columns_of(e_ref, at, leaf)
+        here = e_ref[:, at * leaf : (at + 1) * leaf]
         high = here.astype(BF16)
         points[at, :features] = high
         points[at, features:] = (here - high.astype(F32)).astype(BF16)
         coef = leaf_coefficients(basis_ref[at], rounded)
-        coefs[pl.ds(pl.multiple_of(at * rank, rank), rank)] = coef
-        cp_ref[pl.ds(pl.multiple_of(at * size, size), size)] = pack_pair(coef)
-
-    leaf_loop(per, UNROLL, one)
+        coefs[pl.ds(at * rank, rank)] = coef
+        cp_ref[pl.ds(at * size, size)] = pack_pair(coef)
+
+    for group in range(groups):
+        for copy in copies[group]:
+            copy.wait()
+        for u in range(UNROLL):
+            one(group * UNROLL + u)
     store_share(share_of(trans_ref[...], coefs[...]), part_ref, cp_ref)
     odd = pos_ref[0] % 2
     half = per // 2
@@ -250,63 +261,47 @@
 
 def build_lists(near_ref, lists, pos, half):
     slots = near_ref.shape[0] - 1
-    total = near_ref.shape[1] * slots
+    per = near_ref.shape[1]
     base = pos * 2 * half - half
-
-    def put(entry, counts):
-        m = near_ref[1 + entry % slots, entry // slots] - base
-        own = (m >= half) & (m < 3 * half)
-        low = (m < half) == (pos % 2 == 1)
-        takes = (own, ~own & low, ~own & ~low, own | low)
-        for kind, count in enumerate(counts):
-            lists[kind, count] = entry * 4 * half + m
-        return tuple(count + jnp.where(take, 1, 0) for count, take in zip(counts, takes))
-
-    counts = lax.fori_loop(0, total, put, (0, 0, 0, 0))
+    odd = pos % 2 == 1
+
+    def put(leaf, counts):
+        for slot in range(slots):
+            m = near_ref[1 + slot, leaf] - base
+            own = (m >= half) & (m < 3 * half)
+            low = (m < half) == odd
+            value = (leaf << 16) | ((leaf * slots + slot) << 8) | m
+            for kind, count in enumerate(counts):
+                lists[kind, count] = value
+            takes = (own, ~own & low, ~own & ~low, own | low)
+            counts = tuple(count + jnp.where(take, 1, 0) for count, take in zip(counts, takes))
+        return counts
+
+    counts = lax.fori_loop(0, per, put, (0, 0, 0, 0))
     for kind, count in enumerate(counts):
         for u in range(UNROLL):
-            lists[kind, count + u] = total * 4 * half + half
+            lists[kind, count + u] = (per << 16) | ((per * slots) << 8) | half
         lists[kind, lists.shape[1] - 1] = count
 
 
-def near_entry(lists, kind, at, tile_ref, half):
-    slots = (tile_ref.shape[0] - 1) // (2 * half)
+def near_entry(lists, kind, at, half):
     value = lists[kind, at]
-    entry = value // (4 * half)
-    leaf_at = entry // slots
-    return entry, leaf_at, jnp.minimum(leaf_at, 2 * half - 1), value % (4 * half)
+    leaf_at = value >> 16
+    return (value >> 8) & 255, leaf_at, jnp.minimum(leaf_at, 2 * half - 1), value & 255
 
 
 def self_kernel(e_ref, v_ref, wait_ref, self_ref, near_out, buffer, sems):
     per, _, leaf = v_ref.shape
-
-    def copy_out(slot, at):
-        return pltpu.make_async_copy(buffer.at[slot], self_ref.at[at], sems.at[slot])
-
-    def trip(i, carry):
-        for u in range(UNROLL):
-            at = i * UNROLL + u
-            slot = (i % 2) * UNROLL + u
-
-            @pl.when(i >= 2)
-            def _():
-                copy_out(slot, at - 2 * UNROLL).wait()
-
-        for u in range(UNROLL):
-            at = i * UNROLL + u
-            points = columns_of(e_ref, at, leaf)
-            tile = tile_of(other_rows(points), own_rows(points))
-            buffer[(i % 2) * UNROLL + u] = tile
-            near_out[at] = dot(v_ref[at], tile, 1, 0)
-        for u in range(UNROLL):
-            copy_out((i % 2) * UNROLL + u, i * UNROLL + u).start()
-        return carry
-
-    trips = per // UNROLL
-    lax.fori_loop(0, trips, trip, 0)
-    for i in range(max(trips - 2, 0), trips):
-        for u in range(UNROLL):
-            copy_out((i % 2) * UNROLL + u, i * UNROLL + u).wait()
+    copies = []
+    for at in range(per):
+        points = e_ref[:, at * leaf : (at + 1) * leaf]
+        tile = tile_of(other_rows(points), own_rows(points))
+        buffer[at] = tile
+        near_out[at] = dot(v_ref[at], tile, 1, 0)
+        copies.append(pltpu.make_async_copy(buffer.at[at], self_ref.at[at], sems.at[at]))
+        copies[-1].start()
+    for copy in copies:
+        copy.wait()
 
 
 def points_of(ref, at, columns, features):
@@ -323,7 +318,7 @@
 
     def trip(i, carry):
         for u in range(UNROLL):
-            entry, leaf_at, row, m = near_entry(lists, 3, i * UNROLL + u, tile_ref, half)
+            entry, leaf_at, row, m = near_entry(lists, 3, i * UNROLL + u, half)
             own = (m >= half) & (m < 3 * half)
             place = jnp.clip(m - half, 0, per - 1)
             points = jnp.where(
@@ -344,7 +339,7 @@
 
     def trip(i, carry):
         for u in range(UNROLL):
-            entry, leaf_at, _, m = near_entry(lists, 0, i * UNROLL + u, tile_ref, half)
+            entry, leaf_at, _, m = near_entry(lists, 0, i * UNROLL + u, half)
             place = jnp.clip(m - half, 0, 2 * half - 1)
             near_out[leaf_at] += dot(v_ref[place], tile_ref[entry], 1, 0)
         return carry
@@ -367,7 +362,7 @@
 
     def trip(i, carry):
         for u in range(UNROLL):
-            entry, leaf_at, _, m = near_entry(lists, 1, i * UNROLL + u, tile_ref, half)
+            entry, leaf_at, _, m = near_entry(lists, 1, i * UNROLL + u, half)
             near_out[leaf_at] += dot(vx_ref[m % half], tile_ref[entry], 1, 0)
         return carry
 
@@ -430,7 +425,7 @@
 
     def trip(i, carry):
         for u in range(UNROLL):
-            entry, leaf_at, row, m = near_entry(lists, 2, i * UNROLL + u, tile_ref, half)
+            entry, leaf_at, row, m = near_entry(lists, 2, i * UNROLL + u, half)
             points = points_of(vo_ref, m % half, columns, features)
             tile = tile_of(other_rows(points), own_rows(columns_of(e_ref, row, leaf)))
             tile_ref[entry] = tile
@@ -485,7 +480,7 @@
 
     def trip(i, carry):
         for u in range(UNROLL):
-            entry, leaf_at, _, m = near_entry(lists, 2, i * UNROLL + u, tile_ref, half)
+            entry, leaf_at, _, m = near_entry(lists, 2, i * UNROLL + u, half)
             near_out[leaf_at] += dot(vo_ref[m % half], tile_ref[entry], 1, 0)
         return carry
 
@@ -630,7 +625,7 @@
         [leaf_shape, cp_shape, part_shape, trans_shape, both_shape, both_shape],
         [pltpu.VMEM(right_side.shape, F32), pltpu.VMEM(scale_row.shape, F32), pltpu.VMEM(leaf_basis.shape, BF16),
          pltpu.VMEM(transfer.shape, BF16), pltpu.VMEM(embeddings.shape, F32),
-         pltpu.VMEM((per, 2 * features, leaf), BF16), coefs_shape, pltpu.VMEM((per * rank * rank // 128, 128), F32), pltpu.VMEM((per, rank, 128), F32), pltpu.SemaphoreType.DMA((5,))],
+         pltpu.VMEM((per, 2 * features, leaf), BF16), coefs_shape, pltpu.VMEM((per * rank * rank // 128, 128), F32), pltpu.VMEM((per, rank, 128), F32), pltpu.SemaphoreType.DMA((per // UNROLL + 1, 3))],
         (position, right_side, scale_row, leaf_basis, transfer, embeddings), limit=WIDE_LIMIT,
     )
     got = first_messages(cp)
@@ -651,7 +646,7 @@
     vx = sibling(mx)
     tself, near = call(
         self_kernel, "self_tiles", [WHOLE] * 2 + [ANYWHERE], [self_shape, near_shape],
-        [pltpu.VMEM((2 * UNROLL, leaf, leaf), BF16), pltpu.SemaphoreType.DMA((2 * UNROLL,))],
+        [pltpu.VMEM((per, leaf, leaf), BF16), pltpu.SemaphoreType.DMA((per,))],
         (embeddings, v, mo), out_specs=[OUTSIDE, WHOLE],
     )
     quad, far_quad, mine = second_messages(position, cp, got, part, near)

time: 101 us -> 99.6 us (0.986)
  Pallas kernels: 49.8 us -> 46.4 us
  waiting for transfers between devices: 19.6 us -> 21.3 us
    pallas_call x16, Pallas kernels: 49.8 us -> 46.4 us  [call(): pl.pallas_call(kernel, in_specs=in_specs, out_specs=out_specs or [WHOLE]...]
    ppermute x22, waiting for transfers between devices: 19.6 us -> 21.3 us  [involution(): return lax.ppermute(value, 'leaf', pairs)]
  transfers between devices with their start and end apart: 22 -> 22, of which waited for: 8 -> 8; matrix products, arithmetic and copies ran while one was open for 0% -> 0% of each run, Pallas kernels for 34% -> 33%
where the time goes in v7:
time: 99.6 us; the launch traced here: 99.2 us
  Pallas kernels  46.4 us (47%)
  starting transfers between devices  27.3 us (27%)
  waiting for transfers between devices  21.3 us (21%)
  other arithmetic  2.87 us (3%)
    pallas_call x16, Pallas kernels, call(): pl.pallas_call(kernel, in_specs=in_specs, out_specs=out_specs or [WHOLE]...  46.4 us
    ppermute x22, starting transfers between devices, involution(): return lax.ppermute(value, 'leaf', pairs)  27.3 us
    ppermute x22, waiting for transfers between devices, involution(): return lax.ppermute(value, 'leaf', pairs)  21.3 us
    add x1, other arithmetic, body(): residual = right_side - first_weight * image + second_weight * second  2.64 us
  transfers between devices with their start and end apart: 22, of which 8 were waited for; matrix products, arithmetic and copies ran while one was open for 0% of the time, Pallas kernels for 33%

profile of v7, /device:TPU:0, one launch (start us, length us, event | category | flops | bytes accessed | tf_op | source)
XLA Modules:
  0.0 99.2 jit_solution(14648907999953141063)
XLA Ops:
  0.7 3.1 %prep.1 = (bf16[16,64,512]{2,1,0:T(8,128)(2,1)S(1)}, bf16[608,128]{1,0:T(8,128)(2,1)S(1)}, f32[32,128]{1,0:T(8,128)S(1)}, bf16[16,64,64]{2,1,0:T(8,128)(2,1)S(1)...) custom-call(s32[1]{0:T(128)} %bitcast.pos_ref, f32[64,8192]{1,0:T(8,128)} %rs_ref.3, ...), custom_call_target="tpu_custom_call" | custom-call | tf_op jit(solution)/shard_map/prep/pallas_call | solution.py:521
  3.8 3.0 %collective-permute-start = (bf16[608,128]{1,0:T(8,128)(2,1)S(1)}, bf16[608,128]{1,0:T(8,128)(2,1)S(1)}, u32[]{:S(2)}, u32[]{:S(2)}) collective-permute-start(bf16[608,128]{1,0:T(8,128)(2,1)S(1)} %get-tuple-element.39.wait_ref.own_ref), channel_id=1, source_target_pairs={{0,2},{1,3},{2,0},{3,1},{4,6},{5,7},{6,4},{7,5},{8,10},{9,11},{10,... | collective-permute-start | bytes 466952 | tf_op jit(solution)/shard_map/ppermute | solution.py:33
  6.8 4.0 %relayout.1 = (bf16[16,128,256]{2,1,0:T(8,128)(2,1)S(1)}, bf16[1,64,64]{2,1,0:T(8,128)(2,1)S(1)}, s32[4,40]{1,0:T(4,128)S(1)}) custom-call(s32[1]{0:T(128)} %bitcast.pos_ref, s32[3,16]{1,0:T(4,128)S(1)} %bitcast.9, bf16[16,8,4096]{2,1,0:T(8,128)(2,1)S(1)} %copy-done.3, bf16[2,2,4096]{2,1,0:T(2,128)(2,1)S(1)} %copy-done.5, ...), custom_call_target="tpu_custom_call" | custom-call | tf_op jit(solution)/shard_map/relayout/pallas_call | solution.py:521
  11.4 0.7 collective-permute-start.1
  12.2 6.2 %self_tiles.1 = (bf16[128,512,512]{2,1,0:T(8,128)(2,1)}, f32[17,64,512]{2,1,0:T(8,128)S(1)}) custom-call(f32[32,8192]{1,0:T(8,128)S(1)} %copy-done.1, bf16[16,64,512]{2,1,0:T(8,128)(2,1)S(1)} %get-tuple-element.46.v_ref, bf16[8,128,512]{2,1,0:T(8,128)(2,1)S(1)} %get-tuple-element.45.wait_ref), custom_call_target="tpu_custom_call" | custom-call | tf_op jit(solution)/shard_map/self_tiles/pallas_call | solution.py:521
  18.4 0.7 collective-permute-start.5
  19.1 6.8 %collective-permute-start.6 = (f32[1,32,128]{2,1,0:T(8,128)S(1)}, f32[1,32,128]{2,1,0:T(8,128)S(1)}, u32[]{:S(2)}, u32[]{:S(2)}) collective-permute-start(f32[1,32,128]{2,1,0:T(8,128)S(1)} %get-tuple-element.56), channel_id=1, source_target_pairs={{0,8},{1,13},{2,10},{3,15},{4,12},{5,9},{6,14},{7,11},{8,0},{9,5},... | collective-permute-start | bytes 49160 | tf_op jit(solution)/shard_map/ppermute | solution.py:33
  26.0 12.7 %own_tiles.1 = (bf16[33,512,512]{2,1,0:T(8,128)(2,1)S(1)}, f32[17,64,512]{2,1,0:T(8,128)S(1)}) custom-call(s32[1]{0:T(128)} %bitcast.pos_ref, s32[4,40]{1,0:T(4,128)S(1)} %get-tuple-element.42.lists, f32[32,8192]{1,0:T(8,128)S(1)} %copy-done.1, bf16[16,64,512]{2,1,0:T(8,128)(2,1)S(1)} %get-tuple-element.46.v_ref, ...), custom_call_target="tpu_custom_call", output_to_operand_aliasing={{1}: (5, {})} | custom-call | tf_op jit(solution)/shard_map/own_tiles/pallas_call | solution.py:521
  39.3 0.8 foreign_tiles.1
  41.2 6.7 %far_first.1 = (f32[64,8192]{1,0:T(8,128)S(1)}, bf16[16,64,512]{2,1,0:T(8,128)(2,1)S(1)}, bf16[608,128]{1,0:T(8,128)(2,1)S(1)}, f32[32,128]{1,0:T(8,128)S(1)}, f...) custom-call(s32[1]{0:T(128)} %bitcast.pos_ref, s32[8,16]{1,0:T(8,128)S(1)} %bitcast.7, ...), custom_call_target="tpu_custom_call" | custom-call | tf_op jit(solution)/shard_map/far_first/pallas_call | solution.py:521
  47.9 3.2 %collective-permute-start.10 = (bf16[608,128]{1,0:T(8,128)(2,1)S(1)}, bf16[608,128]{1,0:T(8,128)(2,1)S(1)}, u32[]{:S(2)}, u32[]{:S(2)}) collective-permute-start(bf16[608,128]{1,0:T(8,128)(2,1)S(1)} %get-tuple-element.60.own_ref), channel_id=1, source_target_pairs={{0,2},{1,3},{2,0},{3,1},{4,6},{5,7},{6,4},{7,5},{8,10},{9,11},{10,... | collective-permute-start | bytes 466952 | tf_op jit(solution)/shard_map/ppermute | solution.py:33
  51.7 3.6 %own_again.1.refs_2_.near_in = f32[17,64,512]{2,1,0:T(8,128)S(1)} custom-call(s32[1]{0:T(128)} %bitcast.pos_ref, s32[4,40]{1,0:T(4,128)S(1)} %get-tuple-element.42.lists, bf16[16,64,512]{2,1,0:T(8,128)(2,1)S(1)} %get-tuple-element.62.v_ref, bf16[33,512,512]{2,1,0:T(8,128)(2,1)S(1)} %get-tuple-element.63.tile_ref), custom_call_target="tpu_custom_call" | custom-call | tf_op jit(solution)/shard_map/own_again/pallas_call | solution.py:521
  56.8 0.7 collective-permute-start.12
  57.5 7.5 %collective-permute-start.13 = (f32[1,32,128]{2,1,0:T(8,128)S(1)}, f32[1,32,128]{2,1,0:T(8,128)S(1)}, u32[]{:S(2)}, u32[]{:S(2)}) collective-permute-start(f32[1,32,128]{2,1,0:T(8,128)S(1)} %get-tuple-element.67), channel_id=1, source_target_pairs={{0,8},{1,13},{2,10},{3,15},{4,12},{5,9},{6,14},{7,11},{8,0},{9,5},... | collective-permute-start | bytes 49160 | tf_op jit(solution)/shard_map/ppermute | solution.py:33
  65.1 4.5 %self_again.1.refs_2_.near_in = f32[17,64,512]{2,1,0:T(8,128)S(1)} custom-call(s32[1]{0:T(128)} %bitcast.pos_ref, s32[4,40]{1,0:T(4,128)S(1)} %get-tuple-element.42.lists, bf16[16,64,512]{2,1,0:T(8,128)(2,1)S(1)} %get-tuple-element.62.v_ref, bf16[8,64,512]{2,1,0:T(8,128)(2,1)S(1)} %collective-permute-done.14.vx_ref, ...), custom_call_target="tpu_custom_call", output_to_operand_aliasing={{}: (6, {})} | custom-call | tf_op jit(solution)/shard_map/self_again/pallas_call | solution.py:521
  69.6 6.2 %collective-permute-done.13.refs_1_ = f32[1,32,128]{2,1,0:T(8,128)S(1)} collective-permute-done((f32[1,32,128]{2,1,0:T(8,128)S(1)}, f32[1,32,128]{2,1,0:T(8,128)S(1)}, u32[]{:S(2)}, u32[]{:S(2)}) %collective-permute-start.13) | collective-permute-done | bytes 16416 | tf_op jit(solution)/shard_map/ppermute | solution.py:33
  77.0 0.8 collective-permute-done.16.sum_b
  77.8 4.1 %far_again.1 = (f32[64,8192]{1,0:T(8,128)S(1)}, f32[64,128]{1,0:T(8,128)S(1)}) custom-call(s32[1]{0:T(128)} %bitcast.pos_ref, s32[8,16]{1,0:T(8,128)S(1)} %bitcast.8, f32[64,8192]{1,0:T(8,128)S(1)} %copy-done, f32[1,8192]{1,0:T(1,128)S(1)} %bitcast.6, f32[64,8192]{1,0:T(8,128)S(1)} %get-tuple-element.59.u_ref, bf16[16,64,512]{2,1,0:T(8,128)(2,1)S(1)} %copy-done.2, ...), custom_call_target="tpu_custom_call" | custom-call | tf_op jit(solution)/shard_map/far_again/pallas_call | solution.py:521
  82.0 0.8 collective-permute-start.18
  82.8 0.9 collective-permute-done.18
  83.6 3.9 %collective-permute-done.19 = f32[64,128]{1,0:T(8,128)S(1)} collective-permute-done((f32[64,128]{1,0:T(8,128)S(1)}, f32[64,128]{1,0:T(8,128)S(1)}, u32[]{:S(2)}, u32[]{:S(2)}) %collective-permute-start.19) | collective-permute-done | bytes 32800 | tf_op jit(solution)/shard_map/ppermute | solution.py:33
  87.9 3.6 %collective-permute-done.20 = f32[64,128]{1,0:T(8,128)S(1)} collective-permute-done((f32[64,128]{1,0:T(8,128)S(1)}, f32[64,128]{1,0:T(8,128)S(1)}, u32[]{:S(2)}, u32[]{:S(2)}) %collective-permute-start.20) | collective-permute-done | bytes 32800 | tf_op jit(solution)/shard_map/ppermute | solution.py:33
  91.5 4.9 %collective-permute-done.21 = f32[64,128]{1,0:T(8,128)S(1)} collective-permute-done((f32[64,128]{1,0:T(8,128)S(1)}, f32[64,128]{1,0:T(8,128)S(1)}, u32[]{:S(2)}, u32[]{:S(2)}) %collective-permute-start.21) | collective-permute-done | bytes 32800 | tf_op jit(solution)/shard_map/ppermute | solution.py:33
  96.6 2.6 %multiply_add_fusion = (f32[64,8192]{1,0:T(8,128)}, f32[64,8192]{1,0:T(8,128)}) fusion(f32[64,8192]{1,0:T(8,128)S(1)} %get-tuple-element.75, f32[64,8192]{1,0:T(8,128)S(1)} %copy-done, f32[64,8192]{1,0:T(8,128)S(1)} %get-tuple-element.59.u_ref, f32[64]{0:T(128)S(1)} %get-tuple-element.77, f32[64]{0:T(128)S(1)} %get-tuple-element.76, f32[8192]{0:T(1024)S(1)} %copy-done.4), kind=kLoop, calls=%fused_computation | loop fusion | flops 4194304 | bytes 10519040 | tf_op jit(solution)/shard_map/add | solution.py:710
  (58 shorter events, 6.2 us)
Async XLA Ops:
  0.6 6.1 %copy-start.3 = (bf16[16,8,4096]{2,1,0:T(8,128)(2,1)S(1)}, bf16[16,8,4096]{2,1,0:T(8,128)(2,1)}, u32[]{:S(2)}) copy-start(bf16[16,8,4096]{2,1,0:T(8,128)(2,1)} %coup_ref.1) | copy-start | bytes 3145732
  0.6 6.1 %copy-start.5 = (bf16[2,2,4096]{2,1,0:T(2,128)(2,1)S(1)}, bf16[2,2,4096]{2,1,0:T(2,128)(2,1)}, u32[]{:S(2)}) copy-start(bf16[2,2,4096]{2,1,0:T(2,128)(2,1)} %coarse_ref.1) | copy-start | bytes 98308
  3.8 7.0 %collective-permute-start = (bf16[608,128]{1,0:T(8,128)(2,1)S(1)}, bf16[608,128]{1,0:T(8,128)(2,1)S(1)}, u32[]{:S(2)}, u32[]{:S(2)}) collective-permute-start(bf16[608,128]{1,0:T(8,128)(2,1)S(1)} %get-tuple-element.39.wait_ref.own_ref), channel_id=1, source_target_pairs={{0,2},{1,3},{2,0},{3,1},{4,6},{5,7},{6,4},{7,5},{8,10},{9,11},{10,... | collective-permute-start | bytes 466952 | tf_op jit(solution)/shard_map/ppermute | solution.py:33
  10.8 15.2 %collective-permute-start.2 = (bf16[8,128,512]{2,1,0:T(8,128)(2,1)S(1)}, bf16[8,128,512]{2,1,0:T(8,128)(2,1)S(1)}, u32[]{:S(2)}, u32[]{:S(2)}) collective-permute-start(bf16[8,128,512]{2,1,0:T(8,128)(2,1)S(1)} %get-tuple-element.47), channel_id=1, source_target_pairs={{0,1},{1,0},{2,3},{3,2},{4,5},{5,4},{6,7},{7,6},{8,9},{9,8},{10,11... | collective-permute-start | bytes 3145736 | tf_op jit(solution)/shard_map/ppermute | solution.py:33
  10.9 7.5 %collective-permute-start.3 = (bf16[608,128]{1,0:T(8,128)(2,1)S(1)}, bf16[608,128]{1,0:T(8,128)(2,1)S(1)}, u32[]{:S(2)}, u32[]{:S(2)}) collective-permute-start(bf16[608,128]{1,0:T(8,128)(2,1)S(1)} %get-tuple-element.39.wait_ref.own_ref), channel_id=1, source_target_pairs={{0,1},{1,0},{2,3},{3,2},{4,5},{5,4},{6,7},{7,6},{8,9},{9,8},{10,11... | collective-permute-start | bytes 466952 | tf_op jit(solution)/shard_map/ppermute | solution.py:33
  11.4 7.0 %collective-permute-start.4 = (bf16[608,128]{1,0:T(8,128)(2,1)S(1)}, bf16[608,128]{1,0:T(8,128)(2,1)S(1)}, u32[]{:S(2)}, u32[]{:S(2)}) collective-permute-start(bf16[608,128]{1,0:T(8,128)(2,1)S(1)} %get-tuple-element.49.across_ref), channel_id=1, source_target_pairs={{0,1},{1,0},{2,3},{3,2},{4,5},{5,4},{6,7},{7,6},{8,9},{9,8},{10,11... | collective-permute-start | bytes 466952 | tf_op jit(solution)/shard_map/ppermute | solution.py:33
  11.4 27.9 %collective-permute-start.1 = (bf16[8,128,512]{2,1,0:T(8,128)(2,1)S(1)}, bf16[8,128,512]{2,1,0:T(8,128)(2,1)S(1)}, u32[]{:S(2)}, u32[]{:S(2)}) collective-permute-start(bf16[8,128,512]{2,1,0:T(8,128)(2,1)S(1)} %get-tuple-element.45.wait_ref), channel_id=1, source_target_pairs={{1,2},{2,1},{3,4},{4,3},{5,6},{6,5},{7,8},{8,7},{9,10},{10,9},{11,... | collective-permute-start | bytes 3145736 | tf_op jit(solution)/shard_map/ppermute | solution.py:33
  18.4 20.3 %collective-permute-start.5 = (bf16[4,512,128]{2,1,0:T(8,128)(2,1)S(1)}, bf16[4,512,128]{2,1,0:T(8,128)(2,1)S(1)}, u32[]{:S(2)}, u32[]{:S(2)}) collective-permute-start(bf16[4,512,128]{2,1,0:T(8,128)(2,1)S(1)} %get-tuple-element.51.wait_ref.c0), channel_id=1, source_target_pairs={{1,4},{3,6},{4,1},{5,8},{6,3},{7,10},{8,5},{9,12},{10,7},{11,14},{... | collective-permute-start | bytes 1572872 | tf_op jit(solution)/shard_map/ppermute | solution.py:33
  19.1 19.6 %collective-permute-start.6 = (f32[1,32,128]{2,1,0:T(8,128)S(1)}, f32[1,32,128]{2,1,0:T(8,128)S(1)}, u32[]{:S(2)}, u32[]{:S(2)}) collective-permute-start(f32[1,32,128]{2,1,0:T(8,128)S(1)} %get-tuple-element.56), channel_id=1, source_target_pairs={{0,8},{1,13},{2,10},{3,15},{4,12},{5,9},{6,14},{7,11},{8,0},{9,5},... | collective-permute-start | bytes 49160 | tf_op jit(solution)/shard_map/ppermute | solution.py:33
  38.7 2.0 %collective-permute-start.8 = (bf16[4,512,128]{2,1,0:T(8,128)(2,1)S(1)}, bf16[4,512,128]{2,1,0:T(8,128)(2,1)S(1)}, u32[]{:S(2)}, u32[]{:S(2)}) collective-permute-start(bf16[4,512,128]{2,1,0:T(8,128)(2,1)S(1)} %get-tuple-element.58.c1), channel_id=1, source_target_pairs={{0,1},{1,0},{2,3},{3,2},{4,5},{5,4},{6,7},{7,6},{8,9},{9,8},{10,11... | collective-permute-start | bytes 1572872 | tf_op jit(solution)/shard_map/ppermute | solution.py:33
  38.8 1.9 %collective-permute-start.7 = (f32[1,32,128]{2,1,0:T(8,128)S(1)}, f32[1,32,128]{2,1,0:T(8,128)S(1)}, u32[]{:S(2)}, u32[]{:S(2)}) collective-permute-start(f32[1,32,128]{2,1,0:T(8,128)S(1)} %get-tuple-element.57.sum_a), channel_id=1, source_target_pairs={{0,1},{1,0},{2,3},{3,2},{4,5},{5,4},{6,7},{7,6},{8,9},{9,8},{10,11... | collective-permute-start | bytes 49160 | tf_op jit(solution)/shard_map/ppermute | solution.py:33
  47.9 7.4 %collective-permute-start.10 = (bf16[608,128]{1,0:T(8,128)(2,1)S(1)}, bf16[608,128]{1,0:T(8,128)(2,1)S(1)}, u32[]{:S(2)}, u32[]{:S(2)}) collective-permute-start(bf16[608,128]{1,0:T(8,128)(2,1)S(1)} %get-tuple-element.60.own_ref), channel_id=1, source_target_pairs={{0,2},{1,3},{2,0},{3,1},{4,6},{5,7},{6,4},{7,5},{8,10},{9,11},{10,... | collective-permute-start | bytes 466952 | tf_op jit(solution)/shard_map/ppermute | solution.py:33
  51.1 5.5 %collective-permute-start.9 = (bf16[608,128]{1,0:T(8,128)(2,1)S(1)}, bf16[608,128]{1,0:T(8,128)(2,1)S(1)}, u32[]{:S(2)}, u32[]{:S(2)}) collective-permute-start(bf16[608,128]{1,0:T(8,128)(2,1)S(1)} %get-tuple-element.60.own_ref), channel_id=1, source_target_pairs={{0,1},{1,0},{2,3},{3,2},{4,5},{5,4},{6,7},{7,6},{8,9},{9,8},{10,11... | collective-permute-start | bytes 466952 | tf_op jit(solution)/shard_map/ppermute | solution.py:33
  55.3 1.5 %collective-permute-start.11 = (bf16[608,128]{1,0:T(8,128)(2,1)S(1)}, bf16[608,128]{1,0:T(8,128)(2,1)S(1)}, u32[]{:S(2)}, u32[]{:S(2)}) collective-permute-start(bf16[608,128]{1,0:T(8,128)(2,1)S(1)} %get-tuple-element.64.across_ref), channel_id=1, source_target_pairs={{0,1},{1,0},{2,3},{3,2},{4,5},{5,4},{6,7},{7,6},{8,9},{9,8},{10,11... | collective-permute-start | bytes 466952 | tf_op jit(solution)/shard_map/ppermute | solution.py:33
  55.8 9.3 %collective-permute-start.14 = (bf16[8,64,512]{2,1,0:T(8,128)(2,1)S(1)}, bf16[8,64,512]{2,1,0:T(8,128)(2,1)S(1)}, u32[]{:S(2)}, u32[]{:S(2)}) collective-permute-start(bf16[8,64,512]{2,1,0:T(8,128)(2,1)S(1)} %get-tuple-element.68), channel_id=1, source_target_pairs={{0,1},{1,0},{2,3},{3,2},{4,5},{5,4},{6,7},{7,6},{8,9},{9,8},{10,11... | collective-permute-start | bytes 1572872 | tf_op jit(solution)/shard_map/ppermute | solution.py:33
  55.9 19.9 %collective-permute-start.15 = (bf16[8,64,512]{2,1,0:T(8,128)(2,1)S(1)}, bf16[8,64,512]{2,1,0:T(8,128)(2,1)S(1)}, u32[]{:S(2)}, u32[]{:S(2)}) collective-permute-start(bf16[8,64,512]{2,1,0:T(8,128)(2,1)S(1)} %get-tuple-element.70), channel_id=1, source_target_pairs={{1,2},{2,1},{3,4},{4,3},{5,6},{6,5},{7,8},{8,7},{9,10},{10,9},{11,... | collective-permute-start | bytes 1572872 | tf_op jit(solution)/shard_map/ppermute | solution.py:33
  56.8 19.0 %collective-permute-start.12 = (bf16[4,512,128]{2,1,0:T(8,128)(2,1)S(1)}, bf16[4,512,128]{2,1,0:T(8,128)(2,1)S(1)}, u32[]{:S(2)}, u32[]{:S(2)}) collective-permute-start(bf16[4,512,128]{2,1,0:T(8,128)(2,1)S(1)} %get-tuple-element.66.wait_ref.c0), channel_id=1, source_target_pairs={{1,4},{3,6},{4,1},{5,8},{6,3},{7,10},{8,5},{9,12},{10,7},{11,14},{... | collective-permute-start | bytes 1572872 | tf_op jit(solution)/shard_map/ppermute | solution.py:33
  57.5 18.3 %collective-permute-start.13 = (f32[1,32,128]{2,1,0:T(8,128)S(1)}, f32[1,32,128]{2,1,0:T(8,128)S(1)}, u32[]{:S(2)}, u32[]{:S(2)}) collective-permute-start(f32[1,32,128]{2,1,0:T(8,128)S(1)} %get-tuple-element.67), channel_id=1, source_target_pairs={{0,8},{1,13},{2,10},{3,15},{4,12},{5,9},{6,14},{7,11},{8,0},{9,5},... | collective-permute-start | bytes 49160 | tf_op jit(solution)/shard_map/ppermute | solution.py:33
  75.8 2.0 %collective-permute-start.17 = (bf16[4,512,128]{2,1,0:T(8,128)(2,1)S(1)}, bf16[4,512,128]{2,1,0:T(8,128)(2,1)S(1)}, u32[]{:S(2)}, u32[]{:S(2)}) collective-permute-start(bf16[4,512,128]{2,1,0:T(8,128)(2,1)S(1)} %get-tuple-element.72.c1), channel_id=1, source_target_pairs={{0,1},{1,0},{2,3},{3,2},{4,5},{5,4},{6,7},{7,6},{8,9},{9,8},{10,11... | collective-permute-start | bytes 1572872 | tf_op jit(solution)/shard_map/ppermute | solution.py:33
  75.9 1.9 %collective-permute-start.16 = (f32[1,32,128]{2,1,0:T(8,128)S(1)}, f32[1,32,128]{2,1,0:T(8,128)S(1)}, u32[]{:S(2)}, u32[]{:S(2)}) collective-permute-start(f32[1,32,128]{2,1,0:T(8,128)S(1)} %get-tuple-element.71.sum_a), channel_id=1, source_target_pairs={{0,1},{1,0},{2,3},{3,2},{4,5},{5,4},{6,7},{7,6},{8,9},{9,8},{10,11... | collective-permute-start | bytes 49160 | tf_op jit(solution)/shard_map/ppermute | solution.py:33
  82.0 1.7 %collective-permute-start.18 = (f32[64,128]{1,0:T(8,128)S(1)}, f32[64,128]{1,0:T(8,128)S(1)}, u32[]{:S(2)}, u32[]{:S(2)}) collective-permute-start(f32[64,128]{1,0:T(8,128)S(1)} %get-tuple-element.74), channel_id=1, source_target_pairs={{0,1},{1,0},{2,3},{3,2},{4,5},{5,4},{6,7},{7,6},{8,9},{9,8},{10,11... | collective-permute-start | bytes 98312 | tf_op jit(solution)/shard_map/ppermute | solution.py:33
  83.6 3.9 %collective-permute-start.19 = (f32[64,128]{1,0:T(8,128)S(1)}, f32[64,128]{1,0:T(8,128)S(1)}, u32[]{:S(2)}, u32[]{:S(2)}) collective-permute-start(f32[64,128]{1,0:T(8,128)S(1)} %add.34), channel_id=1, source_target_pairs={{0,2},{1,3},{2,0},{3,1},{4,6},{5,7},{6,4},{7,5},{8,10},{9,11},{10,... | collective-permute-start | bytes 98312 | tf_op jit(solution)/shard_map/ppermute | solution.py:33
  87.5 3.9 %collective-permute-start.20 = (f32[64,128]{1,0:T(8,128)S(1)}, f32[64,128]{1,0:T(8,128)S(1)}, u32[]{:S(2)}, u32[]{:S(2)}) collective-permute-start(f32[64,128]{1,0:T(8,128)S(1)} %add.35), channel_id=1, source_target_pairs={{0,4},{1,5},{2,6},{3,7},{4,0},{5,1},{6,2},{7,3},{8,12},{9,13},{10,... | collective-permute-start | bytes 98312 | tf_op jit(solution)/shard_map/ppermute | solution.py:33
  91.5 4.9 %collective-permute-start.21 = (f32[64,128]{1,0:T(8,128)S(1)}, f32[64,128]{1,0:T(8,128)S(1)}, u32[]{:S(2)}, u32[]{:S(2)}) collective-permute-start(f32[64,128]{1,0:T(8,128)S(1)} %add.36), channel_id=1, source_target_pairs={{0,8},{1,9},{2,10},{3,11},{4,12},{5,13},{6,14},{7,15},{8,0},{9,1},... | collective-permute-start | bytes 98312 | tf_op jit(solution)/shard_map/ppermute | solution.py:33
  (6 other events, 18.7 us)

commit v8 on v7

--- a/solution.py
+++ b/solution.py
@@ -105,6 +105,14 @@
     for at in range(128, value.shape[1], 128):
         total += value[:, at : at + 128]
     return total
+
+
+def as_rows(parts, first, count):
+    lane = lax.broadcasted_iota(jnp.int32, parts[0].shape, 1)
+    out = jnp.zeros(parts[0].shape, F32)
+    for at, part in enumerate(parts):
+        out = jnp.where(lane == first + at, jnp.sum(part[...], axis=1, keepdims=True), out)
+    return out.T[:count]
 
 
 def leaf_coefficients(basis, rounded):
@@ -469,9 +477,7 @@
     store_share(share_of(trans_ref[...], coefs[...]), part_ref, cp_ref)
     mx_ref[...] = q_ref[pl.ds(half * (1 - odd), half)]
     mo_ref[...] = q_ref[pl.ds(half * odd, half)]
-    lane = lax.broadcasted_iota(jnp.int32, msg_ref.shape, 1)
-    out = jnp.where(lane == 0, jnp.sum(acc_uu[...], axis=1, keepdims=True), 0.0)
-    msg_ref[...] = jnp.where(lane == 1, jnp.sum(acc_ru[...], axis=1, keepdims=True), out)
+    msg_ref[...] = as_rows((acc_uu, acc_ru), 0, msg_ref.shape[0])
 
 
 def near_again_kernel(pos_ref, lists, vo_ref, tile_ref, near_in, near_out):
@@ -510,11 +516,7 @@
         acc_rw[...] += lane_groups(columns_of(rs_ref, l, leaf) * second)
 
     leaf_loop(per, FAR_UNROLL, one)
-    lane = lax.broadcasted_iota(jnp.int32, msg_ref.shape, 1)
-    out = prev_ref[...]
-    for at, acc in enumerate((acc_uw, acc_ww, acc_rw)):
-        out = jnp.where(lane == 2 + at, jnp.sum(acc[...], axis=1, keepdims=True), out)
-    msg_ref[...] = out
+    msg_ref[...] = prev_ref[...] + as_rows((acc_uw, acc_ww, acc_rw), 2, msg_ref.shape[0])
 
 
 def call(kernel, name, in_specs, out_shape, scratch, args, aliases=None, flops=0, out_specs=None, limit=VMEM_LIMIT):
@@ -611,7 +613,7 @@
     tile_shape = pltpu.VMEM((per * slots + 1, leaf, leaf), BF16)
     near_shape = pltpu.VMEM((per + 1, columns, leaf), F32)
     wide_shape = pltpu.VMEM((columns, local_points), F32)
-    msg_shape = pltpu.VMEM((columns, 128), F32)
+    msg_shape = pltpu.VMEM((8, columns), F32)
     coefs_shape = pltpu.VMEM((per * rank, columns), BF16)
     acc_shape = pltpu.VMEM((columns, 128), F32)
     window = [
@@ -697,7 +699,7 @@
     while mask < count:
         msg = msg + involution(msg, lambda i: i ^ mask)
         mask *= 2
-    uu, ru, uw, ww, rw = [msg[:, k : k + 1] for k in range(5)]
+    uu, ru, uw, ww, rw = [msg[k][:, None] for k in range(5)]
     step_one = ru / (uu + EPSILON)
     beta = -(uu - step_one * uw) / (uu + EPSILON)
     lead = 1.0 + beta

time: 99.6 us -> 98 us (0.984); the launches traced: 99.2 us -> 99.4 us
  starting transfers between devices: 27.3 us -> 29.5 us
  waiting for transfers between devices: 21.3 us -> 19.9 us
    ppermute x22, starting transfers between devices: 27.3 us -> 29.5 us  [involution(): return lax.ppermute(value, 'leaf', pairs)]
    ppermute x22, waiting for transfers between devices: 21.3 us -> 19.9 us  [involution(): return lax.ppermute(value, 'leaf', pairs)]
  transfers between devices with their start and end apart: 22 -> 22, of which waited for: 8 -> 9; matrix products, arithmetic and copies ran while one was open for 0% -> 0% of each run, Pallas kernels for 33% -> 32%
where the time goes in v8:
time: 98 us; the launch traced here: 99.4 us
  Pallas kernels  46 us (47%)
  starting transfers between devices  29.5 us (30%)
  waiting for transfers between devices  19.9 us (20%)
  other arithmetic  2.68 us (3%)
    pallas_call x16, Pallas kernels, call(): pl.pallas_call(kernel, in_specs=in_specs, out_specs=out_specs or [WHOLE]...  46 us
    ppermute x22, starting transfers between devices, involution(): return lax.ppermute(value, 'leaf', pairs)  29.5 us
    ppermute x22, waiting for transfers between devices, involution(): return lax.ppermute(value, 'leaf', pairs)  19.9 us
    add x1, other arithmetic, body(): residual = right_side - first_weight * image + second_weight * second  2.63 us
  transfers between devices with their start and end apart: 22, of which 9 were waited for; matrix products, arithmetic and copies ran while one was open for 0% of the time, Pallas kernels for 32%

profile of v8, /device:TPU:0, one launch (start us, length us, event | category | flops | bytes accessed | tf_op | source)
XLA Modules:
  0.0 99.4 jit_solution(15387284410116188959)
XLA Ops:
  0.7 3.1 %prep.1 = (bf16[16,64,512]{2,1,0:T(8,128)(2,1)S(1)}, bf16[608,128]{1,0:T(8,128)(2,1)S(1)}, f32[32,128]{1,0:T(8,128)S(1)}, bf16[16,64,64]{2,1,0:T(8,128)(2,1)S(1)...) custom-call(s32[1]{0:T(128)} %bitcast.pos_ref, f32[64,8192]{1,0:T(8,128)} %rs_ref.3, ...), custom_call_target="tpu_custom_call" | custom-call | tf_op jit(solution)/shard_map/prep/pallas_call | solution.py:523
  3.8 3.0 %collective-permute-start = (bf16[608,128]{1,0:T(8,128)(2,1)S(1)}, bf16[608,128]{1,0:T(8,128)(2,1)S(1)}, u32[]{:S(2)}, u32[]{:S(2)}) collective-permute-start(bf16[608,128]{1,0:T(8,128)(2,1)S(1)} %get-tuple-element.39.wait_ref.own_ref), channel_id=1, source_target_pairs={{0,2},{1,3},{2,0},{3,1},{4,6},{5,7},{6,4},{7,5},{8,10},{9,11},{10,... | collective-permute-start | bytes 466952 | tf_op jit(solution)/shard_map/ppermute | solution.py:33
  6.8 4.0 %relayout.1 = (bf16[16,128,256]{2,1,0:T(8,128)(2,1)S(1)}, bf16[1,64,64]{2,1,0:T(8,128)(2,1)S(1)}, s32[4,40]{1,0:T(4,128)S(1)}) custom-call(s32[1]{0:T(128)} %bitcast.pos_ref, s32[3,16]{1,0:T(4,128)S(1)} %bitcast.69, bf16[16,8,4096]{2,1,0:T(8,128)(2,1)S(1)} %copy-done.3, bf16[2,2,4096]{2,1,0:T(2,128)(2,1)S(1)} %copy-done.5, ...), custom_call_target="tpu_custom_call" | custom-call | tf_op jit(solution)/shard_map/relayout/pallas_call | solution.py:523
  12.2 6.2 %self_tiles.1 = (bf16[128,512,512]{2,1,0:T(8,128)(2,1)}, f32[17,64,512]{2,1,0:T(8,128)S(1)}) custom-call(f32[32,8192]{1,0:T(8,128)S(1)} %copy-done.1, bf16[16,64,512]{2,1,0:T(8,128)(2,1)S(1)} %get-tuple-element.46.v_ref, bf16[8,128,512]{2,1,0:T(8,128)(2,1)S(1)} %get-tuple-element.45.wait_ref), custom_call_target="tpu_custom_call" | custom-call | tf_op jit(solution)/shard_map/self_tiles/pallas_call | solution.py:523
  19.1 6.8 %collective-permute-start.6 = (f32[1,32,128]{2,1,0:T(8,128)S(1)}, f32[1,32,128]{2,1,0:T(8,128)S(1)}, u32[]{:S(2)}, u32[]{:S(2)}) collective-permute-start(f32[1,32,128]{2,1,0:T(8,128)S(1)} %get-tuple-element.56), channel_id=1, source_target_pairs={{0,8},{1,13},{2,10},{3,15},{4,12},{5,9},{6,14},{7,11},{8,0},{9,5},... | collective-permute-start | bytes 49160 | tf_op jit(solution)/shard_map/ppermute | solution.py:33
  26.0 12.8 %own_tiles.1 = (bf16[33,512,512]{2,1,0:T(8,128)(2,1)S(1)}, f32[17,64,512]{2,1,0:T(8,128)S(1)}) custom-call(s32[1]{0:T(128)} %bitcast.pos_ref, s32[4,40]{1,0:T(4,128)S(1)} %get-tuple-element.42.lists, f32[32,8192]{1,0:T(8,128)S(1)} %copy-done.1, bf16[16,64,512]{2,1,0:T(8,128)(2,1)S(1)} %get-tuple-element.46.v_ref, ...), custom_call_target="tpu_custom_call", output_to_operand_aliasing={{1}: (5, {})} | custom-call | tf_op jit(solution)/shard_map/own_tiles/pallas_call | solution.py:523
  39.4 0.8 foreign_tiles.1
  41.2 6.7 %far_first.1 = (f32[64,8192]{1,0:T(8,128)S(1)}, bf16[16,64,512]{2,1,0:T(8,128)(2,1)S(1)}, bf16[608,128]{1,0:T(8,128)(2,1)S(1)}, f32[32,128]{1,0:T(8,128)S(1)}, f...) custom-call(s32[1]{0:T(128)} %bitcast.pos_ref, s32[8,16]{1,0:T(8,128)S(1)} %bitcast.67, ...), custom_call_target="tpu_custom_call" | custom-call | tf_op jit(solution)/shard_map/far_first/pallas_call | solution.py:523
  47.9 4.7 %collective-permute-start.10 = (bf16[608,128]{1,0:T(8,128)(2,1)S(1)}, bf16[608,128]{1,0:T(8,128)(2,1)S(1)}, u32[]{:S(2)}, u32[]{:S(2)}) collective-permute-start(bf16[608,128]{1,0:T(8,128)(2,1)S(1)} %get-tuple-element.60.own_ref), channel_id=1, source_target_pairs={{0,2},{1,3},{2,0},{3,1},{4,6},{5,7},{6,4},{7,5},{8,10},{9,11},{10,... | collective-permute-start | bytes 466952 | tf_op jit(solution)/shard_map/ppermute | solution.py:33
  52.6 3.1 %own_again.1.refs_2_.near_in = f32[17,64,512]{2,1,0:T(8,128)S(1)} custom-call(s32[1]{0:T(128)} %bitcast.pos_ref, s32[4,40]{1,0:T(4,128)S(1)} %get-tuple-element.42.lists, bf16[16,64,512]{2,1,0:T(8,128)(2,1)S(1)} %get-tuple-element.62.v_ref, bf16[33,512,512]{2,1,0:T(8,128)(2,1)S(1)} %get-tuple-element.63.tile_ref), custom_call_target="tpu_custom_call" | custom-call | tf_op jit(solution)/shard_map/own_again/pallas_call | solution.py:523
  55.7 1.7 %collective-permute-done.10.refs_0_ = bf16[608,128]{1,0:T(8,128)(2,1)S(1)} collective-permute-done((bf16[608,128]{1,0:T(8,128)(2,1)S(1)}, bf16[608,128]{1,0:T(8,128)(2,1)S(1)}, u32[]{:S(2)}, u32[]{:S(2)}) %collective-permute-start.10) | collective-permute-done | bytes 155680 | tf_op jit(solution)/shard_map/ppermute | solution.py:33
  59.5 6.5 %collective-permute-start.13 = (f32[1,32,128]{2,1,0:T(8,128)S(1)}, f32[1,32,128]{2,1,0:T(8,128)S(1)}, u32[]{:S(2)}, u32[]{:S(2)}) collective-permute-start(f32[1,32,128]{2,1,0:T(8,128)S(1)} %get-tuple-element.67), channel_id=1, source_target_pairs={{0,8},{1,13},{2,10},{3,15},{4,12},{5,9},{6,14},{7,11},{8,0},{9,5},... | collective-permute-start | bytes 49160 | tf_op jit(solution)/shard_map/ppermute | solution.py:33
  66.0 4.6 %self_again.1.refs_2_.near_in = f32[17,64,512]{2,1,0:T(8,128)S(1)} custom-call(s32[1]{0:T(128)} %bitcast.pos_ref, s32[4,40]{1,0:T(4,128)S(1)} %get-tuple-element.42.lists, bf16[16,64,512]{2,1,0:T(8,128)(2,1)S(1)} %get-tuple-element.62.v_ref, bf16[8,64,512]{2,1,0:T(8,128)(2,1)S(1)} %collective-permute-done.14.vx_ref, ...), custom_call_target="tpu_custom_call", output_to_operand_aliasing={{}: (6, {})} | custom-call | tf_op jit(solution)/shard_map/self_again/pallas_call | solution.py:523
  70.6 6.7 %collective-permute-done.13.refs_1_ = f32[1,32,128]{2,1,0:T(8,128)S(1)} collective-permute-done((f32[1,32,128]{2,1,0:T(8,128)S(1)}, f32[1,32,128]{2,1,0:T(8,128)S(1)}, u32[]{:S(2)}, u32[]{:S(2)}) %collective-permute-start.13) | collective-permute-done | bytes 16416 | tf_op jit(solution)/shard_map/ppermute | solution.py:33
  78.4 0.8 collective-permute-done.16.sum_b
  79.3 4.2 %far_again.1 = (f32[64,8192]{1,0:T(8,128)S(1)}, f32[8,64]{1,0:T(8,128)S(1)}) custom-call(s32[1]{0:T(128)} %bitcast.pos_ref, s32[8,16]{1,0:T(8,128)S(1)} %bitcast.68, f32[64,8192]{1,0:T(8,128)S(1)} %copy-done, f32[1,8192]{1,0:T(1,128)S(1)} %bitcast.66, f32[64,8192]{1,0:T(8,128)S(1)} %get-tuple-element.59.u_ref, bf16[16,64,512]{2,1,0:T(8,128)(2,1)S(1)} %copy-done.2, ...), custom_call_target="tpu_custom_call" | custom-call | tf_op jit(solution)/shard_map/far_again/pallas_call | solution.py:523
  83.4 0.7 collective-permute-start.18
  84.2 0.8 collective-permute-done.18
  85.0 3.6 %collective-permute-done.19 = f32[8,64]{1,0:T(8,128)S(1)} collective-permute-done((f32[8,64]{1,0:T(8,128)S(1)}, f32[8,64]{1,0:T(8,128)S(1)}, u32[]{:S(2)}, u32[]{:S(2)}) %collective-permute-start.19) | collective-permute-done | bytes 2080 | tf_op jit(solution)/shard_map/ppermute | solution.py:33
  88.6 1.1 %collective-permute-start.20 = (f32[8,64]{1,0:T(8,128)S(1)}, f32[8,64]{1,0:T(8,128)S(1)}, u32[]{:S(2)}, u32[]{:S(2)}) collective-permute-start(f32[8,64]{1,0:T(8,128)S(1)} %add.72), channel_id=1, source_target_pairs={{0,4},{1,5},{2,6},{3,7},{4,0},{5,1},{6,2},{7,3},{8,12},{9,13},{10,... | collective-permute-start | bytes 6152 | tf_op jit(solution)/shard_map/ppermute | solution.py:33
  89.7 2.5 %collective-permute-done.20 = f32[8,64]{1,0:T(8,128)S(1)} collective-permute-done((f32[8,64]{1,0:T(8,128)S(1)}, f32[8,64]{1,0:T(8,128)S(1)}, u32[]{:S(2)}, u32[]{:S(2)}) %collective-permute-start.20) | collective-permute-done | bytes 2080 | tf_op jit(solution)/shard_map/ppermute | solution.py:33
  92.2 1.6 %collective-permute-start.21 = (f32[8,64]{1,0:T(8,128)S(1)}, f32[8,64]{1,0:T(8,128)S(1)}, u32[]{:S(2)}, u32[]{:S(2)}) collective-permute-start(f32[8,64]{1,0:T(8,128)S(1)} %add.73), channel_id=1, source_target_pairs={{0,8},{1,9},{2,10},{3,11},{4,12},{5,13},{6,14},{7,15},{8,0},{9,1},... | collective-permute-start | bytes 6152 | tf_op jit(solution)/shard_map/ppermute | solution.py:33
  93.8 2.9 %collective-permute-done.21 = f32[8,64]{1,0:T(8,128)S(1)} collective-permute-done((f32[8,64]{1,0:T(8,128)S(1)}, f32[8,64]{1,0:T(8,128)S(1)}, u32[]{:S(2)}, u32[]{:S(2)}) %collective-permute-start.21) | collective-permute-done | bytes 2080 | tf_op jit(solution)/shard_map/ppermute | solution.py:33
  96.8 2.6 %multiply_add_fusion = (f32[64,8192]{1,0:T(8,128)}, f32[64,8192]{1,0:T(8,128)}) fusion(f32[64,8192]{1,0:T(8,128)S(1)} %get-tuple-element.75, f32[64,8192]{1,0:T(8,128)S(1)} %copy-done, f32[64,8192]{1,0:T(8,128)S(1)} %get-tuple-element.59.u_ref, f32[64]{0:T(128)S(1)} %mul.193, f32[64]{0:T(128)S(1)} %get-tuple-element.76, f32[8192]{0:T(1024)S(1)} %copy-done.4), kind=kLoop, calls=%fused_computation | loop fusion | flops 4194304 | bytes 10519040 | tf_op jit(solution)/shard_map/add | solution.py:712
  (60 shorter events, 7.1 us)
Async XLA Ops:
  0.6 6.1 %copy-start.3 = (bf16[16,8,4096]{2,1,0:T(8,128)(2,1)S(1)}, bf16[16,8,4096]{2,1,0:T(8,128)(2,1)}, u32[]{:S(2)}) copy-start(bf16[16,8,4096]{2,1,0:T(8,128)(2,1)} %coup_ref.1) | copy-start | bytes 3145732
  0.6 6.1 %copy-start.5 = (bf16[2,2,4096]{2,1,0:T(2,128)(2,1)S(1)}, bf16[2,2,4096]{2,1,0:T(2,128)(2,1)}, u32[]{:S(2)}) copy-start(bf16[2,2,4096]{2,1,0:T(2,128)(2,1)} %coarse_ref.1) | copy-start | bytes 98308
  3.8 7.0 %collective-permute-start = (bf16[608,128]{1,0:T(8,128)(2,1)S(1)}, bf16[608,128]{1,0:T(8,128)(2,1)S(1)}, u32[]{:S(2)}, u32[]{:S(2)}) collective-permute-start(bf16[608,128]{1,0:T(8,128)(2,1)S(1)} %get-tuple-element.39.wait_ref.own_ref), channel_id=1, source_target_pairs={{0,2},{1,3},{2,0},{3,1},{4,6},{5,7},{6,4},{7,5},{8,10},{9,11},{10,... | collective-permute-start | bytes 466952 | tf_op jit(solution)/shard_map/ppermute | solution.py:33
  10.8 15.2 %collective-permute-start.2 = (bf16[8,128,512]{2,1,0:T(8,128)(2,1)S(1)}, bf16[8,128,512]{2,1,0:T(8,128)(2,1)S(1)}, u32[]{:S(2)}, u32[]{:S(2)}) collective-permute-start(bf16[8,128,512]{2,1,0:T(8,128)(2,1)S(1)} %get-tuple-element.47), channel_id=1, source_target_pairs={{0,1},{1,0},{2,3},{3,2},{4,5},{5,4},{6,7},{7,6},{8,9},{9,8},{10,11... | collective-permute-start | bytes 3145736 | tf_op jit(solution)/shard_map/ppermute | solution.py:33
  10.9 7.5 %collective-permute-start.3 = (bf16[608,128]{1,0:T(8,128)(2,1)S(1)}, bf16[608,128]{1,0:T(8,128)(2,1)S(1)}, u32[]{:S(2)}, u32[]{:S(2)}) collective-permute-start(bf16[608,128]{1,0:T(8,128)(2,1)S(1)} %get-tuple-element.39.wait_ref.own_ref), channel_id=1, source_target_pairs={{0,1},{1,0},{2,3},{3,2},{4,5},{5,4},{6,7},{7,6},{8,9},{9,8},{10,11... | collective-permute-start | bytes 466952 | tf_op jit(solution)/shard_map/ppermute | solution.py:33
  11.4 7.0 %collective-permute-start.4 = (bf16[608,128]{1,0:T(8,128)(2,1)S(1)}, bf16[608,128]{1,0:T(8,128)(2,1)S(1)}, u32[]{:S(2)}, u32[]{:S(2)}) collective-permute-start(bf16[608,128]{1,0:T(8,128)(2,1)S(1)} %get-tuple-element.49.across_ref), channel_id=1, source_target_pairs={{0,1},{1,0},{2,3},{3,2},{4,5},{5,4},{6,7},{7,6},{8,9},{9,8},{10,11... | collective-permute-start | bytes 466952 | tf_op jit(solution)/shard_map/ppermute | solution.py:33
  11.4 27.9 %collective-permute-start.1 = (bf16[8,128,512]{2,1,0:T(8,128)(2,1)S(1)}, bf16[8,128,512]{2,1,0:T(8,128)(2,1)S(1)}, u32[]{:S(2)}, u32[]{:S(2)}) collective-permute-start(bf16[8,128,512]{2,1,0:T(8,128)(2,1)S(1)} %get-tuple-element.45.wait_ref), channel_id=1, source_target_pairs={{1,2},{2,1},{3,4},{4,3},{5,6},{6,5},{7,8},{8,7},{9,10},{10,9},{11,... | collective-permute-start | bytes 3145736 | tf_op jit(solution)/shard_map/ppermute | solution.py:33
  18.4 20.3 %collective-permute-start.5 = (bf16[4,512,128]{2,1,0:T(8,128)(2,1)S(1)}, bf16[4,512,128]{2,1,0:T(8,128)(2,1)S(1)}, u32[]{:S(2)}, u32[]{:S(2)}) collective-permute-start(bf16[4,512,128]{2,1,0:T(8,128)(2,1)S(1)} %get-tuple-element.51.wait_ref.c0), channel_id=1, source_target_pairs={{1,4},{3,6},{4,1},{5,8},{6,3},{7,10},{8,5},{9,12},{10,7},{11,14},{... | collective-permute-start | bytes 1572872 | tf_op jit(solution)/shard_map/ppermute | solution.py:33
  19.1 19.6 %collective-permute-start.6 = (f32[1,32,128]{2,1,0:T(8,128)S(1)}, f32[1,32,128]{2,1,0:T(8,128)S(1)}, u32[]{:S(2)}, u32[]{:S(2)}) collective-permute-start(f32[1,32,128]{2,1,0:T(8,128)S(1)} %get-tuple-element.56), channel_id=1, source_target_pairs={{0,8},{1,13},{2,10},{3,15},{4,12},{5,9},{6,14},{7,11},{8,0},{9,5},... | collective-permute-start | bytes 49160 | tf_op jit(solution)/shard_map/ppermute | solution.py:33
  38.8 2.0 %collective-permute-start.8 = (bf16[4,512,128]{2,1,0:T(8,128)(2,1)S(1)}, bf16[4,512,128]{2,1,0:T(8,128)(2,1)S(1)}, u32[]{:S(2)}, u32[]{:S(2)}) collective-permute-start(bf16[4,512,128]{2,1,0:T(8,128)(2,1)S(1)} %get-tuple-element.58.c1), channel_id=1, source_target_pairs={{0,1},{1,0},{2,3},{3,2},{4,5},{5,4},{6,7},{7,6},{8,9},{9,8},{10,11... | collective-permute-start | bytes 1572872 | tf_op jit(solution)/shard_map/ppermute | solution.py:33
  38.9 1.9 %collective-permute-start.7 = (f32[1,32,128]{2,1,0:T(8,128)S(1)}, f32[1,32,128]{2,1,0:T(8,128)S(1)}, u32[]{:S(2)}, u32[]{:S(2)}) collective-permute-start(f32[1,32,128]{2,1,0:T(8,128)S(1)} %get-tuple-element.57.sum_a), channel_id=1, source_target_pairs={{0,1},{1,0},{2,3},{3,2},{4,5},{5,4},{6,7},{7,6},{8,9},{9,8},{10,11... | collective-permute-start | bytes 49160 | tf_op jit(solution)/shard_map/ppermute | solution.py:33
  47.9 9.4 %collective-permute-start.10 = (bf16[608,128]{1,0:T(8,128)(2,1)S(1)}, bf16[608,128]{1,0:T(8,128)(2,1)S(1)}, u32[]{:S(2)}, u32[]{:S(2)}) collective-permute-start(bf16[608,128]{1,0:T(8,128)(2,1)S(1)} %get-tuple-element.60.own_ref), channel_id=1, source_target_pairs={{0,2},{1,3},{2,0},{3,1},{4,6},{5,7},{6,4},{7,5},{8,10},{9,11},{10,... | collective-permute-start | bytes 466952 | tf_op jit(solution)/shard_map/ppermute | solution.py:33
  52.6 6.0 %collective-permute-start.9 = (bf16[608,128]{1,0:T(8,128)(2,1)S(1)}, bf16[608,128]{1,0:T(8,128)(2,1)S(1)}, u32[]{:S(2)}, u32[]{:S(2)}) collective-permute-start(bf16[608,128]{1,0:T(8,128)(2,1)S(1)} %get-tuple-element.60.own_ref), channel_id=1, source_target_pairs={{0,1},{1,0},{2,3},{3,2},{4,5},{5,4},{6,7},{7,6},{8,9},{9,8},{10,11... | collective-permute-start | bytes 466952 | tf_op jit(solution)/shard_map/ppermute | solution.py:33
  57.4 1.4 %collective-permute-start.11 = (bf16[608,128]{1,0:T(8,128)(2,1)S(1)}, bf16[608,128]{1,0:T(8,128)(2,1)S(1)}, u32[]{:S(2)}, u32[]{:S(2)}) collective-permute-start(bf16[608,128]{1,0:T(8,128)(2,1)S(1)} %get-tuple-element.64.across_ref), channel_id=1, source_target_pairs={{0,1},{1,0},{2,3},{3,2},{4,5},{5,4},{6,7},{7,6},{8,9},{9,8},{10,11... | collective-permute-start | bytes 466952 | tf_op jit(solution)/shard_map/ppermute | solution.py:33
  57.5 8.5 %collective-permute-start.14 = (bf16[8,64,512]{2,1,0:T(8,128)(2,1)S(1)}, bf16[8,64,512]{2,1,0:T(8,128)(2,1)S(1)}, u32[]{:S(2)}, u32[]{:S(2)}) collective-permute-start(bf16[8,64,512]{2,1,0:T(8,128)(2,1)S(1)} %get-tuple-element.68), channel_id=1, source_target_pairs={{0,1},{1,0},{2,3},{3,2},{4,5},{5,4},{6,7},{7,6},{8,9},{9,8},{10,11... | collective-permute-start | bytes 1572872 | tf_op jit(solution)/shard_map/ppermute | solution.py:33
  57.9 19.4 %collective-permute-start.15 = (bf16[8,64,512]{2,1,0:T(8,128)(2,1)S(1)}, bf16[8,64,512]{2,1,0:T(8,128)(2,1)S(1)}, u32[]{:S(2)}, u32[]{:S(2)}) collective-permute-start(bf16[8,64,512]{2,1,0:T(8,128)(2,1)S(1)} %get-tuple-element.70), channel_id=1, source_target_pairs={{1,2},{2,1},{3,4},{4,3},{5,6},{6,5},{7,8},{8,7},{9,10},{10,9},{11,... | collective-permute-start | bytes 1572872 | tf_op jit(solution)/shard_map/ppermute | solution.py:33
  58.8 18.5 %collective-permute-start.12 = (bf16[4,512,128]{2,1,0:T(8,128)(2,1)S(1)}, bf16[4,512,128]{2,1,0:T(8,128)(2,1)S(1)}, u32[]{:S(2)}, u32[]{:S(2)}) collective-permute-start(bf16[4,512,128]{2,1,0:T(8,128)(2,1)S(1)} %get-tuple-element.66.wait_ref.c0), channel_id=1, source_target_pairs={{1,4},{3,6},{4,1},{5,8},{6,3},{7,10},{8,5},{9,12},{10,7},{11,14},{... | collective-permute-start | bytes 1572872 | tf_op jit(solution)/shard_map/ppermute | solution.py:33
  59.5 17.8 %collective-permute-start.13 = (f32[1,32,128]{2,1,0:T(8,128)S(1)}, f32[1,32,128]{2,1,0:T(8,128)S(1)}, u32[]{:S(2)}, u32[]{:S(2)}) collective-permute-start(f32[1,32,128]{2,1,0:T(8,128)S(1)} %get-tuple-element.67), channel_id=1, source_target_pairs={{0,8},{1,13},{2,10},{3,15},{4,12},{5,9},{6,14},{7,11},{8,0},{9,5},... | collective-permute-start | bytes 49160 | tf_op jit(solution)/shard_map/ppermute | solution.py:33
  77.3 2.0 %collective-permute-start.17 = (bf16[4,512,128]{2,1,0:T(8,128)(2,1)S(1)}, bf16[4,512,128]{2,1,0:T(8,128)(2,1)S(1)}, u32[]{:S(2)}, u32[]{:S(2)}) collective-permute-start(bf16[4,512,128]{2,1,0:T(8,128)(2,1)S(1)} %get-tuple-element.72.c1), channel_id=1, source_target_pairs={{0,1},{1,0},{2,3},{3,2},{4,5},{5,4},{6,7},{7,6},{8,9},{9,8},{10,11... | collective-permute-start | bytes 1572872 | tf_op jit(solution)/shard_map/ppermute | solution.py:33
  77.4 1.9 %collective-permute-start.16 = (f32[1,32,128]{2,1,0:T(8,128)S(1)}, f32[1,32,128]{2,1,0:T(8,128)S(1)}, u32[]{:S(2)}, u32[]{:S(2)}) collective-permute-start(f32[1,32,128]{2,1,0:T(8,128)S(1)} %get-tuple-element.71.sum_a), channel_id=1, source_target_pairs={{0,1},{1,0},{2,3},{3,2},{4,5},{5,4},{6,7},{7,6},{8,9},{9,8},{10,11... | collective-permute-start | bytes 49160 | tf_op jit(solution)/shard_map/ppermute | solution.py:33
  83.4 1.6 %collective-permute-start.18 = (f32[8,64]{1,0:T(8,128)S(1)}, f32[8,64]{1,0:T(8,128)S(1)}, u32[]{:S(2)}, u32[]{:S(2)}) collective-permute-start(f32[8,64]{1,0:T(8,128)S(1)} %get-tuple-element.74), channel_id=1, source_target_pairs={{0,1},{1,0},{2,3},{3,2},{4,5},{5,4},{6,7},{7,6},{8,9},{9,8},{10,11... | collective-permute-start | bytes 6152 | tf_op jit(solution)/shard_map/ppermute | solution.py:33
  85.0 3.6 %collective-permute-start.19 = (f32[8,64]{1,0:T(8,128)S(1)}, f32[8,64]{1,0:T(8,128)S(1)}, u32[]{:S(2)}, u32[]{:S(2)}) collective-permute-start(f32[8,64]{1,0:T(8,128)S(1)} %add.71), channel_id=1, source_target_pairs={{0,2},{1,3},{2,0},{3,1},{4,6},{5,7},{6,4},{7,5},{8,10},{9,11},{10,... | collective-permute-start | bytes 6152 | tf_op jit(solution)/shard_map/ppermute | solution.py:33
  88.6 3.6 %collective-permute-start.20 = (f32[8,64]{1,0:T(8,128)S(1)}, f32[8,64]{1,0:T(8,128)S(1)}, u32[]{:S(2)}, u32[]{:S(2)}) collective-permute-start(f32[8,64]{1,0:T(8,128)S(1)} %add.72), channel_id=1, source_target_pairs={{0,4},{1,5},{2,6},{3,7},{4,0},{5,1},{6,2},{7,3},{8,12},{9,13},{10,... | collective-permute-start | bytes 6152 | tf_op jit(solution)/shard_map/ppermute | solution.py:33
  92.2 4.5 %collective-permute-start.21 = (f32[8,64]{1,0:T(8,128)S(1)}, f32[8,64]{1,0:T(8,128)S(1)}, u32[]{:S(2)}, u32[]{:S(2)}) collective-permute-start(f32[8,64]{1,0:T(8,128)S(1)} %add.73), channel_id=1, source_target_pairs={{0,8},{1,9},{2,10},{3,11},{4,12},{5,13},{6,14},{7,15},{8,0},{9,1},... | collective-permute-start | bytes 6152 | tf_op jit(solution)/shard_map/ppermute | solution.py:33
  (6 other events, 18.7 us)

commit v9 on v8

--- a/solution.py
+++ b/solution.py
@@ -135,6 +135,21 @@
         return carry
 
     lax.fori_loop(0, count // unroll, trip, 0)
+
+
+def list_loop(count, fn):
+    def four(i, carry):
+        for u in range(UNROLL):
+            fn(i * UNROLL + u)
+        return carry
+
+    def single(i, carry):
+        fn(i)
+        return carry
+
+    whole_trips = count // UNROLL
+    lax.fori_loop(0, whole_trips, four, 0)
+    lax.fori_loop(whole_trips * UNROLL, count, single, 0)
 
 
 def store_share(total, part_ref, cp_ref):
@@ -324,20 +339,18 @@
     vw[per:] = vx_ref[:, :columns]
     n = lists[3, lists.shape[1] - 1]
 
-    def trip(i, carry):
-        for u in range(UNROLL):
-            entry, leaf_at, row, m = near_entry(lists, 3, i * UNROLL + u, half)
-            own = (m >= half) & (m < 3 * half)
-            place = jnp.clip(m - half, 0, per - 1)
-            points = jnp.where(
-                own, columns_of(e_ref, place, leaf), points_of(vx_ref, m % half, columns, e_ref.shape[0])
-            )
-            tile = tile_of(other_rows(points), own_rows(columns_of(e_ref, row, leaf)))
-            tile_ref[entry] = tile
-            near_out[leaf_at] += dot(vw[jnp.where(own, place, per + m % half)], tile, 1, 0)
-        return carry
-
-    lax.fori_loop(0, (n + UNROLL - 1) // UNROLL, trip, 0)
+    def one(at_entry):
+        entry, leaf_at, row, m = near_entry(lists, 3, at_entry, half)
+        own = (m >= half) & (m < 3 * half)
+        place = jnp.clip(m - half, 0, per - 1)
+        points = jnp.where(
+            own, columns_of(e_ref, place, leaf), points_of(vx_ref, m % half, columns, e_ref.shape[0])
+        )
+        tile = tile_of(other_rows(points), own_rows(columns_of(e_ref, row, leaf)))
+        tile_ref[entry] = tile
+        near_out[leaf_at] += dot(vw[jnp.where(own, place, per + m % half)], tile, 1, 0)
+
+    list_loop(n, one)
 
 
 def own_again_kernel(pos_ref, lists, v_ref, tile_ref, near_out):
@@ -345,14 +358,12 @@
     near_out[...] = jnp.zeros_like(near_out)
     n = lists[0, lists.shape[1] - 1]
 
-    def trip(i, carry):
-        for u in range(UNROLL):
-            entry, leaf_at, _, m = near_entry(lists, 0, i * UNROLL + u, half)
-            place = jnp.clip(m - half, 0, 2 * half - 1)
-            near_out[leaf_at] += dot(v_ref[place], tile_ref[entry], 1, 0)
-        return carry
-
-    lax.fori_loop(0, (n + UNROLL - 1) // UNROLL, trip, 0)
+    def one(at_entry):
+        entry, leaf_at, _, m = near_entry(lists, 0, at_entry, half)
+        place = jnp.clip(m - half, 0, 2 * half - 1)
+        near_out[leaf_at] += dot(v_ref[place], tile_ref[entry], 1, 0)
+
+    list_loop(n, one)
 
 
 def self_again_kernel(
@@ -368,13 +379,11 @@
         copy.start()
     n = lists[1, lists.shape[1] - 1]
 
-    def trip(i, carry):
-        for u in range(UNROLL):
-            entry, leaf_at, _, m = near_entry(lists, 1, i * UNROLL + u, half)
-            near_out[leaf_at] += dot(vx_ref[m % half], tile_ref[entry], 1, 0)
-        return carry
-
-    lax.fori_loop(0, (n + UNROLL - 1) // UNROLL, trip, 0)
+    def one(at_entry):
+        entry, leaf_at, _, m = near_entry(lists, 1, at_entry, half)
+        near_out[leaf_at] += dot(vx_ref[m % half], tile_ref[entry], 1, 0)
+
+    list_loop(n, one)
     for i, copy in enumerate(copies):
         copy.wait()
         for u in range(UNROLL):
@@ -431,16 +440,14 @@
     columns = vo_ref.shape[1] - 2 * features
     n = lists[2, lists.shape[1] - 1]
 
-    def trip(i, carry):
-        for u in range(UNROLL):
-            entry, leaf_at, row, m = near_entry(lists, 2, i * UNROLL + u, half)
-            points = points_of(vo_ref, m % half, columns, features)
-            tile = tile_of(other_rows(points), own_rows(columns_of(e_ref, row, leaf)))
-            tile_ref[entry] = tile
-            near_out[leaf_at] += dot(vo_ref[m % half, :columns], tile, 1, 0)
-        return carry
-
-    lax.fori_loop(0, (n + UNROLL - 1) // UNROLL, trip, 0)
+    def one(at_entry):
+        entry, leaf_at, row, m = near_entry(lists, 2, at_entry, half)
+        points = points_of(vo_ref, m % half, columns, features)
+        tile = tile_of(other_rows(points), own_rows(columns_of(e_ref, row, leaf)))
+        tile_ref[entry] = tile
+        near_out[leaf_at] += dot(vo_ref[m % half, :columns], tile, 1, 0)
+
+    list_loop(n, one)
 
 
 def far_first_kernel(
@@ -484,13 +491,11 @@
     half = vo_ref.shape[0]
     n = lists[2, lists.shape[1] - 1]
 
-    def trip(i, carry):
-        for u in range(UNROLL):
-            entry, leaf_at, _, m = near_entry(lists, 2, i * UNROLL + u, half)
-            near_out[leaf_at] += dot(vo_ref[m % half], tile_ref[entry], 1, 0)
-        return carry
-
-    lax.fori_loop(0, (n + UNROLL - 1) // UNROLL, trip, 0)
+    def one(at_entry):
+        entry, leaf_at, _, m = near_entry(lists, 2, at_entry, half)
+        near_out[leaf_at] += dot(vo_ref[m % half], tile_ref[entry], 1, 0)
+
+    list_loop(n, one)
 
 
 def far_again_kernel(

time: 98 us -> 97.5 us (level); the launches traced: 99.4 us -> 97.2 us
  starting transfers between devices: 29.5 us -> 25.9 us
  waiting for transfers between devices: 19.9 us -> 21.2 us
    ppermute x22, starting transfers between devices: 29.5 us -> 25.9 us  [involution(): return lax.ppermute(value, 'leaf', pairs)]
    ppermute x22, waiting for transfers between devices: 19.9 us -> 21.2 us  [involution(): return lax.ppermute(value, 'leaf', pairs)]
  transfers between devices with their start and end apart: 22 -> 22, of which waited for: 9 -> 9; matrix products, arithmetic and copies ran while one was open for 0% -> 0% of each run, Pallas kernels for 32% -> 33%
where the time goes in v9:
time: 97.5 us; the launch traced here: 97.2 us
  Pallas kernels  46 us (47%)
  starting transfers between devices  25.9 us (27%)
  waiting for transfers between devices  21.2 us (22%)
  other arithmetic  2.68 us (3%)
    pallas_call x16, Pallas kernels, call(): pl.pallas_call(kernel, in_specs=in_specs, out_specs=out_specs or [WHOLE]...  46 us
    ppermute x22, starting transfers between devices, involution(): return lax.ppermute(value, 'leaf', pairs)  25.9 us
    ppermute x22, waiting for transfers between devices, involution(): return lax.ppermute(value, 'leaf', pairs)  21.2 us
    add x1, other arithmetic, body(): residual = right_side - first_weight * image + second_weight * second  2.63 us
  transfers between devices with their start and end apart: 22, of which 9 were waited for; matrix products, arithmetic and copies ran while one was open for 0% of the time, Pallas kernels for 33%

profile of v9, /device:TPU:0, one launch (start us, length us, event | category | flops | bytes accessed | tf_op | source)
XLA Modules:
  0.0 97.2 jit_solution(17011824124941394700)
XLA Ops:
  0.7 3.1 %prep.1 = (bf16[16,64,512]{2,1,0:T(8,128)(2,1)S(1)}, bf16[608,128]{1,0:T(8,128)(2,1)S(1)}, f32[32,128]{1,0:T(8,128)S(1)}, bf16[16,64,64]{2,1,0:T(8,128)(2,1)S(1)...) custom-call(s32[1]{0:T(128)} %bitcast.pos_ref, f32[64,8192]{1,0:T(8,128)} %rs_ref.3, ...), custom_call_target="tpu_custom_call" | custom-call | tf_op jit(solution)/shard_map/prep/pallas_call | solution.py:528
  3.8 3.0 %collective-permute-start = (bf16[608,128]{1,0:T(8,128)(2,1)S(1)}, bf16[608,128]{1,0:T(8,128)(2,1)S(1)}, u32[]{:S(2)}, u32[]{:S(2)}) collective-permute-start(bf16[608,128]{1,0:T(8,128)(2,1)S(1)} %get-tuple-element.39.wait_ref.own_ref), channel_id=1, source_target_pairs={{0,2},{1,3},{2,0},{3,1},{4,6},{5,7},{6,4},{7,5},{8,10},{9,11},{10,... | collective-permute-start | bytes 466952 | tf_op jit(solution)/shard_map/ppermute | solution.py:33
  6.8 4.0 %relayout.1 = (bf16[16,128,256]{2,1,0:T(8,128)(2,1)S(1)}, bf16[1,64,64]{2,1,0:T(8,128)(2,1)S(1)}, s32[4,40]{1,0:T(4,128)S(1)}) custom-call(s32[1]{0:T(128)} %bitcast.pos_ref, s32[3,16]{1,0:T(4,128)S(1)} %bitcast.69, bf16[16,8,4096]{2,1,0:T(8,128)(2,1)S(1)} %copy-done.3, bf16[2,2,4096]{2,1,0:T(2,128)(2,1)S(1)} %copy-done.5, ...), custom_call_target="tpu_custom_call" | custom-call | tf_op jit(solution)/shard_map/relayout/pallas_call | solution.py:528
  11.4 0.7 collective-permute-start.1
  12.2 6.2 %self_tiles.1 = (bf16[128,512,512]{2,1,0:T(8,128)(2,1)}, f32[17,64,512]{2,1,0:T(8,128)S(1)}) custom-call(f32[32,8192]{1,0:T(8,128)S(1)} %copy-done.1, bf16[16,64,512]{2,1,0:T(8,128)(2,1)S(1)} %get-tuple-element.46.v_ref, bf16[8,128,512]{2,1,0:T(8,128)(2,1)S(1)} %get-tuple-element.45.wait_ref), custom_call_target="tpu_custom_call" | custom-call | tf_op jit(solution)/shard_map/self_tiles/pallas_call | solution.py:528
  18.4 0.7 collective-permute-start.5
  19.1 6.8 %collective-permute-start.6 = (f32[1,32,128]{2,1,0:T(8,128)S(1)}, f32[1,32,128]{2,1,0:T(8,128)S(1)}, u32[]{:S(2)}, u32[]{:S(2)}) collective-permute-start(f32[1,32,128]{2,1,0:T(8,128)S(1)} %get-tuple-element.56), channel_id=1, source_target_pairs={{0,8},{1,13},{2,10},{3,15},{4,12},{5,9},{6,14},{7,11},{8,0},{9,5},... | collective-permute-start | bytes 49160 | tf_op jit(solution)/shard_map/ppermute | solution.py:33
  26.0 12.8 %own_tiles.1 = (bf16[33,512,512]{2,1,0:T(8,128)(2,1)S(1)}, f32[17,64,512]{2,1,0:T(8,128)S(1)}) custom-call(s32[1]{0:T(128)} %bitcast.pos_ref, s32[4,40]{1,0:T(4,128)S(1)} %get-tuple-element.42.lists, f32[32,8192]{1,0:T(8,128)S(1)} %copy-done.1, bf16[16,64,512]{2,1,0:T(8,128)(2,1)S(1)} %get-tuple-element.46.v_ref, ...), custom_call_target="tpu_custom_call", output_to_operand_aliasing={{1}: (5, {})} | custom-call | tf_op jit(solution)/shard_map/own_tiles/pallas_call | solution.py:528
  39.4 0.8 foreign_tiles.1
  41.2 6.7 %far_first.1 = (f32[64,8192]{1,0:T(8,128)S(1)}, bf16[16,64,512]{2,1,0:T(8,128)(2,1)S(1)}, bf16[608,128]{1,0:T(8,128)(2,1)S(1)}, f32[32,128]{1,0:T(8,128)S(1)}, f...) custom-call(s32[1]{0:T(128)} %bitcast.pos_ref, s32[8,16]{1,0:T(8,128)S(1)} %bitcast.67, ...), custom_call_target="tpu_custom_call" | custom-call | tf_op jit(solution)/shard_map/far_first/pallas_call | solution.py:528
  47.9 3.2 %collective-permute-start.10 = (bf16[608,128]{1,0:T(8,128)(2,1)S(1)}, bf16[608,128]{1,0:T(8,128)(2,1)S(1)}, u32[]{:S(2)}, u32[]{:S(2)}) collective-permute-start(bf16[608,128]{1,0:T(8,128)(2,1)S(1)} %get-tuple-element.60.own_ref), channel_id=1, source_target_pairs={{0,2},{1,3},{2,0},{3,1},{4,6},{5,7},{6,4},{7,5},{8,10},{9,11},{10,... | collective-permute-start | bytes 466952 | tf_op jit(solution)/shard_map/ppermute | solution.py:33
  51.1 3.1 %own_again.1.refs_2_.near_in = f32[17,64,512]{2,1,0:T(8,128)S(1)} custom-call(s32[1]{0:T(128)} %bitcast.pos_ref, s32[4,40]{1,0:T(4,128)S(1)} %get-tuple-element.42.lists, bf16[16,64,512]{2,1,0:T(8,128)(2,1)S(1)} %get-tuple-element.62.v_ref, bf16[33,512,512]{2,1,0:T(8,128)(2,1)S(1)} %get-tuple-element.63.tile_ref), custom_call_target="tpu_custom_call" | custom-call | tf_op jit(solution)/shard_map/own_again/pallas_call | solution.py:528
  54.2 1.6 %collective-permute-done.10.refs_0_ = bf16[608,128]{1,0:T(8,128)(2,1)S(1)} collective-permute-done((bf16[608,128]{1,0:T(8,128)(2,1)S(1)}, bf16[608,128]{1,0:T(8,128)(2,1)S(1)}, u32[]{:S(2)}, u32[]{:S(2)}) %collective-permute-start.10) | collective-permute-done | bytes 155680 | tf_op jit(solution)/shard_map/ppermute | solution.py:33
  58.0 6.5 %collective-permute-start.13 = (f32[1,32,128]{2,1,0:T(8,128)S(1)}, f32[1,32,128]{2,1,0:T(8,128)S(1)}, u32[]{:S(2)}, u32[]{:S(2)}) collective-permute-start(f32[1,32,128]{2,1,0:T(8,128)S(1)} %get-tuple-element.67), channel_id=1, source_target_pairs={{0,8},{1,13},{2,10},{3,15},{4,12},{5,9},{6,14},{7,11},{8,0},{9,5},... | collective-permute-start | bytes 49160 | tf_op jit(solution)/shard_map/ppermute | solution.py:33
  64.6 4.5 %self_again.1.refs_2_.near_in = f32[17,64,512]{2,1,0:T(8,128)S(1)} custom-call(s32[1]{0:T(128)} %bitcast.pos_ref, s32[4,40]{1,0:T(4,128)S(1)} %get-tuple-element.42.lists, bf16[16,64,512]{2,1,0:T(8,128)(2,1)S(1)} %get-tuple-element.62.v_ref, bf16[8,64,512]{2,1,0:T(8,128)(2,1)S(1)} %collective-permute-done.14.vx_ref, ...), custom_call_target="tpu_custom_call", output_to_operand_aliasing={{}: (6, {})} | custom-call | tf_op jit(solution)/shard_map/self_again/pallas_call | solution.py:528
  69.1 6.2 %collective-permute-done.13.refs_1_ = f32[1,32,128]{2,1,0:T(8,128)S(1)} collective-permute-done((f32[1,32,128]{2,1,0:T(8,128)S(1)}, f32[1,32,128]{2,1,0:T(8,128)S(1)}, u32[]{:S(2)}, u32[]{:S(2)}) %collective-permute-start.13) | collective-permute-done | bytes 16416 | tf_op jit(solution)/shard_map/ppermute | solution.py:33
  76.5 0.8 collective-permute-done.16.sum_b
  77.3 4.2 %far_again.1 = (f32[64,8192]{1,0:T(8,128)S(1)}, f32[8,64]{1,0:T(8,128)S(1)}) custom-call(s32[1]{0:T(128)} %bitcast.pos_ref, s32[8,16]{1,0:T(8,128)S(1)} %bitcast.68, f32[64,8192]{1,0:T(8,128)S(1)} %copy-done, f32[1,8192]{1,0:T(1,128)S(1)} %bitcast.66, f32[64,8192]{1,0:T(8,128)S(1)} %get-tuple-element.59.u_ref, bf16[16,64,512]{2,1,0:T(8,128)(2,1)S(1)} %copy-done.2, ...), custom_call_target="tpu_custom_call" | custom-call | tf_op jit(solution)/shard_map/far_again/pallas_call | solution.py:528
  81.9 0.8 collective-permute-done.18
  82.7 3.6 %collective-permute-done.19 = f32[8,64]{1,0:T(8,128)S(1)} collective-permute-done((f32[8,64]{1,0:T(8,128)S(1)}, f32[8,64]{1,0:T(8,128)S(1)}, u32[]{:S(2)}, u32[]{:S(2)}) %collective-permute-start.19) | collective-permute-done | bytes 2080 | tf_op jit(solution)/shard_map/ppermute | solution.py:33
  86.4 0.9 collective-permute-start.20
  87.2 2.7 %collective-permute-done.20 = f32[8,64]{1,0:T(8,128)S(1)} collective-permute-done((f32[8,64]{1,0:T(8,128)S(1)}, f32[8,64]{1,0:T(8,128)S(1)}, u32[]{:S(2)}, u32[]{:S(2)}) %collective-permute-start.20) | collective-permute-done | bytes 2080 | tf_op jit(solution)/shard_map/ppermute | solution.py:33
  90.0 4.5 %collective-permute-done.21 = f32[8,64]{1,0:T(8,128)S(1)} collective-permute-done((f32[8,64]{1,0:T(8,128)S(1)}, f32[8,64]{1,0:T(8,128)S(1)}, u32[]{:S(2)}, u32[]{:S(2)}) %collective-permute-start.21) | collective-permute-done | bytes 2080 | tf_op jit(solution)/shard_map/ppermute | solution.py:33
  94.5 2.6 %multiply_add_fusion = (f32[64,8192]{1,0:T(8,128)}, f32[64,8192]{1,0:T(8,128)}) fusion(f32[64,8192]{1,0:T(8,128)S(1)} %get-tuple-element.75, f32[64,8192]{1,0:T(8,128)S(1)} %copy-done, f32[64,8192]{1,0:T(8,128)S(1)} %get-tuple-element.59.u_ref, f32[64]{0:T(128)S(1)} %mul.193, f32[64]{0:T(128)S(1)} %get-tuple-element.76, f32[8192]{0:T(1024)S(1)} %copy-done.4), kind=kLoop, calls=%fused_computation | loop fusion | flops 4194304 | bytes 10519040 | tf_op jit(solution)/shard_map/add | solution.py:717
  (60 shorter events, 6.1 us)
Async XLA Ops:
  0.6 6.1 %copy-start.3 = (bf16[16,8,4096]{2,1,0:T(8,128)(2,1)S(1)}, bf16[16,8,4096]{2,1,0:T(8,128)(2,1)}, u32[]{:S(2)}) copy-start(bf16[16,8,4096]{2,1,0:T(8,128)(2,1)} %coup_ref.1) | copy-start | bytes 3145732
  0.6 6.1 %copy-start.5 = (bf16[2,2,4096]{2,1,0:T(2,128)(2,1)S(1)}, bf16[2,2,4096]{2,1,0:T(2,128)(2,1)}, u32[]{:S(2)}) copy-start(bf16[2,2,4096]{2,1,0:T(2,128)(2,1)} %coarse_ref.1) | copy-start | bytes 98308
  3.8 7.0 %collective-permute-start = (bf16[608,128]{1,0:T(8,128)(2,1)S(1)}, bf16[608,128]{1,0:T(8,128)(2,1)S(1)}, u32[]{:S(2)}, u32[]{:S(2)}) collective-permute-start(bf16[608,128]{1,0:T(8,128)(2,1)S(1)} %get-tuple-element.39.wait_ref.own_ref), channel_id=1, source_target_pairs={{0,2},{1,3},{2,0},{3,1},{4,6},{5,7},{6,4},{7,5},{8,10},{9,11},{10,... | collective-permute-start | bytes 466952 | tf_op jit(solution)/shard_map/ppermute | solution.py:33
  10.8 15.2 %collective-permute-start.2 = (bf16[8,128,512]{2,1,0:T(8,128)(2,1)S(1)}, bf16[8,128,512]{2,1,0:T(8,128)(2,1)S(1)}, u32[]{:S(2)}, u32[]{:S(2)}) collective-permute-start(bf16[8,128,512]{2,1,0:T(8,128)(2,1)S(1)} %get-tuple-element.47), channel_id=1, source_target_pairs={{0,1},{1,0},{2,3},{3,2},{4,5},{5,4},{6,7},{7,6},{8,9},{9,8},{10,11... | collective-permute-start | bytes 3145736 | tf_op jit(solution)/shard_map/ppermute | solution.py:33
  10.9 7.5 %collective-permute-start.3 = (bf16[608,128]{1,0:T(8,128)(2,1)S(1)}, bf16[608,128]{1,0:T(8,128)(2,1)S(1)}, u32[]{:S(2)}, u32[]{:S(2)}) collective-permute-start(bf16[608,128]{1,0:T(8,128)(2,1)S(1)} %get-tuple-element.39.wait_ref.own_ref), channel_id=1, source_target_pairs={{0,1},{1,0},{2,3},{3,2},{4,5},{5,4},{6,7},{7,6},{8,9},{9,8},{10,11... | collective-permute-start | bytes 466952 | tf_op jit(solution)/shard_map/ppermute | solution.py:33
  11.4 7.0 %collective-permute-start.4 = (bf16[608,128]{1,0:T(8,128)(2,1)S(1)}, bf16[608,128]{1,0:T(8,128)(2,1)S(1)}, u32[]{:S(2)}, u32[]{:S(2)}) collective-permute-start(bf16[608,128]{1,0:T(8,128)(2,1)S(1)} %get-tuple-element.49.across_ref), channel_id=1, source_target_pairs={{0,1},{1,0},{2,3},{3,2},{4,5},{5,4},{6,7},{7,6},{8,9},{9,8},{10,11... | collective-permute-start | bytes 466952 | tf_op jit(solution)/shard_map/ppermute | solution.py:33
  11.4 27.9 %collective-permute-start.1 = (bf16[8,128,512]{2,1,0:T(8,128)(2,1)S(1)}, bf16[8,128,512]{2,1,0:T(8,128)(2,1)S(1)}, u32[]{:S(2)}, u32[]{:S(2)}) collective-permute-start(bf16[8,128,512]{2,1,0:T(8,128)(2,1)S(1)} %get-tuple-element.45.wait_ref), channel_id=1, source_target_pairs={{1,2},{2,1},{3,4},{4,3},{5,6},{6,5},{7,8},{8,7},{9,10},{10,9},{11,... | collective-permute-start | bytes 3145736 | tf_op jit(solution)/shard_map/ppermute | solution.py:33
  18.4 20.3 %collective-permute-start.5 = (bf16[4,512,128]{2,1,0:T(8,128)(2,1)S(1)}, bf16[4,512,128]{2,1,0:T(8,128)(2,1)S(1)}, u32[]{:S(2)}, u32[]{:S(2)}) collective-permute-start(bf16[4,512,128]{2,1,0:T(8,128)(2,1)S(1)} %get-tuple-element.51.wait_ref.c0), channel_id=1, source_target_pairs={{1,4},{3,6},{4,1},{5,8},{6,3},{7,10},{8,5},{9,12},{10,7},{11,14},{... | collective-permute-start | bytes 1572872 | tf_op jit(solution)/shard_map/ppermute | solution.py:33
  19.1 19.6 %collective-permute-start.6 = (f32[1,32,128]{2,1,0:T(8,128)S(1)}, f32[1,32,128]{2,1,0:T(8,128)S(1)}, u32[]{:S(2)}, u32[]{:S(2)}) collective-permute-start(f32[1,32,128]{2,1,0:T(8,128)S(1)} %get-tuple-element.56), channel_id=1, source_target_pairs={{0,8},{1,13},{2,10},{3,15},{4,12},{5,9},{6,14},{7,11},{8,0},{9,5},... | collective-permute-start | bytes 49160 | tf_op jit(solution)/shard_map/ppermute | solution.py:33
  38.8 2.0 %collective-permute-start.8 = (bf16[4,512,128]{2,1,0:T(8,128)(2,1)S(1)}, bf16[4,512,128]{2,1,0:T(8,128)(2,1)S(1)}, u32[]{:S(2)}, u32[]{:S(2)}) collective-permute-start(bf16[4,512,128]{2,1,0:T(8,128)(2,1)S(1)} %get-tuple-element.58.c1), channel_id=1, source_target_pairs={{0,1},{1,0},{2,3},{3,2},{4,5},{5,4},{6,7},{7,6},{8,9},{9,8},{10,11... | collective-permute-start | bytes 1572872 | tf_op jit(solution)/shard_map/ppermute | solution.py:33
  38.9 1.9 %collective-permute-start.7 = (f32[1,32,128]{2,1,0:T(8,128)S(1)}, f32[1,32,128]{2,1,0:T(8,128)S(1)}, u32[]{:S(2)}, u32[]{:S(2)}) collective-permute-start(f32[1,32,128]{2,1,0:T(8,128)S(1)} %get-tuple-element.57.sum_a), channel_id=1, source_target_pairs={{0,1},{1,0},{2,3},{3,2},{4,5},{5,4},{6,7},{7,6},{8,9},{9,8},{10,11... | collective-permute-start | bytes 49160 | tf_op jit(solution)/shard_map/ppermute | solution.py:33
  47.9 7.9 %collective-permute-start.10 = (bf16[608,128]{1,0:T(8,128)(2,1)S(1)}, bf16[608,128]{1,0:T(8,128)(2,1)S(1)}, u32[]{:S(2)}, u32[]{:S(2)}) collective-permute-start(bf16[608,128]{1,0:T(8,128)(2,1)S(1)} %get-tuple-element.60.own_ref), channel_id=1, source_target_pairs={{0,2},{1,3},{2,0},{3,1},{4,6},{5,7},{6,4},{7,5},{8,10},{9,11},{10,... | collective-permute-start | bytes 466952 | tf_op jit(solution)/shard_map/ppermute | solution.py:33
  51.1 6.0 %collective-permute-start.9 = (bf16[608,128]{1,0:T(8,128)(2,1)S(1)}, bf16[608,128]{1,0:T(8,128)(2,1)S(1)}, u32[]{:S(2)}, u32[]{:S(2)}) collective-permute-start(bf16[608,128]{1,0:T(8,128)(2,1)S(1)} %get-tuple-element.60.own_ref), channel_id=1, source_target_pairs={{0,1},{1,0},{2,3},{3,2},{4,5},{5,4},{6,7},{7,6},{8,9},{9,8},{10,11... | collective-permute-start | bytes 466952 | tf_op jit(solution)/shard_map/ppermute | solution.py:33
  55.9 1.4 %collective-permute-start.11 = (bf16[608,128]{1,0:T(8,128)(2,1)S(1)}, bf16[608,128]{1,0:T(8,128)(2,1)S(1)}, u32[]{:S(2)}, u32[]{:S(2)}) collective-permute-start(bf16[608,128]{1,0:T(8,128)(2,1)S(1)} %get-tuple-element.64.across_ref), channel_id=1, source_target_pairs={{0,1},{1,0},{2,3},{3,2},{4,5},{5,4},{6,7},{7,6},{8,9},{9,8},{10,11... | collective-permute-start | bytes 466952 | tf_op jit(solution)/shard_map/ppermute | solution.py:33
  56.0 8.6 %collective-permute-start.14 = (bf16[8,64,512]{2,1,0:T(8,128)(2,1)S(1)}, bf16[8,64,512]{2,1,0:T(8,128)(2,1)S(1)}, u32[]{:S(2)}, u32[]{:S(2)}) collective-permute-start(bf16[8,64,512]{2,1,0:T(8,128)(2,1)S(1)} %get-tuple-element.68), channel_id=1, source_target_pairs={{0,1},{1,0},{2,3},{3,2},{4,5},{5,4},{6,7},{7,6},{8,9},{9,8},{10,11... | collective-permute-start | bytes 1572872 | tf_op jit(solution)/shard_map/ppermute | solution.py:33
  56.4 18.9 %collective-permute-start.15 = (bf16[8,64,512]{2,1,0:T(8,128)(2,1)S(1)}, bf16[8,64,512]{2,1,0:T(8,128)(2,1)S(1)}, u32[]{:S(2)}, u32[]{:S(2)}) collective-permute-start(bf16[8,64,512]{2,1,0:T(8,128)(2,1)S(1)} %get-tuple-element.70), channel_id=1, source_target_pairs={{1,2},{2,1},{3,4},{4,3},{5,6},{6,5},{7,8},{8,7},{9,10},{10,9},{11,... | collective-permute-start | bytes 1572872 | tf_op jit(solution)/shard_map/ppermute | solution.py:33
  57.3 18.0 %collective-permute-start.12 = (bf16[4,512,128]{2,1,0:T(8,128)(2,1)S(1)}, bf16[4,512,128]{2,1,0:T(8,128)(2,1)S(1)}, u32[]{:S(2)}, u32[]{:S(2)}) collective-permute-start(bf16[4,512,128]{2,1,0:T(8,128)(2,1)S(1)} %get-tuple-element.66.wait_ref.c0), channel_id=1, source_target_pairs={{1,4},{3,6},{4,1},{5,8},{6,3},{7,10},{8,5},{9,12},{10,7},{11,14},{... | collective-permute-start | bytes 1572872 | tf_op jit(solution)/shard_map/ppermute | solution.py:33
  58.0 17.3 %collective-permute-start.13 = (f32[1,32,128]{2,1,0:T(8,128)S(1)}, f32[1,32,128]{2,1,0:T(8,128)S(1)}, u32[]{:S(2)}, u32[]{:S(2)}) collective-permute-start(f32[1,32,128]{2,1,0:T(8,128)S(1)} %get-tuple-element.67), channel_id=1, source_target_pairs={{0,8},{1,13},{2,10},{3,15},{4,12},{5,9},{6,14},{7,11},{8,0},{9,5},... | collective-permute-start | bytes 49160 | tf_op jit(solution)/shard_map/ppermute | solution.py:33
  75.3 2.0 %collective-permute-start.17 = (bf16[4,512,128]{2,1,0:T(8,128)(2,1)S(1)}, bf16[4,512,128]{2,1,0:T(8,128)(2,1)S(1)}, u32[]{:S(2)}, u32[]{:S(2)}) collective-permute-start(bf16[4,512,128]{2,1,0:T(8,128)(2,1)S(1)} %get-tuple-element.72.c1), channel_id=1, source_target_pairs={{0,1},{1,0},{2,3},{3,2},{4,5},{5,4},{6,7},{7,6},{8,9},{9,8},{10,11... | collective-permute-start | bytes 1572872 | tf_op jit(solution)/shard_map/ppermute | solution.py:33
  75.4 1.9 %collective-permute-start.16 = (f32[1,32,128]{2,1,0:T(8,128)S(1)}, f32[1,32,128]{2,1,0:T(8,128)S(1)}, u32[]{:S(2)}, u32[]{:S(2)}) collective-permute-start(f32[1,32,128]{2,1,0:T(8,128)S(1)} %get-tuple-element.71.sum_a), channel_id=1, source_target_pairs={{0,1},{1,0},{2,3},{3,2},{4,5},{5,4},{6,7},{7,6},{8,9},{9,8},{10,11... | collective-permute-start | bytes 49160 | tf_op jit(solution)/shard_map/ppermute | solution.py:33
  81.5 1.2 %collective-permute-start.18 = (f32[8,64]{1,0:T(8,128)S(1)}, f32[8,64]{1,0:T(8,128)S(1)}, u32[]{:S(2)}, u32[]{:S(2)}) collective-permute-start(f32[8,64]{1,0:T(8,128)S(1)} %get-tuple-element.74), channel_id=1, source_target_pairs={{0,1},{1,0},{2,3},{3,2},{4,5},{5,4},{6,7},{7,6},{8,9},{9,8},{10,11... | collective-permute-start | bytes 6152 | tf_op jit(solution)/shard_map/ppermute | solution.py:33
  82.7 3.6 %collective-permute-start.19 = (f32[8,64]{1,0:T(8,128)S(1)}, f32[8,64]{1,0:T(8,128)S(1)}, u32[]{:S(2)}, u32[]{:S(2)}) collective-permute-start(f32[8,64]{1,0:T(8,128)S(1)} %add.71), channel_id=1, source_target_pairs={{0,2},{1,3},{2,0},{3,1},{4,6},{5,7},{6,4},{7,5},{8,10},{9,11},{10,... | collective-permute-start | bytes 6152 | tf_op jit(solution)/shard_map/ppermute | solution.py:33
  86.4 3.6 %collective-permute-start.20 = (f32[8,64]{1,0:T(8,128)S(1)}, f32[8,64]{1,0:T(8,128)S(1)}, u32[]{:S(2)}, u32[]{:S(2)}) collective-permute-start(f32[8,64]{1,0:T(8,128)S(1)} %add.72), channel_id=1, source_target_pairs={{0,4},{1,5},{2,6},{3,7},{4,0},{5,1},{6,2},{7,3},{8,12},{9,13},{10,... | collective-permute-start | bytes 6152 | tf_op jit(solution)/shard_map/ppermute | solution.py:33
  90.0 4.5 %collective-permute-start.21 = (f32[8,64]{1,0:T(8,128)S(1)}, f32[8,64]{1,0:T(8,128)S(1)}, u32[]{:S(2)}, u32[]{:S(2)}) collective-permute-start(f32[8,64]{1,0:T(8,128)S(1)} %add.73), channel_id=1, source_target_pairs={{0,8},{1,9},{2,10},{3,11},{4,12},{5,13},{6,14},{7,15},{8,0},{9,1},... | collective-permute-start | bytes 6152 | tf_op jit(solution)/shard_map/ppermute | solution.py:33
  (6 other events, 18.7 us)

commit v10 on v9

--- a/solution.py
+++ b/solution.py
@@ -137,19 +137,19 @@
     lax.fori_loop(0, count // unroll, trip, 0)
 
 
-def list_loop(count, fn):
+def list_loop(count, fn, group=UNROLL):
     def four(i, carry):
-        for u in range(UNROLL):
-            fn(i * UNROLL + u)
+        for u in range(group):
+            fn(i * group + u)
         return carry
 
     def single(i, carry):
         fn(i)
         return carry
 
-    whole_trips = count // UNROLL
+    whole_trips = count // group
     lax.fori_loop(0, whole_trips, four, 0)
-    lax.fori_loop(whole_trips * UNROLL, count, single, 0)
+    lax.fori_loop(whole_trips * group, count, single, 0)
 
 
 def store_share(total, part_ref, cp_ref):
@@ -350,7 +350,7 @@
         tile_ref[entry] = tile
         near_out[leaf_at] += dot(vw[jnp.where(own, place, per + m % half)], tile, 1, 0)
 
-    list_loop(n, one)
+    list_loop(n, one, 8)
 
 
 def own_again_kernel(pos_ref, lists, v_ref, tile_ref, near_out):
@@ -434,7 +434,7 @@
     mv[...] = wide[:, :rank] + wide[:, rank : 2 * rank] + wide[:, 2 * rank :]
 
 
-def foreign_kernel(pos_ref, lists, e_ref, vo_ref, tile_in, near_in, tile_ref, near_out):
+def foreign_kernel(pos_ref, lists, e_ref, vo_ref, tile_in, near_in, wait_ref, tile_ref, near_out):
     half, _, leaf = vo_ref.shape
     features = e_ref.shape[0]
     columns = vo_ref.shape[1] - 2 * features
@@ -450,18 +450,21 @@
     list_loop(n, one)
 
 
+def setup_kernel(trans_ref, coarse_ref, sum_a, sum_b, c0, c1, c2, cw, mv, fc):
+    load_coefficients(cw, (c0, c1, c2))
+    coarse_rows(coarse_ref, (sum_a, sum_b), fc)
+    store_moved(trans_ref[...], fc, mv)
+
+
 def far_first_kernel(
-    pos_ref, far_ref, rs_ref, sc_ref, basis_ref, coup_ref, trans_ref, near_ref, coarse_ref, sum_a, sum_b, c0, c1, c2,
-    u_ref, q_ref, cp_ref, part_ref, msg_ref, mx_ref, mo_ref, cw, fc, mv, coefs, acc_uu, acc_ru,
+    pos_ref, far_ref, rs_ref, sc_ref, basis_ref, coup_ref, trans_ref, near_ref, cw, mv,
+    u_ref, q_ref, cp_ref, part_ref, msg_ref, mx_ref, mo_ref, coefs, acc_uu, acc_ru,
 ):
     per, rank, leaf = basis_ref.shape
     half = per // 2
     size = rank // 2
     pos = pos_ref[0]
     odd = pos % 2
-    load_coefficients(cw, (c0, c1, c2))
-    coarse_rows(coarse_ref, (sum_a, sum_b), fc)
-    store_moved(trans_ref[...], fc, mv)
     acc_uu[...] = jnp.zeros_like(acc_uu)
     acc_ru[...] = jnp.zeros_like(acc_ru)
 
@@ -663,15 +666,19 @@
         (position, lists, embeddings, v, vx, near, quad), aliases={5: 1},
     )
     coefs, sums = last_messages(*after((far_quad, mine), near))
+    cw, mv = call(
+        setup_kernel, "far_setup", [WHOLE] * 7, [window[0], moved_shape], [window[1]],
+        (trans, coarse, *sums, quad, *coefs),
+    )
     tiles, near = call(
-        foreign_kernel, "foreign_tiles", [SCALAR] * 2 + [WHOLE] * 4, [tile_shape, near_shape], [],
-        (position, lists, embeddings, vo, tiles, near), aliases={4: 0, 5: 1},
+        foreign_kernel, "foreign_tiles", [SCALAR] * 2 + [WHOLE] * 4 + [ANYWHERE], [tile_shape, near_shape], [],
+        (position, lists, embeddings, vo, tiles, near, mv), aliases={4: 0, 5: 1},
     )
     image, q, cp, part, msg, mx, mo = call(
-        far_first_kernel, "far_first", [SCALAR] * 2 + [WHOLE] * 12,
+        far_first_kernel, "far_first", [SCALAR] * 2 + [WHOLE] * 8,
         [wide_shape, leaf_shape, cp_shape, part_shape, msg_shape, half_shape, half_shape],
-        [*window, moved_shape, coefs_shape, acc_shape, acc_shape],
-        (position, far_rows, right_side, scale_row, leaf_basis, coup, trans, near, coarse, *sums, quad, *coefs),
+        [coefs_shape, acc_shape, acc_shape],
+        (position, far_rows, right_side, scale_row, leaf_basis, coup, trans, near, cw, mv),
     )
     got = first_messages(cp)
     (near,) = call(

time: 97.5 us -> 106 us (1.087)
  starting transfers between devices: 25.9 us -> 34.5 us
    ppermute x22, starting transfers between devices: 25.9 us -> 34.5 us  [involution(): return lax.ppermute(value, 'leaf', pairs)]
    pallas_call x16 -> x17, Pallas kernels: 46 us -> 45.3 us  [call(): pl.pallas_call(kernel, in_specs=in_specs, out_specs=out_specs or [WHOLE]...]
  transfers between devices with their start and end apart: 22 -> 22, of which waited for: 9 -> 10; matrix products, arithmetic and copies ran while one was open for 0% -> 0% of each run, Pallas kernels for 33% -> 29%
where the time goes in v10:
time: 106 us
  Pallas kernels  45.3 us (43%)
  starting transfers between devices  34.5 us (33%)
  waiting for transfers between devices  21.3 us (20%)
  other arithmetic  2.68 us (3%)
  local copies, waits for them, and re-layouts  1.07 us (1%)
    pallas_call x17, Pallas kernels, call(): pl.pallas_call(kernel, in_specs=in_specs, out_specs=out_specs or [WHOLE]...  45.3 us
    ppermute x22, starting transfers between devices, involution(): return lax.ppermute(value, 'leaf', pairs)  34.5 us
    ppermute x22, waiting for transfers between devices, involution(): return lax.ppermute(value, 'leaf', pairs)  21.3 us
    add x1, other arithmetic, body(): residual = right_side - first_weight * image + second_weight * second  2.63 us
  transfers between devices with their start and end apart: 22, of which 10 were waited for; matrix products, arithmetic and copies ran while one was open for 0% of the time, Pallas kernels for 29%

profile of v10, /device:TPU:0, one launch (start us, length us, event | category | flops | bytes accessed | tf_op | source)
XLA Modules:
  0.0 105.8 jit_solution(9966492885948896348)
XLA Ops:
  0.7 3.1 %prep.1 = (bf16[16,64,512]{2,1,0:T(8,128)(2,1)S(1)}, bf16[608,128]{1,0:T(8,128)(2,1)S(1)}, f32[32,128]{1,0:T(8,128)S(1)}, bf16[16,64,64]{2,1,0:T(8,128)(2,1)S(1)...) custom-call(s32[1]{0:T(128)} %bitcast.pos_ref, f32[64,8192]{1,0:T(8,128)} %rs_ref.3, ...), custom_call_target="tpu_custom_call" | custom-call | tf_op jit(solution)/shard_map/prep/pallas_call | solution.py:531
  3.8 3.0 %collective-permute-start = (bf16[608,128]{1,0:T(8,128)(2,1)S(1)}, bf16[608,128]{1,0:T(8,128)(2,1)S(1)}, u32[]{:S(2)}, u32[]{:S(2)}) collective-permute-start(bf16[608,128]{1,0:T(8,128)(2,1)S(1)} %get-tuple-element.41.wait_ref.own_ref), channel_id=1, source_target_pairs={{0,2},{1,3},{2,0},{3,1},{4,6},{5,7},{6,4},{7,5},{8,10},{9,11},{10,... | collective-permute-start | bytes 466952 | tf_op jit(solution)/shard_map/ppermute | solution.py:33
  6.8 4.0 %relayout.1 = (bf16[16,128,256]{2,1,0:T(8,128)(2,1)S(1)}, bf16[1,64,64]{2,1,0:T(8,128)(2,1)S(1)}, s32[4,40]{1,0:T(4,128)S(1)}) custom-call(s32[1]{0:T(128)} %bitcast.pos_ref, s32[3,16]{1,0:T(4,128)S(1)} %bitcast.69, bf16[16,8,4096]{2,1,0:T(8,128)(2,1)S(1)} %copy-done.3, bf16[2,2,4096]{2,1,0:T(2,128)(2,1)S(1)} %copy-done.5, ...), custom_call_target="tpu_custom_call" | custom-call | tf_op jit(solution)/shard_map/relayout/pallas_call | solution.py:531
  11.4 6.2 %self_tiles.1 = (bf16[128,512,512]{2,1,0:T(8,128)(2,1)}, f32[17,64,512]{2,1,0:T(8,128)S(1)}) custom-call(f32[32,8192]{1,0:T(8,128)S(1)} %copy-done.1, bf16[16,64,512]{2,1,0:T(8,128)(2,1)S(1)} %get-tuple-element.48.v_ref, bf16[8,128,512]{2,1,0:T(8,128)(2,1)S(1)} %get-tuple-element.47.wait_ref), custom_call_target="tpu_custom_call" | custom-call | tf_op jit(solution)/shard_map/self_tiles/pallas_call | solution.py:531
  19.1 7.8 %collective-permute-start.6 = (f32[1,32,128]{2,1,0:T(8,128)S(1)}, f32[1,32,128]{2,1,0:T(8,128)S(1)}, u32[]{:S(2)}, u32[]{:S(2)}) collective-permute-start(f32[1,32,128]{2,1,0:T(8,128)S(1)} %get-tuple-element.57), channel_id=1, source_target_pairs={{0,8},{1,13},{2,10},{3,15},{4,12},{5,9},{6,14},{7,11},{8,0},{9,5},... | collective-permute-start | bytes 49160 | tf_op jit(solution)/shard_map/ppermute | solution.py:33
  27.0 12.0 %own_tiles.1 = (bf16[33,512,512]{2,1,0:T(8,128)(2,1)S(1)}, f32[17,64,512]{2,1,0:T(8,128)S(1)}) custom-call(s32[1]{0:T(128)} %bitcast.pos_ref, s32[4,40]{1,0:T(4,128)S(1)} %get-tuple-element.44.lists, f32[32,8192]{1,0:T(8,128)S(1)} %copy-done.1, bf16[16,64,512]{2,1,0:T(8,128)(2,1)S(1)} %get-tuple-element.48.v_ref, ...), custom_call_target="tpu_custom_call", output_to_operand_aliasing={{1}: (5, {})} | custom-call | tf_op jit(solution)/shard_map/own_tiles/pallas_call | solution.py:531
  39.0 2.9 %collective-permute-done.6.refs_1_ = f32[1,32,128]{2,1,0:T(8,128)S(1)} collective-permute-done((f32[1,32,128]{2,1,0:T(8,128)S(1)}, f32[1,32,128]{2,1,0:T(8,128)S(1)}, u32[]{:S(2)}, u32[]{:S(2)}) %collective-permute-start.6) | collective-permute-done | bytes 16416 | tf_op jit(solution)/shard_map/ppermute | solution.py:33
  42.3 1.4 %collective-permute-done.7.sum_b = f32[1,32,128]{2,1,0:T(8,128)S(1)} collective-permute-done((f32[1,32,128]{2,1,0:T(8,128)S(1)}, f32[1,32,128]{2,1,0:T(8,128)S(1)}, u32[]{:S(2)}, u32[]{:S(2)}) %collective-permute-start.7) | collective-permute-done | bytes 16416 | tf_op jit(solution)/shard_map/ppermute | solution.py:33
  45.3 0.8 copy-done
  46.3 6.2 %far_first.1 = (f32[64,8192]{1,0:T(8,128)S(1)}, bf16[16,64,512]{2,1,0:T(8,128)(2,1)S(1)}, bf16[608,128]{1,0:T(8,128)(2,1)S(1)}, f32[32,128]{1,0:T(8,128)S(1)}, f...) custom-call(s32[1]{0:T(128)} %bitcast.pos_ref, s32[8,16]{1,0:T(8,128)S(1)} %bitcast.67, ...), custom_call_target="tpu_custom_call" | custom-call | tf_op jit(solution)/shard_map/far_first/pallas_call | solution.py:531
  52.5 7.8 %collective-permute-start.10 = (bf16[608,128]{1,0:T(8,128)(2,1)S(1)}, bf16[608,128]{1,0:T(8,128)(2,1)S(1)}, u32[]{:S(2)}, u32[]{:S(2)}) collective-permute-start(bf16[608,128]{1,0:T(8,128)(2,1)S(1)} %get-tuple-element.64.own_ref), channel_id=1, source_target_pairs={{0,2},{1,3},{2,0},{3,1},{4,6},{5,7},{6,4},{7,5},{8,10},{9,11},{10,... | collective-permute-start | bytes 466952 | tf_op jit(solution)/shard_map/ppermute | solution.py:33
  60.3 3.1 %own_again.1.refs_2_.near_in = f32[17,64,512]{2,1,0:T(8,128)S(1)} custom-call(s32[1]{0:T(128)} %bitcast.pos_ref, s32[4,40]{1,0:T(4,128)S(1)} %get-tuple-element.44.lists, bf16[16,64,512]{2,1,0:T(8,128)(2,1)S(1)} %get-tuple-element.66.v_ref, bf16[33,512,512]{2,1,0:T(8,128)(2,1)S(1)} %get-tuple-element.67.tile_ref), custom_call_target="tpu_custom_call" | custom-call | tf_op jit(solution)/shard_map/own_again/pallas_call | solution.py:531
  65.7 7.2 %collective-permute-start.13 = (f32[1,32,128]{2,1,0:T(8,128)S(1)}, f32[1,32,128]{2,1,0:T(8,128)S(1)}, u32[]{:S(2)}, u32[]{:S(2)}) collective-permute-start(f32[1,32,128]{2,1,0:T(8,128)S(1)} %get-tuple-element.71), channel_id=1, source_target_pairs={{0,8},{1,13},{2,10},{3,15},{4,12},{5,9},{6,14},{7,11},{8,0},{9,5},... | collective-permute-start | bytes 49160 | tf_op jit(solution)/shard_map/ppermute | solution.py:33
  72.8 4.5 %self_again.1.refs_2_.near_in = f32[17,64,512]{2,1,0:T(8,128)S(1)} custom-call(s32[1]{0:T(128)} %bitcast.pos_ref, s32[4,40]{1,0:T(4,128)S(1)} %get-tuple-element.44.lists, bf16[16,64,512]{2,1,0:T(8,128)(2,1)S(1)} %get-tuple-element.66.v_ref, bf16[8,64,512]{2,1,0:T(8,128)(2,1)S(1)} %collective-permute-done.14.vx_ref, ...), custom_call_target="tpu_custom_call", output_to_operand_aliasing={{}: (6, {})} | custom-call | tf_op jit(solution)/shard_map/self_again/pallas_call | solution.py:531
  77.4 6.0 %collective-permute-done.13.refs_1_ = f32[1,32,128]{2,1,0:T(8,128)S(1)} collective-permute-done((f32[1,32,128]{2,1,0:T(8,128)S(1)}, f32[1,32,128]{2,1,0:T(8,128)S(1)}, u32[]{:S(2)}, u32[]{:S(2)}) %collective-permute-start.13) | collective-permute-done | bytes 16416 | tf_op jit(solution)/shard_map/ppermute | solution.py:33
  84.6 0.8 collective-permute-done.16.sum_b
  85.4 4.2 %far_again.1 = (f32[64,8192]{1,0:T(8,128)S(1)}, f32[8,64]{1,0:T(8,128)S(1)}) custom-call(s32[1]{0:T(128)} %bitcast.pos_ref, s32[8,16]{1,0:T(8,128)S(1)} %bitcast.68, f32[64,8192]{1,0:T(8,128)S(1)} %copy-done, f32[1,8192]{1,0:T(1,128)S(1)} %bitcast.66, f32[64,8192]{1,0:T(8,128)S(1)} %get-tuple-element.63.u_ref, bf16[16,64,512]{2,1,0:T(8,128)(2,1)S(1)} %copy-done.2, ...), custom_call_target="tpu_custom_call" | custom-call | tf_op jit(solution)/shard_map/far_again/pallas_call | solution.py:531
  89.8 1.0 collective-permute-done.18
  90.8 3.6 %collective-permute-done.19 = f32[8,64]{1,0:T(8,128)S(1)} collective-permute-done((f32[8,64]{1,0:T(8,128)S(1)}, f32[8,64]{1,0:T(8,128)S(1)}, u32[]{:S(2)}, u32[]{:S(2)}) %collective-permute-start.19) | collective-permute-done | bytes 2080 | tf_op jit(solution)/shard_map/ppermute | solution.py:33
  94.4 2.6 %collective-permute-start.20 = (f32[8,64]{1,0:T(8,128)S(1)}, f32[8,64]{1,0:T(8,128)S(1)}, u32[]{:S(2)}, u32[]{:S(2)}) collective-permute-start(f32[8,64]{1,0:T(8,128)S(1)} %add.72), channel_id=1, source_target_pairs={{0,4},{1,5},{2,6},{3,7},{4,0},{5,1},{6,2},{7,3},{8,12},{9,13},{10,... | collective-permute-start | bytes 6152 | tf_op jit(solution)/shard_map/ppermute | solution.py:33
  97.0 1.6 %collective-permute-done.20 = f32[8,64]{1,0:T(8,128)S(1)} collective-permute-done((f32[8,64]{1,0:T(8,128)S(1)}, f32[8,64]{1,0:T(8,128)S(1)}, u32[]{:S(2)}, u32[]{:S(2)}) %collective-permute-start.20) | collective-permute-done | bytes 2080 | tf_op jit(solution)/shard_map/ppermute | solution.py:33
  98.6 0.9 collective-permute-start.21
  99.5 3.6 %collective-permute-done.21 = f32[8,64]{1,0:T(8,128)S(1)} collective-permute-done((f32[8,64]{1,0:T(8,128)S(1)}, f32[8,64]{1,0:T(8,128)S(1)}, u32[]{:S(2)}, u32[]{:S(2)}) %collective-permute-start.21) | collective-permute-done | bytes 2080 | tf_op jit(solution)/shard_map/ppermute | solution.py:33
  103.1 2.6 %multiply_add_fusion = (f32[64,8192]{1,0:T(8,128)}, f32[64,8192]{1,0:T(8,128)}) fusion(f32[64,8192]{1,0:T(8,128)S(1)} %get-tuple-element.79, f32[64,8192]{1,0:T(8,128)S(1)} %copy-done, f32[64,8192]{1,0:T(8,128)S(1)} %get-tuple-element.63.u_ref, f32[64]{0:T(128)S(1)} %mul.193, f32[64]{0:T(128)S(1)} %get-tuple-element.80, f32[8192]{0:T(1024)S(1)} %copy-done.4), kind=kLoop, calls=%fused_computation | loop fusion | flops 4194304 | bytes 10519040 | tf_op jit(solution)/shard_map/add | solution.py:724
  (61 shorter events, 8.0 us)
Async XLA Ops:
  0.6 6.1 %copy-start.3 = (bf16[16,8,4096]{2,1,0:T(8,128)(2,1)S(1)}, bf16[16,8,4096]{2,1,0:T(8,128)(2,1)}, u32[]{:S(2)}) copy-start(bf16[16,8,4096]{2,1,0:T(8,128)(2,1)} %coup_ref.1) | copy-start | bytes 3145732
  0.6 6.1 %copy-start.5 = (bf16[2,2,4096]{2,1,0:T(2,128)(2,1)S(1)}, bf16[2,2,4096]{2,1,0:T(2,128)(2,1)}, u32[]{:S(2)}) copy-start(bf16[2,2,4096]{2,1,0:T(2,128)(2,1)} %coarse_ref.1) | copy-start | bytes 98308
  3.8 7.0 %collective-permute-start = (bf16[608,128]{1,0:T(8,128)(2,1)S(1)}, bf16[608,128]{1,0:T(8,128)(2,1)S(1)}, u32[]{:S(2)}, u32[]{:S(2)}) collective-permute-start(bf16[608,128]{1,0:T(8,128)(2,1)S(1)} %get-tuple-element.41.wait_ref.own_ref), channel_id=1, source_target_pairs={{0,2},{1,3},{2,0},{3,1},{4,6},{5,7},{6,4},{7,5},{8,10},{9,11},{10,... | collective-permute-start | bytes 466952 | tf_op jit(solution)/shard_map/ppermute | solution.py:33
  10.8 16.2 %collective-permute-start.2 = (bf16[8,128,512]{2,1,0:T(8,128)(2,1)S(1)}, bf16[8,128,512]{2,1,0:T(8,128)(2,1)S(1)}, u32[]{:S(2)}, u32[]{:S(2)}) collective-permute-start(bf16[8,128,512]{2,1,0:T(8,128)(2,1)S(1)} %get-tuple-element.49), channel_id=1, source_target_pairs={{0,1},{1,0},{2,3},{3,2},{4,5},{5,4},{6,7},{7,6},{8,9},{9,8},{10,11... | collective-permute-start | bytes 3145736 | tf_op jit(solution)/shard_map/ppermute | solution.py:33
  10.9 6.7 %collective-permute-start.3 = (bf16[608,128]{1,0:T(8,128)(2,1)S(1)}, bf16[608,128]{1,0:T(8,128)(2,1)S(1)}, u32[]{:S(2)}, u32[]{:S(2)}) collective-permute-start(bf16[608,128]{1,0:T(8,128)(2,1)S(1)} %get-tuple-element.41.wait_ref.own_ref), channel_id=1, source_target_pairs={{0,1},{1,0},{2,3},{3,2},{4,5},{5,4},{6,7},{7,6},{8,9},{9,8},{10,11... | collective-permute-start | bytes 466952 | tf_op jit(solution)/shard_map/ppermute | solution.py:33
  11.4 6.3 %collective-permute-start.4 = (bf16[608,128]{1,0:T(8,128)(2,1)S(1)}, bf16[608,128]{1,0:T(8,128)(2,1)S(1)}, u32[]{:S(2)}, u32[]{:S(2)}) collective-permute-start(bf16[608,128]{1,0:T(8,128)(2,1)S(1)} %get-tuple-element.51.across_ref), channel_id=1, source_target_pairs={{0,1},{1,0},{2,3},{3,2},{4,5},{5,4},{6,7},{7,6},{8,9},{9,8},{10,11... | collective-permute-start | bytes 466952 | tf_op jit(solution)/shard_map/ppermute | solution.py:33
  17.7 24.1 %collective-permute-start.5 = (bf16[4,512,128]{2,1,0:T(8,128)(2,1)S(1)}, bf16[4,512,128]{2,1,0:T(8,128)(2,1)S(1)}, u32[]{:S(2)}, u32[]{:S(2)}) collective-permute-start(bf16[4,512,128]{2,1,0:T(8,128)(2,1)S(1)} %get-tuple-element.53.wait_ref.c0), channel_id=1, source_target_pairs={{1,4},{3,6},{4,1},{5,8},{6,3},{7,10},{8,5},{9,12},{10,7},{11,14},{... | collective-permute-start | bytes 1572872 | tf_op jit(solution)/shard_map/ppermute | solution.py:33
  18.4 26.0 %collective-permute-start.1 = (bf16[8,128,512]{2,1,0:T(8,128)(2,1)S(1)}, bf16[8,128,512]{2,1,0:T(8,128)(2,1)S(1)}, u32[]{:S(2)}, u32[]{:S(2)}) collective-permute-start(bf16[8,128,512]{2,1,0:T(8,128)(2,1)S(1)} %get-tuple-element.47.wait_ref), channel_id=1, source_target_pairs={{1,2},{2,1},{3,4},{4,3},{5,6},{6,5},{7,8},{8,7},{9,10},{10,9},{11,... | collective-permute-start | bytes 3145736 | tf_op jit(solution)/shard_map/ppermute | solution.py:33
  19.1 22.7 %collective-permute-start.6 = (f32[1,32,128]{2,1,0:T(8,128)S(1)}, f32[1,32,128]{2,1,0:T(8,128)S(1)}, u32[]{:S(2)}, u32[]{:S(2)}) collective-permute-start(f32[1,32,128]{2,1,0:T(8,128)S(1)} %get-tuple-element.57), channel_id=1, source_target_pairs={{0,8},{1,13},{2,10},{3,15},{4,12},{5,9},{6,14},{7,11},{8,0},{9,5},... | collective-permute-start | bytes 49160 | tf_op jit(solution)/shard_map/ppermute | solution.py:33
  41.8 1.9 %collective-permute-start.8 = (bf16[4,512,128]{2,1,0:T(8,128)(2,1)S(1)}, bf16[4,512,128]{2,1,0:T(8,128)(2,1)S(1)}, u32[]{:S(2)}, u32[]{:S(2)}) collective-permute-start(bf16[4,512,128]{2,1,0:T(8,128)(2,1)S(1)} %get-tuple-element.59.c1), channel_id=1, source_target_pairs={{0,1},{1,0},{2,3},{3,2},{4,5},{5,4},{6,7},{7,6},{8,9},{9,8},{10,11... | collective-permute-start | bytes 1572872 | tf_op jit(solution)/shard_map/ppermute | solution.py:33
  41.8 1.9 %collective-permute-start.7 = (f32[1,32,128]{2,1,0:T(8,128)S(1)}, f32[1,32,128]{2,1,0:T(8,128)S(1)}, u32[]{:S(2)}, u32[]{:S(2)}) collective-permute-start(f32[1,32,128]{2,1,0:T(8,128)S(1)} %get-tuple-element.58.sum_a), channel_id=1, source_target_pairs={{0,1},{1,0},{2,3},{3,2},{4,5},{5,4},{6,7},{7,6},{8,9},{9,8},{10,11... | collective-permute-start | bytes 49160 | tf_op jit(solution)/shard_map/ppermute | solution.py:33
  52.5 11.0 %collective-permute-start.10 = (bf16[608,128]{1,0:T(8,128)(2,1)S(1)}, bf16[608,128]{1,0:T(8,128)(2,1)S(1)}, u32[]{:S(2)}, u32[]{:S(2)}) collective-permute-start(bf16[608,128]{1,0:T(8,128)(2,1)S(1)} %get-tuple-element.64.own_ref), channel_id=1, source_target_pairs={{0,2},{1,3},{2,0},{3,1},{4,6},{5,7},{6,4},{7,5},{8,10},{9,11},{10,... | collective-permute-start | bytes 466952 | tf_op jit(solution)/shard_map/ppermute | solution.py:33
  60.3 4.4 %collective-permute-start.9 = (bf16[608,128]{1,0:T(8,128)(2,1)S(1)}, bf16[608,128]{1,0:T(8,128)(2,1)S(1)}, u32[]{:S(2)}, u32[]{:S(2)}) collective-permute-start(bf16[608,128]{1,0:T(8,128)(2,1)S(1)} %get-tuple-element.64.own_ref), channel_id=1, source_target_pairs={{0,1},{1,0},{2,3},{3,2},{4,5},{5,4},{6,7},{7,6},{8,9},{9,8},{10,11... | collective-permute-start | bytes 466952 | tf_op jit(solution)/shard_map/ppermute | solution.py:33
  63.5 1.4 %collective-permute-start.11 = (bf16[608,128]{1,0:T(8,128)(2,1)S(1)}, bf16[608,128]{1,0:T(8,128)(2,1)S(1)}, u32[]{:S(2)}, u32[]{:S(2)}) collective-permute-start(bf16[608,128]{1,0:T(8,128)(2,1)S(1)} %get-tuple-element.68.across_ref), channel_id=1, source_target_pairs={{0,1},{1,0},{2,3},{3,2},{4,5},{5,4},{6,7},{7,6},{8,9},{9,8},{10,11... | collective-permute-start | bytes 466952 | tf_op jit(solution)/shard_map/ppermute | solution.py:33
  63.7 9.1 %collective-permute-start.14 = (bf16[8,64,512]{2,1,0:T(8,128)(2,1)S(1)}, bf16[8,64,512]{2,1,0:T(8,128)(2,1)S(1)}, u32[]{:S(2)}, u32[]{:S(2)}) collective-permute-start(bf16[8,64,512]{2,1,0:T(8,128)(2,1)S(1)} %get-tuple-element.72), channel_id=1, source_target_pairs={{0,1},{1,0},{2,3},{3,2},{4,5},{5,4},{6,7},{7,6},{8,9},{9,8},{10,11... | collective-permute-start | bytes 1572872 | tf_op jit(solution)/shard_map/ppermute | solution.py:33
  64.0 19.4 %collective-permute-start.15 = (bf16[8,64,512]{2,1,0:T(8,128)(2,1)S(1)}, bf16[8,64,512]{2,1,0:T(8,128)(2,1)S(1)}, u32[]{:S(2)}, u32[]{:S(2)}) collective-permute-start(bf16[8,64,512]{2,1,0:T(8,128)(2,1)S(1)} %get-tuple-element.74), channel_id=1, source_target_pairs={{1,2},{2,1},{3,4},{4,3},{5,6},{6,5},{7,8},{8,7},{9,10},{10,9},{11,... | collective-permute-start | bytes 1572872 | tf_op jit(solution)/shard_map/ppermute | solution.py:33
  65.0 18.5 %collective-permute-start.12 = (bf16[4,512,128]{2,1,0:T(8,128)(2,1)S(1)}, bf16[4,512,128]{2,1,0:T(8,128)(2,1)S(1)}, u32[]{:S(2)}, u32[]{:S(2)}) collective-permute-start(bf16[4,512,128]{2,1,0:T(8,128)(2,1)S(1)} %get-tuple-element.70.wait_ref.c0), channel_id=1, source_target_pairs={{1,4},{3,6},{4,1},{5,8},{6,3},{7,10},{8,5},{9,12},{10,7},{11,14},{... | collective-permute-start | bytes 1572872 | tf_op jit(solution)/shard_map/ppermute | solution.py:33
  65.7 17.8 %collective-permute-start.13 = (f32[1,32,128]{2,1,0:T(8,128)S(1)}, f32[1,32,128]{2,1,0:T(8,128)S(1)}, u32[]{:S(2)}, u32[]{:S(2)}) collective-permute-start(f32[1,32,128]{2,1,0:T(8,128)S(1)} %get-tuple-element.71), channel_id=1, source_target_pairs={{0,8},{1,13},{2,10},{3,15},{4,12},{5,9},{6,14},{7,11},{8,0},{9,5},... | collective-permute-start | bytes 49160 | tf_op jit(solution)/shard_map/ppermute | solution.py:33
  83.4 2.0 %collective-permute-start.17 = (bf16[4,512,128]{2,1,0:T(8,128)(2,1)S(1)}, bf16[4,512,128]{2,1,0:T(8,128)(2,1)S(1)}, u32[]{:S(2)}, u32[]{:S(2)}) collective-permute-start(bf16[4,512,128]{2,1,0:T(8,128)(2,1)S(1)} %get-tuple-element.76.c1), channel_id=1, source_target_pairs={{0,1},{1,0},{2,3},{3,2},{4,5},{5,4},{6,7},{7,6},{8,9},{9,8},{10,11... | collective-permute-start | bytes 1572872 | tf_op jit(solution)/shard_map/ppermute | solution.py:33
  83.5 1.9 %collective-permute-start.16 = (f32[1,32,128]{2,1,0:T(8,128)S(1)}, f32[1,32,128]{2,1,0:T(8,128)S(1)}, u32[]{:S(2)}, u32[]{:S(2)}) collective-permute-start(f32[1,32,128]{2,1,0:T(8,128)S(1)} %get-tuple-element.75.sum_a), channel_id=1, source_target_pairs={{0,1},{1,0},{2,3},{3,2},{4,5},{5,4},{6,7},{7,6},{8,9},{9,8},{10,11... | collective-permute-start | bytes 49160 | tf_op jit(solution)/shard_map/ppermute | solution.py:33
  89.6 1.2 %collective-permute-start.18 = (f32[8,64]{1,0:T(8,128)S(1)}, f32[8,64]{1,0:T(8,128)S(1)}, u32[]{:S(2)}, u32[]{:S(2)}) collective-permute-start(f32[8,64]{1,0:T(8,128)S(1)} %get-tuple-element.78), channel_id=1, source_target_pairs={{0,1},{1,0},{2,3},{3,2},{4,5},{5,4},{6,7},{7,6},{8,9},{9,8},{10,11... | collective-permute-start | bytes 6152 | tf_op jit(solution)/shard_map/ppermute | solution.py:33
  90.8 3.6 %collective-permute-start.19 = (f32[8,64]{1,0:T(8,128)S(1)}, f32[8,64]{1,0:T(8,128)S(1)}, u32[]{:S(2)}, u32[]{:S(2)}) collective-permute-start(f32[8,64]{1,0:T(8,128)S(1)} %add.71), channel_id=1, source_target_pairs={{0,2},{1,3},{2,0},{3,1},{4,6},{5,7},{6,4},{7,5},{8,10},{9,11},{10,... | collective-permute-start | bytes 6152 | tf_op jit(solution)/shard_map/ppermute | solution.py:33
  94.4 4.2 %collective-permute-start.20 = (f32[8,64]{1,0:T(8,128)S(1)}, f32[8,64]{1,0:T(8,128)S(1)}, u32[]{:S(2)}, u32[]{:S(2)}) collective-permute-start(f32[8,64]{1,0:T(8,128)S(1)} %add.72), channel_id=1, source_target_pairs={{0,4},{1,5},{2,6},{3,7},{4,0},{5,1},{6,2},{7,3},{8,12},{9,13},{10,... | collective-permute-start | bytes 6152 | tf_op jit(solution)/shard_map/ppermute | solution.py:33
  98.6 4.5 %collective-permute-start.21 = (f32[8,64]{1,0:T(8,128)S(1)}, f32[8,64]{1,0:T(8,128)S(1)}, u32[]{:S(2)}, u32[]{:S(2)}) collective-permute-start(f32[8,64]{1,0:T(8,128)S(1)} %add.73), channel_id=1, source_target_pairs={{0,8},{1,9},{2,10},{3,11},{4,12},{5,13},{6,14},{7,15},{8,0},{9,1},... | collective-permute-start | bytes 6152 | tf_op jit(solution)/shard_map/ppermute | solution.py:33
  (6 other events, 17.9 us)
